TPU v7x, 32 devices: a whole 2x2x4 slice. The times are simulated.
32 devices in a mesh: dp: 4 (over y, x), tensor: 8 (over z, core).
Axes of the slice: x: 2, y: 2, z: 4, core: 2. Of those that a mesh axis runs over, the one named last changes fastest.
Arguments:
- tokens: bfloat16 [1024, 2048], P('dp'), may hold values from -6 to 6
- gate_weight: bfloat16 [8, 2048, 2816], P(None, 'dp', 'tensor'), may hold values from -0.25 to 0.25
- up_weight: bfloat16 [8, 2048, 2816], P(None, 'dp', 'tensor'), may hold values from -0.25 to 0.25
- down_weight: bfloat16 [8, 2816, 2048], P(None, 'tensor', 'dp'), may hold values from -0.3125 to 0.3125
- router_weight: float32 [2048, 8], replicated, may hold values from -6 to 6
- carry_mean: float32 [2048], replicated, may hold values from -0.375 to 0.375
Outputs:
- mixed: bfloat16 [1024, 2048], P(('dp', 'tensor'))
All inputs are finite; a program needn't handle non-finite values.
Results may differ from a plain program's by a relative error of at most 0.028.
Values may be sent and summed in bfloat16 or wider, within the bound.
No kernel may reach another device: no remote copies, remote signals or barrier semaphores. Data moves between devices by JAX's collectives and lax.ppermute only.
A program may use at most 64 MiB of HBM per device.

v0:
```python
import jax
import jax.numpy as jnp
from jax import lax
from jax.sharding import PartitionSpec as P

SEG = 256


soft_cap = 8.0


def on_device(tokens, gate_weight, up_weight, down_weight, router_weight, carry_mean):
    dp_count = lax.axis_size("dp")
    tensor_count = lax.axis_size("tensor")
    my_dp = lax.axis_index("dp")
    own_rows, model_width = tokens.shape
    own_segs = own_rows // SEG
    all_segs = own_segs * dp_count
    experts, slice_rows, hidden_cols = gate_weight.shape
    gathered = lax.all_to_all(tokens, "dp", split_axis=1, concat_axis=0, tiled=True)
    slice_means = (
        jnp.sum(gathered.reshape(all_segs, SEG, slice_rows), axis=1, dtype=jnp.float32) / SEG
    )
    router_rows = lax.dynamic_slice_in_dim(router_weight, my_dp * slice_rows, slice_rows, 0)
    carry_rows = lax.dynamic_slice_in_dim(carry_mean, my_dp * slice_rows, slice_rows, 0)
    part_segs = jnp.dot(
        slice_means,
        router_rows,
        precision=lax.Precision.HIGHEST,
        preferred_element_type=jnp.float32,
    )
    part_carry = jnp.dot(
        carry_rows[None, :],
        router_rows,
        precision=lax.Precision.HIGHEST,
        preferred_element_type=jnp.float32,
    )
    seg_logits, carry_logits = lax.psum((part_segs, part_carry), "dp")
    raw_logits = jnp.concatenate([carry_logits, seg_logits[:-1]], axis=0)
    logits = soft_cap * jnp.tanh(raw_logits / soft_cap)
    scores = jnp.exp(logits)
    probs_bf = (scores / jnp.sum(scores, axis=1, keepdims=True)).astype(jnp.bfloat16)
    gate_flat = gate_weight.reshape(experts, slice_rows * hidden_cols)
    up_flat = up_weight.reshape(experts, slice_rows * hidden_cols)
    count = own_rows * lax.axis_size("dp")
    seg_total = count // SEG
    merged_gate = jnp.dot(probs_bf, gate_flat, preferred_element_type=jnp.float32).astype(
        jnp.bfloat16
    )
    merged_up = jnp.dot(probs_bf, up_flat, preferred_element_type=jnp.float32).astype(jnp.bfloat16)
    merged_gate = merged_gate.reshape(seg_total, slice_rows, hidden_cols)
    merged_up = merged_up.reshape(seg_total, slice_rows, hidden_cols)
    rows_in = gathered.reshape(seg_total, SEG, slice_rows)
    gate_part = jnp.einsum("str,src->stc", rows_in, merged_gate, preferred_element_type=jnp.float32)
    up_part = jnp.einsum("str,src->stc", rows_in, merged_up, preferred_element_type=jnp.float32)
    preact = lax.psum_scatter(
        jnp.concatenate([gate_part, up_part], axis=2)
        .reshape(count, 2 * hidden_cols)
        .astype(jnp.bfloat16),
        "dp",
        scatter_dimension=0,
        tiled=True,
    ).astype(jnp.float32)
    hidden = (jax.nn.silu(preact[:, :hidden_cols]) * preact[:, hidden_cols:]).astype(jnp.bfloat16)
    down_cols = down_weight.shape[2]
    all_hidden = lax.all_gather(hidden, "dp", axis=0, tiled=True)
    merged_down = jnp.dot(
        probs_bf,
        down_weight.reshape(experts, hidden_cols * down_cols),
        preferred_element_type=jnp.float32,
    )
    merged_down = merged_down.astype(jnp.bfloat16).reshape(all_segs, hidden_cols, down_cols)
    partial_value = jnp.einsum(
        "stf,sfc->stc",
        all_hidden.reshape(all_segs, SEG, hidden_cols),
        merged_down,
        preferred_element_type=jnp.float32,
    )
    block_rows = own_rows // tensor_count
    partial_value = partial_value.reshape(dp_count, tensor_count, block_rows, down_cols)
    summed = lax.psum_scatter(
        partial_value.astype(jnp.bfloat16), "tensor", scatter_dimension=1, tiled=True
    )
    moved = lax.all_to_all(summed, "dp", split_axis=0, concat_axis=3, tiled=True)
    return moved.reshape(block_rows, dp_count * down_cols)


def solution(mesh):
    placed = (
        P("dp", None),
        P(None, "dp", "tensor"),
        P(None, "dp", "tensor"),
        P(None, "tensor", "dp"),
        P(),
        P(),
    )
    return jax.shard_map(
        on_device, mesh=mesh, in_specs=placed, out_specs=P(("dp", "tensor"), None), check_vma=False
    )
```

profile of v0, /device:TPU:0, one launch (start us, length us, event | category | flops | bytes accessed | tf_op | source)
XLA Modules:
  0.0 209.3 jit_solution(12313443155066367053)
XLA Ops:
  6.5 0.0 copy-start
  6.5 1.5 copy.27
  8.1 1.3 copy.28
  9.4 5.2 %all-to-all-start = ((bf16[256,4,512]{2,0,1:T(8,128)(2,1)}), bf16[256,4,512]{2,0,1:T(8,128)(2,1)}, u32[]{:S(2)}, u32[]{:S(2)}) async-start(bf16[256,4,512]{2,0,1:T(8,128)(2,1)} %copy.28), calls=%async_computation | async-start | bytes 2097152 | tf_op jit(solution)/shard_map/all_to_all | solution.py:20
  14.5 0.0 reduce-scatter.5.cloned.1.call-start
  14.5 3.4 %copy.29 = bf16[8,512,352]{2,1,0:T(8,128)(2,1)S(1)} copy(bf16[8,512,352]{1,2,0:T(8,128)(2,1)} %param.7) | data formatting | bytes 5767168 | tf_op args[1]
  17.9 6.9 %reshape.56 = bf16[1441792]{0:T(1024)(128)(2,1)} reshape(bf16[8,512,352]{2,1,0:T(8,128)(2,1)S(1)} %copy.29) | data formatting | bytes 5767168
  24.8 4.6 %reshape.39 = bf16[8,180224]{1,0:T(8,128)(2,1)} reshape(bf16[1441792]{0:T(1024)(128)(2,1)} %reshape.56) | data formatting | bytes 5767168 | tf_op jit(solution)/shard_map/reshape | solution.py:43
  29.4 3.5 %copy.31 = bf16[8,512,352]{2,1,0:T(8,128)(2,1)S(1)} copy(bf16[8,512,352]{1,2,0:T(8,128)(2,1)} %param.8) | data formatting | bytes 5767168 | tf_op args[2]
  33.0 6.9 %reshape.52 = bf16[1441792]{0:T(1024)(128)(2,1)} reshape(bf16[8,512,352]{2,1,0:T(8,128)(2,1)S(1)} %copy.31) | data formatting | bytes 5767168
  39.9 3.0 %reshape.41 = bf16[8,180224]{1,0:T(8,128)(2,1)S(1)} reshape(bf16[1441792]{0:T(1024)(128)(2,1)} %reshape.52) | data formatting | bytes 5767168 | tf_op jit(solution)/shard_map/reshape | solution.py:44
  42.9 0.8 dynamic_slice.6
  43.7 0.0 copy-done
  43.7 0.1 fusion.11
  43.8 0.0 all-to-all-done
  43.8 1.4 convert_reduce_fusion
  45.2 0.1 fusion.9
  45.4 10.5 %all-reduce.1 = (f32[4,8]{1,0:T(4,128)S(1)}, f32[1,8]{1,0:T(1,128)S(1)}) all-reduce(f32[4,8]{1,0:T(4,128)S(1)} %fusion.9, f32[1,8]{1,0:T(1,128)S(1)} %fusion.11), channel_id=1, replica_groups=mesh['dp'=4,'tensor'=8] {'dp'}, use_global_device_ids=true, to_apply=%region_2.0 | all-reduce | flops 40 | bytes 320 | tf_op jit(solution)/shard_map/psum | solution.py:38
  55.8 0.1 fusion.20
  56.0 3.9 %convolution_convert_fusion.2 = bf16[4,180224]{1,0:T(4,128)(2,1)} fusion(bf16[8,180224]{1,0:T(8,128)(2,1)} %reshape.39, f32[4]{0:T(128)S(1)} %fusion.20, f32[3,8]{1,0:T(4,128)S(1)} %bitcast.57, f32[1,8]{1,0:T(1,128)S(1)} %get-tuple-element.6), kind=kOutput, calls=%fused_computation.2 | convolution fusion | flops 12255392 | bytes 4325520 | tf_op jit(solution)/shard_map/dot_general | solution.py:47
  59.9 3.9 %reshape.58 = bf16[720896]{0:T(1024)(128)(2,1)} reshape(bf16[4,180224]{1,0:T(4,128)(2,1)} %convolution_convert_fusion.2) | data formatting | bytes 2883584
  63.8 4.3 %reshape.40 = bf16[4,512,352]{2,1,0:T(8,128)(2,1)} reshape(bf16[720896]{0:T(1024)(128)(2,1)} %reshape.58) | data formatting | bytes 2883584 | tf_op jit(solution)/shard_map/reshape | solution.py:51
  68.2 2.1 convolution_convert_fusion.1
  70.2 3.9 %reshape.54 = bf16[720896]{0:T(1024)(128)(2,1)} reshape(bf16[4,180224]{1,0:T(4,128)(2,1)} %convolution_convert_fusion.1) | data formatting | bytes 2883584
  74.1 3.5 %reshape.42 = bf16[4,512,352]{2,1,0:T(8,128)(2,1)S(1)} reshape(bf16[720896]{0:T(1024)(128)(2,1)} %reshape.54) | data formatting | bytes 2883584 | tf_op jit(solution)/shard_map/reshape | solution.py:52
  77.6 0.0 copy-done.1
  77.6 1.9 fusion.2
  79.5 1.9 fusion.3
  81.5 0.1 maximum_bitcast_fusion
  81.6 0.0 copy-start.2
  81.6 1.3 copy.41
  82.9 0.0 reduce-scatter.5.cloned.1.call-update
  82.9 0.3 all-reduce.4.cloned.1.call-start
  83.2 0.7 copy-done.2
  83.9 1.6 copy.42
  85.5 1.0 convolution_convert_fusion
  86.5 26.5 %reduce-scatter.5.cloned.1.call-done = bf16[256,704]{0,1:T(8,128)(2,1)} async-done(((bf16[1024,704]{0,1:T(8,128)(2,1)}), bf16[256,704]{0,1:T(8,128)(2,1)}) %reduce-scatter.5.cloned.1.call-update) | async-done | bytes 360464 | tf_op jit(solution)/shard_map/reduce_scatter | solution.py:56
  113.0 1.0 convert_element_type.36
  114.0 0.1 fusion.8
  114.1 16.6 %all_gather.3 = bf16[1024,352]{0,1:T(8,128)(2,1)S(1)} all-gather(bf16[256,352]{0,1:T(8,128)(2,1)S(1)} %fusion.8), channel_id=1, replica_groups=mesh['dp'=4,'tensor'=8] {'dp'}, dimensions={0}, use_global_device_ids=true | all-gather | bytes 901120 | tf_op jit(solution)/shard_map/all_gather | solution.py:66
  130.7 1.9 convolution_convert_fusion.3
  132.6 0.0 all-reduce.4.cloned.1.call-update
  132.6 0.6 dynamic-slice
  133.2 58.5 %all-reduce.4.cloned.1.call-done = bf16[4,8,32,512]{3,2,1,0:T(8,128)(2,1)} async-done(((bf16[4,8,32,512]{3,2,1,0:T(8,128)(2,1)}), bf16[4,8,32,512]{3,2,1,0:T(8,128)(2,1)}) %all-reduce.4.cloned.1.call-update) | async-done | bytes 1048592
  191.7 1.6 constant_dynamic-slice_fusion
  193.2 8.4 %all_to_all.31 = bf16[4,1,32,512]{3,2,1,0:T(8,128)(2,1)S(1)} all-to-all(bf16[4,1,32,512]{3,2,1,0:T(8,128)(2,1)S(1)} %constant_dynamic-slice_fusion), channel_id=1, replica_groups=mesh['dp'=4,'tensor'=8] {'dp'}, dimensions={0} | all-to-all | bytes 262144 | tf_op jit(solution)/shard_map/all_to_all | solution.py:84
  201.7 0.1 copy.35
  201.8 0.7 copy.44
  (3 shorter events, 0.0 us)
Async XLA Ops:
  6.5 37.1 %copy-start = (f32[2048,8]{0,1:T(8,128)S(1)}, f32[2048,8]{0,1:T(8,128)}, u32[]{:S(2)}) copy-start(f32[2048,8]{0,1:T(8,128)} %param.10) | copy-start | bytes 196612
  9.4 34.4 %all-to-all-start = ((bf16[256,4,512]{2,0,1:T(8,128)(2,1)}), bf16[256,4,512]{2,0,1:T(8,128)(2,1)}, u32[]{:S(2)}, u32[]{:S(2)}) async-start(bf16[256,4,512]{2,0,1:T(8,128)(2,1)} %copy.28), calls=%async_computation | async-start | bytes 2097152 | tf_op jit(solution)/shard_map/all_to_all | solution.py:20
  14.5 98.5 %reduce-scatter.5.cloned.1.call-start = ((), (), s32[]{:S(2)}) async-start(), calls=%async_computation.3 | async-start | bytes 1802240 | tf_op jit(solution)/shard_map/reduce_scatter | solution.py:56
  74.1 3.5 %copy-start.1 = (bf16[4,512,352]{2,1,0:T(8,128)(2,1)S(1)}, bf16[4,512,352]{2,1,0:T(8,128)(2,1)}, u32[]{:S(2)}) copy-start(bf16[4,512,352]{2,1,0:T(8,128)(2,1)} %reshape.40) | copy-start | bytes 4325380
  81.6 2.3 %copy-start.2 = (bf16[8,352,512]{2,1,0:T(8,128)(2,1)S(1)}, bf16[8,352,512]{2,1,0:T(8,128)(2,1)}, u32[]{:S(2)}) copy-start(bf16[8,352,512]{2,1,0:T(8,128)(2,1)} %param.9) | copy-start | bytes 8650756
  82.9 108.7 %all-reduce.4.cloned.1.call-start = ((), (), s32[]{:S(2)}) async-start(), calls=%async_computation.4 | async-start | bytes 2097152
  130.7 1.9 copy-start.3
Sparse Core Ops, SparseCore 0:
  83.0 29.8 reduce-scatter.4
  132.7 58.8 all-reduce.3
where the time goes:
time: 210 us; the launch traced here: 209 us
  waiting for transfers between devices  85 us (40%)
  local copies, waits for them, and re-layouts  54.2 us (26%)
  blocking collectives  35.5 us (17%)
  between operations  13.5 us (6%)
  matrix products  12.9 us (6%)
  starting transfers between devices  5.47 us (3%)
  other arithmetic  2.78 us (1%)
    unnamed x3, waiting for transfers between devices  58.5 us
    unnamed x19, local copies, waits for them, and re-layouts  35.2 us
    reduce_scatter x1, waiting for transfers between devices, on_device(): lax.psum_scatter(jnp.concatenate([gate_part, up_part], axis=2).reshape(co...  26.5 us
    all_gather x1, blocking collectives, on_device(): all_hidden = lax.all_gather(hidden, 'dp', axis=0, tiled=True)  16.6 us
    psum x1, blocking collectives, on_device(): seg_logits, carry_logits = lax.psum((part_segs, part_carry), 'dp')  10.5 us
    all_to_all x1, blocking collectives, on_device(): lax.all_to_all(summed, 'dp', split_axis=0, concat_axis=3, tiled=True)  8.44 us
    all_to_all x1, starting transfers between devices, on_device(): lax.all_to_all(tokens, 'dp', split_axis=1, concat_axis=0, tiled=True)  5.16 us
    reshape x1, local copies, waits for them, and re-layouts, on_device(): gate_flat = gate_weight.reshape(experts, slice_rows * hidden_cols)  4.6 us
  transfers between devices with their start and end apart: 3, of which 2 were waited for; matrix products, arithmetic and copies ran while one was open for 15% of the time, Pallas kernels for 0%

commit v1 on v0

v1 whole, which is shorter than its diff:
```python
import functools

import jax
import jax.numpy as jnp
from jax import lax
from jax.experimental import pallas as pl
from jax.experimental.pallas import tpu as pltpu
from jax.sharding import PartitionSpec as P

SEG = 256
SOFT_CAP = 8.0
VMEM = pl.BlockSpec(memory_space=pltpu.VMEM)


def swap(value, axis, step):
    count = lax.axis_size(axis)
    return lax.ppermute(value, axis, [(i, i ^ step) for i in range(count)])


def merge_kernel(block, probs_ref, *refs):
    weights, merged_ref = refs[:-1], refs[-1]
    segs, experts = probs_ref.shape
    cols = weights[0].shape[2]
    spread_row = lax.broadcasted_iota(jnp.int32, (experts, experts * block), 0)
    spread_col = lax.broadcasted_iota(jnp.int32, (experts, experts * block), 1)
    spread = jnp.where(spread_col // block == spread_row, 1.0, 0.0)
    wide = jnp.dot(probs_ref[...], spread, preferred_element_type=jnp.float32)
    place = lax.broadcasted_iota(jnp.int32, (block, experts * block), 1) % block
    row = lax.broadcasted_iota(jnp.int32, (block, experts * block), 0)
    mix = jnp.concatenate(
        [jnp.where(place == row, wide[s : s + 1, :], 0.0) for s in range(segs)], axis=0
    ).astype(jnp.bfloat16)
    at = 0
    for weight in weights:
        for start in range(0, weight.shape[1], block):
            tile = weight[:, start : start + block, :].reshape(experts * block, cols)
            out = jnp.dot(mix, tile, preferred_element_type=jnp.float32).astype(jnp.bfloat16)
            merged_ref[:, at + start : at + start + block, :] = out.reshape(segs, block, cols)
        at += weight.shape[1]


def merge(probs, *weights):
    experts, rows, cols = weights[0].shape
    segs = probs.shape[0]
    block = 32 if rows % 32 == 0 else 16
    total = rows * len(weights)
    return pl.pallas_call(
        functools.partial(merge_kernel, block),
        out_shape=jax.ShapeDtypeStruct((segs, total, cols), jnp.bfloat16),
        in_specs=[VMEM] * (1 + len(weights)),
        out_specs=VMEM,
        compiler_params=pltpu.CompilerParams(vmem_limit_bytes=28 * 2**20),
        cost_estimate=pl.CostEstimate(
            flops=2 * segs * total * cols * experts * block,
            bytes_accessed=2 * total * cols * (experts + segs),
            transcendentals=0,
        ),
    )(probs, *weights)


def preact_kernel(merged_ref, tokens_ref, out_ref):
    for s in range(merged_ref.shape[0]):
        out_ref[s] = lax.dot_general(
            merged_ref[s],
            tokens_ref[s],
            (((1,), (1,)), ((), ())),
            preferred_element_type=jnp.float32,
        ).astype(jnp.bfloat16)


def preact(merged, tokens):
    segs, rows, depth = merged.shape
    cols = tokens.shape[1]
    return pl.pallas_call(
        preact_kernel,
        out_shape=jax.ShapeDtypeStruct((segs, rows, cols), jnp.bfloat16),
        in_specs=[VMEM, VMEM],
        out_specs=VMEM,
        compiler_params=pltpu.CompilerParams(vmem_limit_bytes=28 * 2**20),
        cost_estimate=pl.CostEstimate(
            flops=2 * segs * rows * cols * depth,
            bytes_accessed=2 * segs * (rows * depth + cols * depth + rows * cols),
            transcendentals=0,
        ),
    )(merged, tokens)


def down_kernel(count, mine_ref, *refs):
    parts, downs, out_ref = refs[:count], refs[count : 2 * count], refs[-1]
    own_segs, both, seg = parts[0].shape
    half = both // 2
    cols = downs[0].shape[2]
    for j in range(own_segs):
        total = parts[0][j].astype(jnp.float32)
        for part in parts[1:]:
            total += part[j].astype(jnp.float32)
        gate, up = total[:half], total[half:]
        hidden = (gate / (1.0 + jnp.exp(-gate)) * up).astype(jnp.bfloat16)
        for k in range(count):
            out = lax.dot_general(
                hidden, downs[k][j], (((0,), (0,)), ((), ())), preferred_element_type=jnp.float32
            )
            start = pl.multiple_of((mine_ref[0] ^ k) * cols, 128)
            out_ref[j * seg : (j + 1) * seg, pl.ds(start, cols)] = out.astype(jnp.bfloat16)


def down_product(mine, parts, downs):
    count = len(parts)
    own_segs, both, seg = parts[0].shape
    cols = downs[0].shape[2]
    return pl.pallas_call(
        functools.partial(down_kernel, count),
        out_shape=jax.ShapeDtypeStruct((own_segs * seg, count * cols), jnp.bfloat16),
        in_specs=[pl.BlockSpec(memory_space=pltpu.SMEM)] + [VMEM] * (2 * count),
        out_specs=VMEM,
        compiler_params=pltpu.CompilerParams(vmem_limit_bytes=28 * 2**20),
        cost_estimate=pl.CostEstimate(
            flops=own_segs * seg * both * cols * count,
            bytes_accessed=2 * count * own_segs * (both * seg + both * cols // 2 + seg * cols),
            transcendentals=own_segs * seg * both // 2,
        ),
    )(mine, *parts, *downs)


def on_device(tokens, gate_weight, up_weight, down_weight, router_weight, carry_mean):
    dp = lax.axis_size("dp")
    tensor = lax.axis_size("tensor")
    my_dp = lax.axis_index("dp")
    my_tensor = lax.axis_index("tensor")
    core = my_tensor % 2
    own_rows, width = tokens.shape
    own_segs = own_rows // SEG
    segs = own_segs * dp
    experts, depth, hidden = gate_weight.shape
    gate_t = jnp.swapaxes(gate_weight, 1, 2)
    up_t = jnp.swapaxes(up_weight, 1, 2)

    own_means = jnp.sum(tokens.reshape(own_segs, SEG, width), axis=1, dtype=jnp.float32) / SEG
    own_logits = jnp.dot(
        own_means,
        router_weight,
        precision=lax.Precision.HIGHEST,
        preferred_element_type=jnp.float32,
    )
    carry_logits = jnp.dot(
        carry_mean[None, :],
        router_weight,
        precision=lax.Precision.HIGHEST,
        preferred_element_type=jnp.float32,
    )
    table = jnp.concatenate(
        [own_logits] + [swap(own_logits, "dp", k) for k in range(1, dp)] + [carry_logits], axis=0
    )
    order = jnp.arange(segs, dtype=jnp.int32)
    seg_index = ((order // own_segs) ^ my_dp) * own_segs + order % own_segs
    prior = seg_index - 1
    row = jnp.where(
        seg_index == 0, segs, ((prior // own_segs) ^ my_dp) * own_segs + prior % own_segs
    )
    pick = row[:, None, None] == jnp.arange(segs + 1, dtype=jnp.int32)[None, :, None]
    raw_logits = jnp.sum(jnp.where(pick, table[None], 0.0), axis=1)
    scores = jnp.exp(SOFT_CAP * jnp.tanh(raw_logits / SOFT_CAP))
    probs = (scores / jnp.sum(scores, axis=1, keepdims=True)).astype(jnp.bfloat16)
    probs = probs.astype(jnp.float32)

    half = own_rows // 2
    brought = jnp.stack(
        [
            swap(
                lax.dynamic_slice(tokens, (core * half, (my_dp ^ k) * depth), (half, depth)),
                "dp",
                k,
            )
            for k in range(1, dp)
        ]
    )
    other = swap(brought, "tensor", 1)
    rest = jnp.where(
        core == 0,
        jnp.concatenate([brought, other], axis=1),
        jnp.concatenate([other, brought], axis=1),
    )
    own_block = lax.dynamic_slice(tokens, (0, my_dp * depth), (own_rows, depth))
    rows_in = jnp.concatenate([own_block[None], rest], axis=0).reshape(segs, SEG, depth)

    merged_down = merge(probs, down_weight)
    merged_down = merged_down.reshape(dp, own_segs, hidden, down_weight.shape[2])
    downs = [merged_down[0]] + [swap(merged_down[k], "dp", k) for k in range(1, dp)]

    partial_pre = preact(merge(probs, gate_t, up_t), rows_in)
    partial_pre = partial_pre.reshape(dp, own_segs, 2 * hidden, SEG)
    parts = [partial_pre[0]] + [swap(partial_pre[k], "dp", k) for k in range(1, dp)]

    mixed = down_product(my_dp.reshape(1), parts, downs)

    lines = tensor // 2
    my_line = my_tensor // 2
    mixed = mixed.reshape(lines, 2, own_rows // tensor, width)
    mine = lax.dynamic_index_in_dim(mixed, core, 1, keepdims=False)
    theirs = lax.dynamic_index_in_dim(mixed, 1 - core, 1, keepdims=False)
    pair = mine.astype(jnp.float32) + swap(theirs, "tensor", 1).astype(jnp.float32)
    pair = pair.astype(jnp.bfloat16)
    out = lax.dynamic_index_in_dim(pair, my_line, 0, keepdims=False).astype(jnp.float32)
    for k in range(1, lines):
        piece = lax.dynamic_index_in_dim(pair, my_line ^ k, 0, keepdims=False)
        out = out + swap(piece, "tensor", 2 * k).astype(jnp.float32)
    return out.astype(jnp.bfloat16)


def solution(mesh):
    placed = (
        P("dp", None),
        P(None, "dp", "tensor"),
        P(None, "dp", "tensor"),
        P(None, "tensor", "dp"),
        P(),
        P(),
    )
    return jax.shard_map(
        on_device, mesh=mesh, in_specs=placed, out_specs=P(("dp", "tensor"), None), check_vma=False
    )
```

time: 210 us -> 78.4 us (0.37)
  local copies, waits for them, and re-layouts: 54.2 us -> 8.26 us
  waiting for transfers between devices: 85 us -> 40.6 us
  blocking collectives: 35.5 us -> 0 us
  starting transfers between devices: 5.47 us -> 20.1 us
  between operations: 13.5 us -> 0.24 us
  matrix products: 12.9 us -> 0.42 us
  Pallas kernels: 0 us -> 3.54 us
  other arithmetic: 2.78 us -> 5.01 us
    unnamed x3 -> x0, waiting for transfers between devices: 58.5 us -> none
    ppermute x0 -> x17, waiting for transfers between devices: none -> 40.6 us  [swap(): return lax.ppermute(value, axis, [(i, i ^ step) for i in range(count)])]
    unnamed x19 -> x18, local copies, waits for them, and re-layouts: 35.2 us -> 3.46 us
    reduce_scatter x1 -> x0, waiting for transfers between devices: 26.5 us -> none  [on_device(): lax.psum_scatter(jnp.concatenate([gate_part, up_part], axis=2).reshape(co...]
    ppermute x0 -> x17, starting transfers between devices: none -> 20.1 us  [swap(): return lax.ppermute(value, axis, [(i, i ^ step) for i in range(count)])]
    all_gather x1 -> x0, blocking collectives: 16.6 us -> none  [on_device(): all_hidden = lax.all_gather(hidden, 'dp', axis=0, tiled=True)]
    reshape x4 -> x0, local copies, waits for them, and re-layouts: 15.4 us -> none  [the longest x1 4.6 us: on_device(): gate_flat = gate_weight.reshape(experts, slice_rows * hidden_cols)]
    dot_general x8 -> x2, matrix products: 12.9 us -> 0.42 us  [the longest x1 0.21 us: on_device(): jnp.dot(own_means, router_weight, precision=lax.Precision.HIGHEST, prefer...]
  transfers between devices with their start and end apart: 3 -> 17, of which waited for: 2 -> 10; matrix products, arithmetic and copies ran while one was open for 15% -> 8% of each run, Pallas kernels for 0% -> 3%
where the time goes in v1:
time: 78.4 us; the launch traced here: 78.1 us
  waiting for transfers between devices  40.6 us (52%)
  starting transfers between devices  20.1 us (26%)
  local copies, waits for them, and re-layouts  8.26 us (11%)
  other arithmetic  5.01 us (6%)
  Pallas kernels  3.54 us (5%)
    ppermute x17, waiting for transfers between devices, swap(): return lax.ppermute(value, axis, [(i, i ^ step) for i in range(count)])  40.6 us
    ppermute x17, starting transfers between devices, swap(): return lax.ppermute(value, axis, [(i, i ^ step) for i in range(count)])  20.1 us
    unnamed x18, local copies, waits for them, and re-layouts  3.46 us
    dynamic_slice x1, local copies, waits for them, and re-layouts, on_device(): lax.dynamic_slice(tokens, (core * half, (my_dp ^ k) * depth), (half, depth))  1.77 us
    pallas_call x2, Pallas kernels, merge(): pl.pallas_call(functools.partial(merge_kernel, block), out_shape=jax.Shap...  1.66 us
  transfers between devices with their start and end apart: 17, of which 10 were waited for; matrix products, arithmetic and copies ran while one was open for 8% of the time, Pallas kernels for 3%

profile of v1, /device:TPU:0, one launch (start us, length us, event | category | flops | bytes accessed | tf_op | source)
XLA Modules:
  0.0 78.1 jit_solution(12458066568307044142)
XLA Ops:
  0.0 1.5 %convert_reduce_fusion = f32[2048]{0:T(1024)S(1)} fusion(bf16[256,2048]{1,0:T(8,128)(2,1)} %param.6), kind=kLoop, calls=%fused_computation | loop fusion | flops 1046528 | bytes 1056768 | tf_op jit(solution)/shard_map/reduce_sum | solution.py:138
  1.6 0.2 fusion.9
  1.8 3.0 %collective-permute-start = (f32[1,8]{1,0:T(1,128)S(1)}, f32[1,8]{1,0:T(1,128)S(1)}, u32[]{:S(2)}, u32[]{:S(2)}) collective-permute-start(f32[1,8]{1,0:T(1,128)S(1)} %fusion.9), channel_id=1, source_target_pairs={{0,8},{8,0},{16,24},{24,16},{1,9},{9,1},{17,25},{25,17},{2,10},{10... | collective-permute-start | bytes 104 | tf_op jit(solution)/shard_map/ppermute | solution.py:17
  4.8 1.5 %collective-permute-start.1 = (f32[1,8]{1,0:T(1,128)S(1)}, f32[1,8]{1,0:T(1,128)S(1)}, u32[]{:S(2)}, u32[]{:S(2)}) collective-permute-start(f32[1,8]{1,0:T(1,128)S(1)} %fusion.9), channel_id=1, source_target_pairs={{0,16},{8,24},{16,0},{24,8},{1,17},{9,25},{17,1},{25,9},{2,18},{10... | collective-permute-start | bytes 104 | tf_op jit(solution)/shard_map/ppermute | solution.py:17
  6.3 1.8 %fusion.8 = (bf16[128,512]{1,0:T(8,128)(2,1)}, bf16[128,512]{1,0:T(8,128)(2,1)}, bf16[128,512]{1,0:T(8,128)(2,1)}) fusion(bf16[256,2048]{1,0:T(8,128)(2,1)} %param.6, s32[]{:T(128)S(6)} %select_n.92, s32[]{:T(128)S(6)} %select_n.93, s32[]{:T(128)S(6)} %select_n.95, s32[]{:T(128)S(6)} %select_n.94), kind=kLoop, calls=%fused_computation.25 | loop fusion | bytes 786448 | tf_op jit(solution)/shard_map/dynamic_slice | solution.py:170
  8.1 2.9 %collective-permute-start.5 = (bf16[128,512]{1,0:T(8,128)(2,1)}, bf16[128,512]{1,0:T(8,128)(2,1)S(1)}, u32[]{:S(2)}, u32[]{:S(2)}) collective-permute-start(bf16[128,512]{1,0:T(8,128)(2,1)} %get-tuple-element.14), channel_id=1, source_target_pairs={{0,24},{8,16},{16,8},{24,0},{1,25},{9,17},{17,9},{25,1},{2,26},{10... | collective-permute-start | bytes 393224 | tf_op jit(solution)/shard_map/ppermute | solution.py:17
  11.0 0.5 collective-permute-start.3
  11.5 1.0 %dynamic-slice_bitcast_fusion.1 = bf16[1,256,512]{2,1,0:T(8,128)(2,1)S(1)} fusion(bf16[256,2048]{1,0:T(8,128)(2,1)} %param.6, s32[]{:T(128)S(6)} %select_n.89), kind=kLoop, calls=%fused_computation.11 | loop fusion | bytes 524292 | tf_op jit(solution)/shard_map/broadcast_in_dim | solution.py:184
  12.5 0.2 fusion.10
  12.8 0.1 collective-permute-start.4
  12.9 0.1 select_reduce_fusion
  13.0 0.1 fusion.4
  13.1 2.2 %collective-permute-done.5 = bf16[128,512]{1,0:T(8,128)(2,1)S(1)} collective-permute-done((bf16[128,512]{1,0:T(8,128)(2,1)}, bf16[128,512]{1,0:T(8,128)(2,1)S(1)}, u32[]{:S(2)}, u32[]{:S(2)}) %collective-permute-start.5) | collective-permute-done | bytes 131104 | tf_op jit(solution)/shard_map/ppermute | solution.py:17
  15.4 1.6 %collective-permute-done.3 = bf16[128,512]{1,0:T(8,128)(2,1)S(1)} collective-permute-done((bf16[128,512]{1,0:T(8,128)(2,1)}, bf16[128,512]{1,0:T(8,128)(2,1)S(1)}, u32[]{:S(2)}, u32[]{:S(2)}) %collective-permute-start.3) | collective-permute-done | bytes 131104 | tf_op jit(solution)/shard_map/ppermute | solution.py:17
  16.9 1.2 %collective-permute-done.4 = bf16[128,512]{1,0:T(8,128)(2,1)} collective-permute-done((bf16[128,512]{1,0:T(8,128)(2,1)}, bf16[128,512]{1,0:T(8,128)(2,1)}, u32[]{:S(2)}, u32[]{:S(2)}) %collective-permute-start.4) | collective-permute-done | bytes 131104 | tf_op jit(solution)/shard_map/ppermute | solution.py:17
  18.2 0.9 %pad_maximum_fusion.1 = bf16[3,128,512]{2,1,0:T(8,128)(2,1)S(1)} fusion(bf16[1,128,512]{2,1,0:T(8,128)(2,1)S(1)} %bitcast.37, bf16[1,128,512]{2,1,0:T(8,128)(2,1)} %bitcast.9, bf16[1,128,512]{2,1,0:T(8,128)(2,1)S(1)} %bitcast.39), kind=kLoop, calls=%fused_computation.6 | loop fusion | flops 393216 | bytes 786432 | tf_op jit(solution)/shard_map/stack | solution.py:167
  19.1 0.1 collective-permute-start.6
  19.3 0.7 shard_map.66
  19.9 1.0 %fusion.6 = (bf16[1,352,512]{2,1,0:T(8,128)(2,1)}, bf16[1,352,512]{2,1,0:T(8,128)(2,1)}, bf16[1,352,512]{2,1,0:T(8,128)(2,1)S(1)}, bf16[1,352,512]{2,1,0:T(8,128)(2,1)S(1)}) fusion(bf16[4,352,512]{2,1,0:T(8,128)(2,1)S(1)} %shard_map.66), kind=kLoop, calls=%fused_computation.23 | loop fusion | bytes 2883584 | tf_op jit(solution)/shard_map/slice | solution.py:188
  20.9 1.5 %collective-permute-start.10 = (bf16[1,352,512]{2,1,0:T(8,128)(2,1)S(1)}, bf16[1,352,512]{2,1,0:T(8,128)(2,1)S(1)}, u32[]{:S(2)}, u32[]{:S(2)}) collective-permute-start(bf16[1,352,512]{2,1,0:T(8,128)(2,1)S(1)} %get-tuple-element.7), channel_id=1, source_target_pairs={{0,8},{8,0},{16,24},{24,16},{1,9},{9,1},{17,25},{25,17},{2,10},{10... | collective-permute-start | bytes 1081352 | tf_op jit(solution)/shard_map/ppermute | solution.py:17
  22.4 0.8 collective-permute-start.11
  23.1 1.2 %collective-permute-start.12 = (bf16[1,352,512]{2,1,0:T(8,128)(2,1)}, bf16[1,352,512]{2,1,0:T(8,128)(2,1)S(1)}, u32[]{:S(2)}, u32[]{:S(2)}) collective-permute-start(bf16[1,352,512]{2,1,0:T(8,128)(2,1)} %get-tuple-element.5), channel_id=1, source_target_pairs={{0,24},{8,16},{16,8},{24,0},{1,25},{9,17},{17,9},{25,1},{2,26},{10... | collective-permute-start | bytes 1081352 | tf_op jit(solution)/shard_map/ppermute | solution.py:17
  24.4 1.0 %shard_map.64.merged_ref = bf16[4,704,512]{2,1,0:T(8,128)(2,1)S(1)} custom-call(f32[4,8]{1,0:T(4,128)S(1)} %fusion.5.probs_ref, bf16[8,352,512]{2,1,0:T(8,128)(2,1)S(1)} %bitcast.35, bf16[8,352,512]{2,1,0:T(8,128)(2,1)S(1)} %bitcast.36), custom_call_target="tpu_custom_call" | custom-call | flops 738197504 | bytes 8650752 | tf_op jit(solution)/shard_map/pallas_call | solution.py:47
  25.4 1.3 %maximum_select_fusion = bf16[3,256,512]{2,1,0:T(8,128)(2,1)S(1)} fusion(bf16[3,128,512]{2,1,0:T(8,128)(2,1)S(1)} %collective-permute-done.6, bf16[1,128,512]{2,1,0:T(8,128)(2,1)S(1)} %bitcast.38, bf16[1,128,512]{2,1,0:T(8,128)(2,1)} %bitcast.9, bf16[1,128,512]{2,1,0:T(8,128)(2,1)S(1)} %bitcast.40, pred[]{:T(512)S(6)} %eq.37), kind=kLoop, calls=%fused_computation.4 | loop fusion | flops 6684672 | bytes 1572865 | tf_op jit(solution)/shard_map/jit(_where)/select_n | solution.py:178
  26.7 0.1 pad_maximum_fusion.tokens_ref
  26.8 0.9 %shard_map.65 = bf16[4,704,256]{2,1,0:T(8,128)(2,1)S(1)} custom-call(bf16[4,704,512]{2,1,0:T(8,128)(2,1)S(1)} %shard_map.64.merged_ref, bf16[4,256,512]{2,1,0:T(8,128)(2,1)S(1)} %pad_maximum_fusion.tokens_ref), custom_call_target="tpu_custom_call" | custom-call | flops 738197504 | bytes 5373952 | tf_op jit(solution)/shard_map/pallas_call | solution.py:74
  27.7 1.0 %fusion.7 = (bf16[1,704,256]{2,1,0:T(8,128)(2,1)}, bf16[1,704,256]{2,1,0:T(8,128)(2,1)}, bf16[1,704,256]{2,1,0:T(8,128)(2,1)}, bf16[1,704,256]{2,1,0:T(8,128)(2,1)S(1)}) fusion(bf16[4,704,256]{2,1,0:T(8,128)(2,1)S(1)} %shard_map.65), kind=kLoop, calls=%fused_computation.24 | loop fusion | bytes 2883584 | tf_op jit(solution)/shard_map/slice | solution.py:192
  28.7 1.5 %collective-permute-start.7 = (bf16[1,704,256]{2,1,0:T(8,128)(2,1)}, bf16[1,704,256]{2,1,0:T(8,128)(2,1)S(1)}, u32[]{:S(2)}, u32[]{:S(2)}) collective-permute-start(bf16[1,704,256]{2,1,0:T(8,128)(2,1)} %get-tuple-element.11), channel_id=1, source_target_pairs={{0,8},{8,0},{16,24},{24,16},{1,9},{9,1},{17,25},{25,17},{2,10},{10... | collective-permute-start | bytes 1081352 | tf_op jit(solution)/shard_map/ppermute | solution.py:17
  30.2 0.8 %collective-permute-start.8 = (bf16[1,704,256]{2,1,0:T(8,128)(2,1)}, bf16[1,704,256]{2,1,0:T(8,128)(2,1)S(1)}, u32[]{:S(2)}, u32[]{:S(2)}) collective-permute-start(bf16[1,704,256]{2,1,0:T(8,128)(2,1)} %get-tuple-element.10), channel_id=1, source_target_pairs={{0,16},{8,24},{16,0},{24,8},{1,17},{9,25},{17,1},{25,9},{2,18},{10... | collective-permute-start | bytes 1081352 | tf_op jit(solution)/shard_map/ppermute | solution.py:17
  31.0 1.1 %collective-permute-done.10.refs_5_ = bf16[1,352,512]{2,1,0:T(8,128)(2,1)S(1)} collective-permute-done((bf16[1,352,512]{2,1,0:T(8,128)(2,1)S(1)}, bf16[1,352,512]{2,1,0:T(8,128)(2,1)S(1)}, u32[]{:S(2)}, u32[]{:S(2)}) %collective-permute-start.10) | collective-permute-done | bytes 360480 | tf_op jit(solution)/shard_map/ppermute | solution.py:17
  32.1 1.7 %collective-permute-start.9 = (bf16[1,704,256]{2,1,0:T(8,128)(2,1)}, bf16[1,704,256]{2,1,0:T(8,128)(2,1)S(1)}, u32[]{:S(2)}, u32[]{:S(2)}) collective-permute-start(bf16[1,704,256]{2,1,0:T(8,128)(2,1)} %get-tuple-element.9), channel_id=1, source_target_pairs={{0,24},{8,16},{16,8},{24,0},{1,25},{9,17},{17,9},{25,1},{2,26},{10... | collective-permute-start | bytes 1081352 | tf_op jit(solution)/shard_map/ppermute | solution.py:17
  33.8 7.8 %collective-permute-done.11.refs_6_ = bf16[1,352,512]{2,1,0:T(8,128)(2,1)S(1)} collective-permute-done((bf16[1,352,512]{2,1,0:T(8,128)(2,1)}, bf16[1,352,512]{2,1,0:T(8,128)(2,1)S(1)}, u32[]{:S(2)}, u32[]{:S(2)}) %collective-permute-start.11) | collective-permute-done | bytes 360480 | tf_op jit(solution)/shard_map/ppermute | solution.py:17
  41.6 6.0 %collective-permute-done.7.refs_1_ = bf16[1,704,256]{2,1,0:T(8,128)(2,1)S(1)} collective-permute-done((bf16[1,704,256]{2,1,0:T(8,128)(2,1)}, bf16[1,704,256]{2,1,0:T(8,128)(2,1)S(1)}, u32[]{:S(2)}, u32[]{:S(2)}) %collective-permute-start.7) | collective-permute-done | bytes 360480 | tf_op jit(solution)/shard_map/ppermute | solution.py:17
  47.6 8.7 %collective-permute-done.8.refs_2_ = bf16[1,704,256]{2,1,0:T(8,128)(2,1)S(1)} collective-permute-done((bf16[1,704,256]{2,1,0:T(8,128)(2,1)}, bf16[1,704,256]{2,1,0:T(8,128)(2,1)S(1)}, u32[]{:S(2)}, u32[]{:S(2)}) %collective-permute-start.8) | collective-permute-done | bytes 360480 | tf_op jit(solution)/shard_map/ppermute | solution.py:17
  56.3 0.7 copy-done.4
  57.0 0.7 copy-done.6
  57.8 1.0 %copy-done.5 = bf16[1,704,256]{2,1,0:T(8,128)(2,1)S(1)} copy-done((bf16[1,704,256]{2,1,0:T(8,128)(2,1)S(1)}, bf16[1,704,256]{2,1,0:T(8,128)(2,1)}, u32[]{:S(2)}) %copy-start.5) | copy-done | bytes 360472
  58.7 1.0 %copy-done.7 = bf16[1,704,256]{2,1,0:T(8,128)(2,1)S(1)} copy-done((bf16[1,704,256]{2,1,0:T(8,128)(2,1)S(1)}, bf16[1,704,256]{2,1,0:T(8,128)(2,1)}, u32[]{:S(2)}) %copy-start.7) | copy-done | bytes 360472
  59.7 0.9 %shard_map.67 = bf16[256,2048]{1,0:T(8,128)(2,1)S(1)} custom-call(s32[1]{0:T(128)} %bitcast.mine_ref, bf16[1,704,256]{2,1,0:T(8,128)(2,1)S(1)} %get-tuple-element.12.refs_0_, bf16[1,704,256]{2,1,0:T(8,128)(2,1)S(1)} %collective-permute-done.7.refs_1_, bf16[1,704,256]{2,1,0:T(8,128)(2,1)S(1)} %copy-done.5, bf16[1,704,256]{2,1,0:T(8,128)(2,1)S(1)} %copy-done.7, ...), custom_call_target="tpu_custom_call" | custom-call | flops 369098752 | bytes 3932160 | tf_op jit(solution)/shard_map/pallas_call | solution.py:111
  60.7 0.1 collective-permute-start.13
  60.8 1.9 %collective-permute-done.13 = bf16[4,32,2048]{2,1,0:T(8,128)(2,1)S(1)} collective-permute-done((bf16[4,32,2048]{2,1,0:T(8,128)(2,1)S(1)}, bf16[4,32,2048]{2,1,0:T(8,128)(2,1)S(1)}, u32[]{:S(2)}, u32[]{:S(2)}) %collective-permute-start.13) | collective-permute-done | bytes 524320 | tf_op jit(solution)/shard_map/ppermute | solution.py:17
  62.7 0.1 fusion
  62.9 1.6 %collective-permute-start.14 = (bf16[32,2048]{1,0:T(8,128)(2,1)S(1)}, bf16[32,2048]{1,0:T(8,128)(2,1)S(1)}, u32[]{:S(2)}, u32[]{:S(2)}) collective-permute-start(bf16[32,2048]{1,0:T(8,128)(2,1)S(1)} %get-tuple-element.16), channel_id=1, source_target_pairs={{0,2},{1,3},{2,0},{3,1},{4,6},{5,7},{6,4},{7,5},{8,10},{9,11},{10,... | collective-permute-start | bytes 393224 | tf_op jit(solution)/shard_map/ppermute | solution.py:17
  64.5 2.6 %collective-permute-start.15 = (bf16[32,2048]{1,0:T(8,128)(2,1)S(1)}, bf16[32,2048]{1,0:T(8,128)(2,1)S(1)}, u32[]{:S(2)}, u32[]{:S(2)}) collective-permute-start(bf16[32,2048]{1,0:T(8,128)(2,1)S(1)} %get-tuple-element.18), channel_id=1, source_target_pairs={{0,4},{1,5},{2,6},{3,7},{4,0},{5,1},{6,2},{7,3},{8,12},{9,13},{10,... | collective-permute-start | bytes 393224 | tf_op jit(solution)/shard_map/ppermute | solution.py:17
  67.1 0.2 collective-permute-start.16
  67.3 3.1 %collective-permute-done.14 = bf16[32,2048]{1,0:T(8,128)(2,1)S(1)} collective-permute-done((bf16[32,2048]{1,0:T(8,128)(2,1)S(1)}, bf16[32,2048]{1,0:T(8,128)(2,1)S(1)}, u32[]{:S(2)}, u32[]{:S(2)}) %collective-permute-start.14) | collective-permute-done | bytes 131104 | tf_op jit(solution)/shard_map/ppermute | solution.py:17
  70.4 7.0 %collective-permute-done.15 = bf16[32,2048]{1,0:T(8,128)(2,1)S(1)} collective-permute-done((bf16[32,2048]{1,0:T(8,128)(2,1)S(1)}, bf16[32,2048]{1,0:T(8,128)(2,1)S(1)}, u32[]{:S(2)}, u32[]{:S(2)}) %collective-permute-start.15) | collective-permute-done | bytes 131104 | tf_op jit(solution)/shard_map/ppermute | solution.py:17
  77.4 0.7 fusion.3
  (29 shorter events, 0.3 us)
Async XLA Ops:
  0.0 1.6 %copy-start = (f32[2048,8]{0,1:T(8,128)S(1)}, f32[2048,8]{0,1:T(8,128)}, u32[]{:S(2)}) copy-start(f32[2048,8]{0,1:T(8,128)} %param.10) | copy-start | bytes 196612
  0.0 12.5 %copy-start.8 = (f32[2048]{0:T(1024)S(1)}, f32[2048]{0:T(1024)}, u32[]{:S(2)}) copy-start(f32[2048]{0:T(1024)} %param.11) | copy-start | bytes 24580
  0.0 19.2 %copy-start.3 = (bf16[8,352,512]{2,1,0:T(8,128)(2,1)S(1)}, bf16[8,352,512]{2,1,0:T(8,128)(2,1)}, u32[]{:S(2)}) copy-start(bf16[8,352,512]{2,1,0:T(8,128)(2,1)} %refs_0_.1) | copy-start | bytes 8650756
  1.8 11.0 %collective-permute-start = (f32[1,8]{1,0:T(1,128)S(1)}, f32[1,8]{1,0:T(1,128)S(1)}, u32[]{:S(2)}, u32[]{:S(2)}) collective-permute-start(f32[1,8]{1,0:T(1,128)S(1)} %fusion.9), channel_id=1, source_target_pairs={{0,8},{8,0},{16,24},{24,16},{1,9},{9,1},{17,25},{25,17},{2,10},{10... | collective-permute-start | bytes 104 | tf_op jit(solution)/shard_map/ppermute | solution.py:17
  4.8 8.1 %collective-permute-start.1 = (f32[1,8]{1,0:T(1,128)S(1)}, f32[1,8]{1,0:T(1,128)S(1)}, u32[]{:S(2)}, u32[]{:S(2)}) collective-permute-start(f32[1,8]{1,0:T(1,128)S(1)} %fusion.9), channel_id=1, source_target_pairs={{0,16},{8,24},{16,0},{24,8},{1,17},{9,25},{17,1},{25,9},{2,18},{10... | collective-permute-start | bytes 104 | tf_op jit(solution)/shard_map/ppermute | solution.py:17
  6.3 6.6 %collective-permute-start.2 = (f32[1,8]{1,0:T(1,128)S(1)}, f32[1,8]{1,0:T(1,128)S(1)}, u32[]{:S(2)}, u32[]{:S(2)}) collective-permute-start(f32[1,8]{1,0:T(1,128)S(1)} %fusion.9), channel_id=1, source_target_pairs={{0,24},{8,16},{16,8},{24,0},{1,25},{9,17},{17,9},{25,1},{2,26},{10... | collective-permute-start | bytes 104 | tf_op jit(solution)/shard_map/ppermute | solution.py:17
  8.1 7.3 %collective-permute-start.5 = (bf16[128,512]{1,0:T(8,128)(2,1)}, bf16[128,512]{1,0:T(8,128)(2,1)S(1)}, u32[]{:S(2)}, u32[]{:S(2)}) collective-permute-start(bf16[128,512]{1,0:T(8,128)(2,1)} %get-tuple-element.14), channel_id=1, source_target_pairs={{0,24},{8,16},{16,8},{24,0},{1,25},{9,17},{17,9},{25,1},{2,26},{10... | collective-permute-start | bytes 393224 | tf_op jit(solution)/shard_map/ppermute | solution.py:17
  11.0 5.9 %collective-permute-start.3 = (bf16[128,512]{1,0:T(8,128)(2,1)}, bf16[128,512]{1,0:T(8,128)(2,1)S(1)}, u32[]{:S(2)}, u32[]{:S(2)}) collective-permute-start(bf16[128,512]{1,0:T(8,128)(2,1)} %get-tuple-element.13), channel_id=1, source_target_pairs={{0,8},{8,0},{16,24},{24,16},{1,9},{9,1},{17,25},{25,17},{2,10},{10... | collective-permute-start | bytes 393224 | tf_op jit(solution)/shard_map/ppermute | solution.py:17
  12.8 5.3 %collective-permute-start.4 = (bf16[128,512]{1,0:T(8,128)(2,1)}, bf16[128,512]{1,0:T(8,128)(2,1)}, u32[]{:S(2)}, u32[]{:S(2)}) collective-permute-start(bf16[128,512]{1,0:T(8,128)(2,1)} %get-tuple-element.15), channel_id=1, source_target_pairs={{0,16},{8,24},{16,0},{24,8},{1,17},{9,25},{17,1},{25,9},{2,18},{10... | collective-permute-start | bytes 393224 | tf_op jit(solution)/shard_map/ppermute | solution.py:17
  19.1 6.3 %collective-permute-start.6 = (bf16[3,128,512]{2,1,0:T(8,128)(2,1)S(1)}, bf16[3,128,512]{2,1,0:T(8,128)(2,1)S(1)}, u32[]{:S(2)}, u32[]{:S(2)}) collective-permute-start(bf16[3,128,512]{2,1,0:T(8,128)(2,1)S(1)} %pad_maximum_fusion.1), channel_id=1, source_target_pairs={{0,1},{1,0},{2,3},{3,2},{4,5},{5,4},{6,7},{7,6},{8,9},{9,8},{10,11... | collective-permute-start | bytes 1179656 | tf_op jit(solution)/shard_map/ppermute | solution.py:17
  19.2 5.1 %copy-start.2 = (bf16[8,512,352]{1,2,0:T(8,128)(2,1)S(1)}, bf16[8,512,352]{1,2,0:T(8,128)(2,1)}, u32[]{:S(2)}) copy-start(bf16[8,512,352]{1,2,0:T(8,128)(2,1)} %param.8) | copy-start | bytes 8650756
  19.9 4.5 %copy-start.1 = (bf16[8,512,352]{1,2,0:T(8,128)(2,1)S(1)}, bf16[8,512,352]{1,2,0:T(8,128)(2,1)}, u32[]{:S(2)}) copy-start(bf16[8,512,352]{1,2,0:T(8,128)(2,1)} %param.7) | copy-start | bytes 8650756
  20.9 11.2 %collective-permute-start.10 = (bf16[1,352,512]{2,1,0:T(8,128)(2,1)S(1)}, bf16[1,352,512]{2,1,0:T(8,128)(2,1)S(1)}, u32[]{:S(2)}, u32[]{:S(2)}) collective-permute-start(bf16[1,352,512]{2,1,0:T(8,128)(2,1)S(1)} %get-tuple-element.7), channel_id=1, source_target_pairs={{0,8},{8,0},{16,24},{24,16},{1,9},{9,1},{17,25},{25,17},{2,10},{10... | collective-permute-start | bytes 1081352 | tf_op jit(solution)/shard_map/ppermute | solution.py:17
  22.4 19.2 %collective-permute-start.11 = (bf16[1,352,512]{2,1,0:T(8,128)(2,1)}, bf16[1,352,512]{2,1,0:T(8,128)(2,1)S(1)}, u32[]{:S(2)}, u32[]{:S(2)}) collective-permute-start(bf16[1,352,512]{2,1,0:T(8,128)(2,1)} %get-tuple-element.6), channel_id=1, source_target_pairs={{0,16},{8,24},{16,0},{24,8},{1,17},{9,25},{17,1},{25,9},{2,18},{10... | collective-permute-start | bytes 1081352 | tf_op jit(solution)/shard_map/ppermute | solution.py:17
  23.1 18.4 %collective-permute-start.12 = (bf16[1,352,512]{2,1,0:T(8,128)(2,1)}, bf16[1,352,512]{2,1,0:T(8,128)(2,1)S(1)}, u32[]{:S(2)}, u32[]{:S(2)}) collective-permute-start(bf16[1,352,512]{2,1,0:T(8,128)(2,1)} %get-tuple-element.5), channel_id=1, source_target_pairs={{0,24},{8,16},{16,8},{24,0},{1,25},{9,17},{17,9},{25,1},{2,26},{10... | collective-permute-start | bytes 1081352 | tf_op jit(solution)/shard_map/ppermute | solution.py:17
  28.7 18.9 %collective-permute-start.7 = (bf16[1,704,256]{2,1,0:T(8,128)(2,1)}, bf16[1,704,256]{2,1,0:T(8,128)(2,1)S(1)}, u32[]{:S(2)}, u32[]{:S(2)}) collective-permute-start(bf16[1,704,256]{2,1,0:T(8,128)(2,1)} %get-tuple-element.11), channel_id=1, source_target_pairs={{0,8},{8,0},{16,24},{24,16},{1,9},{9,1},{17,25},{25,17},{2,10},{10... | collective-permute-start | bytes 1081352 | tf_op jit(solution)/shard_map/ppermute | solution.py:17
  30.2 26.1 %collective-permute-start.8 = (bf16[1,704,256]{2,1,0:T(8,128)(2,1)}, bf16[1,704,256]{2,1,0:T(8,128)(2,1)S(1)}, u32[]{:S(2)}, u32[]{:S(2)}) collective-permute-start(bf16[1,704,256]{2,1,0:T(8,128)(2,1)} %get-tuple-element.10), channel_id=1, source_target_pairs={{0,16},{8,24},{16,0},{24,8},{1,17},{9,25},{17,1},{25,9},{2,18},{10... | collective-permute-start | bytes 1081352 | tf_op jit(solution)/shard_map/ppermute | solution.py:17
  32.1 24.9 %collective-permute-start.9 = (bf16[1,704,256]{2,1,0:T(8,128)(2,1)}, bf16[1,704,256]{2,1,0:T(8,128)(2,1)S(1)}, u32[]{:S(2)}, u32[]{:S(2)}) collective-permute-start(bf16[1,704,256]{2,1,0:T(8,128)(2,1)} %get-tuple-element.9), channel_id=1, source_target_pairs={{0,24},{8,16},{16,8},{24,0},{1,25},{9,17},{17,9},{25,1},{2,26},{10... | collective-permute-start | bytes 1081352 | tf_op jit(solution)/shard_map/ppermute | solution.py:17
  56.3 0.7 copy-start.4
  57.0 0.7 copy-start.6
  57.8 1.0 %copy-start.5 = (bf16[1,704,256]{2,1,0:T(8,128)(2,1)S(1)}, bf16[1,704,256]{2,1,0:T(8,128)(2,1)}, u32[]{:S(2)}) copy-start(bf16[1,704,256]{2,1,0:T(8,128)(2,1)} %copy-done.4) | copy-start | bytes 1081348
  58.7 1.0 %copy-start.7 = (bf16[1,704,256]{2,1,0:T(8,128)(2,1)S(1)}, bf16[1,704,256]{2,1,0:T(8,128)(2,1)}, u32[]{:S(2)}) copy-start(bf16[1,704,256]{2,1,0:T(8,128)(2,1)} %copy-done.6) | copy-start | bytes 1081348
  60.7 2.0 %collective-permute-start.13 = (bf16[4,32,2048]{2,1,0:T(8,128)(2,1)S(1)}, bf16[4,32,2048]{2,1,0:T(8,128)(2,1)S(1)}, u32[]{:S(2)}, u32[]{:S(2)}) collective-permute-start(bf16[4,32,2048]{2,1,0:T(8,128)(2,1)S(1)} %dynamic-slice_bitcast_fusion), channel_id=1, source_target_pairs={{0,1},{1,0},{2,3},{3,2},{4,5},{5,4},{6,7},{7,6},{8,9},{9,8},{10,11... | collective-permute-start | bytes 1572872 | tf_op jit(solution)/shard_map/ppermute | solution.py:17
  62.9 7.5 %collective-permute-start.14 = (bf16[32,2048]{1,0:T(8,128)(2,1)S(1)}, bf16[32,2048]{1,0:T(8,128)(2,1)S(1)}, u32[]{:S(2)}, u32[]{:S(2)}) collective-permute-start(bf16[32,2048]{1,0:T(8,128)(2,1)S(1)} %get-tuple-element.16), channel_id=1, source_target_pairs={{0,2},{1,3},{2,0},{3,1},{4,6},{5,7},{6,4},{7,5},{8,10},{9,11},{10,... | collective-permute-start | bytes 393224 | tf_op jit(solution)/shard_map/ppermute | solution.py:17
  64.5 12.9 %collective-permute-start.15 = (bf16[32,2048]{1,0:T(8,128)(2,1)S(1)}, bf16[32,2048]{1,0:T(8,128)(2,1)S(1)}, u32[]{:S(2)}, u32[]{:S(2)}) collective-permute-start(bf16[32,2048]{1,0:T(8,128)(2,1)S(1)} %get-tuple-element.18), channel_id=1, source_target_pairs={{0,4},{1,5},{2,6},{3,7},{4,0},{5,1},{6,2},{7,3},{8,12},{9,13},{10,... | collective-permute-start | bytes 393224 | tf_op jit(solution)/shard_map/ppermute | solution.py:17
  67.1 10.3 %collective-permute-start.16 = (bf16[32,2048]{1,0:T(8,128)(2,1)S(1)}, bf16[32,2048]{1,0:T(8,128)(2,1)S(1)}, u32[]{:S(2)}, u32[]{:S(2)}) collective-permute-start(bf16[32,2048]{1,0:T(8,128)(2,1)S(1)} %get-tuple-element.17), channel_id=1, source_target_pairs={{0,6},{1,7},{2,4},{3,5},{4,2},{5,3},{6,0},{7,1},{8,14},{9,15},{10,... | collective-permute-start | bytes 393224 | tf_op jit(solution)/shard_map/ppermute | solution.py:17

commit v2 on v0

v2 whole, which is shorter than its diff:
```python
import functools

import jax
import jax.numpy as jnp
from jax import lax
from jax.experimental import pallas as pl
from jax.experimental.pallas import tpu as pltpu
from jax.sharding import PartitionSpec as P

SEG = 256
SOFT_CAP = 8.0
VMEM = pl.BlockSpec(memory_space=pltpu.VMEM)
SMEM = pl.BlockSpec(memory_space=pltpu.SMEM)
F32 = jnp.float32
BF16 = jnp.bfloat16


def swap(value, axis, step):
    count = lax.axis_size(axis)
    return lax.ppermute(value, axis, [(i, i ^ step) for i in range(count)])


def call(kernel, outs, in_specs, args, flops, moved, scratch=()):
    return pl.pallas_call(
        kernel,
        out_shape=[jax.ShapeDtypeStruct(shape, dtype) for shape, dtype in outs],
        in_specs=in_specs,
        out_specs=[VMEM] * len(outs),
        scratch_shapes=list(scratch),
        compiler_params=pltpu.CompilerParams(vmem_limit_bytes=20 * 2**20),
        cost_estimate=pl.CostEstimate(flops=flops, bytes_accessed=moved, transcendentals=0),
    )(*args)


def prepare_kernel(dp, own_segs, my_dp, core, tokens, router, carry, logits, own, *sends):
    rows, width = tokens.shape
    half, depth = rows // 2, own.shape[1]
    shape = (logits.shape[0], rows)
    member = lax.broadcasted_iota(jnp.int32, shape, 1) // SEG
    ones = jnp.where(member == lax.broadcasted_iota(jnp.int32, shape, 0), 1.0, 0.0).astype(BF16)
    means = jnp.dot(ones, tokens[...], preferred_element_type=F32) / SEG
    place = lax.broadcasted_iota(jnp.int32, means.shape, 0)
    means = jnp.where(place == own_segs, carry[...], means)
    logits[...] = lax.dot_general(
        means,
        router[...],
        (((1,), (1,)), ((), ())),
        precision=lax.Precision.HIGHEST,
        preferred_element_type=F32,
    )
    start = pl.multiple_of(core[0] * half, half)
    for k in range(1, dp):
        column = pl.multiple_of((my_dp[0] ^ k) * depth, depth)
        sends[k - 1][...] = tokens[pl.ds(start, half), pl.ds(column, depth)]
    own[...] = tokens[:, pl.ds(pl.multiple_of(my_dp[0] * depth, depth), depth)]


def spread_probs(my_dp, tables, own_segs, steps, block):
    experts = tables[0].shape[1]
    raws = []
    for k in steps:
        for j in range(own_segs):
            prior = (my_dp ^ k) * own_segs + j - 1
            raw = tables[0][own_segs : own_segs + 1, :]
            for q, table in enumerate(tables):
                for i in range(own_segs):
                    here = (my_dp ^ q) * own_segs + i == prior
                    raw = jnp.where(here, table[i : i + 1, :], raw)
            raws.append(raw)
    logits = SOFT_CAP * jnp.tanh(jnp.concatenate(raws, axis=0) / SOFT_CAP)
    scores = jnp.exp(logits)
    probs = (scores / jnp.sum(scores, axis=1, keepdims=True)).astype(BF16).astype(F32)
    shape = (experts, experts * block)
    ahead = lax.broadcasted_iota(jnp.int32, shape, 1) // block
    spread = jnp.where(ahead == lax.broadcasted_iota(jnp.int32, shape, 0), 1.0, 0.0)
    wide = jnp.dot(probs, spread, preferred_element_type=F32)
    shape = (block, experts * block)
    diagonal = lax.broadcasted_iota(jnp.int32, shape, 1) % block == lax.broadcasted_iota(
        jnp.int32, shape, 0
    )
    return jnp.concatenate(
        [jnp.where(diagonal, wide[s : s + 1, :], 0.0) for s in range(len(raws))], axis=0
    ).astype(BF16)


def merge_kernel(dp, own_segs, steps, block, count, my_dp, *refs):
    tables, weights, outs = refs[:dp], refs[dp : dp + count], refs[-len(steps) :]
    tables = [table[...] for table in tables]
    mix = spread_probs(my_dp[0], tables, own_segs, steps, block)
    experts, rows, cols = weights[0].shape
    for w, weight in enumerate(weights):
        for start in range(0, rows, block):
            tile = weight[:, start : start + block, :].reshape(experts * block, cols)
            out = jnp.dot(mix, tile, preferred_element_type=F32).astype(BF16)
            out = out.reshape(len(steps), own_segs, block, cols)
            at = w * rows + start
            for k in range(len(steps)):
                outs[k][:, at : at + block, :] = out[k]


def merge(my_dp, tables, own_segs, steps, weights, after=()):
    experts, rows, cols = weights[0].shape
    block = 32 if rows % 32 == 0 else 16
    total = rows * len(weights)
    count = len(weights)
    dp = len(tables)

    def kernel(my_dp_ref, *refs):
        merge_kernel(
            dp, own_segs, steps, block, count, my_dp_ref, *refs[: dp + count], *refs[-len(steps) :]
        )

    segs = own_segs * len(steps)
    return call(
        kernel,
        [((own_segs, total, cols), BF16)] * len(steps),
        [SMEM] + [VMEM] * (dp + count) + [pl.BlockSpec(memory_space=pl.ANY)] * len(after),
        (my_dp, *tables, *weights, *after),
        2 * segs * total * cols * experts * block,
        2 * total * cols * (experts + segs),
    )


def preact_kernel(dp, core, own, *refs):
    brought, others, merged, outs = (
        refs[: dp - 1],
        refs[dp - 1 : 2 * dp - 2],
        refs[2 * dp - 2 : 3 * dp - 2],
        refs[3 * dp - 2 : 4 * dp - 2],
    )
    whole = refs[-1]
    half = own.shape[0] // 2
    near = pl.multiple_of(core[0] * half, half)
    far = pl.multiple_of((1 - core[0]) * half, half)
    for k in list(range(dp - 1, -1, -1)):
        if k > 0:
            whole[k - 1, pl.ds(near, half), :] = brought[k - 1][...]
            whole[k - 1, pl.ds(far, half), :] = others[k - 1][...]
        for j in range(merged[k].shape[0]):
            rows = slice(j * SEG, (j + 1) * SEG)
            outs[k][j] = lax.dot_general(
                merged[k][j],
                own[rows, :] if k == 0 else whole[k - 1, rows, :],
                (((1,), (1,)), ((), ())),
                preferred_element_type=F32,
            ).astype(BF16)


def preact(core, own, brought, others, merged):
    dp = len(merged)
    own_segs, total, depth = merged[0].shape
    segs = dp * own_segs
    return call(
        functools.partial(preact_kernel, dp),
        [((own_segs, total, SEG), BF16)] * dp,
        [SMEM] + [VMEM] * (3 * dp - 1),
        (core, own, *brought, *others, *merged),
        2 * segs * total * SEG * depth,
        2 * segs * (total * depth + SEG * depth + total * SEG),
        [pltpu.VMEM((dp - 1, own_segs * SEG, depth), BF16)],
    )


def down_columns(core, hidden, downs, mixed):
    own_segs, cols = downs[0].shape[0], downs[0].shape[2]
    rows = mixed.shape[2]
    for j in range(own_segs):
        for k, down in enumerate(downs):
            out = lax.dot_general(
                hidden[j], down[j], (((0,), (0,)), ((), ())), preferred_element_type=F32
            ).astype(BF16)
            for i in range(SEG // rows):
                at = j * (SEG // rows) + i
                mixed[(at % 2) ^ core, at // 2, :, k * cols : (k + 1) * cols] = out[
                    i * rows : (i + 1) * rows
                ]


def first_kernel(dp, core, *refs):
    parts, downs, (hidden, mixed) = refs[:dp], refs[dp:-2], refs[-2:]
    half = hidden.shape[1]
    kept = []
    for j in range(hidden.shape[0]):
        total = parts[0][j].astype(F32)
        for part in parts[1:]:
            total += part[j].astype(F32)
        gate, up = total[:half], total[half:]
        kept.append((gate / (1.0 + jnp.exp(-gate)) * up).astype(BF16))
        hidden[j] = kept[j]
    down_columns(core[0], kept, downs, mixed)


def second_kernel(core, hidden, *refs):
    down_columns(core[0], hidden, refs[:-1], refs[-1])


def finish_kernel(groups, lines, my_dp, *refs):
    out = refs[-1]
    for g, steps in enumerate(groups):
        pieces = refs[g * lines : (g + 1) * lines]
        cols = pieces[0].shape[1] // len(steps)
        total = pieces[0][...].astype(F32)
        for piece in pieces[1:]:
            total += piece[...].astype(F32)
        total = total.astype(BF16)
        for k, step in enumerate(steps):
            at = pl.multiple_of((my_dp[0] ^ step) * cols, cols)
            out[:, pl.ds(at, cols)] = total[:, k * cols : (k + 1) * cols]


def tensor_sum_pieces(mixed, lines):
    my_line = lax.axis_index("tensor") // 2
    pair = mixed[0].astype(F32) + swap(mixed[1], "tensor", 1).astype(F32)
    pair = pair.astype(BF16)
    pieces = [lax.dynamic_index_in_dim(pair, my_line ^ k, 0, keepdims=False) for k in range(lines)]
    return [pieces[0]] + [swap(pieces[k], "tensor", 2 * k) for k in range(1, lines)]


def on_device(tokens, gate_weight, up_weight, down_weight, router_weight, carry_mean):
    dp = lax.axis_size("dp")
    tensor = lax.axis_size("tensor")
    lines = tensor // 2
    my_dp = lax.axis_index("dp").reshape(1)
    core = (lax.axis_index("tensor") % 2).reshape(1)
    own_rows, width = tokens.shape
    own_segs = own_rows // SEG
    experts, depth, hidden_count = gate_weight.shape
    cols = down_weight.shape[2]
    steps = tuple(range(dp))
    late = tuple(k for k in steps if k.bit_count() == 1)
    early = tuple(k for k in steps if k not in late)

    table_rows = -(-(own_segs + 1) // 8) * 8
    logits, own, *sends = call(
        functools.partial(prepare_kernel, dp, own_segs),
        [((table_rows, experts), F32), ((own_rows, depth), BF16)]
        + [((own_rows // 2, depth), BF16)] * (dp - 1),
        [SMEM, SMEM, VMEM, VMEM, VMEM],
        (my_dp, core, tokens, router_weight.T, carry_mean.reshape(1, width)),
        2 * table_rows * own_rows * width,
        4 * own_rows * width,
    )
    tables = [logits] + [swap(logits, "dp", k) for k in range(1, dp)]
    brought = [swap(sends[k - 1], "dp", k) for k in range(1, dp)]
    others = [swap(piece, "tensor", 1) for piece in brought]

    merged_early = merge(my_dp, tables, own_segs, early, (down_weight,))
    downs = {k: block if k == 0 else swap(block, "dp", k) for k, block in zip(early, merged_early)}

    gate_up = (jnp.swapaxes(gate_weight, 1, 2), jnp.swapaxes(up_weight, 1, 2))
    merged = merge(my_dp, tables, own_segs, steps, gate_up)
    partial_pre = preact(core, own, brought, others, merged)
    parts = [partial_pre[0]] + [swap(partial_pre[k], "dp", k) for k in range(1, dp)]

    merged_late = merge(my_dp, tables, own_segs, late, (down_weight,), (partial_pre[0],))
    for k, block in zip(late, merged_late):
        downs[k] = swap(block, "dp", k)

    rows = own_rows // tensor
    half_flops = own_rows * hidden_count * cols
    hidden, mixed_early = call(
        functools.partial(first_kernel, dp),
        [
            ((own_segs, hidden_count, SEG), BF16),
            ((2, lines, rows, len(early) * cols), BF16),
        ],
        [SMEM] + [VMEM] * (dp + len(early)),
        (core, *parts, *[downs[k] for k in early]),
        2 * half_flops * len(early),
        2 * (own_rows * hidden_count * 3 + hidden_count * cols * len(early)),
    )
    early_pieces = tensor_sum_pieces(mixed_early, lines)
    (mixed_late,) = call(
        second_kernel,
        [((2, lines, rows, len(late) * cols), BF16)],
        [SMEM] + [VMEM] * (1 + len(late)),
        (core, hidden, *[downs[k] for k in late]),
        2 * half_flops * len(late),
        2 * (own_rows * hidden_count + hidden_count * cols * len(late)),
    )
    late_pieces = tensor_sum_pieces(mixed_late, lines)
    (out,) = call(
        functools.partial(finish_kernel, (early, late), lines),
        [((rows, width), BF16)],
        [SMEM] + [VMEM] * (2 * lines),
        (my_dp, *early_pieces, *late_pieces),
        rows * width * lines,
        2 * rows * width * (lines + 1),
    )
    return out


def solution(mesh):
    placed = (
        P("dp", None),
        P(None, "dp", "tensor"),
        P(None, "dp", "tensor"),
        P(None, "tensor", "dp"),
        P(),
        P(),
    )
    return jax.shard_map(
        on_device, mesh=mesh, in_specs=placed, out_specs=P(("dp", "tensor"), None), check_vma=False
    )
```

time: 210 us -> 80.2 us (0.38)
  local copies, waits for them, and re-layouts: 54.2 us -> 6.49 us
  waiting for transfers between devices: 85 us -> 45 us
  blocking collectives: 35.5 us -> 0 us
  starting transfers between devices: 5.47 us -> 22.1 us
  between operations: 13.5 us -> 0.19 us
  matrix products: 12.9 us -> 0 us
  Pallas kernels: 0 us -> 6.03 us
  other arithmetic: 2.78 us -> 0.13 us
    unnamed x3 -> x0, waiting for transfers between devices: 58.5 us -> none
    ppermute x0 -> x23, waiting for transfers between devices: none -> 45 us  [swap(): return lax.ppermute(value, axis, [(i, i ^ step) for i in range(count)])]
    unnamed x19 -> x14, local copies, waits for them, and re-layouts: 35.2 us -> 6.4 us
    reduce_scatter x1 -> x0, waiting for transfers between devices: 26.5 us -> none  [on_device(): lax.psum_scatter(jnp.concatenate([gate_part, up_part], axis=2).reshape(co...]
    ppermute x0 -> x23, starting transfers between devices: none -> 22.1 us  [swap(): return lax.ppermute(value, axis, [(i, i ^ step) for i in range(count)])]
    all_gather x1 -> x0, blocking collectives: 16.6 us -> none  [on_device(): all_hidden = lax.all_gather(hidden, 'dp', axis=0, tiled=True)]
    reshape x4 -> x0, local copies, waits for them, and re-layouts: 15.4 us -> none  [the longest x1 4.6 us: on_device(): gate_flat = gate_weight.reshape(experts, slice_rows * hidden_cols)]
    dot_general x8 -> x0, matrix products: 12.9 us -> none  [the longest x1 3.89 us: on_device(): jnp.dot(probs_bf, gate_flat, preferred_element_type=jnp.float32)]
  transfers between devices with their start and end apart: 3 -> 23, of which waited for: 2 -> 13; matrix products, arithmetic and copies ran while one was open for 15% -> 0% of each run, Pallas kernels for 0% -> 4%
where the time goes in v2:
time: 80.2 us; the launch traced here: 79.9 us
  waiting for transfers between devices  45 us (56%)
  starting transfers between devices  22.1 us (28%)
  local copies, waits for them, and re-layouts  6.49 us (8%)
  Pallas kernels  6.03 us (8%)
    ppermute x23, waiting for transfers between devices, swap(): return lax.ppermute(value, axis, [(i, i ^ step) for i in range(count)])  45 us
    ppermute x23, starting transfers between devices, swap(): return lax.ppermute(value, axis, [(i, i ^ step) for i in range(count)])  22.1 us
    unnamed x14, local copies, waits for them, and re-layouts  6.4 us
    pallas_call x8, Pallas kernels, call(): pl.pallas_call(kernel, out_shape=[jax.ShapeDtypeStruct(shape, dtype) for...  6.03 us
  transfers between devices with their start and end apart: 23, of which 13 were waited for; matrix products, arithmetic and copies ran while one was open for 0% of the time, Pallas kernels for 4%

profile of v2, /device:TPU:0, one launch (start us, length us, event | category | flops | bytes accessed | tf_op | source)
XLA Modules:
  0.0 79.9 jit_solution(14183182226704106064)
XLA Ops:
  0.0 1.2 %copy-done.4 = bf16[256,2048]{1,0:T(8,128)(2,1)S(1)} copy-done((bf16[256,2048]{1,0:T(8,128)(2,1)S(1)}, bf16[256,2048]{1,0:T(8,128)(2,1)}, u32[]{:S(2)}) %copy-start.4) | copy-done | bytes 1048600
  1.2 0.8 %copy-done.5 = f32[2048,8]{0,1:T(8,128)S(1)} copy-done((f32[2048,8]{0,1:T(8,128)S(1)}, f32[2048,8]{0,1:T(8,128)}, u32[]{:S(2)}) %copy-start.5) | copy-done | bytes 65560
  2.1 0.7 copy-done.6
  2.8 0.5 shard_map.64
  3.3 2.9 %collective-permute-start.6 = (f32[8,8]{1,0:T(8,128)S(1)}, f32[8,8]{1,0:T(8,128)S(1)}, u32[]{:S(2)}, u32[]{:S(2)}) collective-permute-start(f32[8,8]{1,0:T(8,128)S(1)} %get-tuple-element.28.refs_0_), channel_id=1, source_target_pairs={{0,8},{8,0},{16,24},{24,16},{1,9},{9,1},{17,25},{25,17},{2,10},{10... | collective-permute-start | bytes 776 | tf_op jit(solution)/shard_map/ppermute | solution.py:20
  6.2 1.5 %collective-permute-start.7 = (f32[8,8]{1,0:T(8,128)S(1)}, f32[8,8]{1,0:T(8,128)S(1)}, u32[]{:S(2)}, u32[]{:S(2)}) collective-permute-start(f32[8,8]{1,0:T(8,128)S(1)} %get-tuple-element.28.refs_0_), channel_id=1, source_target_pairs={{0,16},{8,24},{16,0},{24,8},{1,17},{9,25},{17,1},{25,9},{2,18},{10... | collective-permute-start | bytes 776 | tf_op jit(solution)/shard_map/ppermute | solution.py:20
  7.7 0.1 collective-permute-done.6.refs_1_
  7.8 2.0 %collective-permute-done.7.refs_2_ = f32[8,8]{1,0:T(8,128)S(1)} collective-permute-done((f32[8,8]{1,0:T(8,128)S(1)}, f32[8,8]{1,0:T(8,128)S(1)}, u32[]{:S(2)}, u32[]{:S(2)}) %collective-permute-start.7) | collective-permute-done | bytes 288 | tf_op jit(solution)/shard_map/ppermute | solution.py:20
  9.8 2.4 %collective-permute-done.8.refs_3_ = f32[8,8]{1,0:T(8,128)S(1)} collective-permute-done((f32[8,8]{1,0:T(8,128)S(1)}, f32[8,8]{1,0:T(8,128)S(1)}, u32[]{:S(2)}, u32[]{:S(2)}) %collective-permute-start.8) | collective-permute-done | bytes 288 | tf_op jit(solution)/shard_map/ppermute | solution.py:20
  12.2 1.8 %copy-done = bf16[8,352,512]{2,1,0:T(8,128)(2,1)S(1)} copy-done((bf16[8,352,512]{2,1,0:T(8,128)(2,1)S(1)}, bf16[8,352,512]{2,1,0:T(8,128)(2,1)}, u32[]{:S(2)}) %copy-start) | copy-done | bytes 2883608
  14.0 0.8 %shard_map.67 = (bf16[1,352,512]{2,1,0:T(8,128)(2,1)S(1)}, bf16[1,352,512]{2,1,0:T(8,128)(2,1)S(1)}) custom-call(s32[1]{0:T(128)} %bitcast.my_dp.my_dp_ref, f32[8,8]{1,0:T(8,128)S(1)} %get-tuple-element.28.refs_0_, f32[8,8]{1,0:T(8,128)S(1)} %collective-permute-done.6.refs_1_, f32[8,8]{1,0:T(8,128)S(1)} %collective-permute-done.7.refs_2_, ...), custom_call_target="tpu_custom_call" | custom-call | flops 184549376 | bytes 3604480 | tf_op jit(solution)/shard_map/pallas_call | solution.py:24
  14.9 0.1 collective-permute-start.12
  14.9 2.0 %collective-permute-start = (bf16[128,512]{1,0:T(8,128)(2,1)S(1)}, bf16[128,512]{1,0:T(8,128)(2,1)S(1)}, u32[]{:S(2)}, u32[]{:S(2)}) collective-permute-start(bf16[128,512]{1,0:T(8,128)(2,1)S(1)} %get-tuple-element.25), channel_id=1, source_target_pairs={{0,8},{8,0},{16,24},{24,16},{1,9},{9,1},{17,25},{25,17},{2,10},{10... | collective-permute-start | bytes 393224 | tf_op jit(solution)/shard_map/ppermute | solution.py:20
  16.9 1.5 %collective-permute-start.1 = (bf16[128,512]{1,0:T(8,128)(2,1)S(1)}, bf16[128,512]{1,0:T(8,128)(2,1)S(1)}, u32[]{:S(2)}, u32[]{:S(2)}) collective-permute-start(bf16[128,512]{1,0:T(8,128)(2,1)S(1)} %get-tuple-element.26), channel_id=1, source_target_pairs={{0,16},{8,24},{16,0},{24,8},{1,17},{9,25},{17,1},{25,9},{2,18},{10... | collective-permute-start | bytes 393224 | tf_op jit(solution)/shard_map/ppermute | solution.py:20
  18.4 0.1 collective-permute-start.2
  18.5 9.1 %collective-permute-done.refs_0_ = bf16[128,512]{1,0:T(8,128)(2,1)S(1)} collective-permute-done((bf16[128,512]{1,0:T(8,128)(2,1)S(1)}, bf16[128,512]{1,0:T(8,128)(2,1)S(1)}, u32[]{:S(2)}, u32[]{:S(2)}) %collective-permute-start) | collective-permute-done | bytes 131104 | tf_op jit(solution)/shard_map/ppermute | solution.py:20
  27.6 0.9 %collective-permute-done.1.refs_1_ = bf16[128,512]{1,0:T(8,128)(2,1)S(1)} collective-permute-done((bf16[128,512]{1,0:T(8,128)(2,1)S(1)}, bf16[128,512]{1,0:T(8,128)(2,1)S(1)}, u32[]{:S(2)}, u32[]{:S(2)}) %collective-permute-start.1) | collective-permute-done | bytes 131104 | tf_op jit(solution)/shard_map/ppermute | solution.py:20
  28.5 0.0 collective-permute-start.4
  28.5 1.4 %collective-permute-done.2.refs_2_ = bf16[128,512]{1,0:T(8,128)(2,1)S(1)} collective-permute-done((bf16[128,512]{1,0:T(8,128)(2,1)S(1)}, bf16[128,512]{1,0:T(8,128)(2,1)S(1)}, u32[]{:S(2)}, u32[]{:S(2)}) %collective-permute-start.2) | collective-permute-done | bytes 131104 | tf_op jit(solution)/shard_map/ppermute | solution.py:20
  29.9 1.8 %copy-done.3 = bf16[8,512,352]{1,2,0:T(8,128)(2,1)S(1)} copy-done((bf16[8,512,352]{1,2,0:T(8,128)(2,1)S(1)}, bf16[8,512,352]{1,2,0:T(8,128)(2,1)}, u32[]{:S(2)}) %copy-start.3) | copy-done | bytes 2883608
  31.7 1.1 %shard_map.65 = (bf16[1,704,512]{2,1,0:T(8,128)(2,1)S(1)}, bf16[1,704,512]{2,1,0:T(8,128)(2,1)S(1)}, bf16[1,704,512]{2,1,0:T(8,128)(2,1)S(1)}, bf16[1,704,512]{2,1,0:T(8,128)(2,1)S(1)}) custom-call(s32[1]{0:T(128)} %bitcast.my_dp.my_dp_ref, f32[8,8]{1,0:T(8,128)S(1)} %get-tuple-element.28.refs_0_, f32[8,8]{1,0:T(8,128)S(1)} %collective-permute-done.6.refs_1_, ...), custom_call_target="tpu_custom_call" | custom-call | flops 738197504 | bytes 8650752 | tf_op jit(solution)/shard_map/pallas_call | solution.py:24
  32.9 1.0 %shard_map.66 = (bf16[1,704,256]{2,1,0:T(8,128)(2,1)S(1)}, bf16[1,704,256]{2,1,0:T(8,128)(2,1)S(1)}, bf16[1,704,256]{2,1,0:T(8,128)(2,1)S(1)}, bf16[1,704,256]{2,1,0:T(8,128)(2,1)S(1)}) custom-call(s32[1]{0:T(128)} %bitcast.1.core, bf16[256,512]{1,0:T(8,128)(2,1)S(1)} %get-tuple-element.24.own, bf16[128,512]{1,0:T(8,128)(2,1)S(1)} %collective-permute-done.refs_0_, ...), custom_call_target="tpu_custom_call" | custom-call | flops 738197504 | bytes 5373952 | tf_op jit(solution)/shard_map/pallas_call | solution.py:24
  33.9 0.6 collective-permute-start.10
  34.5 1.5 %collective-permute-start.11 = (bf16[1,704,256]{2,1,0:T(8,128)(2,1)S(1)}, bf16[1,704,256]{2,1,0:T(8,128)(2,1)S(1)}, u32[]{:S(2)}, u32[]{:S(2)}) collective-permute-start(bf16[1,704,256]{2,1,0:T(8,128)(2,1)S(1)} %get-tuple-element.36), channel_id=1, source_target_pairs={{0,24},{8,16},{16,8},{24,0},{1,25},{9,17},{17,9},{25,1},{2,26},{10... | collective-permute-start | bytes 1081352 | tf_op jit(solution)/shard_map/ppermute | solution.py:20
  36.0 1.5 %collective-permute-start.9 = (bf16[1,704,256]{2,1,0:T(8,128)(2,1)S(1)}, bf16[1,704,256]{2,1,0:T(8,128)(2,1)S(1)}, u32[]{:S(2)}, u32[]{:S(2)}) collective-permute-start(bf16[1,704,256]{2,1,0:T(8,128)(2,1)S(1)} %get-tuple-element.34), channel_id=1, source_target_pairs={{0,8},{8,0},{16,24},{24,16},{1,9},{9,1},{17,25},{25,17},{2,10},{10... | collective-permute-start | bytes 1081352 | tf_op jit(solution)/shard_map/ppermute | solution.py:20
  37.5 0.8 %shard_map.69 = (bf16[1,352,512]{2,1,0:T(8,128)(2,1)S(1)}, bf16[1,352,512]{2,1,0:T(8,128)(2,1)S(1)}) custom-call(s32[1]{0:T(128)} %bitcast.my_dp.my_dp_ref, f32[8,8]{1,0:T(8,128)S(1)} %get-tuple-element.28.refs_0_, f32[8,8]{1,0:T(8,128)S(1)} %collective-permute-done.6.refs_1_, f32[8,8]{1,0:T(8,128)S(1)} %collective-permute-done.7.refs_2_, ...), custom_call_target="tpu_custom_call" | custom-call | flops 184549376 | bytes 3604480 | tf_op jit(solution)/shard_map/pallas_call | solution.py:24
  38.3 0.6 collective-permute-start.17
  38.9 0.3 collective-permute-start.18
  39.2 13.7 %collective-permute-done.10.refs_2_ = bf16[1,704,256]{2,1,0:T(8,128)(2,1)S(1)} collective-permute-done((bf16[1,704,256]{2,1,0:T(8,128)(2,1)S(1)}, bf16[1,704,256]{2,1,0:T(8,128)(2,1)S(1)}, u32[]{:S(2)}, u32[]{:S(2)}) %collective-permute-start.10) | collective-permute-done | bytes 360480 | tf_op jit(solution)/shard_map/ppermute | solution.py:20
  52.9 1.5 %collective-permute-done.9.refs_1_ = bf16[1,704,256]{2,1,0:T(8,128)(2,1)S(1)} collective-permute-done((bf16[1,704,256]{2,1,0:T(8,128)(2,1)S(1)}, bf16[1,704,256]{2,1,0:T(8,128)(2,1)S(1)}, u32[]{:S(2)}, u32[]{:S(2)}) %collective-permute-start.9) | collective-permute-done | bytes 360480 | tf_op jit(solution)/shard_map/ppermute | solution.py:20
  54.5 0.6 shard_map.68
  55.1 6.4 %collective-permute-done.17.refs_0_ = bf16[1,352,512]{2,1,0:T(8,128)(2,1)S(1)} collective-permute-done((bf16[1,352,512]{2,1,0:T(8,128)(2,1)S(1)}, bf16[1,352,512]{2,1,0:T(8,128)(2,1)S(1)}, u32[]{:S(2)}, u32[]{:S(2)}) %collective-permute-start.17) | collective-permute-done | bytes 360480 | tf_op jit(solution)/shard_map/ppermute | solution.py:20
  61.5 0.5 shard_map.70
  62.0 0.1 collective-permute-start.19
  62.1 0.5 collective-permute-start.13
  62.6 0.9 %collective-permute-done.19 = bf16[4,32,1024]{2,1,0:T(8,128)(2,1)S(1)} collective-permute-done((bf16[4,32,1024]{2,1,0:T(8,128)(2,1)S(1)}, bf16[4,32,1024]{2,1,0:T(8,128)(2,1)S(1)}, u32[]{:S(2)}, u32[]{:S(2)}) %collective-permute-start.19) | collective-permute-done | bytes 262176 | tf_op jit(solution)/shard_map/ppermute | solution.py:20
  63.6 0.1 fusion
  63.7 1.6 %collective-permute-start.20 = (bf16[32,1024]{1,0:T(8,128)(2,1)S(1)}, bf16[32,1024]{1,0:T(8,128)(2,1)S(1)}, u32[]{:S(2)}, u32[]{:S(2)}) collective-permute-start(bf16[32,1024]{1,0:T(8,128)(2,1)S(1)} %get-tuple-element.45), channel_id=1, source_target_pairs={{0,2},{1,3},{2,0},{3,1},{4,6},{5,7},{6,4},{7,5},{8,10},{9,11},{10,... | collective-permute-start | bytes 196616 | tf_op jit(solution)/shard_map/ppermute | solution.py:20
  65.3 2.6 %collective-permute-start.21 = (bf16[32,1024]{1,0:T(8,128)(2,1)S(1)}, bf16[32,1024]{1,0:T(8,128)(2,1)S(1)}, u32[]{:S(2)}, u32[]{:S(2)}) collective-permute-start(bf16[32,1024]{1,0:T(8,128)(2,1)S(1)} %get-tuple-element.44), channel_id=1, source_target_pairs={{0,4},{1,5},{2,6},{3,7},{4,0},{5,1},{6,2},{7,3},{8,12},{9,13},{10,... | collective-permute-start | bytes 196616 | tf_op jit(solution)/shard_map/ppermute | solution.py:20
  67.9 0.2 collective-permute-start.22
  68.1 0.1 fusion.1
  68.2 0.7 collective-permute-start.14
  69.0 3.5 %collective-permute-start.15 = (bf16[32,1024]{1,0:T(8,128)(2,1)S(1)}, bf16[32,1024]{1,0:T(8,128)(2,1)S(1)}, u32[]{:S(2)}, u32[]{:S(2)}) collective-permute-start(bf16[32,1024]{1,0:T(8,128)(2,1)S(1)} %get-tuple-element.48), channel_id=1, source_target_pairs={{0,4},{1,5},{2,6},{3,7},{4,0},{5,1},{6,2},{7,3},{8,12},{9,13},{10,... | collective-permute-start | bytes 196616 | tf_op jit(solution)/shard_map/ppermute | solution.py:20
  72.5 0.2 collective-permute-start.16
  72.7 0.2 collective-permute-done.21.refs_6_
  72.9 1.9 %collective-permute-done.22.refs_7_ = bf16[32,1024]{1,0:T(8,128)(2,1)S(1)} collective-permute-done((bf16[32,1024]{1,0:T(8,128)(2,1)S(1)}, bf16[32,1024]{1,0:T(8,128)(2,1)S(1)}, u32[]{:S(2)}, u32[]{:S(2)}) %collective-permute-start.22) | collective-permute-done | bytes 65568 | tf_op jit(solution)/shard_map/ppermute | solution.py:20
  74.8 4.4 %collective-permute-done.15.refs_2_ = bf16[32,1024]{1,0:T(8,128)(2,1)S(1)} collective-permute-done((bf16[32,1024]{1,0:T(8,128)(2,1)S(1)}, bf16[32,1024]{1,0:T(8,128)(2,1)S(1)}, u32[]{:S(2)}, u32[]{:S(2)}) %collective-permute-start.15) | collective-permute-done | bytes 65568 | tf_op jit(solution)/shard_map/ppermute | solution.py:20
  79.2 0.7 shard_map.71
  (26 shorter events, 0.1 us)
Async XLA Ops:
  0.0 1.2 %copy-start.4 = (bf16[256,2048]{1,0:T(8,128)(2,1)S(1)}, bf16[256,2048]{1,0:T(8,128)(2,1)}, u32[]{:S(2)}) copy-start(bf16[256,2048]{1,0:T(8,128)(2,1)} %tokens.1) | copy-start | bytes 3145732
  1.2 0.8 %copy-start.5 = (f32[2048,8]{0,1:T(8,128)S(1)}, f32[2048,8]{0,1:T(8,128)}, u32[]{:S(2)}) copy-start(f32[2048,8]{0,1:T(8,128)} %param.10) | copy-start | bytes 196612
  2.1 0.7 copy-start.6
  3.3 4.5 %collective-permute-start.6 = (f32[8,8]{1,0:T(8,128)S(1)}, f32[8,8]{1,0:T(8,128)S(1)}, u32[]{:S(2)}, u32[]{:S(2)}) collective-permute-start(f32[8,8]{1,0:T(8,128)S(1)} %get-tuple-element.28.refs_0_), channel_id=1, source_target_pairs={{0,8},{8,0},{16,24},{24,16},{1,9},{9,1},{17,25},{25,17},{2,10},{10... | collective-permute-start | bytes 776 | tf_op jit(solution)/shard_map/ppermute | solution.py:20
  6.2 3.6 %collective-permute-start.7 = (f32[8,8]{1,0:T(8,128)S(1)}, f32[8,8]{1,0:T(8,128)S(1)}, u32[]{:S(2)}, u32[]{:S(2)}) collective-permute-start(f32[8,8]{1,0:T(8,128)S(1)} %get-tuple-element.28.refs_0_), channel_id=1, source_target_pairs={{0,16},{8,24},{16,0},{24,8},{1,17},{9,25},{17,1},{25,9},{2,18},{10... | collective-permute-start | bytes 776 | tf_op jit(solution)/shard_map/ppermute | solution.py:20
  7.7 4.5 %collective-permute-start.8 = (f32[8,8]{1,0:T(8,128)S(1)}, f32[8,8]{1,0:T(8,128)S(1)}, u32[]{:S(2)}, u32[]{:S(2)}) collective-permute-start(f32[8,8]{1,0:T(8,128)S(1)} %get-tuple-element.28.refs_0_), channel_id=1, source_target_pairs={{0,24},{8,16},{16,8},{24,0},{1,25},{9,17},{17,9},{25,1},{2,26},{10... | collective-permute-start | bytes 776 | tf_op jit(solution)/shard_map/ppermute | solution.py:20
  12.2 1.8 %copy-start = (bf16[8,352,512]{2,1,0:T(8,128)(2,1)S(1)}, bf16[8,352,512]{2,1,0:T(8,128)(2,1)}, u32[]{:S(2)}) copy-start(bf16[8,352,512]{2,1,0:T(8,128)(2,1)} %refs_4_.3) | copy-start | bytes 8650756
  14.0 15.9 %copy-start.2 = (bf16[8,512,352]{1,2,0:T(8,128)(2,1)S(1)}, bf16[8,512,352]{1,2,0:T(8,128)(2,1)}, u32[]{:S(2)}) copy-start(bf16[8,512,352]{1,2,0:T(8,128)(2,1)} %param.7) | copy-start | bytes 8650756
  14.9 24.0 %collective-permute-start.12 = (bf16[1,352,512]{2,1,0:T(8,128)(2,1)S(1)}, bf16[1,352,512]{2,1,0:T(8,128)(2,1)S(1)}, u32[]{:S(2)}, u32[]{:S(2)}) collective-permute-start(bf16[1,352,512]{2,1,0:T(8,128)(2,1)S(1)} %get-tuple-element.38), channel_id=1, source_target_pairs={{0,24},{8,16},{16,8},{24,0},{1,25},{9,17},{17,9},{25,1},{2,26},{10... | collective-permute-start | bytes 1081352 | tf_op jit(solution)/shard_map/ppermute | solution.py:20
  14.9 12.6 %collective-permute-start = (bf16[128,512]{1,0:T(8,128)(2,1)S(1)}, bf16[128,512]{1,0:T(8,128)(2,1)S(1)}, u32[]{:S(2)}, u32[]{:S(2)}) collective-permute-start(bf16[128,512]{1,0:T(8,128)(2,1)S(1)} %get-tuple-element.25), channel_id=1, source_target_pairs={{0,8},{8,0},{16,24},{24,16},{1,9},{9,1},{17,25},{25,17},{2,10},{10... | collective-permute-start | bytes 393224 | tf_op jit(solution)/shard_map/ppermute | solution.py:20
  16.9 11.6 %collective-permute-start.1 = (bf16[128,512]{1,0:T(8,128)(2,1)S(1)}, bf16[128,512]{1,0:T(8,128)(2,1)S(1)}, u32[]{:S(2)}, u32[]{:S(2)}) collective-permute-start(bf16[128,512]{1,0:T(8,128)(2,1)S(1)} %get-tuple-element.26), channel_id=1, source_target_pairs={{0,16},{8,24},{16,0},{24,8},{1,17},{9,25},{17,1},{25,9},{2,18},{10... | collective-permute-start | bytes 393224 | tf_op jit(solution)/shard_map/ppermute | solution.py:20
  18.4 11.5 %collective-permute-start.2 = (bf16[128,512]{1,0:T(8,128)(2,1)S(1)}, bf16[128,512]{1,0:T(8,128)(2,1)S(1)}, u32[]{:S(2)}, u32[]{:S(2)}) collective-permute-start(bf16[128,512]{1,0:T(8,128)(2,1)S(1)} %get-tuple-element.27), channel_id=1, source_target_pairs={{0,24},{8,16},{16,8},{24,0},{1,25},{9,17},{17,9},{25,1},{2,26},{10... | collective-permute-start | bytes 393224 | tf_op jit(solution)/shard_map/ppermute | solution.py:20
  27.6 5.3 %collective-permute-start.3 = (bf16[128,512]{1,0:T(8,128)(2,1)S(1)}, bf16[128,512]{1,0:T(8,128)(2,1)S(1)}, u32[]{:S(2)}, u32[]{:S(2)}) collective-permute-start(bf16[128,512]{1,0:T(8,128)(2,1)S(1)} %collective-permute-done.refs_0_), channel_id=1, source_target_pairs={{0,1},{1,0},{2,3},{3,2},{4,5},{5,4},{6,7},{7,6},{8,9},{9,8},{10,11... | collective-permute-start | bytes 393224 | tf_op jit(solution)/shard_map/ppermute | solution.py:20
  28.5 4.4 %collective-permute-start.4 = (bf16[128,512]{1,0:T(8,128)(2,1)S(1)}, bf16[128,512]{1,0:T(8,128)(2,1)S(1)}, u32[]{:S(2)}, u32[]{:S(2)}) collective-permute-start(bf16[128,512]{1,0:T(8,128)(2,1)S(1)} %collective-permute-done.1.refs_1_), channel_id=1, source_target_pairs={{0,1},{1,0},{2,3},{3,2},{4,5},{5,4},{6,7},{7,6},{8,9},{9,8},{10,11... | collective-permute-start | bytes 393224 | tf_op jit(solution)/shard_map/ppermute | solution.py:20
  29.9 3.0 %collective-permute-start.5 = (bf16[128,512]{1,0:T(8,128)(2,1)S(1)}, bf16[128,512]{1,0:T(8,128)(2,1)S(1)}, u32[]{:S(2)}, u32[]{:S(2)}) collective-permute-start(bf16[128,512]{1,0:T(8,128)(2,1)S(1)} %collective-permute-done.2.refs_2_), channel_id=1, source_target_pairs={{0,1},{1,0},{2,3},{3,2},{4,5},{5,4},{6,7},{7,6},{8,9},{9,8},{10,11... | collective-permute-start | bytes 393224 | tf_op jit(solution)/shard_map/ppermute | solution.py:20
  29.9 1.8 %copy-start.3 = (bf16[8,512,352]{1,2,0:T(8,128)(2,1)S(1)}, bf16[8,512,352]{1,2,0:T(8,128)(2,1)}, u32[]{:S(2)}) copy-start(bf16[8,512,352]{1,2,0:T(8,128)(2,1)} %param.8) | copy-start | bytes 8650756
  32.9 4.6 %copy-start.1 = (bf16[8,352,512]{2,1,0:T(8,128)(2,1)S(1)}, bf16[8,352,512]{2,1,0:T(8,128)(2,1)}, u32[]{:S(2)}) copy-start(bf16[8,352,512]{2,1,0:T(8,128)(2,1)} %refs_4_.3) | copy-start | bytes 8650756
  33.9 19.0 %collective-permute-start.10 = (bf16[1,704,256]{2,1,0:T(8,128)(2,1)S(1)}, bf16[1,704,256]{2,1,0:T(8,128)(2,1)S(1)}, u32[]{:S(2)}, u32[]{:S(2)}) collective-permute-start(bf16[1,704,256]{2,1,0:T(8,128)(2,1)S(1)} %get-tuple-element.35), channel_id=1, source_target_pairs={{0,16},{8,24},{16,0},{24,8},{1,17},{9,25},{17,1},{25,9},{2,18},{10... | collective-permute-start | bytes 1081352 | tf_op jit(solution)/shard_map/ppermute | solution.py:20
  34.5 18.4 %collective-permute-start.11 = (bf16[1,704,256]{2,1,0:T(8,128)(2,1)S(1)}, bf16[1,704,256]{2,1,0:T(8,128)(2,1)S(1)}, u32[]{:S(2)}, u32[]{:S(2)}) collective-permute-start(bf16[1,704,256]{2,1,0:T(8,128)(2,1)S(1)} %get-tuple-element.36), channel_id=1, source_target_pairs={{0,24},{8,16},{16,8},{24,0},{1,25},{9,17},{17,9},{25,1},{2,26},{10... | collective-permute-start | bytes 1081352 | tf_op jit(solution)/shard_map/ppermute | solution.py:20
  36.0 18.5 %collective-permute-start.9 = (bf16[1,704,256]{2,1,0:T(8,128)(2,1)S(1)}, bf16[1,704,256]{2,1,0:T(8,128)(2,1)S(1)}, u32[]{:S(2)}, u32[]{:S(2)}) collective-permute-start(bf16[1,704,256]{2,1,0:T(8,128)(2,1)S(1)} %get-tuple-element.34), channel_id=1, source_target_pairs={{0,8},{8,0},{16,24},{24,16},{1,9},{9,1},{17,25},{25,17},{2,10},{10... | collective-permute-start | bytes 1081352 | tf_op jit(solution)/shard_map/ppermute | solution.py:20
  38.3 23.2 %collective-permute-start.17 = (bf16[1,352,512]{2,1,0:T(8,128)(2,1)S(1)}, bf16[1,352,512]{2,1,0:T(8,128)(2,1)S(1)}, u32[]{:S(2)}, u32[]{:S(2)}) collective-permute-start(bf16[1,352,512]{2,1,0:T(8,128)(2,1)S(1)} %get-tuple-element.41), channel_id=1, source_target_pairs={{0,8},{8,0},{16,24},{24,16},{1,9},{9,1},{17,25},{25,17},{2,10},{10... | collective-permute-start | bytes 1081352 | tf_op jit(solution)/shard_map/ppermute | solution.py:20
  38.9 22.6 %collective-permute-start.18 = (bf16[1,352,512]{2,1,0:T(8,128)(2,1)S(1)}, bf16[1,352,512]{2,1,0:T(8,128)(2,1)S(1)}, u32[]{:S(2)}, u32[]{:S(2)}) collective-permute-start(bf16[1,352,512]{2,1,0:T(8,128)(2,1)S(1)} %get-tuple-element.42), channel_id=1, source_target_pairs={{0,16},{8,24},{16,0},{24,8},{1,17},{9,25},{17,1},{25,9},{2,18},{10... | collective-permute-start | bytes 1081352 | tf_op jit(solution)/shard_map/ppermute | solution.py:20
  62.0 1.6 %collective-permute-start.19 = (bf16[4,32,1024]{2,1,0:T(8,128)(2,1)S(1)}, bf16[4,32,1024]{2,1,0:T(8,128)(2,1)S(1)}, u32[]{:S(2)}, u32[]{:S(2)}) collective-permute-start(bf16[4,32,1024]{2,1,0:T(8,128)(2,1)S(1)} %slice_bitcast_fusion), channel_id=1, source_target_pairs={{0,1},{1,0},{2,3},{3,2},{4,5},{5,4},{6,7},{7,6},{8,9},{9,8},{10,11... | collective-permute-start | bytes 786440 | tf_op jit(solution)/shard_map/ppermute | solution.py:20
  62.1 6.0 %collective-permute-start.13 = (bf16[4,32,1024]{2,1,0:T(8,128)(2,1)S(1)}, bf16[4,32,1024]{2,1,0:T(8,128)(2,1)S(1)}, u32[]{:S(2)}, u32[]{:S(2)}) collective-permute-start(bf16[4,32,1024]{2,1,0:T(8,128)(2,1)S(1)} %slice_bitcast_fusion.2), channel_id=1, source_target_pairs={{0,1},{1,0},{2,3},{3,2},{4,5},{5,4},{6,7},{7,6},{8,9},{9,8},{10,11... | collective-permute-start | bytes 786440 | tf_op jit(solution)/shard_map/ppermute | solution.py:20
  63.7 8.8 %collective-permute-start.20 = (bf16[32,1024]{1,0:T(8,128)(2,1)S(1)}, bf16[32,1024]{1,0:T(8,128)(2,1)S(1)}, u32[]{:S(2)}, u32[]{:S(2)}) collective-permute-start(bf16[32,1024]{1,0:T(8,128)(2,1)S(1)} %get-tuple-element.45), channel_id=1, source_target_pairs={{0,2},{1,3},{2,0},{3,1},{4,6},{5,7},{6,4},{7,5},{8,10},{9,11},{10,... | collective-permute-start | bytes 196616 | tf_op jit(solution)/shard_map/ppermute | solution.py:20
  65.3 7.5 %collective-permute-start.21 = (bf16[32,1024]{1,0:T(8,128)(2,1)S(1)}, bf16[32,1024]{1,0:T(8,128)(2,1)S(1)}, u32[]{:S(2)}, u32[]{:S(2)}) collective-permute-start(bf16[32,1024]{1,0:T(8,128)(2,1)S(1)} %get-tuple-element.44), channel_id=1, source_target_pairs={{0,4},{1,5},{2,6},{3,7},{4,0},{5,1},{6,2},{7,3},{8,12},{9,13},{10,... | collective-permute-start | bytes 196616 | tf_op jit(solution)/shard_map/ppermute | solution.py:20
  67.9 6.9 %collective-permute-start.22 = (bf16[32,1024]{1,0:T(8,128)(2,1)S(1)}, bf16[32,1024]{1,0:T(8,128)(2,1)S(1)}, u32[]{:S(2)}, u32[]{:S(2)}) collective-permute-start(bf16[32,1024]{1,0:T(8,128)(2,1)S(1)} %get-tuple-element.43), channel_id=1, source_target_pairs={{0,6},{1,7},{2,4},{3,5},{4,2},{5,3},{6,0},{7,1},{8,14},{9,15},{10,... | collective-permute-start | bytes 196616 | tf_op jit(solution)/shard_map/ppermute | solution.py:20
  68.2 6.6 %collective-permute-start.14 = (bf16[32,1024]{1,0:T(8,128)(2,1)S(1)}, bf16[32,1024]{1,0:T(8,128)(2,1)S(1)}, u32[]{:S(2)}, u32[]{:S(2)}) collective-permute-start(bf16[32,1024]{1,0:T(8,128)(2,1)S(1)} %get-tuple-element.49), channel_id=1, source_target_pairs={{0,2},{1,3},{2,0},{3,1},{4,6},{5,7},{6,4},{7,5},{8,10},{9,11},{10,... | collective-permute-start | bytes 196616 | tf_op jit(solution)/shard_map/ppermute | solution.py:20
  69.0 10.2 %collective-permute-start.15 = (bf16[32,1024]{1,0:T(8,128)(2,1)S(1)}, bf16[32,1024]{1,0:T(8,128)(2,1)S(1)}, u32[]{:S(2)}, u32[]{:S(2)}) collective-permute-start(bf16[32,1024]{1,0:T(8,128)(2,1)S(1)} %get-tuple-element.48), channel_id=1, source_target_pairs={{0,4},{1,5},{2,6},{3,7},{4,0},{5,1},{6,2},{7,3},{8,12},{9,13},{10,... | collective-permute-start | bytes 196616 | tf_op jit(solution)/shard_map/ppermute | solution.py:20
  72.5 6.7 %collective-permute-start.16 = (bf16[32,1024]{1,0:T(8,128)(2,1)S(1)}, bf16[32,1024]{1,0:T(8,128)(2,1)S(1)}, u32[]{:S(2)}, u32[]{:S(2)}) collective-permute-start(bf16[32,1024]{1,0:T(8,128)(2,1)S(1)} %get-tuple-element.47), channel_id=1, source_target_pairs={{0,6},{1,7},{2,4},{3,5},{4,2},{5,3},{6,0},{7,1},{8,14},{9,15},{10,... | collective-permute-start | bytes 196616 | tf_op jit(solution)/shard_map/ppermute | solution.py:20

commit v3 on v2

--- a/solution.py
+++ b/solution.py
@@ -13,11 +13,18 @@
 SMEM = pl.BlockSpec(memory_space=pltpu.SMEM)
 F32 = jnp.float32
 BF16 = jnp.bfloat16
+LANES = 128
+HBM = pl.BlockSpec(memory_space=pltpu.HBM)
+ANY = pl.BlockSpec(memory_space=pl.ANY)
 
 
 def swap(value, axis, step):
     count = lax.axis_size(axis)
     return lax.ppermute(value, axis, [(i, i ^ step) for i in range(count)])
+
+
+def in_hbm(value):
+    return pltpu.with_memory_space_constraint(value, pltpu.HBM)
 
 
 def call(kernel, outs, in_specs, args, flops, moved, scratch=()):
@@ -27,32 +34,88 @@
         in_specs=in_specs,
         out_specs=[VMEM] * len(outs),
         scratch_shapes=list(scratch),
-        compiler_params=pltpu.CompilerParams(vmem_limit_bytes=20 * 2**20),
+        compiler_params=pltpu.CompilerParams(vmem_limit_bytes=24 * 2**20),
         cost_estimate=pl.CostEstimate(flops=flops, bytes_accessed=moved, transcendentals=0),
     )(*args)
 
 
-def prepare_kernel(dp, own_segs, my_dp, core, tokens, router, carry, logits, own, *sends):
-    rows, width = tokens.shape
-    half, depth = rows // 2, own.shape[1]
-    shape = (logits.shape[0], rows)
-    member = lax.broadcasted_iota(jnp.int32, shape, 1) // SEG
-    ones = jnp.where(member == lax.broadcasted_iota(jnp.int32, shape, 0), 1.0, 0.0).astype(BF16)
-    means = jnp.dot(ones, tokens[...], preferred_element_type=F32) / SEG
-    place = lax.broadcasted_iota(jnp.int32, means.shape, 0)
-    means = jnp.where(place == own_segs, carry[...], means)
-    logits[...] = lax.dot_general(
-        means,
-        router[...],
-        (((1,), (1,)), ((), ())),
+def prepare_kernel(dp, own_segs, my_dp, core, tokens, router, carry, own, *refs):
+    sends, (blocks, routers, carries, sems) = refs[: dp - 1], refs[dp - 1 :]
+    rows, depth = own.shape
+    half = rows // 2
+    extra = sends[0].shape[0] - half
+    experts = router.shape[0]
+    columns = [pl.multiple_of((my_dp[0] ^ k) * depth, depth) for k in range(dp)]
+    copies = [
+        pltpu.make_async_copy(
+            tokens.at[:, pl.ds(columns[k], depth)],
+            own if k == 0 else blocks.at[k - 1],
+            sems.at[k],
+        )
+        for k in range(dp)
+    ]
+    copies.append(pltpu.make_async_copy(router, routers, sems.at[dp]))
+    copies.append(pltpu.make_async_copy(carry, carries, sems.at[dp + 1]))
+    for copy in copies[dp:] + copies[:dp]:
+        copy.start()
+    member = lax.broadcasted_iota(jnp.int32, (extra, rows), 1) // SEG
+    ones = member == lax.broadcasted_iota(jnp.int32, (extra, rows), 0)
+    ones = jnp.where(ones, 1.0, 0.0).astype(BF16)
+    start = pl.multiple_of(core[0] * half, half)
+    copies[dp].wait()
+    copies[dp + 1].wait()
+    logits = jnp.zeros((extra, experts), F32)
+    for k in range(dp):
+        copies[k].wait()
+        block = own[...] if k == 0 else blocks[k - 1]
+        means = jnp.dot(ones, block, preferred_element_type=F32) / SEG
+        place = lax.broadcasted_iota(jnp.int32, means.shape, 0)
+        means = jnp.where(place == own_segs, carries[:, pl.ds(columns[k], depth)], means)
+        logits += lax.dot_general(
+            means,
+            routers[:, pl.ds(columns[k], depth)],
+            (((1,), (1,)), ((), ())),
+            precision=lax.Precision.HIGHEST,
+            preferred_element_type=F32,
+        )
+        if k > 0:
+            sends[k - 1][:half] = blocks[k - 1, pl.ds(start, half), :]
+    lane = lax.broadcasted_iota(jnp.int32, (experts, LANES), 1)
+    copied = lane % experts == lax.broadcasted_iota(jnp.int32, (experts, LANES), 0)
+    logits = jnp.dot(
+        logits,
+        jnp.where(copied, 1.0, 0.0),
         precision=lax.Precision.HIGHEST,
         preferred_element_type=F32,
     )
-    start = pl.multiple_of(core[0] * half, half)
-    for k in range(1, dp):
-        column = pl.multiple_of((my_dp[0] ^ k) * depth, depth)
-        sends[k - 1][...] = tokens[pl.ds(start, half), pl.ds(column, depth)]
-    own[...] = tokens[:, pl.ds(pl.multiple_of(my_dp[0] * depth, depth), depth)]
+    high = logits.astype(BF16).astype(F32)
+    middle = (logits - high).astype(BF16).astype(F32)
+    low = logits - high - middle
+    lane = lax.broadcasted_iota(jnp.int32, logits.shape, 1)
+    terms = jnp.where(lane < experts, high, jnp.where(lane < 2 * experts, middle, low))
+    terms = jnp.where(lane < 3 * experts, terms, 0.0).astype(BF16)
+    for send in sends:
+        send[half:] = jnp.zeros((extra, depth), BF16)
+        send[half:, :LANES] = terms
+
+
+def load_kernel(count, *refs):
+    sources, targets, sems = refs[:count], refs[-count - 1 : -1], refs[-1]
+    copies = [
+        pltpu.make_async_copy(source, target, sems.at[i])
+        for i, (source, target) in enumerate(zip(sources, targets))
+    ]
+    for copy in copies:
+        copy.start()
+    for copy in copies:
+        copy.wait()
+
+
+def read_table(piece, half, experts):
+    lane = lax.broadcasted_iota(jnp.int32, (LANES, experts), 0)
+    summed = lane % experts == lax.broadcasted_iota(jnp.int32, (LANES, experts), 1)
+    summed = jnp.where(summed & (lane < 3 * experts), 1.0, 0.0).astype(BF16)
+    return jnp.dot(piece[half:, :LANES], summed, preferred_element_type=F32)
 
 
 def spread_probs(my_dp, tables, own_segs, steps, block):
@@ -83,59 +146,58 @@
     ).astype(BF16)
 
 
-def merge_kernel(dp, own_segs, steps, block, count, my_dp, *refs):
-    tables, weights, outs = refs[:dp], refs[dp : dp + count], refs[-len(steps) :]
-    tables = [table[...] for table in tables]
-    mix = spread_probs(my_dp[0], tables, own_segs, steps, block)
+def route_kernel(dp, own_segs, block, my_dp, sent, *refs):
+    pieces, (stacked, mix) = refs[: dp - 1], refs[-2:]
+    half = stacked.shape[1]
+    for k, piece in enumerate(pieces):
+        stacked[k] = piece[:half]
+    experts = mix.shape[1] // block
+    tables = [read_table(piece, half, experts) for piece in (sent, *pieces)]
+    mix[...] = spread_probs(my_dp[0], tables, own_segs, tuple(range(dp)), block)
+
+
+def merge_kernel(own_segs, mix, *refs):
+    weights, outs = refs
     experts, rows, cols = weights[0].shape
+    block = mix.shape[1] // experts
     for w, weight in enumerate(weights):
         for start in range(0, rows, block):
             tile = weight[:, start : start + block, :].reshape(experts * block, cols)
-            out = jnp.dot(mix, tile, preferred_element_type=F32).astype(BF16)
-            out = out.reshape(len(steps), own_segs, block, cols)
+            out = jnp.dot(mix[...], tile, preferred_element_type=F32).astype(BF16)
+            out = out.reshape(len(outs), own_segs, block, cols)
             at = w * rows + start
-            for k in range(len(steps)):
+            for k in range(len(outs)):
                 outs[k][:, at : at + block, :] = out[k]
 
 
-def merge(my_dp, tables, own_segs, steps, weights, after=()):
+def merge(mix, dp, own_segs, weights, after=()):
     experts, rows, cols = weights[0].shape
-    block = 32 if rows % 32 == 0 else 16
     total = rows * len(weights)
     count = len(weights)
-    dp = len(tables)
-
-    def kernel(my_dp_ref, *refs):
-        merge_kernel(
-            dp, own_segs, steps, block, count, my_dp_ref, *refs[: dp + count], *refs[-len(steps) :]
-        )
-
-    segs = own_segs * len(steps)
+
+    def kernel(mix_ref, *refs):
+        merge_kernel(own_segs, mix_ref, refs[:count], refs[-dp:])
+
     return call(
         kernel,
-        [((own_segs, total, cols), BF16)] * len(steps),
-        [SMEM] + [VMEM] * (dp + count) + [pl.BlockSpec(memory_space=pl.ANY)] * len(after),
-        (my_dp, *tables, *weights, *after),
-        2 * segs * total * cols * experts * block,
-        2 * total * cols * (experts + segs),
+        [((own_segs, total, cols), BF16)] * dp,
+        [VMEM] * (1 + count) + [ANY] * len(after),
+        (mix, *weights, *after),
+        2 * mix.size * total * cols // rows,
+        2 * total * cols * (experts + dp * own_segs),
     )
 
 
 def preact_kernel(dp, core, own, *refs):
-    brought, others, merged, outs = (
-        refs[: dp - 1],
-        refs[dp - 1 : 2 * dp - 2],
-        refs[2 * dp - 2 : 3 * dp - 2],
-        refs[3 * dp - 2 : 4 * dp - 2],
-    )
-    whole = refs[-1]
+    brought, other = refs[: dp - 1], refs[dp - 1]
+    merged, outs, whole = refs[dp : 2 * dp], refs[2 * dp : 3 * dp], refs[-1]
     half = own.shape[0] // 2
     near = pl.multiple_of(core[0] * half, half)
     far = pl.multiple_of((1 - core[0]) * half, half)
     for k in list(range(dp - 1, -1, -1)):
         if k > 0:
-            whole[k - 1, pl.ds(near, half), :] = brought[k - 1][...]
-            whole[k - 1, pl.ds(far, half), :] = others[k - 1][...]
+            whole[k - 1, pl.ds(near, half), :] = brought[k - 1][:half]
+            whole[k - 1, pl.ds(far, half), :] = other[k - 1]
         for j in range(merged[k].shape[0]):
             rows = slice(j * SEG, (j + 1) * SEG)
             outs[k][j] = lax.dot_general(
@@ -146,15 +208,15 @@
             ).astype(BF16)
 
 
-def preact(core, own, brought, others, merged):
+def preact(core, own, brought, other, merged):
     dp = len(merged)
     own_segs, total, depth = merged[0].shape
     segs = dp * own_segs
     return call(
         functools.partial(preact_kernel, dp),
         [((own_segs, total, SEG), BF16)] * dp,
-        [SMEM] + [VMEM] * (3 * dp - 1),
-        (core, own, *brought, *others, *merged),
+        [SMEM] + [VMEM] * (2 * dp + 1),
+        (core, own, *brought, other, *merged),
         2 * segs * total * SEG * depth,
         2 * segs * (total * depth + SEG * depth + total * SEG),
         [pltpu.VMEM((dp - 1, own_segs * SEG, depth), BF16)],
@@ -190,8 +252,8 @@
     down_columns(core[0], kept, downs, mixed)
 
 
-def second_kernel(core, hidden, *refs):
-    down_columns(core[0], hidden, refs[:-1], refs[-1])
+def second_kernel(count, core, hidden, *refs):
+    down_columns(core[0], hidden, refs[:count], refs[-1])
 
 
 def finish_kernel(groups, lines, my_dp, *refs):
@@ -227,34 +289,52 @@
     experts, depth, hidden_count = gate_weight.shape
     cols = down_weight.shape[2]
     steps = tuple(range(dp))
+    segs = dp * own_segs
     late = tuple(k for k in steps if k.bit_count() == 1)
     early = tuple(k for k in steps if k not in late)
 
-    table_rows = -(-(own_segs + 1) // 8) * 8
-    logits, own, *sends = call(
+    extra = -(-(own_segs + 1) // 16) * 16
+    own, *sends = call(
         functools.partial(prepare_kernel, dp, own_segs),
-        [((table_rows, experts), F32), ((own_rows, depth), BF16)]
-        + [((own_rows // 2, depth), BF16)] * (dp - 1),
-        [SMEM, SMEM, VMEM, VMEM, VMEM],
-        (my_dp, core, tokens, router_weight.T, carry_mean.reshape(1, width)),
-        2 * table_rows * own_rows * width,
+        [((own_rows, depth), BF16)] + [((own_rows // 2 + extra, depth), BF16)] * (dp - 1),
+        [SMEM, SMEM, HBM, HBM, HBM],
+        (my_dp, core, *map(in_hbm, (tokens, router_weight.T, carry_mean.reshape(1, width)))),
+        2 * extra * own_rows * width,
         4 * own_rows * width,
-    )
-    tables = [logits] + [swap(logits, "dp", k) for k in range(1, dp)]
+        [
+            pltpu.VMEM((dp - 1, own_rows, depth), BF16),
+            pltpu.VMEM((experts, width), F32),
+            pltpu.VMEM((1, width), F32),
+            pltpu.SemaphoreType.DMA((dp + 2,)),
+        ],
+    )
     brought = [swap(sends[k - 1], "dp", k) for k in range(1, dp)]
-    others = [swap(piece, "tensor", 1) for piece in brought]
-
-    merged_early = merge(my_dp, tables, own_segs, early, (down_weight,))
-    downs = {k: block if k == 0 else swap(block, "dp", k) for k, block in zip(early, merged_early)}
-
-    gate_up = (jnp.swapaxes(gate_weight, 1, 2), jnp.swapaxes(up_weight, 1, 2))
-    merged = merge(my_dp, tables, own_segs, steps, gate_up)
-    partial_pre = preact(core, own, brought, others, merged)
+    weights = (jnp.swapaxes(gate_weight, 1, 2), jnp.swapaxes(up_weight, 1, 2), down_weight)
+    gate_t, up_t, down = call(
+        functools.partial(load_kernel, len(weights)),
+        [(weight.shape, BF16) for weight in weights],
+        [HBM] * len(weights) + [ANY],
+        (*[in_hbm(weight) for weight in weights], own),
+        0,
+        12 * gate_weight.size,
+        [pltpu.SemaphoreType.DMA((len(weights),))],
+    )
+    block = 32 if hidden_count % 32 == 0 else 16
+    stacked, mix = call(
+        functools.partial(route_kernel, dp, own_segs, block),
+        [((dp - 1, own_rows // 2, depth), BF16), ((segs * block, experts * block), BF16)],
+        [SMEM] + [VMEM] * dp + [ANY],
+        (my_dp, sends[0], *brought, down),
+        0,
+        2 * own_rows * width,
+    )
+    other = swap(stacked, "tensor", 1)
+    merged = merge(mix, dp, own_segs, (gate_t, up_t))
+    partial_pre = preact(core, own, brought, other, merged)
     parts = [partial_pre[0]] + [swap(partial_pre[k], "dp", k) for k in range(1, dp)]
 
-    merged_late = merge(my_dp, tables, own_segs, late, (down_weight,), (partial_pre[0],))
-    for k, block in zip(late, merged_late):
-        downs[k] = swap(block, "dp", k)
+    merged_down = merge(mix, dp, own_segs, (down,), (partial_pre[0],))
+    downs = [block if k == 0 else swap(block, "dp", k) for k, block in enumerate(merged_down)]
 
     rows = own_rows // tensor
     half_flops = own_rows * hidden_count * cols
@@ -271,10 +351,10 @@
     )
     early_pieces = tensor_sum_pieces(mixed_early, lines)
     (mixed_late,) = call(
-        second_kernel,
+        functools.partial(second_kernel, len(late)),
         [((2, lines, rows, len(late) * cols), BF16)],
-        [SMEM] + [VMEM] * (1 + len(late)),
-        (core, hidden, *[downs[k] for k in late]),
+        [SMEM] + [VMEM] * (1 + len(late)) + [ANY],
+        (core, hidden, *[downs[k] for k in late], early_pieces[0]),
         2 * half_flops * len(late),
         2 * (own_rows * hidden_count + hidden_count * cols * len(late)),
     )

time: 80.2 us -> 73.1 us (0.911)
  local copies, waits for them, and re-layouts: 6.49 us -> 0.1 us
  Pallas kernels: 6.03 us -> 10.6 us
  waiting for transfers between devices: 45 us -> 40.9 us
  starting transfers between devices: 22.1 us -> 21.1 us
    unnamed x14 -> x0, local copies, waits for them, and re-layouts: 6.4 us -> none
    pallas_call x8 -> x9, Pallas kernels: 6.03 us -> 10.6 us  [call(): pl.pallas_call(kernel, out_shape=[jax.ShapeDtypeStruct(shape, dtype) for...]
    ppermute x23 -> x18, waiting for transfers between devices: 45 us -> 40.9 us  [swap(): return lax.ppermute(value, axis, [(i, i ^ step) for i in range(count)])]
    ppermute x23 -> x18, starting transfers between devices: 22.1 us -> 21.1 us  [swap(): return lax.ppermute(value, axis, [(i, i ^ step) for i in range(count)])]
  transfers between devices with their start and end apart: 23 -> 18, of which waited for: 13 -> 10; matrix products, arithmetic and copies ran while one was open for 0% -> 0% of each run, Pallas kernels for 4% -> 7%
where the time goes in v3:
time: 73.1 us; the launch traced here: 73 us
  waiting for transfers between devices  40.9 us (56%)
  starting transfers between devices  21.1 us (29%)
  Pallas kernels  10.6 us (15%)
    ppermute x18, waiting for transfers between devices, swap(): return lax.ppermute(value, axis, [(i, i ^ step) for i in range(count)])  40.9 us
    ppermute x18, starting transfers between devices, swap(): return lax.ppermute(value, axis, [(i, i ^ step) for i in range(count)])  21.1 us
    pallas_call x9, Pallas kernels, call(): pl.pallas_call(kernel, out_shape=[jax.ShapeDtypeStruct(shape, dtype) for...  10.6 us
  transfers between devices with their start and end apart: 18, of which 10 were waited for; matrix products, arithmetic and copies ran while one was open for 0% of the time, Pallas kernels for 7%

profile of v3, /device:TPU:0, one launch (start us, length us, event | category | flops | bytes accessed | tf_op | source)
XLA Modules:
  0.0 73.0 jit_solution(9218169953783149309)
XLA Ops:
  0.0 2.4 %shard_map.64 = (bf16[256,512]{1,0:T(8,128)(2,1)S(1)}, bf16[144,512]{1,0:T(8,128)(2,1)S(1)}, bf16[144,512]{1,0:T(8,128)(2,1)S(1)}, bf16[144,512]{1,0:T(8,128)(2,1)S(1)}) custom-call(s32[1]{0:T(128)} %bitcast.my_dp, s32[1]{0:T(128)} %bitcast.1.core, bf16[256,2048]{1,0:T(8,128)(2,1)} %tokens.1, f32[8,2048]{1,0:T(8,128)} %bitcast.36, f32[1,2048]{1,0:T(1,128)} %bitcast.37), custom_call_target="tpu_custom_call" | custom-call | flops 16777216 | bytes 2097152 | tf_op jit(solution)/shard_map/pallas_call | solution.py:31
  2.4 3.0 %collective-permute-start = (bf16[144,512]{1,0:T(8,128)(2,1)S(1)}, bf16[144,512]{1,0:T(8,128)(2,1)S(1)}, u32[]{:S(2)}, u32[]{:S(2)}) collective-permute-start(bf16[144,512]{1,0:T(8,128)(2,1)S(1)} %get-tuple-element.29.sent), channel_id=1, source_target_pairs={{0,8},{8,0},{16,24},{24,16},{1,9},{9,1},{17,25},{25,17},{2,10},{10... | collective-permute-start | bytes 442376 | tf_op jit(solution)/shard_map/ppermute | solution.py:23
  5.4 1.5 %collective-permute-start.1 = (bf16[144,512]{1,0:T(8,128)(2,1)S(1)}, bf16[144,512]{1,0:T(8,128)(2,1)S(1)}, u32[]{:S(2)}, u32[]{:S(2)}) collective-permute-start(bf16[144,512]{1,0:T(8,128)(2,1)S(1)} %get-tuple-element.30), channel_id=1, source_target_pairs={{0,16},{8,24},{16,0},{24,8},{1,17},{9,25},{17,1},{25,9},{2,18},{10... | collective-permute-start | bytes 442376 | tf_op jit(solution)/shard_map/ppermute | solution.py:23
  6.9 0.0 collective-permute-start.2
  6.9 3.6 %shard_map.65 = (bf16[8,352,512]{2,1,0:T(8,128)(2,1)S(1)}, bf16[8,352,512]{2,1,0:T(8,128)(2,1)S(1)}, bf16[8,352,512]{2,1,0:T(8,128)(2,1)S(1)}) custom-call(bf16[8,352,512]{2,1,0:T(8,128)(2,1)} %bitcast.34, bf16[8,352,512]{2,1,0:T(8,128)(2,1)} %bitcast.35, bf16[8,352,512]{2,1,0:T(8,128)(2,1)} %refs_2_.1, bf16[256,512]{1,0:T(8,128)(2,1)S(1)} %get-tuple-element.28.refs_3_.own), custom_call_target="tpu_custom_call" | custom-call | bytes 17301504 | tf_op jit(solution)/shard_map/pallas_call | solution.py:31
  10.5 0.0 collective-permute-done.refs_0_
  10.5 3.3 %collective-permute-done.1.refs_1_ = bf16[144,512]{1,0:T(8,128)(2,1)S(1)} collective-permute-done((bf16[144,512]{1,0:T(8,128)(2,1)S(1)}, bf16[144,512]{1,0:T(8,128)(2,1)S(1)}, u32[]{:S(2)}, u32[]{:S(2)}) %collective-permute-start.1) | collective-permute-done | bytes 147488 | tf_op jit(solution)/shard_map/ppermute | solution.py:23
  13.8 0.0 collective-permute-done.2.refs_2_
  13.8 0.4 shard_map.66
  14.2 0.1 collective-permute-start.3
  14.3 0.9 %shard_map.67 = (bf16[1,704,512]{2,1,0:T(8,128)(2,1)S(1)}, bf16[1,704,512]{2,1,0:T(8,128)(2,1)S(1)}, bf16[1,704,512]{2,1,0:T(8,128)(2,1)S(1)}, bf16[1,704,512]{2,1,0:T(8,128)(2,1)S(1)}) custom-call(bf16[128,256]{1,0:T(8,128)(2,1)S(1)} %get-tuple-element.34.mix_ref, bf16[8,352,512]{2,1,0:T(8,128)(2,1)S(1)} %get-tuple-element.35.refs_0_, ...), custom_call_target="tpu_custom_call" | custom-call | flops 67108864 | bytes 8650752 | tf_op jit(solution)/shard_map/pallas_call | solution.py:31
  15.2 0.8 %collective-permute-done.3.refs_3_ = bf16[3,128,512]{2,1,0:T(8,128)(2,1)S(1)} collective-permute-done((bf16[3,128,512]{2,1,0:T(8,128)(2,1)S(1)}, bf16[3,128,512]{2,1,0:T(8,128)(2,1)S(1)}, u32[]{:S(2)}, u32[]{:S(2)}) %collective-permute-start.3) | collective-permute-done | bytes 393248 | tf_op jit(solution)/shard_map/ppermute | solution.py:23
  16.0 1.0 %shard_map.68 = (bf16[1,704,256]{2,1,0:T(8,128)(2,1)S(1)}, bf16[1,704,256]{2,1,0:T(8,128)(2,1)S(1)}, bf16[1,704,256]{2,1,0:T(8,128)(2,1)S(1)}, bf16[1,704,256]{2,1,0:T(8,128)(2,1)S(1)}) custom-call(s32[1]{0:T(128)} %bitcast.1.core, bf16[256,512]{1,0:T(8,128)(2,1)S(1)} %get-tuple-element.28.refs_3_.own, bf16[144,512]{1,0:T(8,128)(2,1)S(1)} %collective-permute-done.refs_0_, ...), custom_call_target="tpu_custom_call" | custom-call | flops 738197504 | bytes 5373952 | tf_op jit(solution)/shard_map/pallas_call | solution.py:31
  17.0 1.3 %collective-permute-start.4 = (bf16[1,704,256]{2,1,0:T(8,128)(2,1)S(1)}, bf16[1,704,256]{2,1,0:T(8,128)(2,1)S(1)}, u32[]{:S(2)}, u32[]{:S(2)}) collective-permute-start(bf16[1,704,256]{2,1,0:T(8,128)(2,1)S(1)} %get-tuple-element.42), channel_id=1, source_target_pairs={{0,8},{8,0},{16,24},{24,16},{1,9},{9,1},{17,25},{25,17},{2,10},{10... | collective-permute-start | bytes 1081352 | tf_op jit(solution)/shard_map/ppermute | solution.py:23
  18.3 0.8 %collective-permute-start.5 = (bf16[1,704,256]{2,1,0:T(8,128)(2,1)S(1)}, bf16[1,704,256]{2,1,0:T(8,128)(2,1)S(1)}, u32[]{:S(2)}, u32[]{:S(2)}) collective-permute-start(bf16[1,704,256]{2,1,0:T(8,128)(2,1)S(1)} %get-tuple-element.43), channel_id=1, source_target_pairs={{0,16},{8,24},{16,0},{24,8},{1,17},{9,25},{17,1},{25,9},{2,18},{10... | collective-permute-start | bytes 1081352 | tf_op jit(solution)/shard_map/ppermute | solution.py:23
  19.1 1.4 %collective-permute-start.6 = (bf16[1,704,256]{2,1,0:T(8,128)(2,1)S(1)}, bf16[1,704,256]{2,1,0:T(8,128)(2,1)S(1)}, u32[]{:S(2)}, u32[]{:S(2)}) collective-permute-start(bf16[1,704,256]{2,1,0:T(8,128)(2,1)S(1)} %get-tuple-element.44), channel_id=1, source_target_pairs={{0,24},{8,16},{16,8},{24,0},{1,25},{9,17},{17,9},{25,1},{2,26},{10... | collective-permute-start | bytes 1081352 | tf_op jit(solution)/shard_map/ppermute | solution.py:23
  20.6 0.5 shard_map.69
  21.1 1.5 %collective-permute-start.7 = (bf16[1,352,512]{2,1,0:T(8,128)(2,1)S(1)}, bf16[1,352,512]{2,1,0:T(8,128)(2,1)S(1)}, u32[]{:S(2)}, u32[]{:S(2)}) collective-permute-start(bf16[1,352,512]{2,1,0:T(8,128)(2,1)S(1)} %get-tuple-element.46), channel_id=1, source_target_pairs={{0,24},{8,16},{16,8},{24,0},{1,25},{9,17},{17,9},{25,1},{2,26},{10... | collective-permute-start | bytes 1081352 | tf_op jit(solution)/shard_map/ppermute | solution.py:23
  22.6 5.7 %collective-permute-done.4.refs_1_ = bf16[1,704,256]{2,1,0:T(8,128)(2,1)S(1)} collective-permute-done((bf16[1,704,256]{2,1,0:T(8,128)(2,1)S(1)}, bf16[1,704,256]{2,1,0:T(8,128)(2,1)S(1)}, u32[]{:S(2)}, u32[]{:S(2)}) %collective-permute-start.4) | collective-permute-done | bytes 360480 | tf_op jit(solution)/shard_map/ppermute | solution.py:23
  28.3 14.0 %collective-permute-done.5.refs_2_ = bf16[1,704,256]{2,1,0:T(8,128)(2,1)S(1)} collective-permute-done((bf16[1,704,256]{2,1,0:T(8,128)(2,1)S(1)}, bf16[1,704,256]{2,1,0:T(8,128)(2,1)S(1)}, u32[]{:S(2)}, u32[]{:S(2)}) %collective-permute-start.5) | collective-permute-done | bytes 360480 | tf_op jit(solution)/shard_map/ppermute | solution.py:23
  42.3 0.0 collective-permute-done.6.refs_3_
  42.3 1.6 %collective-permute-done.7.refs_5_ = bf16[1,352,512]{2,1,0:T(8,128)(2,1)S(1)} collective-permute-done((bf16[1,352,512]{2,1,0:T(8,128)(2,1)S(1)}, bf16[1,352,512]{2,1,0:T(8,128)(2,1)S(1)}, u32[]{:S(2)}, u32[]{:S(2)}) %collective-permute-start.7) | collective-permute-done | bytes 360480 | tf_op jit(solution)/shard_map/ppermute | solution.py:23
  43.9 0.6 shard_map.70
  44.6 0.1 collective-permute-start.8
  44.7 0.9 %collective-permute-start.12 = (bf16[1,352,512]{2,1,0:T(8,128)(2,1)S(1)}, bf16[1,352,512]{2,1,0:T(8,128)(2,1)S(1)}, u32[]{:S(2)}, u32[]{:S(2)}) collective-permute-start(bf16[1,352,512]{2,1,0:T(8,128)(2,1)S(1)} %get-tuple-element.49), channel_id=1, source_target_pairs={{0,8},{8,0},{16,24},{24,16},{1,9},{9,1},{17,25},{25,17},{2,10},{10... | collective-permute-start | bytes 1081352 | tf_op jit(solution)/shard_map/ppermute | solution.py:23
  45.6 1.5 %collective-permute-start.13 = (bf16[1,352,512]{2,1,0:T(8,128)(2,1)S(1)}, bf16[1,352,512]{2,1,0:T(8,128)(2,1)S(1)}, u32[]{:S(2)}, u32[]{:S(2)}) collective-permute-start(bf16[1,352,512]{2,1,0:T(8,128)(2,1)S(1)} %get-tuple-element.50), channel_id=1, source_target_pairs={{0,16},{8,24},{16,0},{24,8},{1,17},{9,25},{17,1},{25,9},{2,18},{10... | collective-permute-start | bytes 1081352 | tf_op jit(solution)/shard_map/ppermute | solution.py:23
  47.1 0.0 collective-permute-done.8
  47.1 0.1 fusion.1
  47.2 8.3 %collective-permute-done.12.refs_0_ = bf16[1,352,512]{2,1,0:T(8,128)(2,1)S(1)} collective-permute-done((bf16[1,352,512]{2,1,0:T(8,128)(2,1)S(1)}, bf16[1,352,512]{2,1,0:T(8,128)(2,1)S(1)}, u32[]{:S(2)}, u32[]{:S(2)}) %collective-permute-start.12) | collective-permute-done | bytes 360480 | tf_op jit(solution)/shard_map/ppermute | solution.py:23
  55.5 0.5 collective-permute-done.13.refs_1_
  56.0 0.5 shard_map.71
  56.5 0.1 collective-permute-start.14
  56.6 1.6 %collective-permute-start.9 = (bf16[32,1024]{1,0:T(8,128)(2,1)S(1)}, bf16[32,1024]{1,0:T(8,128)(2,1)S(1)}, u32[]{:S(2)}, u32[]{:S(2)}) collective-permute-start(bf16[32,1024]{1,0:T(8,128)(2,1)S(1)} %get-tuple-element.57), channel_id=1, source_target_pairs={{0,2},{1,3},{2,0},{3,1},{4,6},{5,7},{6,4},{7,5},{8,10},{9,11},{10,... | collective-permute-start | bytes 196616 | tf_op jit(solution)/shard_map/ppermute | solution.py:23
  58.2 2.6 %collective-permute-start.10 = (bf16[32,1024]{1,0:T(8,128)(2,1)S(1)}, bf16[32,1024]{1,0:T(8,128)(2,1)S(1)}, u32[]{:S(2)}, u32[]{:S(2)}) collective-permute-start(bf16[32,1024]{1,0:T(8,128)(2,1)S(1)} %get-tuple-element.56), channel_id=1, source_target_pairs={{0,4},{1,5},{2,6},{3,7},{4,0},{5,1},{6,2},{7,3},{8,12},{9,13},{10,... | collective-permute-start | bytes 196616 | tf_op jit(solution)/shard_map/ppermute | solution.py:23
  60.8 0.2 collective-permute-start.11
  61.1 0.0 collective-permute-done.14
  61.1 0.1 fusion
  61.2 0.8 %collective-permute-start.15 = (bf16[32,1024]{1,0:T(8,128)(2,1)S(1)}, bf16[32,1024]{1,0:T(8,128)(2,1)S(1)}, u32[]{:S(2)}, u32[]{:S(2)}) collective-permute-start(bf16[32,1024]{1,0:T(8,128)(2,1)S(1)} %get-tuple-element.53), channel_id=1, source_target_pairs={{0,2},{1,3},{2,0},{3,1},{4,6},{5,7},{6,4},{7,5},{8,10},{9,11},{10,... | collective-permute-start | bytes 196616 | tf_op jit(solution)/shard_map/ppermute | solution.py:23
  61.9 3.5 %collective-permute-start.16 = (bf16[32,1024]{1,0:T(8,128)(2,1)S(1)}, bf16[32,1024]{1,0:T(8,128)(2,1)S(1)}, u32[]{:S(2)}, u32[]{:S(2)}) collective-permute-start(bf16[32,1024]{1,0:T(8,128)(2,1)S(1)} %get-tuple-element.52), channel_id=1, source_target_pairs={{0,4},{1,5},{2,6},{3,7},{4,0},{5,1},{6,2},{7,3},{8,12},{9,13},{10,... | collective-permute-start | bytes 196616 | tf_op jit(solution)/shard_map/ppermute | solution.py:23
  65.4 0.0 collective-permute-done.9.refs_1_
  65.4 0.2 collective-permute-start.17
  65.6 0.4 collective-permute-done.10.refs_2_
  66.0 1.6 %collective-permute-done.11.refs_3_ = bf16[32,1024]{1,0:T(8,128)(2,1)S(1)} collective-permute-done((bf16[32,1024]{1,0:T(8,128)(2,1)S(1)}, bf16[32,1024]{1,0:T(8,128)(2,1)S(1)}, u32[]{:S(2)}, u32[]{:S(2)}) %collective-permute-start.11) | collective-permute-done | bytes 65568 | tf_op jit(solution)/shard_map/ppermute | solution.py:23
  67.6 0.0 collective-permute-done.15.refs_5_
  67.6 4.7 %collective-permute-done.16.refs_6_ = bf16[32,1024]{1,0:T(8,128)(2,1)S(1)} collective-permute-done((bf16[32,1024]{1,0:T(8,128)(2,1)S(1)}, bf16[32,1024]{1,0:T(8,128)(2,1)S(1)}, u32[]{:S(2)}, u32[]{:S(2)}) %collective-permute-start.16) | collective-permute-done | bytes 65568 | tf_op jit(solution)/shard_map/ppermute | solution.py:23
  72.3 0.0 collective-permute-done.17.refs_7_
  72.3 0.7 shard_map.72
  (4 shorter events, 0.1 us)
Async XLA Ops:
  2.4 8.1 %collective-permute-start = (bf16[144,512]{1,0:T(8,128)(2,1)S(1)}, bf16[144,512]{1,0:T(8,128)(2,1)S(1)}, u32[]{:S(2)}, u32[]{:S(2)}) collective-permute-start(bf16[144,512]{1,0:T(8,128)(2,1)S(1)} %get-tuple-element.29.sent), channel_id=1, source_target_pairs={{0,8},{8,0},{16,24},{24,16},{1,9},{9,1},{17,25},{25,17},{2,10},{10... | collective-permute-start | bytes 442376 | tf_op jit(solution)/shard_map/ppermute | solution.py:23
  5.4 8.5 %collective-permute-start.1 = (bf16[144,512]{1,0:T(8,128)(2,1)S(1)}, bf16[144,512]{1,0:T(8,128)(2,1)S(1)}, u32[]{:S(2)}, u32[]{:S(2)}) collective-permute-start(bf16[144,512]{1,0:T(8,128)(2,1)S(1)} %get-tuple-element.30), channel_id=1, source_target_pairs={{0,16},{8,24},{16,0},{24,8},{1,17},{9,25},{17,1},{25,9},{2,18},{10... | collective-permute-start | bytes 442376 | tf_op jit(solution)/shard_map/ppermute | solution.py:23
  6.9 7.0 %collective-permute-start.2 = (bf16[144,512]{1,0:T(8,128)(2,1)S(1)}, bf16[144,512]{1,0:T(8,128)(2,1)S(1)}, u32[]{:S(2)}, u32[]{:S(2)}) collective-permute-start(bf16[144,512]{1,0:T(8,128)(2,1)S(1)} %get-tuple-element.31), channel_id=1, source_target_pairs={{0,24},{8,16},{16,8},{24,0},{1,25},{9,17},{17,9},{25,1},{2,26},{10... | collective-permute-start | bytes 442376 | tf_op jit(solution)/shard_map/ppermute | solution.py:23
  14.2 1.8 %collective-permute-start.3 = (bf16[3,128,512]{2,1,0:T(8,128)(2,1)S(1)}, bf16[3,128,512]{2,1,0:T(8,128)(2,1)S(1)}, u32[]{:S(2)}, u32[]{:S(2)}) collective-permute-start(bf16[3,128,512]{2,1,0:T(8,128)(2,1)S(1)} %get-tuple-element.33), channel_id=1, source_target_pairs={{0,1},{1,0},{2,3},{3,2},{4,5},{5,4},{6,7},{7,6},{8,9},{9,8},{10,11... | collective-permute-start | bytes 1179656 | tf_op jit(solution)/shard_map/ppermute | solution.py:23
  17.0 11.3 %collective-permute-start.4 = (bf16[1,704,256]{2,1,0:T(8,128)(2,1)S(1)}, bf16[1,704,256]{2,1,0:T(8,128)(2,1)S(1)}, u32[]{:S(2)}, u32[]{:S(2)}) collective-permute-start(bf16[1,704,256]{2,1,0:T(8,128)(2,1)S(1)} %get-tuple-element.42), channel_id=1, source_target_pairs={{0,8},{8,0},{16,24},{24,16},{1,9},{9,1},{17,25},{25,17},{2,10},{10... | collective-permute-start | bytes 1081352 | tf_op jit(solution)/shard_map/ppermute | solution.py:23
  18.3 24.0 %collective-permute-start.5 = (bf16[1,704,256]{2,1,0:T(8,128)(2,1)S(1)}, bf16[1,704,256]{2,1,0:T(8,128)(2,1)S(1)}, u32[]{:S(2)}, u32[]{:S(2)}) collective-permute-start(bf16[1,704,256]{2,1,0:T(8,128)(2,1)S(1)} %get-tuple-element.43), channel_id=1, source_target_pairs={{0,16},{8,24},{16,0},{24,8},{1,17},{9,25},{17,1},{25,9},{2,18},{10... | collective-permute-start | bytes 1081352 | tf_op jit(solution)/shard_map/ppermute | solution.py:23
  19.1 23.2 %collective-permute-start.6 = (bf16[1,704,256]{2,1,0:T(8,128)(2,1)S(1)}, bf16[1,704,256]{2,1,0:T(8,128)(2,1)S(1)}, u32[]{:S(2)}, u32[]{:S(2)}) collective-permute-start(bf16[1,704,256]{2,1,0:T(8,128)(2,1)S(1)} %get-tuple-element.44), channel_id=1, source_target_pairs={{0,24},{8,16},{16,8},{24,0},{1,25},{9,17},{17,9},{25,1},{2,26},{10... | collective-permute-start | bytes 1081352 | tf_op jit(solution)/shard_map/ppermute | solution.py:23
  21.1 22.8 %collective-permute-start.7 = (bf16[1,352,512]{2,1,0:T(8,128)(2,1)S(1)}, bf16[1,352,512]{2,1,0:T(8,128)(2,1)S(1)}, u32[]{:S(2)}, u32[]{:S(2)}) collective-permute-start(bf16[1,352,512]{2,1,0:T(8,128)(2,1)S(1)} %get-tuple-element.46), channel_id=1, source_target_pairs={{0,24},{8,16},{16,8},{24,0},{1,25},{9,17},{17,9},{25,1},{2,26},{10... | collective-permute-start | bytes 1081352 | tf_op jit(solution)/shard_map/ppermute | solution.py:23
  44.6 2.5 %collective-permute-start.8 = (bf16[4,32,1024]{2,1,0:T(8,128)(2,1)S(1)}, bf16[4,32,1024]{2,1,0:T(8,128)(2,1)S(1)}, u32[]{:S(2)}, u32[]{:S(2)}) collective-permute-start(bf16[4,32,1024]{2,1,0:T(8,128)(2,1)S(1)} %slice_bitcast_fusion.2), channel_id=1, source_target_pairs={{0,1},{1,0},{2,3},{3,2},{4,5},{5,4},{6,7},{7,6},{8,9},{9,8},{10,11... | collective-permute-start | bytes 786440 | tf_op jit(solution)/shard_map/ppermute | solution.py:23
  44.7 10.8 %collective-permute-start.12 = (bf16[1,352,512]{2,1,0:T(8,128)(2,1)S(1)}, bf16[1,352,512]{2,1,0:T(8,128)(2,1)S(1)}, u32[]{:S(2)}, u32[]{:S(2)}) collective-permute-start(bf16[1,352,512]{2,1,0:T(8,128)(2,1)S(1)} %get-tuple-element.49), channel_id=1, source_target_pairs={{0,8},{8,0},{16,24},{24,16},{1,9},{9,1},{17,25},{25,17},{2,10},{10... | collective-permute-start | bytes 1081352 | tf_op jit(solution)/shard_map/ppermute | solution.py:23
  45.6 10.5 %collective-permute-start.13 = (bf16[1,352,512]{2,1,0:T(8,128)(2,1)S(1)}, bf16[1,352,512]{2,1,0:T(8,128)(2,1)S(1)}, u32[]{:S(2)}, u32[]{:S(2)}) collective-permute-start(bf16[1,352,512]{2,1,0:T(8,128)(2,1)S(1)} %get-tuple-element.50), channel_id=1, source_target_pairs={{0,16},{8,24},{16,0},{24,8},{1,17},{9,25},{17,1},{25,9},{2,18},{10... | collective-permute-start | bytes 1081352 | tf_op jit(solution)/shard_map/ppermute | solution.py:23
  56.5 4.5 %collective-permute-start.14 = (bf16[4,32,1024]{2,1,0:T(8,128)(2,1)S(1)}, bf16[4,32,1024]{2,1,0:T(8,128)(2,1)S(1)}, u32[]{:S(2)}, u32[]{:S(2)}) collective-permute-start(bf16[4,32,1024]{2,1,0:T(8,128)(2,1)S(1)} %slice_bitcast_fusion), channel_id=1, source_target_pairs={{0,1},{1,0},{2,3},{3,2},{4,5},{5,4},{6,7},{7,6},{8,9},{9,8},{10,11... | collective-permute-start | bytes 786440 | tf_op jit(solution)/shard_map/ppermute | solution.py:23
  56.6 8.8 %collective-permute-start.9 = (bf16[32,1024]{1,0:T(8,128)(2,1)S(1)}, bf16[32,1024]{1,0:T(8,128)(2,1)S(1)}, u32[]{:S(2)}, u32[]{:S(2)}) collective-permute-start(bf16[32,1024]{1,0:T(8,128)(2,1)S(1)} %get-tuple-element.57), channel_id=1, source_target_pairs={{0,2},{1,3},{2,0},{3,1},{4,6},{5,7},{6,4},{7,5},{8,10},{9,11},{10,... | collective-permute-start | bytes 196616 | tf_op jit(solution)/shard_map/ppermute | solution.py:23
  58.2 7.7 %collective-permute-start.10 = (bf16[32,1024]{1,0:T(8,128)(2,1)S(1)}, bf16[32,1024]{1,0:T(8,128)(2,1)S(1)}, u32[]{:S(2)}, u32[]{:S(2)}) collective-permute-start(bf16[32,1024]{1,0:T(8,128)(2,1)S(1)} %get-tuple-element.56), channel_id=1, source_target_pairs={{0,4},{1,5},{2,6},{3,7},{4,0},{5,1},{6,2},{7,3},{8,12},{9,13},{10,... | collective-permute-start | bytes 196616 | tf_op jit(solution)/shard_map/ppermute | solution.py:23
  60.8 6.8 %collective-permute-start.11 = (bf16[32,1024]{1,0:T(8,128)(2,1)S(1)}, bf16[32,1024]{1,0:T(8,128)(2,1)S(1)}, u32[]{:S(2)}, u32[]{:S(2)}) collective-permute-start(bf16[32,1024]{1,0:T(8,128)(2,1)S(1)} %get-tuple-element.55), channel_id=1, source_target_pairs={{0,6},{1,7},{2,4},{3,5},{4,2},{5,3},{6,0},{7,1},{8,14},{9,15},{10,... | collective-permute-start | bytes 196616 | tf_op jit(solution)/shard_map/ppermute | solution.py:23
  61.2 6.4 %collective-permute-start.15 = (bf16[32,1024]{1,0:T(8,128)(2,1)S(1)}, bf16[32,1024]{1,0:T(8,128)(2,1)S(1)}, u32[]{:S(2)}, u32[]{:S(2)}) collective-permute-start(bf16[32,1024]{1,0:T(8,128)(2,1)S(1)} %get-tuple-element.53), channel_id=1, source_target_pairs={{0,2},{1,3},{2,0},{3,1},{4,6},{5,7},{6,4},{7,5},{8,10},{9,11},{10,... | collective-permute-start | bytes 196616 | tf_op jit(solution)/shard_map/ppermute | solution.py:23
  61.9 10.4 %collective-permute-start.16 = (bf16[32,1024]{1,0:T(8,128)(2,1)S(1)}, bf16[32,1024]{1,0:T(8,128)(2,1)S(1)}, u32[]{:S(2)}, u32[]{:S(2)}) collective-permute-start(bf16[32,1024]{1,0:T(8,128)(2,1)S(1)} %get-tuple-element.52), channel_id=1, source_target_pairs={{0,4},{1,5},{2,6},{3,7},{4,0},{5,1},{6,2},{7,3},{8,12},{9,13},{10,... | collective-permute-start | bytes 196616 | tf_op jit(solution)/shard_map/ppermute | solution.py:23
  65.4 6.9 %collective-permute-start.17 = (bf16[32,1024]{1,0:T(8,128)(2,1)S(1)}, bf16[32,1024]{1,0:T(8,128)(2,1)S(1)}, u32[]{:S(2)}, u32[]{:S(2)}) collective-permute-start(bf16[32,1024]{1,0:T(8,128)(2,1)S(1)} %get-tuple-element.51), channel_id=1, source_target_pairs={{0,6},{1,7},{2,4},{3,5},{4,2},{5,3},{6,0},{7,1},{8,14},{9,15},{10,... | collective-permute-start | bytes 196616 | tf_op jit(solution)/shard_map/ppermute | solution.py:23

commit v4 on v3

--- a/solution.py
+++ b/solution.py
@@ -170,7 +170,7 @@
                 outs[k][:, at : at + block, :] = out[k]
 
 
-def merge(mix, dp, own_segs, weights, after=()):
+def merge(mix, dp, own_segs, weights):
     experts, rows, cols = weights[0].shape
     total = rows * len(weights)
     count = len(weights)
@@ -181,8 +181,8 @@
     return call(
         kernel,
         [((own_segs, total, cols), BF16)] * dp,
-        [VMEM] * (1 + count) + [ANY] * len(after),
-        (mix, *weights, *after),
+        [VMEM] * (1 + count),
+        (mix, *weights),
         2 * mix.size * total * cols // rows,
         2 * total * cols * (experts + dp * own_segs),
     )
@@ -223,51 +223,100 @@
     )
 
 
-def down_columns(core, hidden, downs, mixed):
-    own_segs, cols = downs[0].shape[0], downs[0].shape[2]
+def down_kernel(dp, core, *refs):
+    parts, downs, mixed = refs[:dp], refs[dp:-1], refs[-1]
+    own_segs, half, cols = downs[0].shape
     rows = mixed.shape[2]
     for j in range(own_segs):
-        for k, down in enumerate(downs):
-            out = lax.dot_general(
-                hidden[j], down[j], (((0,), (0,)), ((), ())), preferred_element_type=F32
-            ).astype(BF16)
-            for i in range(SEG // rows):
-                at = j * (SEG // rows) + i
-                mixed[(at % 2) ^ core, at // 2, :, k * cols : (k + 1) * cols] = out[
-                    i * rows : (i + 1) * rows
-                ]
-
-
-def first_kernel(dp, core, *refs):
-    parts, downs, (hidden, mixed) = refs[:dp], refs[dp:-2], refs[-2:]
-    half = hidden.shape[1]
-    kept = []
-    for j in range(hidden.shape[0]):
         total = parts[0][j].astype(F32)
         for part in parts[1:]:
             total += part[j].astype(F32)
         gate, up = total[:half], total[half:]
-        kept.append((gate / (1.0 + jnp.exp(-gate)) * up).astype(BF16))
-        hidden[j] = kept[j]
-    down_columns(core[0], kept, downs, mixed)
-
-
-def second_kernel(count, core, hidden, *refs):
-    down_columns(core[0], hidden, refs[:count], refs[-1])
-
-
-def finish_kernel(groups, lines, my_dp, *refs):
-    out = refs[-1]
-    for g, steps in enumerate(groups):
-        pieces = refs[g * lines : (g + 1) * lines]
-        cols = pieces[0].shape[1] // len(steps)
-        total = pieces[0][...].astype(F32)
-        for piece in pieces[1:]:
-            total += piece[...].astype(F32)
-        total = total.astype(BF16)
-        for k, step in enumerate(steps):
-            at = pl.multiple_of((my_dp[0] ^ step) * cols, cols)
-            out[:, pl.ds(at, cols)] = total[:, k * cols : (k + 1) * cols]
+        hidden = (gate / (1.0 + jnp.exp(-gate)) * up).astype(BF16)
+        for k, down in enumerate(downs):
+            out = lax.dot_general(
+                hidden, down[j], (((0,), (0,)), ((), ())), preferred_element_type=F32
+            ).astype(BF16)
+            for i in range(SEG // rows):
+                at = j * (SEG // rows) + i
+                mixed[(at % 2) ^ core[0], at // 2, :, k * cols : (k + 1) * cols] = out[
+                    i * rows : (i + 1) * rows
+                ]
+
+
+def finish_kernel(dp, my_dp, *refs):
+    pieces, out = refs[:-1], refs[-1]
+    cols = out.shape[1] // dp
+    total = pieces[0][...].astype(F32)
+    for piece in pieces[1:]:
+        total += piece[...].astype(F32)
+    total = total.astype(BF16)
+    for k in range(dp):
+        at = pl.multiple_of((my_dp[0] ^ k) * cols, cols)
+        out[:, pl.ds(at, cols)] = total[:, k * cols : (k + 1) * cols]
+
+
+def tensor_sum_pieces(mixed, lines):
+    my_line = lax.axis_index("tensor") // 2
+    pair = mixed[0].astype(F32) + swap(mixed[1], "tensor", 1).astype(F32)
+    pair = pair.astype(BF16)
+    pieces = [lax.dynamic_index_in_dim(pair, my_line ^ k, 0, keepdims=False) for k in range(lines)]
+    return [pieces[0]] + [swap(pieces[k], "tensor", 2 * k) for k in range(1, lines)]
+
+
+def on_device(tokens, gate_weight, up_weight, down_weight, router_weight, carry_mean):
+    dp = lax.axis_size("dp")
+    tensor = lax.axis_size("tensor")
+    lines = tensor // 2
+    my_dp = lax.axis_index("dp").reshape(1)
+    core = (lax.axis_index("tensor") % 2).reshape(1)
+    own_rows, width = tokens.shape
+    own_segs = own_rows // SEG
+    experts, depth, hidden_count = gate_weight.shape
+    cols = down_weight.shape[2]
+    segs = dp * own_segs
+    return call(
+        functools.partial(preact_kernel, dp),
+        [((own_segs, total, SEG), BF16)] * dp,
+        [SMEM] + [VMEM] * (2 * dp + 1),
+        (core, own, *brought, other, *merged),
+        2 * segs * total * SEG * depth,
+        2 * segs * (total * depth + SEG * depth + total * SEG),
+        [pltpu.VMEM((dp - 1, own_segs * SEG, depth), BF16)],
+    )
+
+
+def down_kernel(dp, core, *refs):
+    parts, downs, mixed = refs[:dp], refs[dp:-1], refs[-1]
+    own_segs, half, cols = downs[0].shape
+    rows = mixed.shape[2]
+    for j in range(own_segs):
+        total = parts[0][j].astype(F32)
+        for part in parts[1:]:
+            total += part[j].astype(F32)
+        gate, up = total[:half], total[half:]
+        hidden = (gate / (1.0 + jnp.exp(-gate)) * up).astype(BF16)
+        for k, down in enumerate(downs):
+            out = lax.dot_general(
+                hidden, down[j], (((0,), (0,)), ((), ())), preferred_element_type=F32
+            ).astype(BF16)
+            for i in range(SEG // rows):
+                at = j * (SEG // rows) + i
+                mixed[(at % 2) ^ core[0], at // 2, :, k * cols : (k + 1) * cols] = out[
+                    i * rows : (i + 1) * rows
+                ]
+
+
+def finish_kernel(dp, my_dp, *refs):
+    pieces, out = refs[:-1], refs[-1]
+    cols = out.shape[1] // dp
+    total = pieces[0][...].astype(F32)
+    for piece in pieces[1:]:
+        total += piece[...].astype(F32)
+    total = total.astype(BF16)
+    for k in range(dp):
+        at = pl.multiple_of((my_dp[0] ^ k) * cols, cols)
+        out[:, pl.ds(at, cols)] = total[:, k * cols : (k + 1) * cols]
 
 
 def tensor_sum_pieces(mixed, lines):
@@ -329,41 +378,28 @@
         2 * own_rows * width,
     )
     other = swap(stacked, "tensor", 1)
+    merged_down = merge(mix, dp, own_segs, (down,))
+    downs = [block if k == 0 else swap(block, "dp", k) for k, block in enumerate(merged_down)]
     merged = merge(mix, dp, own_segs, (gate_t, up_t))
     partial_pre = preact(core, own, brought, other, merged)
     parts = [partial_pre[0]] + [swap(partial_pre[k], "dp", k) for k in range(1, dp)]
 
-    merged_down = merge(mix, dp, own_segs, (down,), (partial_pre[0],))
-    downs = [block if k == 0 else swap(block, "dp", k) for k, block in enumerate(merged_down)]
 
     rows = own_rows // tensor
-    half_flops = own_rows * hidden_count * cols
-    hidden, mixed_early = call(
-        functools.partial(first_kernel, dp),
-        [
-            ((own_segs, hidden_count, SEG), BF16),
-            ((2, lines, rows, len(early) * cols), BF16),
-        ],
-        [SMEM] + [VMEM] * (dp + len(early)),
-        (core, *parts, *[downs[k] for k in early]),
-        2 * half_flops * len(early),
-        2 * (own_rows * hidden_count * 3 + hidden_count * cols * len(early)),
-    )
-    early_pieces = tensor_sum_pieces(mixed_early, lines)
-    (mixed_late,) = call(
-        functools.partial(second_kernel, len(late)),
-        [((2, lines, rows, len(late) * cols), BF16)],
-        [SMEM] + [VMEM] * (1 + len(late)) + [ANY],
-        (core, hidden, *[downs[k] for k in late], early_pieces[0]),
-        2 * half_flops * len(late),
-        2 * (own_rows * hidden_count + hidden_count * cols * len(late)),
-    )
-    late_pieces = tensor_sum_pieces(mixed_late, lines)
+    (mixed,) = call(
+        functools.partial(down_kernel, dp),
+        [((2, lines, rows, width), BF16)],
+        [SMEM] + [VMEM] * (2 * dp),
+        (core, *parts, *downs),
+        2 * own_rows * hidden_count * width,
+        2 * (own_rows * hidden_count * dp * 2 + hidden_count * width),
+    )
+    pieces = tensor_sum_pieces(mixed, lines)
     (out,) = call(
-        functools.partial(finish_kernel, (early, late), lines),
+        functools.partial(finish_kernel, dp),
         [((rows, width), BF16)],
-        [SMEM] + [VMEM] * (2 * lines),
-        (my_dp, *early_pieces, *late_pieces),
+        [SMEM] + [VMEM] * lines,
+        (my_dp, *pieces),
         rows * width * lines,
         2 * rows * width * (lines + 1),
     )

time: 73.1 us -> 68.5 us (0.937)
  starting transfers between devices: 21.1 us -> 16.3 us
    ppermute x18 -> x14, starting transfers between devices: 21.1 us -> 16.3 us  [swap(): return lax.ppermute(value, axis, [(i, i ^ step) for i in range(count)])]
    ppermute x18 -> x14, waiting for transfers between devices: 40.9 us -> 41.3 us  [swap(): return lax.ppermute(value, axis, [(i, i ^ step) for i in range(count)])]
    pallas_call x9 -> x8, Pallas kernels: 10.6 us -> 10.4 us  [call(): pl.pallas_call(kernel, out_shape=[jax.ShapeDtypeStruct(shape, dtype) for...]
  transfers between devices with their start and end apart: 18 -> 14, of which waited for: 10 -> 9; matrix products, arithmetic and copies ran while one was open for 0% -> 0% of each run, Pallas kernels for 7% -> 9%
where the time goes in v4:
time: 68.5 us; the launch traced here: 68.3 us
  waiting for transfers between devices  41.3 us (60%)
  starting transfers between devices  16.3 us (24%)
  Pallas kernels  10.4 us (15%)
    ppermute x14, waiting for transfers between devices, swap(): return lax.ppermute(value, axis, [(i, i ^ step) for i in range(count)])  41.3 us
    ppermute x14, starting transfers between devices, swap(): return lax.ppermute(value, axis, [(i, i ^ step) for i in range(count)])  16.3 us
    pallas_call x8, Pallas kernels, call(): pl.pallas_call(kernel, out_shape=[jax.ShapeDtypeStruct(shape, dtype) for...  10.4 us
  transfers between devices with their start and end apart: 14, of which 9 were waited for; matrix products, arithmetic and copies ran while one was open for 0% of the time, Pallas kernels for 9%

profile of v4, /device:TPU:0, one launch (start us, length us, event | category | flops | bytes accessed | tf_op | source)
XLA Modules:
  0.0 68.3 jit_solution(12070603437170277540)
XLA Ops:
  0.0 2.4 %shard_map.64 = (bf16[256,512]{1,0:T(8,128)(2,1)S(1)}, bf16[144,512]{1,0:T(8,128)(2,1)S(1)}, bf16[144,512]{1,0:T(8,128)(2,1)S(1)}, bf16[144,512]{1,0:T(8,128)(2,1)S(1)}) custom-call(s32[1]{0:T(128)} %bitcast.my_dp, s32[1]{0:T(128)} %bitcast.1.core, bf16[256,2048]{1,0:T(8,128)(2,1)} %tokens.1, f32[8,2048]{1,0:T(8,128)} %bitcast.23, f32[1,2048]{1,0:T(1,128)} %bitcast.24), custom_call_target="tpu_custom_call" | custom-call | flops 16777216 | bytes 2097152 | tf_op jit(solution)/shard_map/pallas_call | solution.py:31
  2.4 3.0 %collective-permute-start = (bf16[144,512]{1,0:T(8,128)(2,1)S(1)}, bf16[144,512]{1,0:T(8,128)(2,1)S(1)}, u32[]{:S(2)}, u32[]{:S(2)}) collective-permute-start(bf16[144,512]{1,0:T(8,128)(2,1)S(1)} %get-tuple-element.27.sent), channel_id=1, source_target_pairs={{0,8},{8,0},{16,24},{24,16},{1,9},{9,1},{17,25},{25,17},{2,10},{10... | collective-permute-start | bytes 442376 | tf_op jit(solution)/shard_map/ppermute | solution.py:23
  5.4 1.5 %collective-permute-start.1 = (bf16[144,512]{1,0:T(8,128)(2,1)S(1)}, bf16[144,512]{1,0:T(8,128)(2,1)S(1)}, u32[]{:S(2)}, u32[]{:S(2)}) collective-permute-start(bf16[144,512]{1,0:T(8,128)(2,1)S(1)} %get-tuple-element.28), channel_id=1, source_target_pairs={{0,16},{8,24},{16,0},{24,8},{1,17},{9,25},{17,1},{25,9},{2,18},{10... | collective-permute-start | bytes 442376 | tf_op jit(solution)/shard_map/ppermute | solution.py:23
  6.9 0.0 collective-permute-start.2
  6.9 3.6 %shard_map.65 = (bf16[8,352,512]{2,1,0:T(8,128)(2,1)S(1)}, bf16[8,352,512]{2,1,0:T(8,128)(2,1)S(1)}, bf16[8,352,512]{2,1,0:T(8,128)(2,1)S(1)}) custom-call(bf16[8,352,512]{2,1,0:T(8,128)(2,1)} %bitcast.21, bf16[8,352,512]{2,1,0:T(8,128)(2,1)} %bitcast.22, bf16[8,352,512]{2,1,0:T(8,128)(2,1)} %refs_2_.1, bf16[256,512]{1,0:T(8,128)(2,1)S(1)} %get-tuple-element.26.refs_3_.own), custom_call_target="tpu_custom_call" | custom-call | bytes 17301504 | tf_op jit(solution)/shard_map/pallas_call | solution.py:31
  10.5 0.0 collective-permute-done.refs_0_
  10.5 3.3 %collective-permute-done.1.refs_1_ = bf16[144,512]{1,0:T(8,128)(2,1)S(1)} collective-permute-done((bf16[144,512]{1,0:T(8,128)(2,1)S(1)}, bf16[144,512]{1,0:T(8,128)(2,1)S(1)}, u32[]{:S(2)}, u32[]{:S(2)}) %collective-permute-start.1) | collective-permute-done | bytes 147488 | tf_op jit(solution)/shard_map/ppermute | solution.py:23
  13.8 0.0 collective-permute-done.2.refs_2_
  13.8 0.4 shard_map.66
  14.2 0.1 collective-permute-start.3
  14.3 0.5 shard_map.69
  14.8 1.3 %collective-permute-start.7 = (bf16[1,352,512]{2,1,0:T(8,128)(2,1)S(1)}, bf16[1,352,512]{2,1,0:T(8,128)(2,1)S(1)}, u32[]{:S(2)}, u32[]{:S(2)}) collective-permute-start(bf16[1,352,512]{2,1,0:T(8,128)(2,1)S(1)} %get-tuple-element.44), channel_id=1, source_target_pairs={{0,8},{8,0},{16,24},{24,16},{1,9},{9,1},{17,25},{25,17},{2,10},{10... | collective-permute-start | bytes 1081352 | tf_op jit(solution)/shard_map/ppermute | solution.py:23
  16.1 0.8 %collective-permute-start.8 = (bf16[1,352,512]{2,1,0:T(8,128)(2,1)S(1)}, bf16[1,352,512]{2,1,0:T(8,128)(2,1)S(1)}, u32[]{:S(2)}, u32[]{:S(2)}) collective-permute-start(bf16[1,352,512]{2,1,0:T(8,128)(2,1)S(1)} %get-tuple-element.45), channel_id=1, source_target_pairs={{0,16},{8,24},{16,0},{24,8},{1,17},{9,25},{17,1},{25,9},{2,18},{10... | collective-permute-start | bytes 1081352 | tf_op jit(solution)/shard_map/ppermute | solution.py:23
  17.0 1.4 %collective-permute-start.9 = (bf16[1,352,512]{2,1,0:T(8,128)(2,1)S(1)}, bf16[1,352,512]{2,1,0:T(8,128)(2,1)S(1)}, u32[]{:S(2)}, u32[]{:S(2)}) collective-permute-start(bf16[1,352,512]{2,1,0:T(8,128)(2,1)S(1)} %get-tuple-element.46), channel_id=1, source_target_pairs={{0,24},{8,16},{16,8},{24,0},{1,25},{9,17},{17,9},{25,1},{2,26},{10... | collective-permute-start | bytes 1081352 | tf_op jit(solution)/shard_map/ppermute | solution.py:23
  18.4 0.9 %shard_map.67 = (bf16[1,704,512]{2,1,0:T(8,128)(2,1)S(1)}, bf16[1,704,512]{2,1,0:T(8,128)(2,1)S(1)}, bf16[1,704,512]{2,1,0:T(8,128)(2,1)S(1)}, bf16[1,704,512]{2,1,0:T(8,128)(2,1)S(1)}) custom-call(bf16[128,256]{1,0:T(8,128)(2,1)S(1)} %get-tuple-element.32.mix_ref, bf16[8,352,512]{2,1,0:T(8,128)(2,1)S(1)} %get-tuple-element.33.refs_0_, ...), custom_call_target="tpu_custom_call" | custom-call | flops 67108864 | bytes 8650752 | tf_op jit(solution)/shard_map/pallas_call | solution.py:31
  19.3 0.0 collective-permute-done.3.refs_3_
  19.3 1.0 %shard_map.68 = (bf16[1,704,256]{2,1,0:T(8,128)(2,1)S(1)}, bf16[1,704,256]{2,1,0:T(8,128)(2,1)S(1)}, bf16[1,704,256]{2,1,0:T(8,128)(2,1)S(1)}, bf16[1,704,256]{2,1,0:T(8,128)(2,1)S(1)}) custom-call(s32[1]{0:T(128)} %bitcast.1.core, bf16[256,512]{1,0:T(8,128)(2,1)S(1)} %get-tuple-element.26.refs_3_.own, bf16[144,512]{1,0:T(8,128)(2,1)S(1)} %collective-permute-done.refs_0_, ...), custom_call_target="tpu_custom_call" | custom-call | flops 738197504 | bytes 5373952 | tf_op jit(solution)/shard_map/pallas_call | solution.py:31
  20.3 1.3 %collective-permute-start.4 = (bf16[1,704,256]{2,1,0:T(8,128)(2,1)S(1)}, bf16[1,704,256]{2,1,0:T(8,128)(2,1)S(1)}, u32[]{:S(2)}, u32[]{:S(2)}) collective-permute-start(bf16[1,704,256]{2,1,0:T(8,128)(2,1)S(1)} %get-tuple-element.40), channel_id=1, source_target_pairs={{0,8},{8,0},{16,24},{24,16},{1,9},{9,1},{17,25},{25,17},{2,10},{10... | collective-permute-start | bytes 1081352 | tf_op jit(solution)/shard_map/ppermute | solution.py:23
  21.6 0.8 %collective-permute-start.5 = (bf16[1,704,256]{2,1,0:T(8,128)(2,1)S(1)}, bf16[1,704,256]{2,1,0:T(8,128)(2,1)S(1)}, u32[]{:S(2)}, u32[]{:S(2)}) collective-permute-start(bf16[1,704,256]{2,1,0:T(8,128)(2,1)S(1)} %get-tuple-element.41), channel_id=1, source_target_pairs={{0,16},{8,24},{16,0},{24,8},{1,17},{9,25},{17,1},{25,9},{2,18},{10... | collective-permute-start | bytes 1081352 | tf_op jit(solution)/shard_map/ppermute | solution.py:23
  22.4 3.7 %collective-permute-done.7.refs_5_ = bf16[1,352,512]{2,1,0:T(8,128)(2,1)S(1)} collective-permute-done((bf16[1,352,512]{2,1,0:T(8,128)(2,1)S(1)}, bf16[1,352,512]{2,1,0:T(8,128)(2,1)S(1)}, u32[]{:S(2)}, u32[]{:S(2)}) %collective-permute-start.7) | collective-permute-done | bytes 360480 | tf_op jit(solution)/shard_map/ppermute | solution.py:23
  26.1 1.5 %collective-permute-start.6 = (bf16[1,704,256]{2,1,0:T(8,128)(2,1)S(1)}, bf16[1,704,256]{2,1,0:T(8,128)(2,1)S(1)}, u32[]{:S(2)}, u32[]{:S(2)}) collective-permute-start(bf16[1,704,256]{2,1,0:T(8,128)(2,1)S(1)} %get-tuple-element.42), channel_id=1, source_target_pairs={{0,24},{8,16},{16,8},{24,0},{1,25},{9,17},{17,9},{25,1},{2,26},{10... | collective-permute-start | bytes 1081352 | tf_op jit(solution)/shard_map/ppermute | solution.py:23
  27.6 7.5 %collective-permute-done.8.refs_6_ = bf16[1,352,512]{2,1,0:T(8,128)(2,1)S(1)} collective-permute-done((bf16[1,352,512]{2,1,0:T(8,128)(2,1)S(1)}, bf16[1,352,512]{2,1,0:T(8,128)(2,1)S(1)}, u32[]{:S(2)}, u32[]{:S(2)}) %collective-permute-start.8) | collective-permute-done | bytes 360480 | tf_op jit(solution)/shard_map/ppermute | solution.py:23
  35.1 0.0 collective-permute-done.9.refs_7_
  35.1 6.5 %collective-permute-done.4.refs_1_ = bf16[1,704,256]{2,1,0:T(8,128)(2,1)S(1)} collective-permute-done((bf16[1,704,256]{2,1,0:T(8,128)(2,1)S(1)}, bf16[1,704,256]{2,1,0:T(8,128)(2,1)S(1)}, u32[]{:S(2)}, u32[]{:S(2)}) %collective-permute-start.4) | collective-permute-done | bytes 360480 | tf_op jit(solution)/shard_map/ppermute | solution.py:23
  41.6 0.9 %collective-permute-done.5.refs_2_ = bf16[1,704,256]{2,1,0:T(8,128)(2,1)S(1)} collective-permute-done((bf16[1,704,256]{2,1,0:T(8,128)(2,1)S(1)}, bf16[1,704,256]{2,1,0:T(8,128)(2,1)S(1)}, u32[]{:S(2)}, u32[]{:S(2)}) %collective-permute-start.5) | collective-permute-done | bytes 360480 | tf_op jit(solution)/shard_map/ppermute | solution.py:23
  42.5 7.4 %collective-permute-done.6.refs_3_ = bf16[1,704,256]{2,1,0:T(8,128)(2,1)S(1)} collective-permute-done((bf16[1,704,256]{2,1,0:T(8,128)(2,1)S(1)}, bf16[1,704,256]{2,1,0:T(8,128)(2,1)S(1)}, u32[]{:S(2)}, u32[]{:S(2)}) %collective-permute-start.6) | collective-permute-done | bytes 360480 | tf_op jit(solution)/shard_map/ppermute | solution.py:23
  49.9 0.9 %shard_map.70 = bf16[2,4,32,2048]{3,2,1,0:T(8,128)(2,1)S(1)} custom-call(s32[1]{0:T(128)} %bitcast.1.core, bf16[1,704,256]{2,1,0:T(8,128)(2,1)S(1)} %get-tuple-element.39.refs_0_, bf16[1,704,256]{2,1,0:T(8,128)(2,1)S(1)} %collective-permute-done.4.refs_1_, bf16[1,704,256]{2,1,0:T(8,128)(2,1)S(1)} %collective-permute-done.5.refs_2_, ...), custom_call_target="tpu_custom_call" | custom-call | flops 369098752 | bytes 2883584 | tf_op jit(solution)/shard_map/pallas_call | solution.py:31
  50.9 0.1 collective-permute-start.10
  51.0 1.9 %collective-permute-done.10 = bf16[4,32,2048]{2,1,0:T(8,128)(2,1)S(1)} collective-permute-done((bf16[4,32,2048]{2,1,0:T(8,128)(2,1)S(1)}, bf16[4,32,2048]{2,1,0:T(8,128)(2,1)S(1)}, u32[]{:S(2)}, u32[]{:S(2)}) %collective-permute-start.10) | collective-permute-done | bytes 524320 | tf_op jit(solution)/shard_map/ppermute | solution.py:23
  52.9 0.1 fusion
  53.1 1.6 %collective-permute-start.11 = (bf16[32,2048]{1,0:T(8,128)(2,1)S(1)}, bf16[32,2048]{1,0:T(8,128)(2,1)S(1)}, u32[]{:S(2)}, u32[]{:S(2)}) collective-permute-start(bf16[32,2048]{1,0:T(8,128)(2,1)S(1)} %get-tuple-element.49), channel_id=1, source_target_pairs={{0,2},{1,3},{2,0},{3,1},{4,6},{5,7},{6,4},{7,5},{8,10},{9,11},{10,... | collective-permute-start | bytes 393224 | tf_op jit(solution)/shard_map/ppermute | solution.py:23
  54.7 2.6 %collective-permute-start.12 = (bf16[32,2048]{1,0:T(8,128)(2,1)S(1)}, bf16[32,2048]{1,0:T(8,128)(2,1)S(1)}, u32[]{:S(2)}, u32[]{:S(2)}) collective-permute-start(bf16[32,2048]{1,0:T(8,128)(2,1)S(1)} %get-tuple-element.48), channel_id=1, source_target_pairs={{0,4},{1,5},{2,6},{3,7},{4,0},{5,1},{6,2},{7,3},{8,12},{9,13},{10,... | collective-permute-start | bytes 393224 | tf_op jit(solution)/shard_map/ppermute | solution.py:23
  57.3 0.2 collective-permute-start.13
  57.5 3.1 %collective-permute-done.11.refs_1_ = bf16[32,2048]{1,0:T(8,128)(2,1)S(1)} collective-permute-done((bf16[32,2048]{1,0:T(8,128)(2,1)S(1)}, bf16[32,2048]{1,0:T(8,128)(2,1)S(1)}, u32[]{:S(2)}, u32[]{:S(2)}) %collective-permute-start.11) | collective-permute-done | bytes 131104 | tf_op jit(solution)/shard_map/ppermute | solution.py:23
  60.6 7.0 %collective-permute-done.12.refs_2_ = bf16[32,2048]{1,0:T(8,128)(2,1)S(1)} collective-permute-done((bf16[32,2048]{1,0:T(8,128)(2,1)S(1)}, bf16[32,2048]{1,0:T(8,128)(2,1)S(1)}, u32[]{:S(2)}, u32[]{:S(2)}) %collective-permute-start.12) | collective-permute-done | bytes 131104 | tf_op jit(solution)/shard_map/ppermute | solution.py:23
  67.6 0.0 collective-permute-done.13.refs_3_
  67.6 0.7 %shard_map.71 = bf16[32,2048]{1,0:T(8,128)(2,1)} custom-call(s32[1]{0:T(128)} %bitcast.my_dp, bf16[32,2048]{1,0:T(8,128)(2,1)S(1)} %get-tuple-element.50.refs_0_, bf16[32,2048]{1,0:T(8,128)(2,1)S(1)} %collective-permute-done.11.refs_1_, bf16[32,2048]{1,0:T(8,128)(2,1)S(1)} %collective-permute-done.12.refs_2_, ...), custom_call_target="tpu_custom_call" | custom-call | flops 262144 | bytes 655360 | tf_op jit(solution)/shard_map/pallas_call | solution.py:31
  (2 shorter events, 0.1 us)
Async XLA Ops:
  2.4 8.1 %collective-permute-start = (bf16[144,512]{1,0:T(8,128)(2,1)S(1)}, bf16[144,512]{1,0:T(8,128)(2,1)S(1)}, u32[]{:S(2)}, u32[]{:S(2)}) collective-permute-start(bf16[144,512]{1,0:T(8,128)(2,1)S(1)} %get-tuple-element.27.sent), channel_id=1, source_target_pairs={{0,8},{8,0},{16,24},{24,16},{1,9},{9,1},{17,25},{25,17},{2,10},{10... | collective-permute-start | bytes 442376 | tf_op jit(solution)/shard_map/ppermute | solution.py:23
  5.4 8.5 %collective-permute-start.1 = (bf16[144,512]{1,0:T(8,128)(2,1)S(1)}, bf16[144,512]{1,0:T(8,128)(2,1)S(1)}, u32[]{:S(2)}, u32[]{:S(2)}) collective-permute-start(bf16[144,512]{1,0:T(8,128)(2,1)S(1)} %get-tuple-element.28), channel_id=1, source_target_pairs={{0,16},{8,24},{16,0},{24,8},{1,17},{9,25},{17,1},{25,9},{2,18},{10... | collective-permute-start | bytes 442376 | tf_op jit(solution)/shard_map/ppermute | solution.py:23
  6.9 7.0 %collective-permute-start.2 = (bf16[144,512]{1,0:T(8,128)(2,1)S(1)}, bf16[144,512]{1,0:T(8,128)(2,1)S(1)}, u32[]{:S(2)}, u32[]{:S(2)}) collective-permute-start(bf16[144,512]{1,0:T(8,128)(2,1)S(1)} %get-tuple-element.29), channel_id=1, source_target_pairs={{0,24},{8,16},{16,8},{24,0},{1,25},{9,17},{17,9},{25,1},{2,26},{10... | collective-permute-start | bytes 442376 | tf_op jit(solution)/shard_map/ppermute | solution.py:23
  14.2 5.1 %collective-permute-start.3 = (bf16[3,128,512]{2,1,0:T(8,128)(2,1)S(1)}, bf16[3,128,512]{2,1,0:T(8,128)(2,1)S(1)}, u32[]{:S(2)}, u32[]{:S(2)}) collective-permute-start(bf16[3,128,512]{2,1,0:T(8,128)(2,1)S(1)} %get-tuple-element.31), channel_id=1, source_target_pairs={{0,1},{1,0},{2,3},{3,2},{4,5},{5,4},{6,7},{7,6},{8,9},{9,8},{10,11... | collective-permute-start | bytes 1179656 | tf_op jit(solution)/shard_map/ppermute | solution.py:23
  14.8 11.3 %collective-permute-start.7 = (bf16[1,352,512]{2,1,0:T(8,128)(2,1)S(1)}, bf16[1,352,512]{2,1,0:T(8,128)(2,1)S(1)}, u32[]{:S(2)}, u32[]{:S(2)}) collective-permute-start(bf16[1,352,512]{2,1,0:T(8,128)(2,1)S(1)} %get-tuple-element.44), channel_id=1, source_target_pairs={{0,8},{8,0},{16,24},{24,16},{1,9},{9,1},{17,25},{25,17},{2,10},{10... | collective-permute-start | bytes 1081352 | tf_op jit(solution)/shard_map/ppermute | solution.py:23
  16.1 19.0 %collective-permute-start.8 = (bf16[1,352,512]{2,1,0:T(8,128)(2,1)S(1)}, bf16[1,352,512]{2,1,0:T(8,128)(2,1)S(1)}, u32[]{:S(2)}, u32[]{:S(2)}) collective-permute-start(bf16[1,352,512]{2,1,0:T(8,128)(2,1)S(1)} %get-tuple-element.45), channel_id=1, source_target_pairs={{0,16},{8,24},{16,0},{24,8},{1,17},{9,25},{17,1},{25,9},{2,18},{10... | collective-permute-start | bytes 1081352 | tf_op jit(solution)/shard_map/ppermute | solution.py:23
  17.0 18.1 %collective-permute-start.9 = (bf16[1,352,512]{2,1,0:T(8,128)(2,1)S(1)}, bf16[1,352,512]{2,1,0:T(8,128)(2,1)S(1)}, u32[]{:S(2)}, u32[]{:S(2)}) collective-permute-start(bf16[1,352,512]{2,1,0:T(8,128)(2,1)S(1)} %get-tuple-element.46), channel_id=1, source_target_pairs={{0,24},{8,16},{16,8},{24,0},{1,25},{9,17},{17,9},{25,1},{2,26},{10... | collective-permute-start | bytes 1081352 | tf_op jit(solution)/shard_map/ppermute | solution.py:23
  20.3 21.3 %collective-permute-start.4 = (bf16[1,704,256]{2,1,0:T(8,128)(2,1)S(1)}, bf16[1,704,256]{2,1,0:T(8,128)(2,1)S(1)}, u32[]{:S(2)}, u32[]{:S(2)}) collective-permute-start(bf16[1,704,256]{2,1,0:T(8,128)(2,1)S(1)} %get-tuple-element.40), channel_id=1, source_target_pairs={{0,8},{8,0},{16,24},{24,16},{1,9},{9,1},{17,25},{25,17},{2,10},{10... | collective-permute-start | bytes 1081352 | tf_op jit(solution)/shard_map/ppermute | solution.py:23
  21.6 20.9 %collective-permute-start.5 = (bf16[1,704,256]{2,1,0:T(8,128)(2,1)S(1)}, bf16[1,704,256]{2,1,0:T(8,128)(2,1)S(1)}, u32[]{:S(2)}, u32[]{:S(2)}) collective-permute-start(bf16[1,704,256]{2,1,0:T(8,128)(2,1)S(1)} %get-tuple-element.41), channel_id=1, source_target_pairs={{0,16},{8,24},{16,0},{24,8},{1,17},{9,25},{17,1},{25,9},{2,18},{10... | collective-permute-start | bytes 1081352 | tf_op jit(solution)/shard_map/ppermute | solution.py:23
  26.1 23.8 %collective-permute-start.6 = (bf16[1,704,256]{2,1,0:T(8,128)(2,1)S(1)}, bf16[1,704,256]{2,1,0:T(8,128)(2,1)S(1)}, u32[]{:S(2)}, u32[]{:S(2)}) collective-permute-start(bf16[1,704,256]{2,1,0:T(8,128)(2,1)S(1)} %get-tuple-element.42), channel_id=1, source_target_pairs={{0,24},{8,16},{16,8},{24,0},{1,25},{9,17},{17,9},{25,1},{2,26},{10... | collective-permute-start | bytes 1081352 | tf_op jit(solution)/shard_map/ppermute | solution.py:23
  50.9 2.0 %collective-permute-start.10 = (bf16[4,32,2048]{2,1,0:T(8,128)(2,1)S(1)}, bf16[4,32,2048]{2,1,0:T(8,128)(2,1)S(1)}, u32[]{:S(2)}, u32[]{:S(2)}) collective-permute-start(bf16[4,32,2048]{2,1,0:T(8,128)(2,1)S(1)} %slice_bitcast_fusion), channel_id=1, source_target_pairs={{0,1},{1,0},{2,3},{3,2},{4,5},{5,4},{6,7},{7,6},{8,9},{9,8},{10,11... | collective-permute-start | bytes 1572872 | tf_op jit(solution)/shard_map/ppermute | solution.py:23
  53.1 7.5 %collective-permute-start.11 = (bf16[32,2048]{1,0:T(8,128)(2,1)S(1)}, bf16[32,2048]{1,0:T(8,128)(2,1)S(1)}, u32[]{:S(2)}, u32[]{:S(2)}) collective-permute-start(bf16[32,2048]{1,0:T(8,128)(2,1)S(1)} %get-tuple-element.49), channel_id=1, source_target_pairs={{0,2},{1,3},{2,0},{3,1},{4,6},{5,7},{6,4},{7,5},{8,10},{9,11},{10,... | collective-permute-start | bytes 393224 | tf_op jit(solution)/shard_map/ppermute | solution.py:23
  54.7 12.9 %collective-permute-start.12 = (bf16[32,2048]{1,0:T(8,128)(2,1)S(1)}, bf16[32,2048]{1,0:T(8,128)(2,1)S(1)}, u32[]{:S(2)}, u32[]{:S(2)}) collective-permute-start(bf16[32,2048]{1,0:T(8,128)(2,1)S(1)} %get-tuple-element.48), channel_id=1, source_target_pairs={{0,4},{1,5},{2,6},{3,7},{4,0},{5,1},{6,2},{7,3},{8,12},{9,13},{10,... | collective-permute-start | bytes 393224 | tf_op jit(solution)/shard_map/ppermute | solution.py:23
  57.3 10.3 %collective-permute-start.13 = (bf16[32,2048]{1,0:T(8,128)(2,1)S(1)}, bf16[32,2048]{1,0:T(8,128)(2,1)S(1)}, u32[]{:S(2)}, u32[]{:S(2)}) collective-permute-start(bf16[32,2048]{1,0:T(8,128)(2,1)S(1)} %get-tuple-element.47), channel_id=1, source_target_pairs={{0,6},{1,7},{2,4},{3,5},{4,2},{5,3},{6,0},{7,1},{8,14},{9,15},{10,... | collective-permute-start | bytes 393224 | tf_op jit(solution)/shard_map/ppermute | solution.py:23

commit v5 on v4

--- a/solution.py
+++ b/solution.py
@@ -62,36 +62,30 @@
     ones = member == lax.broadcasted_iota(jnp.int32, (extra, rows), 0)
     ones = jnp.where(ones, 1.0, 0.0).astype(BF16)
     start = pl.multiple_of(core[0] * half, half)
-    copies[dp].wait()
-    copies[dp + 1].wait()
-    logits = jnp.zeros((extra, experts), F32)
+    for copy in copies:
+        copy.wait()
+    totals = [jnp.zeros((experts, depth), F32)] * (own_segs + 1)
     for k in range(dp):
-        copies[k].wait()
         block = own[...] if k == 0 else blocks[k - 1]
+        weight = routers[:, pl.ds(columns[k], depth)]
         means = jnp.dot(ones, block, preferred_element_type=F32) / SEG
-        place = lax.broadcasted_iota(jnp.int32, means.shape, 0)
-        means = jnp.where(place == own_segs, carries[:, pl.ds(columns[k], depth)], means)
-        logits += lax.dot_general(
-            means,
-            routers[:, pl.ds(columns[k], depth)],
-            (((1,), (1,)), ((), ())),
-            precision=lax.Precision.HIGHEST,
-            preferred_element_type=F32,
-        )
+        for j in range(own_segs):
+            totals[j] += means[j : j + 1, :] * weight
+        totals[own_segs] += carries[:, pl.ds(columns[k], depth)] * weight
         if k > 0:
             sends[k - 1][:half] = blocks[k - 1, pl.ds(start, half), :]
     lane = lax.broadcasted_iota(jnp.int32, (experts, LANES), 1)
-    copied = lane % experts == lax.broadcasted_iota(jnp.int32, (experts, LANES), 0)
-    logits = jnp.dot(
-        logits,
-        jnp.where(copied, 1.0, 0.0),
-        precision=lax.Precision.HIGHEST,
-        preferred_element_type=F32,
-    )
+    place = lane % experts == lax.broadcasted_iota(jnp.int32, (experts, LANES), 0)
+    row = lax.broadcasted_iota(jnp.int32, (extra, LANES), 0)
+    lane = lax.broadcasted_iota(jnp.int32, (extra, LANES), 1)
+    logits = jnp.zeros((extra, LANES), F32)
+    for j, total in enumerate(totals):
+        column = jnp.sum(total, axis=1, keepdims=True)
+        spread = jnp.sum(jnp.where(place, column, 0.0), axis=0, keepdims=True)
+        logits = jnp.where(row == j, spread, logits)
     high = logits.astype(BF16).astype(F32)
     middle = (logits - high).astype(BF16).astype(F32)
     low = logits - high - middle
-    lane = lax.broadcasted_iota(jnp.int32, logits.shape, 1)
     terms = jnp.where(lane < experts, high, jnp.where(lane < 2 * experts, middle, low))
     terms = jnp.where(lane < 3 * experts, terms, 0.0).astype(BF16)
     for send in sends:
@@ -261,7 +255,7 @@
     pair = mixed[0].astype(F32) + swap(mixed[1], "tensor", 1).astype(F32)
     pair = pair.astype(BF16)
     pieces = [lax.dynamic_index_in_dim(pair, my_line ^ k, 0, keepdims=False) for k in range(lines)]
-    return [pieces[0]] + [swap(pieces[k], "tensor", 2 * k) for k in range(1, lines)]
+    return [swap(pieces[k], "tensor", 2 * k) for k in range(lines - 1, 0, -1)] + [pieces[0]]
 
 
 def on_device(tokens, gate_weight, up_weight, down_weight, router_weight, carry_mean):
@@ -275,72 +269,6 @@
     experts, depth, hidden_count = gate_weight.shape
     cols = down_weight.shape[2]
     segs = dp * own_segs
-    return call(
-        functools.partial(preact_kernel, dp),
-        [((own_segs, total, SEG), BF16)] * dp,
-        [SMEM] + [VMEM] * (2 * dp + 1),
-        (core, own, *brought, other, *merged),
-        2 * segs * total * SEG * depth,
-        2 * segs * (total * depth + SEG * depth + total * SEG),
-        [pltpu.VMEM((dp - 1, own_segs * SEG, depth), BF16)],
-    )
-
-
-def down_kernel(dp, core, *refs):
-    parts, downs, mixed = refs[:dp], refs[dp:-1], refs[-1]
-    own_segs, half, cols = downs[0].shape
-    rows = mixed.shape[2]
-    for j in range(own_segs):
-        total = parts[0][j].astype(F32)
-        for part in parts[1:]:
-            total += part[j].astype(F32)
-        gate, up = total[:half], total[half:]
-        hidden = (gate / (1.0 + jnp.exp(-gate)) * up).astype(BF16)
-        for k, down in enumerate(downs):
-            out = lax.dot_general(
-                hidden, down[j], (((0,), (0,)), ((), ())), preferred_element_type=F32
-            ).astype(BF16)
-            for i in range(SEG // rows):
-                at = j * (SEG // rows) + i
-                mixed[(at % 2) ^ core[0], at // 2, :, k * cols : (k + 1) * cols] = out[
-                    i * rows : (i + 1) * rows
-                ]
-
-
-def finish_kernel(dp, my_dp, *refs):
-    pieces, out = refs[:-1], refs[-1]
-    cols = out.shape[1] // dp
-    total = pieces[0][...].astype(F32)
-    for piece in pieces[1:]:
-        total += piece[...].astype(F32)
-    total = total.astype(BF16)
-    for k in range(dp):
-        at = pl.multiple_of((my_dp[0] ^ k) * cols, cols)
-        out[:, pl.ds(at, cols)] = total[:, k * cols : (k + 1) * cols]
-
-
-def tensor_sum_pieces(mixed, lines):
-    my_line = lax.axis_index("tensor") // 2
-    pair = mixed[0].astype(F32) + swap(mixed[1], "tensor", 1).astype(F32)
-    pair = pair.astype(BF16)
-    pieces = [lax.dynamic_index_in_dim(pair, my_line ^ k, 0, keepdims=False) for k in range(lines)]
-    return [pieces[0]] + [swap(pieces[k], "tensor", 2 * k) for k in range(1, lines)]
-
-
-def on_device(tokens, gate_weight, up_weight, down_weight, router_weight, carry_mean):
-    dp = lax.axis_size("dp")
-    tensor = lax.axis_size("tensor")
-    lines = tensor // 2
-    my_dp = lax.axis_index("dp").reshape(1)
-    core = (lax.axis_index("tensor") % 2).reshape(1)
-    own_rows, width = tokens.shape
-    own_segs = own_rows // SEG
-    experts, depth, hidden_count = gate_weight.shape
-    cols = down_weight.shape[2]
-    steps = tuple(range(dp))
-    segs = dp * own_segs
-    late = tuple(k for k in steps if k.bit_count() == 1)
-    early = tuple(k for k in steps if k not in late)
 
     extra = -(-(own_segs + 1) // 16) * 16
     own, *sends = call(
@@ -379,11 +307,11 @@
     )
     other = swap(stacked, "tensor", 1)
     merged_down = merge(mix, dp, own_segs, (down,))
-    downs = [block if k == 0 else swap(block, "dp", k) for k, block in enumerate(merged_down)]
+    downs = [swap(merged_down[k], "dp", k) for k in range(dp - 1, 0, -1)]
+    downs = [merged_down[0], *reversed(downs)]
     merged = merge(mix, dp, own_segs, (gate_t, up_t))
     partial_pre = preact(core, own, brought, other, merged)
     parts = [partial_pre[0]] + [swap(partial_pre[k], "dp", k) for k in range(1, dp)]
-
 
     rows = own_rows // tensor
     (mixed,) = call(

time: 68.5 us -> 68.3 us (level)
  no operation moved by 1% of the time
where the time goes in v5:
time: 68.3 us; the launch traced here: 68.2 us
  waiting for transfers between devices  41.8 us (61%)
  starting transfers between devices  16.3 us (24%)
  Pallas kernels  9.73 us (14%)
    ppermute x14, waiting for transfers between devices, swap(): return lax.ppermute(value, axis, [(i, i ^ step) for i in range(count)])  41.8 us
    ppermute x14, starting transfers between devices, swap(): return lax.ppermute(value, axis, [(i, i ^ step) for i in range(count)])  16.3 us
    pallas_call x8, Pallas kernels, call(): pl.pallas_call(kernel, out_shape=[jax.ShapeDtypeStruct(shape, dtype) for...  9.73 us
  transfers between devices with their start and end apart: 14, of which 9 were waited for; matrix products, arithmetic and copies ran while one was open for 0% of the time, Pallas kernels for 9%

profile of v5, /device:TPU:0, one launch (start us, length us, event | category | flops | bytes accessed | tf_op | source)
XLA Modules:
  0.0 68.2 jit_solution(10007858861580010503)
XLA Ops:
  0.0 1.7 %shard_map.64 = (bf16[256,512]{1,0:T(8,128)(2,1)S(1)}, bf16[144,512]{1,0:T(8,128)(2,1)S(1)}, bf16[144,512]{1,0:T(8,128)(2,1)S(1)}, bf16[144,512]{1,0:T(8,128)(2,1)S(1)}) custom-call(s32[1]{0:T(128)} %bitcast.my_dp, s32[1]{0:T(128)} %bitcast.1.core, bf16[256,2048]{1,0:T(8,128)(2,1)} %tokens.1, f32[8,2048]{1,0:T(8,128)} %bitcast.23, f32[1,2048]{1,0:T(1,128)} %bitcast.24), custom_call_target="tpu_custom_call" | custom-call | flops 16777216 | bytes 2097152 | tf_op jit(solution)/shard_map/pallas_call | solution.py:31
  1.7 3.0 %collective-permute-start = (bf16[144,512]{1,0:T(8,128)(2,1)S(1)}, bf16[144,512]{1,0:T(8,128)(2,1)S(1)}, u32[]{:S(2)}, u32[]{:S(2)}) collective-permute-start(bf16[144,512]{1,0:T(8,128)(2,1)S(1)} %get-tuple-element.27.sent), channel_id=1, source_target_pairs={{0,8},{8,0},{16,24},{24,16},{1,9},{9,1},{17,25},{25,17},{2,10},{10... | collective-permute-start | bytes 442376 | tf_op jit(solution)/shard_map/ppermute | solution.py:23
  4.7 1.5 %collective-permute-start.1 = (bf16[144,512]{1,0:T(8,128)(2,1)S(1)}, bf16[144,512]{1,0:T(8,128)(2,1)S(1)}, u32[]{:S(2)}, u32[]{:S(2)}) collective-permute-start(bf16[144,512]{1,0:T(8,128)(2,1)S(1)} %get-tuple-element.28), channel_id=1, source_target_pairs={{0,16},{8,24},{16,0},{24,8},{1,17},{9,25},{17,1},{25,9},{2,18},{10... | collective-permute-start | bytes 442376 | tf_op jit(solution)/shard_map/ppermute | solution.py:23
  6.2 0.0 collective-permute-start.2
  6.2 3.6 %shard_map.65 = (bf16[8,352,512]{2,1,0:T(8,128)(2,1)S(1)}, bf16[8,352,512]{2,1,0:T(8,128)(2,1)S(1)}, bf16[8,352,512]{2,1,0:T(8,128)(2,1)S(1)}) custom-call(bf16[8,352,512]{2,1,0:T(8,128)(2,1)} %bitcast.21, bf16[8,352,512]{2,1,0:T(8,128)(2,1)} %bitcast.22, bf16[8,352,512]{2,1,0:T(8,128)(2,1)} %refs_2_.1, bf16[256,512]{1,0:T(8,128)(2,1)S(1)} %get-tuple-element.26.refs_3_.own), custom_call_target="tpu_custom_call" | custom-call | bytes 17301504 | tf_op jit(solution)/shard_map/pallas_call | solution.py:31
  9.8 0.0 collective-permute-done.refs_0_
  9.8 3.3 %collective-permute-done.1.refs_1_ = bf16[144,512]{1,0:T(8,128)(2,1)S(1)} collective-permute-done((bf16[144,512]{1,0:T(8,128)(2,1)S(1)}, bf16[144,512]{1,0:T(8,128)(2,1)S(1)}, u32[]{:S(2)}, u32[]{:S(2)}) %collective-permute-start.1) | collective-permute-done | bytes 147488 | tf_op jit(solution)/shard_map/ppermute | solution.py:23
  13.2 0.0 collective-permute-done.2.refs_2_
  13.2 0.4 shard_map.66
  13.5 0.1 collective-permute-start.3
  13.6 0.5 shard_map.69
  14.2 1.3 %collective-permute-start.7 = (bf16[1,352,512]{2,1,0:T(8,128)(2,1)S(1)}, bf16[1,352,512]{2,1,0:T(8,128)(2,1)S(1)}, u32[]{:S(2)}, u32[]{:S(2)}) collective-permute-start(bf16[1,352,512]{2,1,0:T(8,128)(2,1)S(1)} %get-tuple-element.44), channel_id=1, source_target_pairs={{0,8},{8,0},{16,24},{24,16},{1,9},{9,1},{17,25},{25,17},{2,10},{10... | collective-permute-start | bytes 1081352 | tf_op jit(solution)/shard_map/ppermute | solution.py:23
  15.5 0.8 %collective-permute-start.8 = (bf16[1,352,512]{2,1,0:T(8,128)(2,1)S(1)}, bf16[1,352,512]{2,1,0:T(8,128)(2,1)S(1)}, u32[]{:S(2)}, u32[]{:S(2)}) collective-permute-start(bf16[1,352,512]{2,1,0:T(8,128)(2,1)S(1)} %get-tuple-element.45), channel_id=1, source_target_pairs={{0,16},{8,24},{16,0},{24,8},{1,17},{9,25},{17,1},{25,9},{2,18},{10... | collective-permute-start | bytes 1081352 | tf_op jit(solution)/shard_map/ppermute | solution.py:23
  16.3 1.4 %collective-permute-start.9 = (bf16[1,352,512]{2,1,0:T(8,128)(2,1)S(1)}, bf16[1,352,512]{2,1,0:T(8,128)(2,1)S(1)}, u32[]{:S(2)}, u32[]{:S(2)}) collective-permute-start(bf16[1,352,512]{2,1,0:T(8,128)(2,1)S(1)} %get-tuple-element.46), channel_id=1, source_target_pairs={{0,24},{8,16},{16,8},{24,0},{1,25},{9,17},{17,9},{25,1},{2,26},{10... | collective-permute-start | bytes 1081352 | tf_op jit(solution)/shard_map/ppermute | solution.py:23
  17.7 0.9 %shard_map.67 = (bf16[1,704,512]{2,1,0:T(8,128)(2,1)S(1)}, bf16[1,704,512]{2,1,0:T(8,128)(2,1)S(1)}, bf16[1,704,512]{2,1,0:T(8,128)(2,1)S(1)}, bf16[1,704,512]{2,1,0:T(8,128)(2,1)S(1)}) custom-call(bf16[128,256]{1,0:T(8,128)(2,1)S(1)} %get-tuple-element.32.mix_ref, bf16[8,352,512]{2,1,0:T(8,128)(2,1)S(1)} %get-tuple-element.33.refs_0_, ...), custom_call_target="tpu_custom_call" | custom-call | flops 67108864 | bytes 8650752 | tf_op jit(solution)/shard_map/pallas_call | solution.py:31
  18.6 0.0 collective-permute-done.3.refs_3_
  18.7 1.0 %shard_map.68 = (bf16[1,704,256]{2,1,0:T(8,128)(2,1)S(1)}, bf16[1,704,256]{2,1,0:T(8,128)(2,1)S(1)}, bf16[1,704,256]{2,1,0:T(8,128)(2,1)S(1)}, bf16[1,704,256]{2,1,0:T(8,128)(2,1)S(1)}) custom-call(s32[1]{0:T(128)} %bitcast.1.core, bf16[256,512]{1,0:T(8,128)(2,1)S(1)} %get-tuple-element.26.refs_3_.own, bf16[144,512]{1,0:T(8,128)(2,1)S(1)} %collective-permute-done.refs_0_, ...), custom_call_target="tpu_custom_call" | custom-call | flops 738197504 | bytes 5373952 | tf_op jit(solution)/shard_map/pallas_call | solution.py:31
  19.6 1.3 %collective-permute-start.4 = (bf16[1,704,256]{2,1,0:T(8,128)(2,1)S(1)}, bf16[1,704,256]{2,1,0:T(8,128)(2,1)S(1)}, u32[]{:S(2)}, u32[]{:S(2)}) collective-permute-start(bf16[1,704,256]{2,1,0:T(8,128)(2,1)S(1)} %get-tuple-element.40), channel_id=1, source_target_pairs={{0,8},{8,0},{16,24},{24,16},{1,9},{9,1},{17,25},{25,17},{2,10},{10... | collective-permute-start | bytes 1081352 | tf_op jit(solution)/shard_map/ppermute | solution.py:23
  20.9 0.8 %collective-permute-start.5 = (bf16[1,704,256]{2,1,0:T(8,128)(2,1)S(1)}, bf16[1,704,256]{2,1,0:T(8,128)(2,1)S(1)}, u32[]{:S(2)}, u32[]{:S(2)}) collective-permute-start(bf16[1,704,256]{2,1,0:T(8,128)(2,1)S(1)} %get-tuple-element.41), channel_id=1, source_target_pairs={{0,16},{8,24},{16,0},{24,8},{1,17},{9,25},{17,1},{25,9},{2,18},{10... | collective-permute-start | bytes 1081352 | tf_op jit(solution)/shard_map/ppermute | solution.py:23
  21.8 3.7 %collective-permute-done.7.refs_5_ = bf16[1,352,512]{2,1,0:T(8,128)(2,1)S(1)} collective-permute-done((bf16[1,352,512]{2,1,0:T(8,128)(2,1)S(1)}, bf16[1,352,512]{2,1,0:T(8,128)(2,1)S(1)}, u32[]{:S(2)}, u32[]{:S(2)}) %collective-permute-start.7) | collective-permute-done | bytes 360480 | tf_op jit(solution)/shard_map/ppermute | solution.py:23
  25.4 1.5 %collective-permute-start.6 = (bf16[1,704,256]{2,1,0:T(8,128)(2,1)S(1)}, bf16[1,704,256]{2,1,0:T(8,128)(2,1)S(1)}, u32[]{:S(2)}, u32[]{:S(2)}) collective-permute-start(bf16[1,704,256]{2,1,0:T(8,128)(2,1)S(1)} %get-tuple-element.42), channel_id=1, source_target_pairs={{0,24},{8,16},{16,8},{24,0},{1,25},{9,17},{17,9},{25,1},{2,26},{10... | collective-permute-start | bytes 1081352 | tf_op jit(solution)/shard_map/ppermute | solution.py:23
  26.9 7.5 %collective-permute-done.8.refs_6_ = bf16[1,352,512]{2,1,0:T(8,128)(2,1)S(1)} collective-permute-done((bf16[1,352,512]{2,1,0:T(8,128)(2,1)S(1)}, bf16[1,352,512]{2,1,0:T(8,128)(2,1)S(1)}, u32[]{:S(2)}, u32[]{:S(2)}) %collective-permute-start.8) | collective-permute-done | bytes 360480 | tf_op jit(solution)/shard_map/ppermute | solution.py:23
  34.4 0.0 collective-permute-done.9.refs_7_
  34.4 6.5 %collective-permute-done.4.refs_1_ = bf16[1,704,256]{2,1,0:T(8,128)(2,1)S(1)} collective-permute-done((bf16[1,704,256]{2,1,0:T(8,128)(2,1)S(1)}, bf16[1,704,256]{2,1,0:T(8,128)(2,1)S(1)}, u32[]{:S(2)}, u32[]{:S(2)}) %collective-permute-start.4) | collective-permute-done | bytes 360480 | tf_op jit(solution)/shard_map/ppermute | solution.py:23
  40.9 0.9 %collective-permute-done.5.refs_2_ = bf16[1,704,256]{2,1,0:T(8,128)(2,1)S(1)} collective-permute-done((bf16[1,704,256]{2,1,0:T(8,128)(2,1)S(1)}, bf16[1,704,256]{2,1,0:T(8,128)(2,1)S(1)}, u32[]{:S(2)}, u32[]{:S(2)}) %collective-permute-start.5) | collective-permute-done | bytes 360480 | tf_op jit(solution)/shard_map/ppermute | solution.py:23
  41.8 7.4 %collective-permute-done.6.refs_3_ = bf16[1,704,256]{2,1,0:T(8,128)(2,1)S(1)} collective-permute-done((bf16[1,704,256]{2,1,0:T(8,128)(2,1)S(1)}, bf16[1,704,256]{2,1,0:T(8,128)(2,1)S(1)}, u32[]{:S(2)}, u32[]{:S(2)}) %collective-permute-start.6) | collective-permute-done | bytes 360480 | tf_op jit(solution)/shard_map/ppermute | solution.py:23
  49.2 1.0 %shard_map.70 = bf16[2,4,32,2048]{3,2,1,0:T(8,128)(2,1)S(1)} custom-call(s32[1]{0:T(128)} %bitcast.1.core, bf16[1,704,256]{2,1,0:T(8,128)(2,1)S(1)} %get-tuple-element.39.refs_0_, bf16[1,704,256]{2,1,0:T(8,128)(2,1)S(1)} %collective-permute-done.4.refs_1_, bf16[1,704,256]{2,1,0:T(8,128)(2,1)S(1)} %collective-permute-done.5.refs_2_, ...), custom_call_target="tpu_custom_call" | custom-call | flops 369098752 | bytes 2883584 | tf_op jit(solution)/shard_map/pallas_call | solution.py:31
  50.2 0.1 collective-permute-start.10
  50.3 1.9 %collective-permute-done.10 = bf16[4,32,2048]{2,1,0:T(8,128)(2,1)S(1)} collective-permute-done((bf16[4,32,2048]{2,1,0:T(8,128)(2,1)S(1)}, bf16[4,32,2048]{2,1,0:T(8,128)(2,1)S(1)}, u32[]{:S(2)}, u32[]{:S(2)}) %collective-permute-start.10) | collective-permute-done | bytes 524320 | tf_op jit(solution)/shard_map/ppermute | solution.py:23
  52.2 0.1 fusion
  52.4 3.7 %collective-permute-start.11 = (bf16[32,2048]{1,0:T(8,128)(2,1)S(1)}, bf16[32,2048]{1,0:T(8,128)(2,1)S(1)}, u32[]{:S(2)}, u32[]{:S(2)}) collective-permute-start(bf16[32,2048]{1,0:T(8,128)(2,1)S(1)} %get-tuple-element.50), channel_id=1, source_target_pairs={{0,6},{1,7},{2,4},{3,5},{4,2},{5,3},{6,0},{7,1},{8,14},{9,15},{10,... | collective-permute-start | bytes 393224 | tf_op jit(solution)/shard_map/ppermute | solution.py:23
  56.0 0.0 collective-permute-start.12
  56.1 0.8 %collective-permute-start.13 = (bf16[32,2048]{1,0:T(8,128)(2,1)S(1)}, bf16[32,2048]{1,0:T(8,128)(2,1)S(1)}, u32[]{:S(2)}, u32[]{:S(2)}) collective-permute-start(bf16[32,2048]{1,0:T(8,128)(2,1)S(1)} %get-tuple-element.48), channel_id=1, source_target_pairs={{0,2},{1,3},{2,0},{3,1},{4,6},{5,7},{6,4},{7,5},{8,10},{9,11},{10,... | collective-permute-start | bytes 393224 | tf_op jit(solution)/shard_map/ppermute | solution.py:23
  56.8 3.8 %collective-permute-done.11.refs_0_ = bf16[32,2048]{1,0:T(8,128)(2,1)S(1)} collective-permute-done((bf16[32,2048]{1,0:T(8,128)(2,1)S(1)}, bf16[32,2048]{1,0:T(8,128)(2,1)S(1)}, u32[]{:S(2)}, u32[]{:S(2)}) %collective-permute-start.11) | collective-permute-done | bytes 131104 | tf_op jit(solution)/shard_map/ppermute | solution.py:23
  60.7 6.7 %collective-permute-done.12.refs_1_ = bf16[32,2048]{1,0:T(8,128)(2,1)S(1)} collective-permute-done((bf16[32,2048]{1,0:T(8,128)(2,1)S(1)}, bf16[32,2048]{1,0:T(8,128)(2,1)S(1)}, u32[]{:S(2)}, u32[]{:S(2)}) %collective-permute-start.12) | collective-permute-done | bytes 131104 | tf_op jit(solution)/shard_map/ppermute | solution.py:23
  67.4 0.0 collective-permute-done.13.refs_2_
  67.4 0.7 %shard_map.71 = bf16[32,2048]{1,0:T(8,128)(2,1)} custom-call(s32[1]{0:T(128)} %bitcast.my_dp, bf16[32,2048]{1,0:T(8,128)(2,1)S(1)} %collective-permute-done.11.refs_0_, bf16[32,2048]{1,0:T(8,128)(2,1)S(1)} %collective-permute-done.12.refs_1_, bf16[32,2048]{1,0:T(8,128)(2,1)S(1)} %collective-permute-done.13.refs_2_, ...), custom_call_target="tpu_custom_call" | custom-call | flops 262144 | bytes 655360 | tf_op jit(solution)/shard_map/pallas_call | solution.py:31
  (2 shorter events, 0.1 us)
Async XLA Ops:
  1.7 8.1 %collective-permute-start = (bf16[144,512]{1,0:T(8,128)(2,1)S(1)}, bf16[144,512]{1,0:T(8,128)(2,1)S(1)}, u32[]{:S(2)}, u32[]{:S(2)}) collective-permute-start(bf16[144,512]{1,0:T(8,128)(2,1)S(1)} %get-tuple-element.27.sent), channel_id=1, source_target_pairs={{0,8},{8,0},{16,24},{24,16},{1,9},{9,1},{17,25},{25,17},{2,10},{10... | collective-permute-start | bytes 442376 | tf_op jit(solution)/shard_map/ppermute | solution.py:23
  4.7 8.5 %collective-permute-start.1 = (bf16[144,512]{1,0:T(8,128)(2,1)S(1)}, bf16[144,512]{1,0:T(8,128)(2,1)S(1)}, u32[]{:S(2)}, u32[]{:S(2)}) collective-permute-start(bf16[144,512]{1,0:T(8,128)(2,1)S(1)} %get-tuple-element.28), channel_id=1, source_target_pairs={{0,16},{8,24},{16,0},{24,8},{1,17},{9,25},{17,1},{25,9},{2,18},{10... | collective-permute-start | bytes 442376 | tf_op jit(solution)/shard_map/ppermute | solution.py:23
  6.2 7.0 %collective-permute-start.2 = (bf16[144,512]{1,0:T(8,128)(2,1)S(1)}, bf16[144,512]{1,0:T(8,128)(2,1)S(1)}, u32[]{:S(2)}, u32[]{:S(2)}) collective-permute-start(bf16[144,512]{1,0:T(8,128)(2,1)S(1)} %get-tuple-element.29), channel_id=1, source_target_pairs={{0,24},{8,16},{16,8},{24,0},{1,25},{9,17},{17,9},{25,1},{2,26},{10... | collective-permute-start | bytes 442376 | tf_op jit(solution)/shard_map/ppermute | solution.py:23
  13.5 5.1 %collective-permute-start.3 = (bf16[3,128,512]{2,1,0:T(8,128)(2,1)S(1)}, bf16[3,128,512]{2,1,0:T(8,128)(2,1)S(1)}, u32[]{:S(2)}, u32[]{:S(2)}) collective-permute-start(bf16[3,128,512]{2,1,0:T(8,128)(2,1)S(1)} %get-tuple-element.31), channel_id=1, source_target_pairs={{0,1},{1,0},{2,3},{3,2},{4,5},{5,4},{6,7},{7,6},{8,9},{9,8},{10,11... | collective-permute-start | bytes 1179656 | tf_op jit(solution)/shard_map/ppermute | solution.py:23
  14.2 11.3 %collective-permute-start.7 = (bf16[1,352,512]{2,1,0:T(8,128)(2,1)S(1)}, bf16[1,352,512]{2,1,0:T(8,128)(2,1)S(1)}, u32[]{:S(2)}, u32[]{:S(2)}) collective-permute-start(bf16[1,352,512]{2,1,0:T(8,128)(2,1)S(1)} %get-tuple-element.44), channel_id=1, source_target_pairs={{0,8},{8,0},{16,24},{24,16},{1,9},{9,1},{17,25},{25,17},{2,10},{10... | collective-permute-start | bytes 1081352 | tf_op jit(solution)/shard_map/ppermute | solution.py:23
  15.5 19.0 %collective-permute-start.8 = (bf16[1,352,512]{2,1,0:T(8,128)(2,1)S(1)}, bf16[1,352,512]{2,1,0:T(8,128)(2,1)S(1)}, u32[]{:S(2)}, u32[]{:S(2)}) collective-permute-start(bf16[1,352,512]{2,1,0:T(8,128)(2,1)S(1)} %get-tuple-element.45), channel_id=1, source_target_pairs={{0,16},{8,24},{16,0},{24,8},{1,17},{9,25},{17,1},{25,9},{2,18},{10... | collective-permute-start | bytes 1081352 | tf_op jit(solution)/shard_map/ppermute | solution.py:23
  16.3 18.2 %collective-permute-start.9 = (bf16[1,352,512]{2,1,0:T(8,128)(2,1)S(1)}, bf16[1,352,512]{2,1,0:T(8,128)(2,1)S(1)}, u32[]{:S(2)}, u32[]{:S(2)}) collective-permute-start(bf16[1,352,512]{2,1,0:T(8,128)(2,1)S(1)} %get-tuple-element.46), channel_id=1, source_target_pairs={{0,24},{8,16},{16,8},{24,0},{1,25},{9,17},{17,9},{25,1},{2,26},{10... | collective-permute-start | bytes 1081352 | tf_op jit(solution)/shard_map/ppermute | solution.py:23
  19.6 21.3 %collective-permute-start.4 = (bf16[1,704,256]{2,1,0:T(8,128)(2,1)S(1)}, bf16[1,704,256]{2,1,0:T(8,128)(2,1)S(1)}, u32[]{:S(2)}, u32[]{:S(2)}) collective-permute-start(bf16[1,704,256]{2,1,0:T(8,128)(2,1)S(1)} %get-tuple-element.40), channel_id=1, source_target_pairs={{0,8},{8,0},{16,24},{24,16},{1,9},{9,1},{17,25},{25,17},{2,10},{10... | collective-permute-start | bytes 1081352 | tf_op jit(solution)/shard_map/ppermute | solution.py:23
  20.9 20.9 %collective-permute-start.5 = (bf16[1,704,256]{2,1,0:T(8,128)(2,1)S(1)}, bf16[1,704,256]{2,1,0:T(8,128)(2,1)S(1)}, u32[]{:S(2)}, u32[]{:S(2)}) collective-permute-start(bf16[1,704,256]{2,1,0:T(8,128)(2,1)S(1)} %get-tuple-element.41), channel_id=1, source_target_pairs={{0,16},{8,24},{16,0},{24,8},{1,17},{9,25},{17,1},{25,9},{2,18},{10... | collective-permute-start | bytes 1081352 | tf_op jit(solution)/shard_map/ppermute | solution.py:23
  25.4 23.8 %collective-permute-start.6 = (bf16[1,704,256]{2,1,0:T(8,128)(2,1)S(1)}, bf16[1,704,256]{2,1,0:T(8,128)(2,1)S(1)}, u32[]{:S(2)}, u32[]{:S(2)}) collective-permute-start(bf16[1,704,256]{2,1,0:T(8,128)(2,1)S(1)} %get-tuple-element.42), channel_id=1, source_target_pairs={{0,24},{8,16},{16,8},{24,0},{1,25},{9,17},{17,9},{25,1},{2,26},{10... | collective-permute-start | bytes 1081352 | tf_op jit(solution)/shard_map/ppermute | solution.py:23
  50.2 2.0 %collective-permute-start.10 = (bf16[4,32,2048]{2,1,0:T(8,128)(2,1)S(1)}, bf16[4,32,2048]{2,1,0:T(8,128)(2,1)S(1)}, u32[]{:S(2)}, u32[]{:S(2)}) collective-permute-start(bf16[4,32,2048]{2,1,0:T(8,128)(2,1)S(1)} %slice_bitcast_fusion), channel_id=1, source_target_pairs={{0,1},{1,0},{2,3},{3,2},{4,5},{5,4},{6,7},{7,6},{8,9},{9,8},{10,11... | collective-permute-start | bytes 1572872 | tf_op jit(solution)/shard_map/ppermute | solution.py:23
  52.4 8.3 %collective-permute-start.11 = (bf16[32,2048]{1,0:T(8,128)(2,1)S(1)}, bf16[32,2048]{1,0:T(8,128)(2,1)S(1)}, u32[]{:S(2)}, u32[]{:S(2)}) collective-permute-start(bf16[32,2048]{1,0:T(8,128)(2,1)S(1)} %get-tuple-element.50), channel_id=1, source_target_pairs={{0,6},{1,7},{2,4},{3,5},{4,2},{5,3},{6,0},{7,1},{8,14},{9,15},{10,... | collective-permute-start | bytes 393224 | tf_op jit(solution)/shard_map/ppermute | solution.py:23
  56.0 11.4 %collective-permute-start.12 = (bf16[32,2048]{1,0:T(8,128)(2,1)S(1)}, bf16[32,2048]{1,0:T(8,128)(2,1)S(1)}, u32[]{:S(2)}, u32[]{:S(2)}) collective-permute-start(bf16[32,2048]{1,0:T(8,128)(2,1)S(1)} %get-tuple-element.49), channel_id=1, source_target_pairs={{0,4},{1,5},{2,6},{3,7},{4,0},{5,1},{6,2},{7,3},{8,12},{9,13},{10,... | collective-permute-start | bytes 393224 | tf_op jit(solution)/shard_map/ppermute | solution.py:23
  56.1 11.4 %collective-permute-start.13 = (bf16[32,2048]{1,0:T(8,128)(2,1)S(1)}, bf16[32,2048]{1,0:T(8,128)(2,1)S(1)}, u32[]{:S(2)}, u32[]{:S(2)}) collective-permute-start(bf16[32,2048]{1,0:T(8,128)(2,1)S(1)} %get-tuple-element.48), channel_id=1, source_target_pairs={{0,2},{1,3},{2,0},{3,1},{4,6},{5,7},{6,4},{7,5},{8,10},{9,11},{10,... | collective-permute-start | bytes 393224 | tf_op jit(solution)/shard_map/ppermute | solution.py:23

commit v6 on v3

--- a/solution.py
+++ b/solution.py
@@ -62,36 +62,30 @@
     ones = member == lax.broadcasted_iota(jnp.int32, (extra, rows), 0)
     ones = jnp.where(ones, 1.0, 0.0).astype(BF16)
     start = pl.multiple_of(core[0] * half, half)
-    copies[dp].wait()
-    copies[dp + 1].wait()
-    logits = jnp.zeros((extra, experts), F32)
+    for copy in copies:
+        copy.wait()
+    totals = [jnp.zeros((experts, depth), F32)] * (own_segs + 1)
     for k in range(dp):
-        copies[k].wait()
         block = own[...] if k == 0 else blocks[k - 1]
+        weight = routers[:, pl.ds(columns[k], depth)]
         means = jnp.dot(ones, block, preferred_element_type=F32) / SEG
-        place = lax.broadcasted_iota(jnp.int32, means.shape, 0)
-        means = jnp.where(place == own_segs, carries[:, pl.ds(columns[k], depth)], means)
-        logits += lax.dot_general(
-            means,
-            routers[:, pl.ds(columns[k], depth)],
-            (((1,), (1,)), ((), ())),
-            precision=lax.Precision.HIGHEST,
-            preferred_element_type=F32,
-        )
+        for j in range(own_segs):
+            totals[j] += means[j : j + 1, :] * weight
+        totals[own_segs] += carries[:, pl.ds(columns[k], depth)] * weight
         if k > 0:
             sends[k - 1][:half] = blocks[k - 1, pl.ds(start, half), :]
     lane = lax.broadcasted_iota(jnp.int32, (experts, LANES), 1)
-    copied = lane % experts == lax.broadcasted_iota(jnp.int32, (experts, LANES), 0)
-    logits = jnp.dot(
-        logits,
-        jnp.where(copied, 1.0, 0.0),
-        precision=lax.Precision.HIGHEST,
-        preferred_element_type=F32,
-    )
+    place = lane % experts == lax.broadcasted_iota(jnp.int32, (experts, LANES), 0)
+    row = lax.broadcasted_iota(jnp.int32, (extra, LANES), 0)
+    lane = lax.broadcasted_iota(jnp.int32, (extra, LANES), 1)
+    logits = jnp.zeros((extra, LANES), F32)
+    for j, total in enumerate(totals):
+        column = jnp.sum(total, axis=1, keepdims=True)
+        spread = jnp.sum(jnp.where(place, column, 0.0), axis=0, keepdims=True)
+        logits = jnp.where(row == j, spread, logits)
     high = logits.astype(BF16).astype(F32)
     middle = (logits - high).astype(BF16).astype(F32)
     low = logits - high - middle
-    lane = lax.broadcasted_iota(jnp.int32, logits.shape, 1)
     terms = jnp.where(lane < experts, high, jnp.where(lane < 2 * experts, middle, low))
     terms = jnp.where(lane < 3 * experts, terms, 0.0).astype(BF16)
     for send in sends:
@@ -170,7 +164,7 @@
                 outs[k][:, at : at + block, :] = out[k]
 
 
-def merge(mix, dp, own_segs, weights, after=()):
+def merge(mix, dp, own_segs, weights):
     experts, rows, cols = weights[0].shape
     total = rows * len(weights)
     count = len(weights)
@@ -181,8 +175,8 @@
     return call(
         kernel,
         [((own_segs, total, cols), BF16)] * dp,
-        [VMEM] * (1 + count) + [ANY] * len(after),
-        (mix, *weights, *after),
+        [VMEM] * (1 + count),
+        (mix, *weights),
         2 * mix.size * total * cols // rows,
         2 * total * cols * (experts + dp * own_segs),
     )
@@ -224,12 +218,12 @@
 
 
 def down_columns(core, hidden, downs, mixed):
-    own_segs, cols = downs[0].shape[0], downs[0].shape[2]
+    cols = downs[0].shape[2]
     rows = mixed.shape[2]
-    for j in range(own_segs):
+    for j, part in enumerate(hidden):
         for k, down in enumerate(downs):
             out = lax.dot_general(
-                hidden[j], down[j], (((0,), (0,)), ((), ())), preferred_element_type=F32
+                part, down[j], (((0,), (0,)), ((), ())), preferred_element_type=F32
             ).astype(BF16)
             for i in range(SEG // rows):
                 at = j * (SEG // rows) + i
@@ -239,7 +233,7 @@
 
 
 def first_kernel(dp, core, *refs):
-    parts, downs, (hidden, mixed) = refs[:dp], refs[dp:-2], refs[-2:]
+    parts, downs, hidden, mixed = refs[:dp], refs[dp:-2], refs[-2], refs[-1]
     half = hidden.shape[1]
     kept = []
     for j in range(hidden.shape[0]):
@@ -253,7 +247,8 @@
 
 
 def second_kernel(count, core, hidden, *refs):
-    down_columns(core[0], hidden, refs[:count], refs[-1])
+    kept = [hidden[j] for j in range(hidden.shape[0])]
+    down_columns(core[0], kept, refs[:count], refs[-1])
 
 
 def finish_kernel(groups, lines, my_dp, *refs):
@@ -275,7 +270,7 @@
     pair = mixed[0].astype(F32) + swap(mixed[1], "tensor", 1).astype(F32)
     pair = pair.astype(BF16)
     pieces = [lax.dynamic_index_in_dim(pair, my_line ^ k, 0, keepdims=False) for k in range(lines)]
-    return [pieces[0]] + [swap(pieces[k], "tensor", 2 * k) for k in range(1, lines)]
+    return [swap(pieces[k], "tensor", 2 * k) for k in range(lines - 1, 0, -1)] + [pieces[0]]
 
 
 def on_device(tokens, gate_weight, up_weight, down_weight, router_weight, carry_mean):
@@ -288,10 +283,7 @@
     own_segs = own_rows // SEG
     experts, depth, hidden_count = gate_weight.shape
     cols = down_weight.shape[2]
-    steps = tuple(range(dp))
     segs = dp * own_segs
-    late = tuple(k for k in steps if k.bit_count() == 1)
-    early = tuple(k for k in steps if k not in late)
 
     extra = -(-(own_segs + 1) // 16) * 16
     own, *sends = call(
@@ -329,36 +321,33 @@
         2 * own_rows * width,
     )
     other = swap(stacked, "tensor", 1)
+    merged_down = merge(mix, dp, own_segs, (down,))
+    downs = [block if k == 0 else swap(block, "dp", k) for k, block in enumerate(merged_down)]
     merged = merge(mix, dp, own_segs, (gate_t, up_t))
     partial_pre = preact(core, own, brought, other, merged)
     parts = [partial_pre[0]] + [swap(partial_pre[k], "dp", k) for k in range(1, dp)]
 
-    merged_down = merge(mix, dp, own_segs, (down,), (partial_pre[0],))
-    downs = [block if k == 0 else swap(block, "dp", k) for k, block in enumerate(merged_down)]
-
     rows = own_rows // tensor
-    half_flops = own_rows * hidden_count * cols
-    hidden, mixed_early = call(
+    early, late = tuple(range(dp - 1)), (dp - 1,)
+    flops = 2 * own_rows * hidden_count * cols
+    hidden, mixed = call(
         functools.partial(first_kernel, dp),
-        [
-            ((own_segs, hidden_count, SEG), BF16),
-            ((2, lines, rows, len(early) * cols), BF16),
-        ],
+        [((own_segs, hidden_count, SEG), BF16), ((2, lines, rows, len(early) * cols), BF16)],
         [SMEM] + [VMEM] * (dp + len(early)),
         (core, *parts, *[downs[k] for k in early]),
-        2 * half_flops * len(early),
-        2 * (own_rows * hidden_count * 3 + hidden_count * cols * len(early)),
-    )
-    early_pieces = tensor_sum_pieces(mixed_early, lines)
-    (mixed_late,) = call(
+        flops * len(early),
+        2 * (own_rows * hidden_count * dp * 2 + hidden_count * cols * len(early)),
+    )
+    early_pieces = tensor_sum_pieces(mixed, lines)
+    (mixed,) = call(
         functools.partial(second_kernel, len(late)),
         [((2, lines, rows, len(late) * cols), BF16)],
-        [SMEM] + [VMEM] * (1 + len(late)) + [ANY],
-        (core, hidden, *[downs[k] for k in late], early_pieces[0]),
-        2 * half_flops * len(late),
+        [SMEM] + [VMEM] * (1 + len(late)) + [ANY] * lines,
+        (core, hidden, *[downs[k] for k in late], *early_pieces),
+        flops * len(late),
         2 * (own_rows * hidden_count + hidden_count * cols * len(late)),
     )
-    late_pieces = tensor_sum_pieces(mixed_late, lines)
+    late_pieces = tensor_sum_pieces(mixed, lines)
     (out,) = call(
         functools.partial(finish_kernel, (early, late), lines),
         [((rows, width), BF16)],

time: 73.1 us -> 66.6 us (0.911)
  waiting for transfers between devices: 40.9 us -> 35.1 us
  Pallas kernels: 10.6 us -> 9.86 us
    ppermute x18, waiting for transfers between devices: 40.9 us -> 35.1 us  [swap(): return lax.ppermute(value, axis, [(i, i ^ step) for i in range(count)])]
  transfers between devices with their start and end apart: 18 -> 18, of which waited for: 10 -> 11; matrix products, arithmetic and copies ran while one was open for 0% -> 0% of each run, Pallas kernels for 7% -> 9%
where the time goes in v6:
time: 66.6 us; the launch traced here: 66.5 us
  waiting for transfers between devices  35.1 us (53%)
  starting transfers between devices  21.2 us (32%)
  Pallas kernels  9.86 us (15%)
    ppermute x18, waiting for transfers between devices, swap(): return lax.ppermute(value, axis, [(i, i ^ step) for i in range(count)])  35.1 us
    ppermute x18, starting transfers between devices, swap(): return lax.ppermute(value, axis, [(i, i ^ step) for i in range(count)])  21.2 us
    pallas_call x9, Pallas kernels, call(): pl.pallas_call(kernel, out_shape=[jax.ShapeDtypeStruct(shape, dtype) for...  9.86 us
  transfers between devices with their start and end apart: 18, of which 11 were waited for; matrix products, arithmetic and copies ran while one was open for 0% of the time, Pallas kernels for 9%

profile of v6, /device:TPU:0, one launch (start us, length us, event | category | flops | bytes accessed | tf_op | source)
XLA Modules:
  0.0 66.5 jit_solution(2932690484661509909)
XLA Ops:
  0.0 1.7 %shard_map.64 = (bf16[256,512]{1,0:T(8,128)(2,1)S(1)}, bf16[144,512]{1,0:T(8,128)(2,1)S(1)}, bf16[144,512]{1,0:T(8,128)(2,1)S(1)}, bf16[144,512]{1,0:T(8,128)(2,1)S(1)}) custom-call(s32[1]{0:T(128)} %bitcast.my_dp, s32[1]{0:T(128)} %bitcast.1.core, bf16[256,2048]{1,0:T(8,128)(2,1)} %tokens.1, f32[8,2048]{1,0:T(8,128)} %bitcast.36, f32[1,2048]{1,0:T(1,128)} %bitcast.37), custom_call_target="tpu_custom_call" | custom-call | flops 16777216 | bytes 2097152 | tf_op jit(solution)/shard_map/pallas_call | solution.py:31
  1.7 3.0 %collective-permute-start = (bf16[144,512]{1,0:T(8,128)(2,1)S(1)}, bf16[144,512]{1,0:T(8,128)(2,1)S(1)}, u32[]{:S(2)}, u32[]{:S(2)}) collective-permute-start(bf16[144,512]{1,0:T(8,128)(2,1)S(1)} %get-tuple-element.29.sent), channel_id=1, source_target_pairs={{0,8},{8,0},{16,24},{24,16},{1,9},{9,1},{17,25},{25,17},{2,10},{10... | collective-permute-start | bytes 442376 | tf_op jit(solution)/shard_map/ppermute | solution.py:23
  4.7 1.5 %collective-permute-start.1 = (bf16[144,512]{1,0:T(8,128)(2,1)S(1)}, bf16[144,512]{1,0:T(8,128)(2,1)S(1)}, u32[]{:S(2)}, u32[]{:S(2)}) collective-permute-start(bf16[144,512]{1,0:T(8,128)(2,1)S(1)} %get-tuple-element.30), channel_id=1, source_target_pairs={{0,16},{8,24},{16,0},{24,8},{1,17},{9,25},{17,1},{25,9},{2,18},{10... | collective-permute-start | bytes 442376 | tf_op jit(solution)/shard_map/ppermute | solution.py:23
  6.2 0.0 collective-permute-start.2
  6.2 3.6 %shard_map.65 = (bf16[8,352,512]{2,1,0:T(8,128)(2,1)S(1)}, bf16[8,352,512]{2,1,0:T(8,128)(2,1)S(1)}, bf16[8,352,512]{2,1,0:T(8,128)(2,1)S(1)}) custom-call(bf16[8,352,512]{2,1,0:T(8,128)(2,1)} %bitcast.34, bf16[8,352,512]{2,1,0:T(8,128)(2,1)} %bitcast.35, bf16[8,352,512]{2,1,0:T(8,128)(2,1)} %refs_2_.1, bf16[256,512]{1,0:T(8,128)(2,1)S(1)} %get-tuple-element.28.refs_3_.own), custom_call_target="tpu_custom_call" | custom-call | bytes 17301504 | tf_op jit(solution)/shard_map/pallas_call | solution.py:31
  9.8 0.0 collective-permute-done.refs_0_
  9.8 3.3 %collective-permute-done.1.refs_1_ = bf16[144,512]{1,0:T(8,128)(2,1)S(1)} collective-permute-done((bf16[144,512]{1,0:T(8,128)(2,1)S(1)}, bf16[144,512]{1,0:T(8,128)(2,1)S(1)}, u32[]{:S(2)}, u32[]{:S(2)}) %collective-permute-start.1) | collective-permute-done | bytes 147488 | tf_op jit(solution)/shard_map/ppermute | solution.py:23
  13.2 0.0 collective-permute-done.2.refs_2_
  13.2 0.4 shard_map.66
  13.5 0.1 collective-permute-start.3
  13.6 0.5 shard_map.69
  14.2 1.3 %collective-permute-start.7 = (bf16[1,352,512]{2,1,0:T(8,128)(2,1)S(1)}, bf16[1,352,512]{2,1,0:T(8,128)(2,1)S(1)}, u32[]{:S(2)}, u32[]{:S(2)}) collective-permute-start(bf16[1,352,512]{2,1,0:T(8,128)(2,1)S(1)} %get-tuple-element.46), channel_id=1, source_target_pairs={{0,8},{8,0},{16,24},{24,16},{1,9},{9,1},{17,25},{25,17},{2,10},{10... | collective-permute-start | bytes 1081352 | tf_op jit(solution)/shard_map/ppermute | solution.py:23
  15.5 0.8 %collective-permute-start.8 = (bf16[1,352,512]{2,1,0:T(8,128)(2,1)S(1)}, bf16[1,352,512]{2,1,0:T(8,128)(2,1)S(1)}, u32[]{:S(2)}, u32[]{:S(2)}) collective-permute-start(bf16[1,352,512]{2,1,0:T(8,128)(2,1)S(1)} %get-tuple-element.47), channel_id=1, source_target_pairs={{0,16},{8,24},{16,0},{24,8},{1,17},{9,25},{17,1},{25,9},{2,18},{10... | collective-permute-start | bytes 1081352 | tf_op jit(solution)/shard_map/ppermute | solution.py:23
  16.3 0.9 %shard_map.67 = (bf16[1,704,512]{2,1,0:T(8,128)(2,1)S(1)}, bf16[1,704,512]{2,1,0:T(8,128)(2,1)S(1)}, bf16[1,704,512]{2,1,0:T(8,128)(2,1)S(1)}, bf16[1,704,512]{2,1,0:T(8,128)(2,1)S(1)}) custom-call(bf16[128,256]{1,0:T(8,128)(2,1)S(1)} %get-tuple-element.34.mix_ref, bf16[8,352,512]{2,1,0:T(8,128)(2,1)S(1)} %get-tuple-element.35.refs_0_, ...), custom_call_target="tpu_custom_call" | custom-call | flops 67108864 | bytes 8650752 | tf_op jit(solution)/shard_map/pallas_call | solution.py:31
  17.2 0.0 collective-permute-done.3.refs_3_
  17.2 1.0 %shard_map.68 = (bf16[1,704,256]{2,1,0:T(8,128)(2,1)S(1)}, bf16[1,704,256]{2,1,0:T(8,128)(2,1)S(1)}, bf16[1,704,256]{2,1,0:T(8,128)(2,1)S(1)}, bf16[1,704,256]{2,1,0:T(8,128)(2,1)S(1)}) custom-call(s32[1]{0:T(128)} %bitcast.1.core, bf16[256,512]{1,0:T(8,128)(2,1)S(1)} %get-tuple-element.28.refs_3_.own, bf16[144,512]{1,0:T(8,128)(2,1)S(1)} %collective-permute-done.refs_0_, ...), custom_call_target="tpu_custom_call" | custom-call | flops 738197504 | bytes 5373952 | tf_op jit(solution)/shard_map/pallas_call | solution.py:31
  18.2 1.6 %collective-permute-start.4 = (bf16[1,704,256]{2,1,0:T(8,128)(2,1)S(1)}, bf16[1,704,256]{2,1,0:T(8,128)(2,1)S(1)}, u32[]{:S(2)}, u32[]{:S(2)}) collective-permute-start(bf16[1,704,256]{2,1,0:T(8,128)(2,1)S(1)} %get-tuple-element.42), channel_id=1, source_target_pairs={{0,8},{8,0},{16,24},{24,16},{1,9},{9,1},{17,25},{25,17},{2,10},{10... | collective-permute-start | bytes 1081352 | tf_op jit(solution)/shard_map/ppermute | solution.py:23
  19.8 0.5 collective-permute-start.5
  20.3 1.5 %collective-permute-start.6 = (bf16[1,704,256]{2,1,0:T(8,128)(2,1)S(1)}, bf16[1,704,256]{2,1,0:T(8,128)(2,1)S(1)}, u32[]{:S(2)}, u32[]{:S(2)}) collective-permute-start(bf16[1,704,256]{2,1,0:T(8,128)(2,1)S(1)} %get-tuple-element.44), channel_id=1, source_target_pairs={{0,24},{8,16},{16,8},{24,0},{1,25},{9,17},{17,9},{25,1},{2,26},{10... | collective-permute-start | bytes 1081352 | tf_op jit(solution)/shard_map/ppermute | solution.py:23
  21.8 3.7 %collective-permute-done.7.refs_5_ = bf16[1,352,512]{2,1,0:T(8,128)(2,1)S(1)} collective-permute-done((bf16[1,352,512]{2,1,0:T(8,128)(2,1)S(1)}, bf16[1,352,512]{2,1,0:T(8,128)(2,1)S(1)}, u32[]{:S(2)}, u32[]{:S(2)}) %collective-permute-start.7) | collective-permute-done | bytes 360480 | tf_op jit(solution)/shard_map/ppermute | solution.py:23
  25.4 1.3 %collective-permute-done.8.refs_6_ = bf16[1,352,512]{2,1,0:T(8,128)(2,1)S(1)} collective-permute-done((bf16[1,352,512]{2,1,0:T(8,128)(2,1)S(1)}, bf16[1,352,512]{2,1,0:T(8,128)(2,1)S(1)}, u32[]{:S(2)}, u32[]{:S(2)}) %collective-permute-start.8) | collective-permute-done | bytes 360480 | tf_op jit(solution)/shard_map/ppermute | solution.py:23
  26.7 6.5 %collective-permute-done.4.refs_1_ = bf16[1,704,256]{2,1,0:T(8,128)(2,1)S(1)} collective-permute-done((bf16[1,704,256]{2,1,0:T(8,128)(2,1)S(1)}, bf16[1,704,256]{2,1,0:T(8,128)(2,1)S(1)}, u32[]{:S(2)}, u32[]{:S(2)}) %collective-permute-start.4) | collective-permute-done | bytes 360480 | tf_op jit(solution)/shard_map/ppermute | solution.py:23
  33.2 6.7 %collective-permute-done.5.refs_2_ = bf16[1,704,256]{2,1,0:T(8,128)(2,1)S(1)} collective-permute-done((bf16[1,704,256]{2,1,0:T(8,128)(2,1)S(1)}, bf16[1,704,256]{2,1,0:T(8,128)(2,1)S(1)}, u32[]{:S(2)}, u32[]{:S(2)}) %collective-permute-start.5) | collective-permute-done | bytes 360480 | tf_op jit(solution)/shard_map/ppermute | solution.py:23
  39.8 1.6 %collective-permute-done.6.refs_3_ = bf16[1,704,256]{2,1,0:T(8,128)(2,1)S(1)} collective-permute-done((bf16[1,704,256]{2,1,0:T(8,128)(2,1)S(1)}, bf16[1,704,256]{2,1,0:T(8,128)(2,1)S(1)}, u32[]{:S(2)}, u32[]{:S(2)}) %collective-permute-start.6) | collective-permute-done | bytes 360480 | tf_op jit(solution)/shard_map/ppermute | solution.py:23
  41.4 0.8 %shard_map.70 = (bf16[1,352,256]{2,1,0:T(8,128)(2,1)S(1)}, bf16[2,4,32,1536]{3,2,1,0:T(8,128)(2,1)S(1)}) custom-call(s32[1]{0:T(128)} %bitcast.1.core, bf16[1,704,256]{2,1,0:T(8,128)(2,1)S(1)} %get-tuple-element.41.refs_0_, bf16[1,704,256]{2,1,0:T(8,128)(2,1)S(1)} %collective-permute-done.4.refs_1_, bf16[1,704,256]{2,1,0:T(8,128)(2,1)S(1)} %collective-permute-done.5.refs_2_, ...), custom_call_target="tpu_custom_call" | custom-call | flops 276824064 | bytes 2523136 | tf_op jit(solution)/shard_map/pallas_call | solution.py:31
  42.3 0.1 collective-permute-start.9
  42.4 1.8 %collective-permute-start.13 = (bf16[1,352,512]{2,1,0:T(8,128)(2,1)S(1)}, bf16[1,352,512]{2,1,0:T(8,128)(2,1)S(1)}, u32[]{:S(2)}, u32[]{:S(2)}) collective-permute-start(bf16[1,352,512]{2,1,0:T(8,128)(2,1)S(1)} %get-tuple-element.50), channel_id=1, source_target_pairs={{0,24},{8,16},{16,8},{24,0},{1,25},{9,17},{17,9},{25,1},{2,26},{10... | collective-permute-start | bytes 1081352 | tf_op jit(solution)/shard_map/ppermute | solution.py:23
  44.2 0.0 collective-permute-done.9
  44.2 0.1 fusion
  44.3 3.7 %collective-permute-start.10 = (bf16[32,1536]{1,0:T(8,128)(2,1)S(1)}, bf16[32,1536]{1,0:T(8,128)(2,1)S(1)}, u32[]{:S(2)}, u32[]{:S(2)}) collective-permute-start(bf16[32,1536]{1,0:T(8,128)(2,1)S(1)} %get-tuple-element.54), channel_id=1, source_target_pairs={{0,6},{1,7},{2,4},{3,5},{4,2},{5,3},{6,0},{7,1},{8,14},{9,15},{10,... | collective-permute-start | bytes 294920 | tf_op jit(solution)/shard_map/ppermute | solution.py:23
  48.0 0.0 collective-permute-start.11
  48.0 0.8 %collective-permute-start.12 = (bf16[32,1536]{1,0:T(8,128)(2,1)S(1)}, bf16[32,1536]{1,0:T(8,128)(2,1)S(1)}, u32[]{:S(2)}, u32[]{:S(2)}) collective-permute-start(bf16[32,1536]{1,0:T(8,128)(2,1)S(1)} %get-tuple-element.52), channel_id=1, source_target_pairs={{0,2},{1,3},{2,0},{3,1},{4,6},{5,7},{6,4},{7,5},{8,10},{9,11},{10,... | collective-permute-start | bytes 294920 | tf_op jit(solution)/shard_map/ppermute | solution.py:23
  48.8 5.3 %collective-permute-done.13.refs_0_ = bf16[1,352,512]{2,1,0:T(8,128)(2,1)S(1)} collective-permute-done((bf16[1,352,512]{2,1,0:T(8,128)(2,1)S(1)}, bf16[1,352,512]{2,1,0:T(8,128)(2,1)S(1)}, u32[]{:S(2)}, u32[]{:S(2)}) %collective-permute-start.13) | collective-permute-done | bytes 360480 | tf_op jit(solution)/shard_map/ppermute | solution.py:23
  54.1 0.0 collective-permute-done.10.refs_1_.refs_0_
  54.1 2.5 %collective-permute-done.11.refs_2_.refs_1_ = bf16[32,1536]{1,0:T(8,128)(2,1)S(1)} collective-permute-done((bf16[32,1536]{1,0:T(8,128)(2,1)S(1)}, bf16[32,1536]{1,0:T(8,128)(2,1)S(1)}, u32[]{:S(2)}, u32[]{:S(2)}) %collective-permute-start.11) | collective-permute-done | bytes 98336 | tf_op jit(solution)/shard_map/ppermute | solution.py:23
  56.6 0.0 collective-permute-done.12.refs_3_.refs_2_
  56.6 0.3 shard_map.71
  56.9 0.1 collective-permute-start.14
  57.0 1.3 %collective-permute-done.14 = bf16[4,32,512]{2,1,0:T(8,128)(2,1)S(1)} collective-permute-done((bf16[4,32,512]{2,1,0:T(8,128)(2,1)S(1)}, bf16[4,32,512]{2,1,0:T(8,128)(2,1)S(1)}, u32[]{:S(2)}, u32[]{:S(2)}) %collective-permute-start.14) | collective-permute-done | bytes 131104 | tf_op jit(solution)/shard_map/ppermute | solution.py:23
  58.4 2.5 %collective-permute-start.15 = (bf16[32,512]{1,0:T(8,128)(2,1)S(1)}, bf16[32,512]{1,0:T(8,128)(2,1)S(1)}, u32[]{:S(2)}, u32[]{:S(2)}) collective-permute-start(bf16[32,512]{1,0:T(8,128)(2,1)S(1)} %get-tuple-element.58), channel_id=1, source_target_pairs={{0,6},{1,7},{2,4},{3,5},{4,2},{5,3},{6,0},{7,1},{8,14},{9,15},{10,... | collective-permute-start | bytes 98312 | tf_op jit(solution)/shard_map/ppermute | solution.py:23
  61.0 0.0 collective-permute-start.16
  61.0 1.9 %collective-permute-start.17 = (bf16[32,512]{1,0:T(8,128)(2,1)S(1)}, bf16[32,512]{1,0:T(8,128)(2,1)S(1)}, u32[]{:S(2)}, u32[]{:S(2)}) collective-permute-start(bf16[32,512]{1,0:T(8,128)(2,1)S(1)} %get-tuple-element.56), channel_id=1, source_target_pairs={{0,2},{1,3},{2,0},{3,1},{4,6},{5,7},{6,4},{7,5},{8,10},{9,11},{10,... | collective-permute-start | bytes 98312 | tf_op jit(solution)/shard_map/ppermute | solution.py:23
  62.9 1.3 %collective-permute-done.15.refs_4_ = bf16[32,512]{1,0:T(8,128)(2,1)S(1)} collective-permute-done((bf16[32,512]{1,0:T(8,128)(2,1)S(1)}, bf16[32,512]{1,0:T(8,128)(2,1)S(1)}, u32[]{:S(2)}, u32[]{:S(2)}) %collective-permute-start.15) | collective-permute-done | bytes 32800 | tf_op jit(solution)/shard_map/ppermute | solution.py:23
  64.2 1.6 %collective-permute-done.16.refs_5_ = bf16[32,512]{1,0:T(8,128)(2,1)S(1)} collective-permute-done((bf16[32,512]{1,0:T(8,128)(2,1)S(1)}, bf16[32,512]{1,0:T(8,128)(2,1)S(1)}, u32[]{:S(2)}, u32[]{:S(2)}) %collective-permute-start.16) | collective-permute-done | bytes 32800 | tf_op jit(solution)/shard_map/ppermute | solution.py:23
  65.8 0.0 collective-permute-done.17.refs_6_
  65.8 0.7 %shard_map.72 = bf16[32,2048]{1,0:T(8,128)(2,1)} custom-call(s32[1]{0:T(128)} %bitcast.my_dp, bf16[32,1536]{1,0:T(8,128)(2,1)S(1)} %collective-permute-done.10.refs_1_.refs_0_, bf16[32,1536]{1,0:T(8,128)(2,1)S(1)} %collective-permute-done.11.refs_2_.refs_1_, bf16[32,1536]{1,0:T(8,128)(2,1)S(1)} %collective-permute-done.12.refs_3_.refs_2_, ...), custom_call_target="tpu_custom_call" | custom-call | flops 262144 | bytes 655360 | tf_op jit(solution)/shard_map/pallas_call | solution.py:31
  (5 shorter events, 0.1 us)
Async XLA Ops:
  1.7 8.1 %collective-permute-start = (bf16[144,512]{1,0:T(8,128)(2,1)S(1)}, bf16[144,512]{1,0:T(8,128)(2,1)S(1)}, u32[]{:S(2)}, u32[]{:S(2)}) collective-permute-start(bf16[144,512]{1,0:T(8,128)(2,1)S(1)} %get-tuple-element.29.sent), channel_id=1, source_target_pairs={{0,8},{8,0},{16,24},{24,16},{1,9},{9,1},{17,25},{25,17},{2,10},{10... | collective-permute-start | bytes 442376 | tf_op jit(solution)/shard_map/ppermute | solution.py:23
  4.7 8.5 %collective-permute-start.1 = (bf16[144,512]{1,0:T(8,128)(2,1)S(1)}, bf16[144,512]{1,0:T(8,128)(2,1)S(1)}, u32[]{:S(2)}, u32[]{:S(2)}) collective-permute-start(bf16[144,512]{1,0:T(8,128)(2,1)S(1)} %get-tuple-element.30), channel_id=1, source_target_pairs={{0,16},{8,24},{16,0},{24,8},{1,17},{9,25},{17,1},{25,9},{2,18},{10... | collective-permute-start | bytes 442376 | tf_op jit(solution)/shard_map/ppermute | solution.py:23
  6.2 7.0 %collective-permute-start.2 = (bf16[144,512]{1,0:T(8,128)(2,1)S(1)}, bf16[144,512]{1,0:T(8,128)(2,1)S(1)}, u32[]{:S(2)}, u32[]{:S(2)}) collective-permute-start(bf16[144,512]{1,0:T(8,128)(2,1)S(1)} %get-tuple-element.31), channel_id=1, source_target_pairs={{0,24},{8,16},{16,8},{24,0},{1,25},{9,17},{17,9},{25,1},{2,26},{10... | collective-permute-start | bytes 442376 | tf_op jit(solution)/shard_map/ppermute | solution.py:23
  13.5 3.7 %collective-permute-start.3 = (bf16[3,128,512]{2,1,0:T(8,128)(2,1)S(1)}, bf16[3,128,512]{2,1,0:T(8,128)(2,1)S(1)}, u32[]{:S(2)}, u32[]{:S(2)}) collective-permute-start(bf16[3,128,512]{2,1,0:T(8,128)(2,1)S(1)} %get-tuple-element.33), channel_id=1, source_target_pairs={{0,1},{1,0},{2,3},{3,2},{4,5},{5,4},{6,7},{7,6},{8,9},{9,8},{10,11... | collective-permute-start | bytes 1179656 | tf_op jit(solution)/shard_map/ppermute | solution.py:23
  14.2 11.3 %collective-permute-start.7 = (bf16[1,352,512]{2,1,0:T(8,128)(2,1)S(1)}, bf16[1,352,512]{2,1,0:T(8,128)(2,1)S(1)}, u32[]{:S(2)}, u32[]{:S(2)}) collective-permute-start(bf16[1,352,512]{2,1,0:T(8,128)(2,1)S(1)} %get-tuple-element.46), channel_id=1, source_target_pairs={{0,8},{8,0},{16,24},{24,16},{1,9},{9,1},{17,25},{25,17},{2,10},{10... | collective-permute-start | bytes 1081352 | tf_op jit(solution)/shard_map/ppermute | solution.py:23
  15.5 11.2 %collective-permute-start.8 = (bf16[1,352,512]{2,1,0:T(8,128)(2,1)S(1)}, bf16[1,352,512]{2,1,0:T(8,128)(2,1)S(1)}, u32[]{:S(2)}, u32[]{:S(2)}) collective-permute-start(bf16[1,352,512]{2,1,0:T(8,128)(2,1)S(1)} %get-tuple-element.47), channel_id=1, source_target_pairs={{0,16},{8,24},{16,0},{24,8},{1,17},{9,25},{17,1},{25,9},{2,18},{10... | collective-permute-start | bytes 1081352 | tf_op jit(solution)/shard_map/ppermute | solution.py:23
  18.2 15.0 %collective-permute-start.4 = (bf16[1,704,256]{2,1,0:T(8,128)(2,1)S(1)}, bf16[1,704,256]{2,1,0:T(8,128)(2,1)S(1)}, u32[]{:S(2)}, u32[]{:S(2)}) collective-permute-start(bf16[1,704,256]{2,1,0:T(8,128)(2,1)S(1)} %get-tuple-element.42), channel_id=1, source_target_pairs={{0,8},{8,0},{16,24},{24,16},{1,9},{9,1},{17,25},{25,17},{2,10},{10... | collective-permute-start | bytes 1081352 | tf_op jit(solution)/shard_map/ppermute | solution.py:23
  19.8 20.0 %collective-permute-start.5 = (bf16[1,704,256]{2,1,0:T(8,128)(2,1)S(1)}, bf16[1,704,256]{2,1,0:T(8,128)(2,1)S(1)}, u32[]{:S(2)}, u32[]{:S(2)}) collective-permute-start(bf16[1,704,256]{2,1,0:T(8,128)(2,1)S(1)} %get-tuple-element.43), channel_id=1, source_target_pairs={{0,16},{8,24},{16,0},{24,8},{1,17},{9,25},{17,1},{25,9},{2,18},{10... | collective-permute-start | bytes 1081352 | tf_op jit(solution)/shard_map/ppermute | solution.py:23
  20.3 21.2 %collective-permute-start.6 = (bf16[1,704,256]{2,1,0:T(8,128)(2,1)S(1)}, bf16[1,704,256]{2,1,0:T(8,128)(2,1)S(1)}, u32[]{:S(2)}, u32[]{:S(2)}) collective-permute-start(bf16[1,704,256]{2,1,0:T(8,128)(2,1)S(1)} %get-tuple-element.44), channel_id=1, source_target_pairs={{0,24},{8,16},{16,8},{24,0},{1,25},{9,17},{17,9},{25,1},{2,26},{10... | collective-permute-start | bytes 1081352 | tf_op jit(solution)/shard_map/ppermute | solution.py:23
  42.3 1.9 %collective-permute-start.9 = (bf16[4,32,1536]{2,1,0:T(8,128)(2,1)S(1)}, bf16[4,32,1536]{2,1,0:T(8,128)(2,1)S(1)}, u32[]{:S(2)}, u32[]{:S(2)}) collective-permute-start(bf16[4,32,1536]{2,1,0:T(8,128)(2,1)S(1)} %slice_bitcast_fusion), channel_id=1, source_target_pairs={{0,1},{1,0},{2,3},{3,2},{4,5},{5,4},{6,7},{7,6},{8,9},{9,8},{10,11... | collective-permute-start | bytes 1179656 | tf_op jit(solution)/shard_map/ppermute | solution.py:23
  42.4 11.7 %collective-permute-start.13 = (bf16[1,352,512]{2,1,0:T(8,128)(2,1)S(1)}, bf16[1,352,512]{2,1,0:T(8,128)(2,1)S(1)}, u32[]{:S(2)}, u32[]{:S(2)}) collective-permute-start(bf16[1,352,512]{2,1,0:T(8,128)(2,1)S(1)} %get-tuple-element.50), channel_id=1, source_target_pairs={{0,24},{8,16},{16,8},{24,0},{1,25},{9,17},{17,9},{25,1},{2,26},{10... | collective-permute-start | bytes 1081352 | tf_op jit(solution)/shard_map/ppermute | solution.py:23
  44.3 9.7 %collective-permute-start.10 = (bf16[32,1536]{1,0:T(8,128)(2,1)S(1)}, bf16[32,1536]{1,0:T(8,128)(2,1)S(1)}, u32[]{:S(2)}, u32[]{:S(2)}) collective-permute-start(bf16[32,1536]{1,0:T(8,128)(2,1)S(1)} %get-tuple-element.54), channel_id=1, source_target_pairs={{0,6},{1,7},{2,4},{3,5},{4,2},{5,3},{6,0},{7,1},{8,14},{9,15},{10,... | collective-permute-start | bytes 294920 | tf_op jit(solution)/shard_map/ppermute | solution.py:23
  48.0 8.6 %collective-permute-start.11 = (bf16[32,1536]{1,0:T(8,128)(2,1)S(1)}, bf16[32,1536]{1,0:T(8,128)(2,1)S(1)}, u32[]{:S(2)}, u32[]{:S(2)}) collective-permute-start(bf16[32,1536]{1,0:T(8,128)(2,1)S(1)} %get-tuple-element.53), channel_id=1, source_target_pairs={{0,4},{1,5},{2,6},{3,7},{4,0},{5,1},{6,2},{7,3},{8,12},{9,13},{10,... | collective-permute-start | bytes 294920 | tf_op jit(solution)/shard_map/ppermute | solution.py:23
  48.0 8.6 %collective-permute-start.12 = (bf16[32,1536]{1,0:T(8,128)(2,1)S(1)}, bf16[32,1536]{1,0:T(8,128)(2,1)S(1)}, u32[]{:S(2)}, u32[]{:S(2)}) collective-permute-start(bf16[32,1536]{1,0:T(8,128)(2,1)S(1)} %get-tuple-element.52), channel_id=1, source_target_pairs={{0,2},{1,3},{2,0},{3,1},{4,6},{5,7},{6,4},{7,5},{8,10},{9,11},{10,... | collective-permute-start | bytes 294920 | tf_op jit(solution)/shard_map/ppermute | solution.py:23
  56.9 1.4 %collective-permute-start.14 = (bf16[4,32,512]{2,1,0:T(8,128)(2,1)S(1)}, bf16[4,32,512]{2,1,0:T(8,128)(2,1)S(1)}, u32[]{:S(2)}, u32[]{:S(2)}) collective-permute-start(bf16[4,32,512]{2,1,0:T(8,128)(2,1)S(1)} %slice_bitcast_fusion.1), channel_id=1, source_target_pairs={{0,1},{1,0},{2,3},{3,2},{4,5},{5,4},{6,7},{7,6},{8,9},{9,8},{10,11... | collective-permute-start | bytes 393224 | tf_op jit(solution)/shard_map/ppermute | solution.py:23
  58.4 5.8 %collective-permute-start.15 = (bf16[32,512]{1,0:T(8,128)(2,1)S(1)}, bf16[32,512]{1,0:T(8,128)(2,1)S(1)}, u32[]{:S(2)}, u32[]{:S(2)}) collective-permute-start(bf16[32,512]{1,0:T(8,128)(2,1)S(1)} %get-tuple-element.58), channel_id=1, source_target_pairs={{0,6},{1,7},{2,4},{3,5},{4,2},{5,3},{6,0},{7,1},{8,14},{9,15},{10,... | collective-permute-start | bytes 98312 | tf_op jit(solution)/shard_map/ppermute | solution.py:23
  61.0 4.8 %collective-permute-start.16 = (bf16[32,512]{1,0:T(8,128)(2,1)S(1)}, bf16[32,512]{1,0:T(8,128)(2,1)S(1)}, u32[]{:S(2)}, u32[]{:S(2)}) collective-permute-start(bf16[32,512]{1,0:T(8,128)(2,1)S(1)} %get-tuple-element.57), channel_id=1, source_target_pairs={{0,4},{1,5},{2,6},{3,7},{4,0},{5,1},{6,2},{7,3},{8,12},{9,13},{10,... | collective-permute-start | bytes 98312 | tf_op jit(solution)/shard_map/ppermute | solution.py:23
  61.0 4.8 %collective-permute-start.17 = (bf16[32,512]{1,0:T(8,128)(2,1)S(1)}, bf16[32,512]{1,0:T(8,128)(2,1)S(1)}, u32[]{:S(2)}, u32[]{:S(2)}) collective-permute-start(bf16[32,512]{1,0:T(8,128)(2,1)S(1)} %get-tuple-element.56), channel_id=1, source_target_pairs={{0,2},{1,3},{2,0},{3,1},{4,6},{5,7},{6,4},{7,5},{8,10},{9,11},{10,... | collective-permute-start | bytes 98312 | tf_op jit(solution)/shard_map/ppermute | solution.py:23

commit v7 on v6

--- a/solution.py
+++ b/solution.py
@@ -40,10 +40,12 @@
 
 
 def prepare_kernel(dp, own_segs, my_dp, core, tokens, router, carry, own, *refs):
-    sends, (blocks, routers, carries, sems) = refs[: dp - 1], refs[dp - 1 :]
+    firsts, seconds = refs[: dp - 1], refs[dp - 1 : 2 * dp - 2]
+    blocks, routers, carries, sems = refs[2 * dp - 2 :]
     rows, depth = own.shape
     half = rows // 2
-    extra = sends[0].shape[0] - half
+    quarter = half // 2
+    extra = firsts[0].shape[0] - quarter
     experts = router.shape[0]
     columns = [pl.multiple_of((my_dp[0] ^ k) * depth, depth) for k in range(dp)]
     copies = [
@@ -61,7 +63,7 @@
     member = lax.broadcasted_iota(jnp.int32, (extra, rows), 1) // SEG
     ones = member == lax.broadcasted_iota(jnp.int32, (extra, rows), 0)
     ones = jnp.where(ones, 1.0, 0.0).astype(BF16)
-    start = pl.multiple_of(core[0] * half, half)
+    start = pl.multiple_of(core[0] * half, quarter)
     for copy in copies:
         copy.wait()
     totals = [jnp.zeros((experts, depth), F32)] * (own_segs + 1)
@@ -73,7 +75,8 @@
             totals[j] += means[j : j + 1, :] * weight
         totals[own_segs] += carries[:, pl.ds(columns[k], depth)] * weight
         if k > 0:
-            sends[k - 1][:half] = blocks[k - 1, pl.ds(start, half), :]
+            firsts[k - 1][:quarter] = blocks[k - 1, pl.ds(start, quarter), :]
+            seconds[k - 1][...] = blocks[k - 1, pl.ds(start + quarter, quarter), :]
     lane = lax.broadcasted_iota(jnp.int32, (experts, LANES), 1)
     place = lane % experts == lax.broadcasted_iota(jnp.int32, (experts, LANES), 0)
     row = lax.broadcasted_iota(jnp.int32, (extra, LANES), 0)
@@ -88,9 +91,9 @@
     low = logits - high - middle
     terms = jnp.where(lane < experts, high, jnp.where(lane < 2 * experts, middle, low))
     terms = jnp.where(lane < 3 * experts, terms, 0.0).astype(BF16)
-    for send in sends:
-        send[half:] = jnp.zeros((extra, depth), BF16)
-        send[half:, :LANES] = terms
+    for first in firsts:
+        first[quarter:] = jnp.zeros((extra, depth), BF16)
+        first[quarter:, :LANES] = terms
 
 
 def load_kernel(count, *refs):
@@ -105,15 +108,27 @@
         copy.wait()
 
 
-def read_table(piece, half, experts):
+def read_table(piece, tokens, experts):
     lane = lax.broadcasted_iota(jnp.int32, (LANES, experts), 0)
     summed = lane % experts == lax.broadcasted_iota(jnp.int32, (LANES, experts), 1)
     summed = jnp.where(summed & (lane < 3 * experts), 1.0, 0.0).astype(BF16)
-    return jnp.dot(piece[half:, :LANES], summed, preferred_element_type=F32)
-
-
-def spread_probs(my_dp, tables, own_segs, steps, block):
-    experts = tables[0].shape[1]
+    return jnp.dot(piece[tokens:, :LANES], summed, preferred_element_type=F32)
+
+
+def load(weights, after):
+    count = len(weights)
+    return call(
+        functools.partial(load_kernel, count),
+        [(weight.shape, BF16) for weight in weights],
+        [HBM] * count + [ANY],
+        (*map(in_hbm, weights), after),
+        0,
+        4 * count * weights[0].size,
+        [pltpu.SemaphoreType.DMA((count,))],
+    )
+
+
+def spread_probs(my_dp, tables, own_segs, experts, steps, block):
     raws = []
     for k in steps:
         for j in range(own_segs):
@@ -140,14 +155,19 @@
     ).astype(BF16)
 
 
-def route_kernel(dp, own_segs, block, my_dp, sent, *refs):
-    pieces, (stacked, mix) = refs[: dp - 1], refs[-2:]
-    half = stacked.shape[1]
-    for k, piece in enumerate(pieces):
-        stacked[k] = piece[:half]
+def route_kernel(dp, own_segs, block, my_dp, *refs):
+    pieces, mix = refs[:dp], refs[-1]
     experts = mix.shape[1] // block
-    tables = [read_table(piece, half, experts) for piece in (sent, *pieces)]
-    mix[...] = spread_probs(my_dp[0], tables, own_segs, tuple(range(dp)), block)
+    tables = [read_table(piece, own_segs * SEG // 4, experts) for piece in pieces]
+    mix[...] = spread_probs(my_dp[0], tables, own_segs, experts, tuple(range(dp)), block)
+
+
+def stack_kernel(dp, *refs):
+    firsts, seconds, stacked = refs[: dp - 1], refs[dp - 1 : 2 * dp - 2], refs[-1]
+    quarter = seconds[0].shape[0]
+    for k in range(dp - 1):
+        stacked[k, :quarter] = firsts[k][:quarter]
+        stacked[k, quarter:] = seconds[k][...]
 
 
 def merge_kernel(own_segs, mix, *refs):
@@ -182,15 +202,14 @@
     )
 
 
-def preact_kernel(dp, core, own, *refs):
-    brought, other = refs[: dp - 1], refs[dp - 1]
-    merged, outs, whole = refs[dp : 2 * dp], refs[2 * dp : 3 * dp], refs[-1]
+def preact_kernel(dp, core, own, brought, other, *refs):
+    merged, outs, whole = refs[:dp], refs[dp : 2 * dp], refs[-1]
     half = own.shape[0] // 2
     near = pl.multiple_of(core[0] * half, half)
     far = pl.multiple_of((1 - core[0]) * half, half)
-    for k in list(range(dp - 1, -1, -1)):
+    for k in range(dp - 1, -1, -1):
         if k > 0:
-            whole[k - 1, pl.ds(near, half), :] = brought[k - 1][:half]
+            whole[k - 1, pl.ds(near, half), :] = brought[k - 1]
             whole[k - 1, pl.ds(far, half), :] = other[k - 1]
         for j in range(merged[k].shape[0]):
             rows = slice(j * SEG, (j + 1) * SEG)
@@ -209,8 +228,8 @@
     return call(
         functools.partial(preact_kernel, dp),
         [((own_segs, total, SEG), BF16)] * dp,
-        [SMEM] + [VMEM] * (2 * dp + 1),
-        (core, own, *brought, other, *merged),
+        [SMEM] + [VMEM] * (dp + 3),
+        (core, own, brought, other, *merged),
         2 * segs * total * SEG * depth,
         2 * segs * (total * depth + SEG * depth + total * SEG),
         [pltpu.VMEM((dp - 1, own_segs * SEG, depth), BF16)],
@@ -286,9 +305,12 @@
     segs = dp * own_segs
 
     extra = -(-(own_segs + 1) // 16) * 16
+    quarter = own_rows // 4
     own, *sends = call(
         functools.partial(prepare_kernel, dp, own_segs),
-        [((own_rows, depth), BF16)] + [((own_rows // 2 + extra, depth), BF16)] * (dp - 1),
+        [((own_rows, depth), BF16)]
+        + [((quarter + extra, depth), BF16)] * (dp - 1)
+        + [((quarter, depth), BF16)] * (dp - 1),
         [SMEM, SMEM, HBM, HBM, HBM],
         (my_dp, core, *map(in_hbm, (tokens, router_weight.T, carry_mean.reshape(1, width)))),
         2 * extra * own_rows * width,
@@ -300,31 +322,34 @@
             pltpu.SemaphoreType.DMA((dp + 2,)),
         ],
     )
-    brought = [swap(sends[k - 1], "dp", k) for k in range(1, dp)]
-    weights = (jnp.swapaxes(gate_weight, 1, 2), jnp.swapaxes(up_weight, 1, 2), down_weight)
-    gate_t, up_t, down = call(
-        functools.partial(load_kernel, len(weights)),
-        [(weight.shape, BF16) for weight in weights],
-        [HBM] * len(weights) + [ANY],
-        (*[in_hbm(weight) for weight in weights], own),
+    firsts = [swap(sends[k - 1], "dp", k) for k in range(1, dp)]
+    seconds = [swap(sends[dp + k - 2], "dp", k) for k in range(1, dp)]
+    (down,) = load((down_weight,), own)
+    block = 32 if hidden_count % 32 == 0 else 16
+    (mix,) = call(
+        functools.partial(route_kernel, dp, own_segs, block),
+        [((segs * block, experts * block), BF16)],
+        [SMEM] + [VMEM] * dp + [ANY],
+        (my_dp, sends[0], *firsts, down),
         0,
-        12 * gate_weight.size,
-        [pltpu.SemaphoreType.DMA((len(weights),))],
-    )
-    block = 32 if hidden_count % 32 == 0 else 16
-    stacked, mix = call(
-        functools.partial(route_kernel, dp, own_segs, block),
-        [((dp - 1, own_rows // 2, depth), BF16), ((segs * block, experts * block), BF16)],
-        [SMEM] + [VMEM] * dp + [ANY],
-        (my_dp, sends[0], *brought, down),
+        2 * own_rows * depth,
+    )
+    merged_down = merge(mix, dp, own_segs, (down,))
+    downs = [block if k == 0 else swap(block, "dp", k) for k, block in enumerate(merged_down)]
+    gate_t, up_t = load(
+        (jnp.swapaxes(gate_weight, 1, 2), jnp.swapaxes(up_weight, 1, 2)), merged_down[0]
+    )
+    (stacked,) = call(
+        functools.partial(stack_kernel, dp),
+        [((dp - 1, own_rows // 2, depth), BF16)],
+        [VMEM] * (2 * dp - 2) + [ANY],
+        (*firsts, *seconds, up_t),
         0,
         2 * own_rows * width,
     )
     other = swap(stacked, "tensor", 1)
-    merged_down = merge(mix, dp, own_segs, (down,))
-    downs = [block if k == 0 else swap(block, "dp", k) for k, block in enumerate(merged_down)]
     merged = merge(mix, dp, own_segs, (gate_t, up_t))
-    partial_pre = preact(core, own, brought, other, merged)
+    partial_pre = preact(core, own, stacked, other, merged)
     parts = [partial_pre[0]] + [swap(partial_pre[k], "dp", k) for k in range(1, dp)]
 
     rows = own_rows // tensor

time: 66.6 us -> 70.1 us (1.053)
  starting transfers between devices: 21.2 us -> 25.5 us
  waiting for transfers between devices: 35.1 us -> 33.2 us
  Pallas kernels: 9.86 us -> 10.9 us
    ppermute x18 -> x21, starting transfers between devices: 21.2 us -> 25.5 us  [swap(): return lax.ppermute(value, axis, [(i, i ^ step) for i in range(count)])]
    ppermute x18 -> x21, waiting for transfers between devices: 35.1 us -> 33.2 us  [swap(): return lax.ppermute(value, axis, [(i, i ^ step) for i in range(count)])]
    pallas_call x9 -> x11, Pallas kernels: 9.86 us -> 10.9 us  [call(): pl.pallas_call(kernel, out_shape=[jax.ShapeDtypeStruct(shape, dtype) for...]
  transfers between devices with their start and end apart: 18 -> 21, of which waited for: 11 -> 10; matrix products, arithmetic and copies ran while one was open for 0% -> 0% of each run, Pallas kernels for 9% -> 10%
where the time goes in v7:
time: 70.1 us; the launch traced here: 70 us
  waiting for transfers between devices  33.2 us (47%)
  starting transfers between devices  25.5 us (36%)
  Pallas kernels  10.9 us (16%)
    ppermute x21, waiting for transfers between devices, swap(): return lax.ppermute(value, axis, [(i, i ^ step) for i in range(count)])  33.2 us
    ppermute x21, starting transfers between devices, swap(): return lax.ppermute(value, axis, [(i, i ^ step) for i in range(count)])  25.5 us
    pallas_call x11, Pallas kernels, call(): pl.pallas_call(kernel, out_shape=[jax.ShapeDtypeStruct(shape, dtype) for...  10.9 us
  transfers between devices with their start and end apart: 21, of which 10 were waited for; matrix products, arithmetic and copies ran while one was open for 0% of the time, Pallas kernels for 10%

profile of v7, /device:TPU:0, one launch (start us, length us, event | category | flops | bytes accessed | tf_op | source)
XLA Modules:
  0.0 70.0 jit_solution(12196303511357817869)
XLA Ops:
  0.0 1.7 %shard_map.64 = (bf16[256,512]{1,0:T(8,128)(2,1)S(1)}, bf16[80,512]{1,0:T(8,128)(2,1)S(1)}, bf16[80,512]{1,0:T(8,128)(2,1)S(1)}, bf16[80,512]{1,0:T(8,128)(2,1)S...) custom-call(s32[1]{0:T(128)} %bitcast.my_dp, s32[1]{0:T(128)} %bitcast.1.core, ...), custom_call_target="tpu_custom_call" | custom-call | flops 16777216 | bytes 2097152 | tf_op jit(solution)/shard_map/pallas_call | solution.py:31
  1.7 3.0 %collective-permute-start.1 = (bf16[80,512]{1,0:T(8,128)(2,1)S(1)}, bf16[80,512]{1,0:T(8,128)(2,1)S(1)}, u32[]{:S(2)}, u32[]{:S(2)}) collective-permute-start(bf16[80,512]{1,0:T(8,128)(2,1)S(1)} %get-tuple-element.30), channel_id=1, source_target_pairs={{0,16},{8,24},{16,0},{24,8},{1,17},{9,25},{17,1},{25,9},{2,18},{10... | collective-permute-start | bytes 245768 | tf_op jit(solution)/shard_map/ppermute | solution.py:23
  4.7 1.4 %collective-permute-start.2 = (bf16[80,512]{1,0:T(8,128)(2,1)S(1)}, bf16[80,512]{1,0:T(8,128)(2,1)S(1)}, u32[]{:S(2)}, u32[]{:S(2)}) collective-permute-start(bf16[80,512]{1,0:T(8,128)(2,1)S(1)} %get-tuple-element.31), channel_id=1, source_target_pairs={{0,24},{8,16},{16,8},{24,0},{1,25},{9,17},{17,9},{25,1},{2,26},{10... | collective-permute-start | bytes 245768 | tf_op jit(solution)/shard_map/ppermute | solution.py:23
  6.2 0.1 collective-permute-start
  6.3 1.9 %collective-permute-start.3 = (bf16[64,512]{1,0:T(8,128)(2,1)S(1)}, bf16[64,512]{1,0:T(8,128)(2,1)S(1)}, u32[]{:S(2)}, u32[]{:S(2)}) collective-permute-start(bf16[64,512]{1,0:T(8,128)(2,1)S(1)} %get-tuple-element.32), channel_id=1, source_target_pairs={{0,8},{8,0},{16,24},{24,16},{1,9},{9,1},{17,25},{25,17},{2,10},{10... | collective-permute-start | bytes 196616 | tf_op jit(solution)/shard_map/ppermute | solution.py:23
  8.2 1.5 %collective-permute-start.4 = (bf16[64,512]{1,0:T(8,128)(2,1)S(1)}, bf16[64,512]{1,0:T(8,128)(2,1)S(1)}, u32[]{:S(2)}, u32[]{:S(2)}) collective-permute-start(bf16[64,512]{1,0:T(8,128)(2,1)S(1)} %get-tuple-element.33), channel_id=1, source_target_pairs={{0,16},{8,24},{16,0},{24,8},{1,17},{9,25},{17,1},{25,9},{2,18},{10... | collective-permute-start | bytes 196616 | tf_op jit(solution)/shard_map/ppermute | solution.py:23
  9.7 0.0 collective-permute-done.1.refs_2_.refs_1_
  9.7 1.7 %collective-permute-start.5 = (bf16[64,512]{1,0:T(8,128)(2,1)S(1)}, bf16[64,512]{1,0:T(8,128)(2,1)S(1)}, u32[]{:S(2)}, u32[]{:S(2)}) collective-permute-start(bf16[64,512]{1,0:T(8,128)(2,1)S(1)} %get-tuple-element.34), channel_id=1, source_target_pairs={{0,24},{8,16},{16,8},{24,0},{1,25},{9,17},{17,9},{25,1},{2,26},{10... | collective-permute-start | bytes 196616 | tf_op jit(solution)/shard_map/ppermute | solution.py:23
  11.4 1.8 %shard_map.65.refs_4_.refs_0_ = bf16[8,352,512]{2,1,0:T(8,128)(2,1)S(1)} custom-call(bf16[8,352,512]{2,1,0:T(8,128)(2,1)} %refs_0_.1, bf16[256,512]{1,0:T(8,128)(2,1)S(1)} %get-tuple-element.28.refs_1_.own), custom_call_target="tpu_custom_call" | custom-call | bytes 5767168 | tf_op jit(solution)/shard_map/pallas_call | solution.py:31
  13.2 0.0 collective-permute-done.2.refs_3_.refs_2_
  13.2 0.0 collective-permute-done.refs_1_.refs_0_
  13.2 0.4 shard_map.66.mix_ref
  13.6 0.5 shard_map.67
  14.1 2.7 %shard_map.68 = (bf16[8,352,512]{2,1,0:T(8,128)(2,1)S(1)}, bf16[8,352,512]{2,1,0:T(8,128)(2,1)S(1)}) custom-call(bf16[8,352,512]{2,1,0:T(8,128)(2,1)} %bitcast.34, bf16[8,352,512]{2,1,0:T(8,128)(2,1)} %bitcast.35, bf16[1,352,512]{2,1,0:T(8,128)(2,1)S(1)} %get-tuple-element.35.refs_2_.refs_4_), custom_call_target="tpu_custom_call" | custom-call | bytes 11534336 | tf_op jit(solution)/shard_map/pallas_call | solution.py:31
  16.9 0.0 collective-permute-done.3.refs_3_
  16.9 0.1 collective-permute-start.6
  17.0 0.9 %collective-permute-start.10 = (bf16[1,352,512]{2,1,0:T(8,128)(2,1)S(1)}, bf16[1,352,512]{2,1,0:T(8,128)(2,1)S(1)}, u32[]{:S(2)}, u32[]{:S(2)}) collective-permute-start(bf16[1,352,512]{2,1,0:T(8,128)(2,1)S(1)} %get-tuple-element.46), channel_id=1, source_target_pairs={{0,8},{8,0},{16,24},{24,16},{1,9},{9,1},{17,25},{25,17},{2,10},{10... | collective-permute-start | bytes 1081352 | tf_op jit(solution)/shard_map/ppermute | solution.py:23
  17.9 1.0 %collective-permute-start.11 = (bf16[1,352,512]{2,1,0:T(8,128)(2,1)S(1)}, bf16[1,352,512]{2,1,0:T(8,128)(2,1)S(1)}, u32[]{:S(2)}, u32[]{:S(2)}) collective-permute-start(bf16[1,352,512]{2,1,0:T(8,128)(2,1)S(1)} %get-tuple-element.47), channel_id=1, source_target_pairs={{0,16},{8,24},{16,0},{24,8},{1,17},{9,25},{17,1},{25,9},{2,18},{10... | collective-permute-start | bytes 1081352 | tf_op jit(solution)/shard_map/ppermute | solution.py:23
  18.9 0.9 %shard_map.70 = (bf16[1,704,512]{2,1,0:T(8,128)(2,1)S(1)}, bf16[1,704,512]{2,1,0:T(8,128)(2,1)S(1)}, bf16[1,704,512]{2,1,0:T(8,128)(2,1)S(1)}, bf16[1,704,512]{2,1,0:T(8,128)(2,1)S(1)}) custom-call(bf16[128,256]{1,0:T(8,128)(2,1)S(1)} %shard_map.66.mix_ref, bf16[8,352,512]{2,1,0:T(8,128)(2,1)S(1)} %get-tuple-element.37.refs_0_, ...), custom_call_target="tpu_custom_call" | custom-call | flops 67108864 | bytes 8650752 | tf_op jit(solution)/shard_map/pallas_call | solution.py:31
  19.8 1.0 %shard_map.71 = (bf16[1,704,256]{2,1,0:T(8,128)(2,1)S(1)}, bf16[1,704,256]{2,1,0:T(8,128)(2,1)S(1)}, bf16[1,704,256]{2,1,0:T(8,128)(2,1)S(1)}, bf16[1,704,256]{2,1,0:T(8,128)(2,1)S(1)}) custom-call(s32[1]{0:T(128)} %bitcast.1.core, bf16[256,512]{1,0:T(8,128)(2,1)S(1)} %get-tuple-element.28.refs_1_.own, bf16[3,128,512]{2,1,0:T(8,128)(2,1)S(1)} %shard_map.69.brought, ...), custom_call_target="tpu_custom_call" | custom-call | flops 738197504 | bytes 5373952 | tf_op jit(solution)/shard_map/pallas_call | solution.py:31
  20.8 0.6 collective-permute-start.7
  21.4 1.7 %collective-permute-start.8 = (bf16[1,704,256]{2,1,0:T(8,128)(2,1)S(1)}, bf16[1,704,256]{2,1,0:T(8,128)(2,1)S(1)}, u32[]{:S(2)}, u32[]{:S(2)}) collective-permute-start(bf16[1,704,256]{2,1,0:T(8,128)(2,1)S(1)} %get-tuple-element.44), channel_id=1, source_target_pairs={{0,16},{8,24},{16,0},{24,8},{1,17},{9,25},{17,1},{25,9},{2,18},{10... | collective-permute-start | bytes 1081352 | tf_op jit(solution)/shard_map/ppermute | solution.py:23
  23.1 1.3 %collective-permute-start.9 = (bf16[1,704,256]{2,1,0:T(8,128)(2,1)S(1)}, bf16[1,704,256]{2,1,0:T(8,128)(2,1)S(1)}, u32[]{:S(2)}, u32[]{:S(2)}) collective-permute-start(bf16[1,704,256]{2,1,0:T(8,128)(2,1)S(1)} %get-tuple-element.45), channel_id=1, source_target_pairs={{0,24},{8,16},{16,8},{24,0},{1,25},{9,17},{17,9},{25,1},{2,26},{10... | collective-permute-start | bytes 1081352 | tf_op jit(solution)/shard_map/ppermute | solution.py:23
  24.4 3.9 %collective-permute-done.10.refs_5_ = bf16[1,352,512]{2,1,0:T(8,128)(2,1)S(1)} collective-permute-done((bf16[1,352,512]{2,1,0:T(8,128)(2,1)S(1)}, bf16[1,352,512]{2,1,0:T(8,128)(2,1)S(1)}, u32[]{:S(2)}, u32[]{:S(2)}) %collective-permute-start.10) | collective-permute-done | bytes 360480 | tf_op jit(solution)/shard_map/ppermute | solution.py:23
  28.3 0.9 %collective-permute-done.11.refs_6_ = bf16[1,352,512]{2,1,0:T(8,128)(2,1)S(1)} collective-permute-done((bf16[1,352,512]{2,1,0:T(8,128)(2,1)S(1)}, bf16[1,352,512]{2,1,0:T(8,128)(2,1)S(1)}, u32[]{:S(2)}, u32[]{:S(2)}) %collective-permute-start.11) | collective-permute-done | bytes 360480 | tf_op jit(solution)/shard_map/ppermute | solution.py:23
  29.1 6.9 %collective-permute-done.7.refs_1_ = bf16[1,704,256]{2,1,0:T(8,128)(2,1)S(1)} collective-permute-done((bf16[1,704,256]{2,1,0:T(8,128)(2,1)S(1)}, bf16[1,704,256]{2,1,0:T(8,128)(2,1)S(1)}, u32[]{:S(2)}, u32[]{:S(2)}) %collective-permute-start.7) | collective-permute-done | bytes 360480 | tf_op jit(solution)/shard_map/ppermute | solution.py:23
  36.0 7.8 %collective-permute-done.8.refs_2_ = bf16[1,704,256]{2,1,0:T(8,128)(2,1)S(1)} collective-permute-done((bf16[1,704,256]{2,1,0:T(8,128)(2,1)S(1)}, bf16[1,704,256]{2,1,0:T(8,128)(2,1)S(1)}, u32[]{:S(2)}, u32[]{:S(2)}) %collective-permute-start.8) | collective-permute-done | bytes 360480 | tf_op jit(solution)/shard_map/ppermute | solution.py:23
  43.8 0.8 %shard_map.72 = (bf16[1,352,256]{2,1,0:T(8,128)(2,1)S(1)}, bf16[2,4,32,1536]{3,2,1,0:T(8,128)(2,1)S(1)}) custom-call(s32[1]{0:T(128)} %bitcast.1.core, bf16[1,704,256]{2,1,0:T(8,128)(2,1)S(1)} %get-tuple-element.42.refs_0_, bf16[1,704,256]{2,1,0:T(8,128)(2,1)S(1)} %collective-permute-done.7.refs_1_, bf16[1,704,256]{2,1,0:T(8,128)(2,1)S(1)} %collective-permute-done.8.refs_2_, ...), custom_call_target="tpu_custom_call" | custom-call | flops 276824064 | bytes 2523136 | tf_op jit(solution)/shard_map/pallas_call | solution.py:31
  44.6 0.1 collective-permute-start.12
  44.7 1.2 %collective-permute-start.16 = (bf16[1,352,512]{2,1,0:T(8,128)(2,1)S(1)}, bf16[1,352,512]{2,1,0:T(8,128)(2,1)S(1)}, u32[]{:S(2)}, u32[]{:S(2)}) collective-permute-start(bf16[1,352,512]{2,1,0:T(8,128)(2,1)S(1)} %get-tuple-element.50), channel_id=1, source_target_pairs={{0,24},{8,16},{16,8},{24,0},{1,25},{9,17},{17,9},{25,1},{2,26},{10... | collective-permute-start | bytes 1081352 | tf_op jit(solution)/shard_map/ppermute | solution.py:23
  46.0 0.4 collective-permute-done.12
  46.4 0.1 fusion
  46.6 1.3 %collective-permute-start.15 = (bf16[32,1536]{1,0:T(8,128)(2,1)S(1)}, bf16[32,1536]{1,0:T(8,128)(2,1)S(1)}, u32[]{:S(2)}, u32[]{:S(2)}) collective-permute-start(bf16[32,1536]{1,0:T(8,128)(2,1)S(1)} %get-tuple-element.52), channel_id=1, source_target_pairs={{0,2},{1,3},{2,0},{3,1},{4,6},{5,7},{6,4},{7,5},{8,10},{9,11},{10,... | collective-permute-start | bytes 294920 | tf_op jit(solution)/shard_map/ppermute | solution.py:23
  47.8 2.6 %collective-permute-start.14 = (bf16[32,1536]{1,0:T(8,128)(2,1)S(1)}, bf16[32,1536]{1,0:T(8,128)(2,1)S(1)}, u32[]{:S(2)}, u32[]{:S(2)}) collective-permute-start(bf16[32,1536]{1,0:T(8,128)(2,1)S(1)} %get-tuple-element.53), channel_id=1, source_target_pairs={{0,4},{1,5},{2,6},{3,7},{4,0},{5,1},{6,2},{7,3},{8,12},{9,13},{10,... | collective-permute-start | bytes 294920 | tf_op jit(solution)/shard_map/ppermute | solution.py:23
  50.4 0.6 collective-permute-start.13
  51.0 5.4 %collective-permute-done.16.refs_0_ = bf16[1,352,512]{2,1,0:T(8,128)(2,1)S(1)} collective-permute-done((bf16[1,352,512]{2,1,0:T(8,128)(2,1)S(1)}, bf16[1,352,512]{2,1,0:T(8,128)(2,1)S(1)}, u32[]{:S(2)}, u32[]{:S(2)}) %collective-permute-start.16) | collective-permute-done | bytes 360480 | tf_op jit(solution)/shard_map/ppermute | solution.py:23
  56.5 2.1 %collective-permute-done.14.refs_2_.refs_1_ = bf16[32,1536]{1,0:T(8,128)(2,1)S(1)} collective-permute-done((bf16[32,1536]{1,0:T(8,128)(2,1)S(1)}, bf16[32,1536]{1,0:T(8,128)(2,1)S(1)}, u32[]{:S(2)}, u32[]{:S(2)}) %collective-permute-start.14) | collective-permute-done | bytes 98336 | tf_op jit(solution)/shard_map/ppermute | solution.py:23
  58.5 0.0 collective-permute-done.13.refs_1_.refs_0_
  58.5 0.3 shard_map.73
  58.9 0.1 collective-permute-start.17
  58.9 1.3 %collective-permute-done.17 = bf16[4,32,512]{2,1,0:T(8,128)(2,1)S(1)} collective-permute-done((bf16[4,32,512]{2,1,0:T(8,128)(2,1)S(1)}, bf16[4,32,512]{2,1,0:T(8,128)(2,1)S(1)}, u32[]{:S(2)}, u32[]{:S(2)}) %collective-permute-start.17) | collective-permute-done | bytes 131104 | tf_op jit(solution)/shard_map/ppermute | solution.py:23
  60.3 1.8 %collective-permute-start.20 = (bf16[32,512]{1,0:T(8,128)(2,1)S(1)}, bf16[32,512]{1,0:T(8,128)(2,1)S(1)}, u32[]{:S(2)}, u32[]{:S(2)}) collective-permute-start(bf16[32,512]{1,0:T(8,128)(2,1)S(1)} %get-tuple-element.56), channel_id=1, source_target_pairs={{0,2},{1,3},{2,0},{3,1},{4,6},{5,7},{6,4},{7,5},{8,10},{9,11},{10,... | collective-permute-start | bytes 98312 | tf_op jit(solution)/shard_map/ppermute | solution.py:23
  62.1 1.4 %collective-permute-start.19 = (bf16[32,512]{1,0:T(8,128)(2,1)S(1)}, bf16[32,512]{1,0:T(8,128)(2,1)S(1)}, u32[]{:S(2)}, u32[]{:S(2)}) collective-permute-start(bf16[32,512]{1,0:T(8,128)(2,1)S(1)} %get-tuple-element.57), channel_id=1, source_target_pairs={{0,4},{1,5},{2,6},{3,7},{4,0},{5,1},{6,2},{7,3},{8,12},{9,13},{10,... | collective-permute-start | bytes 98312 | tf_op jit(solution)/shard_map/ppermute | solution.py:23
  63.5 1.2 %collective-permute-start.18 = (bf16[32,512]{1,0:T(8,128)(2,1)S(1)}, bf16[32,512]{1,0:T(8,128)(2,1)S(1)}, u32[]{:S(2)}, u32[]{:S(2)}) collective-permute-start(bf16[32,512]{1,0:T(8,128)(2,1)S(1)} %get-tuple-element.58), channel_id=1, source_target_pairs={{0,6},{1,7},{2,4},{3,5},{4,2},{5,3},{6,0},{7,1},{8,14},{9,15},{10,... | collective-permute-start | bytes 98312 | tf_op jit(solution)/shard_map/ppermute | solution.py:23
  64.8 0.0 collective-permute-done.20.refs_6_
  64.8 2.7 %collective-permute-done.19.refs_5_ = bf16[32,512]{1,0:T(8,128)(2,1)S(1)} collective-permute-done((bf16[32,512]{1,0:T(8,128)(2,1)S(1)}, bf16[32,512]{1,0:T(8,128)(2,1)S(1)}, u32[]{:S(2)}, u32[]{:S(2)}) %collective-permute-start.19) | collective-permute-done | bytes 32800 | tf_op jit(solution)/shard_map/ppermute | solution.py:23
  67.5 1.7 %collective-permute-done.18.refs_4_ = bf16[32,512]{1,0:T(8,128)(2,1)S(1)} collective-permute-done((bf16[32,512]{1,0:T(8,128)(2,1)S(1)}, bf16[32,512]{1,0:T(8,128)(2,1)S(1)}, u32[]{:S(2)}, u32[]{:S(2)}) %collective-permute-start.18) | collective-permute-done | bytes 32800 | tf_op jit(solution)/shard_map/ppermute | solution.py:23
  69.3 0.7 %shard_map.74 = bf16[32,2048]{1,0:T(8,128)(2,1)} custom-call(s32[1]{0:T(128)} %bitcast.my_dp, bf16[32,1536]{1,0:T(8,128)(2,1)S(1)} %collective-permute-done.13.refs_1_.refs_0_, bf16[32,1536]{1,0:T(8,128)(2,1)S(1)} %collective-permute-done.14.refs_2_.refs_1_, bf16[32,1536]{1,0:T(8,128)(2,1)S(1)} %collective-permute-done.15.refs_3_.refs_2_, ...), custom_call_target="tpu_custom_call" | custom-call | flops 262144 | bytes 655360 | tf_op jit(solution)/shard_map/pallas_call | solution.py:31
  (11 shorter events, 0.2 us)
Async XLA Ops:
  1.7 8.0 %collective-permute-start.1 = (bf16[80,512]{1,0:T(8,128)(2,1)S(1)}, bf16[80,512]{1,0:T(8,128)(2,1)S(1)}, u32[]{:S(2)}, u32[]{:S(2)}) collective-permute-start(bf16[80,512]{1,0:T(8,128)(2,1)S(1)} %get-tuple-element.30), channel_id=1, source_target_pairs={{0,16},{8,24},{16,0},{24,8},{1,17},{9,25},{17,1},{25,9},{2,18},{10... | collective-permute-start | bytes 245768 | tf_op jit(solution)/shard_map/ppermute | solution.py:23
  4.7 8.5 %collective-permute-start.2 = (bf16[80,512]{1,0:T(8,128)(2,1)S(1)}, bf16[80,512]{1,0:T(8,128)(2,1)S(1)}, u32[]{:S(2)}, u32[]{:S(2)}) collective-permute-start(bf16[80,512]{1,0:T(8,128)(2,1)S(1)} %get-tuple-element.31), channel_id=1, source_target_pairs={{0,24},{8,16},{16,8},{24,0},{1,25},{9,17},{17,9},{25,1},{2,26},{10... | collective-permute-start | bytes 245768 | tf_op jit(solution)/shard_map/ppermute | solution.py:23
  6.2 7.1 %collective-permute-start = (bf16[80,512]{1,0:T(8,128)(2,1)S(1)}, bf16[80,512]{1,0:T(8,128)(2,1)S(1)}, u32[]{:S(2)}, u32[]{:S(2)}) collective-permute-start(bf16[80,512]{1,0:T(8,128)(2,1)S(1)} %get-tuple-element.29.refs_0_), channel_id=1, source_target_pairs={{0,8},{8,0},{16,24},{24,16},{1,9},{9,1},{17,25},{25,17},{2,10},{10... | collective-permute-start | bytes 245768 | tf_op jit(solution)/shard_map/ppermute | solution.py:23
  6.3 10.6 %collective-permute-start.3 = (bf16[64,512]{1,0:T(8,128)(2,1)S(1)}, bf16[64,512]{1,0:T(8,128)(2,1)S(1)}, u32[]{:S(2)}, u32[]{:S(2)}) collective-permute-start(bf16[64,512]{1,0:T(8,128)(2,1)S(1)} %get-tuple-element.32), channel_id=1, source_target_pairs={{0,8},{8,0},{16,24},{24,16},{1,9},{9,1},{17,25},{25,17},{2,10},{10... | collective-permute-start | bytes 196616 | tf_op jit(solution)/shard_map/ppermute | solution.py:23
  8.2 8.7 %collective-permute-start.4 = (bf16[64,512]{1,0:T(8,128)(2,1)S(1)}, bf16[64,512]{1,0:T(8,128)(2,1)S(1)}, u32[]{:S(2)}, u32[]{:S(2)}) collective-permute-start(bf16[64,512]{1,0:T(8,128)(2,1)S(1)} %get-tuple-element.33), channel_id=1, source_target_pairs={{0,16},{8,24},{16,0},{24,8},{1,17},{9,25},{17,1},{25,9},{2,18},{10... | collective-permute-start | bytes 196616 | tf_op jit(solution)/shard_map/ppermute | solution.py:23
  9.7 7.2 %collective-permute-start.5 = (bf16[64,512]{1,0:T(8,128)(2,1)S(1)}, bf16[64,512]{1,0:T(8,128)(2,1)S(1)}, u32[]{:S(2)}, u32[]{:S(2)}) collective-permute-start(bf16[64,512]{1,0:T(8,128)(2,1)S(1)} %get-tuple-element.34), channel_id=1, source_target_pairs={{0,24},{8,16},{16,8},{24,0},{1,25},{9,17},{17,9},{25,1},{2,26},{10... | collective-permute-start | bytes 196616 | tf_op jit(solution)/shard_map/ppermute | solution.py:23
  16.9 2.9 %collective-permute-start.6 = (bf16[3,128,512]{2,1,0:T(8,128)(2,1)S(1)}, bf16[3,128,512]{2,1,0:T(8,128)(2,1)S(1)}, u32[]{:S(2)}, u32[]{:S(2)}) collective-permute-start(bf16[3,128,512]{2,1,0:T(8,128)(2,1)S(1)} %shard_map.69.brought), channel_id=1, source_target_pairs={{0,1},{1,0},{2,3},{3,2},{4,5},{5,4},{6,7},{7,6},{8,9},{9,8},{10,11... | collective-permute-start | bytes 1179656 | tf_op jit(solution)/shard_map/ppermute | solution.py:23
  17.0 11.3 %collective-permute-start.10 = (bf16[1,352,512]{2,1,0:T(8,128)(2,1)S(1)}, bf16[1,352,512]{2,1,0:T(8,128)(2,1)S(1)}, u32[]{:S(2)}, u32[]{:S(2)}) collective-permute-start(bf16[1,352,512]{2,1,0:T(8,128)(2,1)S(1)} %get-tuple-element.46), channel_id=1, source_target_pairs={{0,8},{8,0},{16,24},{24,16},{1,9},{9,1},{17,25},{25,17},{2,10},{10... | collective-permute-start | bytes 1081352 | tf_op jit(solution)/shard_map/ppermute | solution.py:23
  17.9 11.3 %collective-permute-start.11 = (bf16[1,352,512]{2,1,0:T(8,128)(2,1)S(1)}, bf16[1,352,512]{2,1,0:T(8,128)(2,1)S(1)}, u32[]{:S(2)}, u32[]{:S(2)}) collective-permute-start(bf16[1,352,512]{2,1,0:T(8,128)(2,1)S(1)} %get-tuple-element.47), channel_id=1, source_target_pairs={{0,16},{8,24},{16,0},{24,8},{1,17},{9,25},{17,1},{25,9},{2,18},{10... | collective-permute-start | bytes 1081352 | tf_op jit(solution)/shard_map/ppermute | solution.py:23
  20.8 15.2 %collective-permute-start.7 = (bf16[1,704,256]{2,1,0:T(8,128)(2,1)S(1)}, bf16[1,704,256]{2,1,0:T(8,128)(2,1)S(1)}, u32[]{:S(2)}, u32[]{:S(2)}) collective-permute-start(bf16[1,704,256]{2,1,0:T(8,128)(2,1)S(1)} %get-tuple-element.43), channel_id=1, source_target_pairs={{0,8},{8,0},{16,24},{24,16},{1,9},{9,1},{17,25},{25,17},{2,10},{10... | collective-permute-start | bytes 1081352 | tf_op jit(solution)/shard_map/ppermute | solution.py:23
  21.4 22.4 %collective-permute-start.8 = (bf16[1,704,256]{2,1,0:T(8,128)(2,1)S(1)}, bf16[1,704,256]{2,1,0:T(8,128)(2,1)S(1)}, u32[]{:S(2)}, u32[]{:S(2)}) collective-permute-start(bf16[1,704,256]{2,1,0:T(8,128)(2,1)S(1)} %get-tuple-element.44), channel_id=1, source_target_pairs={{0,16},{8,24},{16,0},{24,8},{1,17},{9,25},{17,1},{25,9},{2,18},{10... | collective-permute-start | bytes 1081352 | tf_op jit(solution)/shard_map/ppermute | solution.py:23
  23.1 20.7 %collective-permute-start.9 = (bf16[1,704,256]{2,1,0:T(8,128)(2,1)S(1)}, bf16[1,704,256]{2,1,0:T(8,128)(2,1)S(1)}, u32[]{:S(2)}, u32[]{:S(2)}) collective-permute-start(bf16[1,704,256]{2,1,0:T(8,128)(2,1)S(1)} %get-tuple-element.45), channel_id=1, source_target_pairs={{0,24},{8,16},{16,8},{24,0},{1,25},{9,17},{17,9},{25,1},{2,26},{10... | collective-permute-start | bytes 1081352 | tf_op jit(solution)/shard_map/ppermute | solution.py:23
  44.6 1.8 %collective-permute-start.12 = (bf16[4,32,1536]{2,1,0:T(8,128)(2,1)S(1)}, bf16[4,32,1536]{2,1,0:T(8,128)(2,1)S(1)}, u32[]{:S(2)}, u32[]{:S(2)}) collective-permute-start(bf16[4,32,1536]{2,1,0:T(8,128)(2,1)S(1)} %slice_bitcast_fusion), channel_id=1, source_target_pairs={{0,1},{1,0},{2,3},{3,2},{4,5},{5,4},{6,7},{7,6},{8,9},{9,8},{10,11... | collective-permute-start | bytes 1179656 | tf_op jit(solution)/shard_map/ppermute | solution.py:23
  44.7 11.7 %collective-permute-start.16 = (bf16[1,352,512]{2,1,0:T(8,128)(2,1)S(1)}, bf16[1,352,512]{2,1,0:T(8,128)(2,1)S(1)}, u32[]{:S(2)}, u32[]{:S(2)}) collective-permute-start(bf16[1,352,512]{2,1,0:T(8,128)(2,1)S(1)} %get-tuple-element.50), channel_id=1, source_target_pairs={{0,24},{8,16},{16,8},{24,0},{1,25},{9,17},{17,9},{25,1},{2,26},{10... | collective-permute-start | bytes 1081352 | tf_op jit(solution)/shard_map/ppermute | solution.py:23
  46.6 9.9 %collective-permute-start.15 = (bf16[32,1536]{1,0:T(8,128)(2,1)S(1)}, bf16[32,1536]{1,0:T(8,128)(2,1)S(1)}, u32[]{:S(2)}, u32[]{:S(2)}) collective-permute-start(bf16[32,1536]{1,0:T(8,128)(2,1)S(1)} %get-tuple-element.52), channel_id=1, source_target_pairs={{0,2},{1,3},{2,0},{3,1},{4,6},{5,7},{6,4},{7,5},{8,10},{9,11},{10,... | collective-permute-start | bytes 294920 | tf_op jit(solution)/shard_map/ppermute | solution.py:23
  47.8 10.7 %collective-permute-start.14 = (bf16[32,1536]{1,0:T(8,128)(2,1)S(1)}, bf16[32,1536]{1,0:T(8,128)(2,1)S(1)}, u32[]{:S(2)}, u32[]{:S(2)}) collective-permute-start(bf16[32,1536]{1,0:T(8,128)(2,1)S(1)} %get-tuple-element.53), channel_id=1, source_target_pairs={{0,4},{1,5},{2,6},{3,7},{4,0},{5,1},{6,2},{7,3},{8,12},{9,13},{10,... | collective-permute-start | bytes 294920 | tf_op jit(solution)/shard_map/ppermute | solution.py:23
  50.4 8.1 %collective-permute-start.13 = (bf16[32,1536]{1,0:T(8,128)(2,1)S(1)}, bf16[32,1536]{1,0:T(8,128)(2,1)S(1)}, u32[]{:S(2)}, u32[]{:S(2)}) collective-permute-start(bf16[32,1536]{1,0:T(8,128)(2,1)S(1)} %get-tuple-element.54), channel_id=1, source_target_pairs={{0,6},{1,7},{2,4},{3,5},{4,2},{5,3},{6,0},{7,1},{8,14},{9,15},{10,... | collective-permute-start | bytes 294920 | tf_op jit(solution)/shard_map/ppermute | solution.py:23
  58.9 1.4 %collective-permute-start.17 = (bf16[4,32,512]{2,1,0:T(8,128)(2,1)S(1)}, bf16[4,32,512]{2,1,0:T(8,128)(2,1)S(1)}, u32[]{:S(2)}, u32[]{:S(2)}) collective-permute-start(bf16[4,32,512]{2,1,0:T(8,128)(2,1)S(1)} %slice_bitcast_fusion.1), channel_id=1, source_target_pairs={{0,1},{1,0},{2,3},{3,2},{4,5},{5,4},{6,7},{7,6},{8,9},{9,8},{10,11... | collective-permute-start | bytes 393224 | tf_op jit(solution)/shard_map/ppermute | solution.py:23
  60.3 4.5 %collective-permute-start.20 = (bf16[32,512]{1,0:T(8,128)(2,1)S(1)}, bf16[32,512]{1,0:T(8,128)(2,1)S(1)}, u32[]{:S(2)}, u32[]{:S(2)}) collective-permute-start(bf16[32,512]{1,0:T(8,128)(2,1)S(1)} %get-tuple-element.56), channel_id=1, source_target_pairs={{0,2},{1,3},{2,0},{3,1},{4,6},{5,7},{6,4},{7,5},{8,10},{9,11},{10,... | collective-permute-start | bytes 98312 | tf_op jit(solution)/shard_map/ppermute | solution.py:23
  62.1 5.4 %collective-permute-start.19 = (bf16[32,512]{1,0:T(8,128)(2,1)S(1)}, bf16[32,512]{1,0:T(8,128)(2,1)S(1)}, u32[]{:S(2)}, u32[]{:S(2)}) collective-permute-start(bf16[32,512]{1,0:T(8,128)(2,1)S(1)} %get-tuple-element.57), channel_id=1, source_target_pairs={{0,4},{1,5},{2,6},{3,7},{4,0},{5,1},{6,2},{7,3},{8,12},{9,13},{10,... | collective-permute-start | bytes 98312 | tf_op jit(solution)/shard_map/ppermute | solution.py:23
  63.5 5.7 %collective-permute-start.18 = (bf16[32,512]{1,0:T(8,128)(2,1)S(1)}, bf16[32,512]{1,0:T(8,128)(2,1)S(1)}, u32[]{:S(2)}, u32[]{:S(2)}) collective-permute-start(bf16[32,512]{1,0:T(8,128)(2,1)S(1)} %get-tuple-element.58), channel_id=1, source_target_pairs={{0,6},{1,7},{2,4},{3,5},{4,2},{5,3},{6,0},{7,1},{8,14},{9,15},{10,... | collective-permute-start | bytes 98312 | tf_op jit(solution)/shard_map/ppermute | solution.py:23

commit v8 on v7

--- a/solution.py
+++ b/solution.py
@@ -14,6 +14,7 @@
 F32 = jnp.float32
 BF16 = jnp.bfloat16
 LANES = 128
+BESIDE = 10**10
 HBM = pl.BlockSpec(memory_space=pltpu.HBM)
 ANY = pl.BlockSpec(memory_space=pl.ANY)
 
@@ -39,7 +40,7 @@
     )(*args)
 
 
-def prepare_kernel(dp, own_segs, my_dp, core, tokens, router, carry, own, *refs):
+def prepare_kernel(dp, own_segs, block, my_dp, core, tokens, router, carry, own, *refs):
     firsts, seconds = refs[: dp - 1], refs[dp - 1 : 2 * dp - 2]
     blocks, routers, carries, sems = refs[2 * dp - 2 :]
     rows, depth = own.shape
@@ -51,7 +52,7 @@
     copies = [
         pltpu.make_async_copy(
             tokens.at[:, pl.ds(columns[k], depth)],
-            own if k == 0 else blocks.at[k - 1],
+            blocks.at[k],
             sems.at[k],
         )
         for k in range(dp)
@@ -63,20 +64,26 @@
     member = lax.broadcasted_iota(jnp.int32, (extra, rows), 1) // SEG
     ones = member == lax.broadcasted_iota(jnp.int32, (extra, rows), 0)
     ones = jnp.where(ones, 1.0, 0.0).astype(BF16)
-    start = pl.multiple_of(core[0] * half, quarter)
+    near = [pl.multiple_of((2 * i + core[0]) * block, block) for i in range(half // block)]
+    far = [pl.multiple_of((2 * i + 1 - core[0]) * block, block) for i in range(half // block)]
     for copy in copies:
         copy.wait()
     totals = [jnp.zeros((experts, depth), F32)] * (own_segs + 1)
     for k in range(dp):
-        block = own[...] if k == 0 else blocks[k - 1]
         weight = routers[:, pl.ds(columns[k], depth)]
-        means = jnp.dot(ones, block, preferred_element_type=F32) / SEG
+        means = jnp.dot(ones, blocks[k], preferred_element_type=F32) / SEG
         for j in range(own_segs):
             totals[j] += means[j : j + 1, :] * weight
         totals[own_segs] += carries[:, pl.ds(columns[k], depth)] * weight
-        if k > 0:
-            firsts[k - 1][:quarter] = blocks[k - 1, pl.ds(start, quarter), :]
-            seconds[k - 1][...] = blocks[k - 1, pl.ds(start + quarter, quarter), :]
+        for i, start in enumerate(near if k > 0 else near + far):
+            at = i * block
+            rows_in = blocks[k, pl.ds(start, block), :]
+            if k == 0:
+                own[at : at + block] = rows_in
+            elif at < quarter:
+                firsts[k - 1][at : at + block] = rows_in
+            else:
+                seconds[k - 1][at - quarter : at - quarter + block] = rows_in
     lane = lax.broadcasted_iota(jnp.int32, (experts, LANES), 1)
     place = lane % experts == lax.broadcasted_iota(jnp.int32, (experts, LANES), 0)
     row = lax.broadcasted_iota(jnp.int32, (extra, LANES), 0)
@@ -184,7 +191,7 @@
                 outs[k][:, at : at + block, :] = out[k]
 
 
-def merge(mix, dp, own_segs, weights):
+def merge(mix, dp, own_segs, weights, flops):
     experts, rows, cols = weights[0].shape
     total = rows * len(weights)
     count = len(weights)
@@ -197,77 +204,67 @@
         [((own_segs, total, cols), BF16)] * dp,
         [VMEM] * (1 + count),
         (mix, *weights),
-        2 * mix.size * total * cols // rows,
+        flops,
         2 * total * cols * (experts + dp * own_segs),
     )
 
 
-def preact_kernel(dp, core, own, brought, other, *refs):
+def preact_kernel(dp, own, brought, other, *refs):
     merged, outs, whole = refs[:dp], refs[dp : 2 * dp], refs[-1]
     half = own.shape[0] // 2
-    near = pl.multiple_of(core[0] * half, half)
-    far = pl.multiple_of((1 - core[0]) * half, half)
     for k in range(dp - 1, -1, -1):
         if k > 0:
-            whole[k - 1, pl.ds(near, half), :] = brought[k - 1]
-            whole[k - 1, pl.ds(far, half), :] = other[k - 1]
-        for j in range(merged[k].shape[0]):
-            rows = slice(j * SEG, (j + 1) * SEG)
-            outs[k][j] = lax.dot_general(
-                merged[k][j],
-                own[rows, :] if k == 0 else whole[k - 1, rows, :],
-                (((1,), (1,)), ((), ())),
-                preferred_element_type=F32,
-            ).astype(BF16)
-
-
-def preact(core, own, brought, other, merged):
+            whole[k - 1, :half] = brought[k - 1]
+            whole[k - 1, half:] = other[k - 1]
+        outs[k][0] = lax.dot_general(
+            merged[k][0],
+            own[...] if k == 0 else whole[k - 1],
+            (((1,), (1,)), ((), ())),
+            preferred_element_type=F32,
+        ).astype(BF16)
+
+
+def preact(own, brought, other, merged):
     dp = len(merged)
     own_segs, total, depth = merged[0].shape
     segs = dp * own_segs
     return call(
         functools.partial(preact_kernel, dp),
         [((own_segs, total, SEG), BF16)] * dp,
-        [SMEM] + [VMEM] * (dp + 3),
-        (core, own, brought, other, *merged),
+        [VMEM] * (dp + 3),
+        (own, brought, other, *merged),
         2 * segs * total * SEG * depth,
         2 * segs * (total * depth + SEG * depth + total * SEG),
         [pltpu.VMEM((dp - 1, own_segs * SEG, depth), BF16)],
     )
 
 
-def down_columns(core, hidden, downs, mixed):
-    cols = downs[0].shape[2]
-    rows = mixed.shape[2]
-    for j, part in enumerate(hidden):
-        for k, down in enumerate(downs):
-            out = lax.dot_general(
-                part, down[j], (((0,), (0,)), ((), ())), preferred_element_type=F32
-            ).astype(BF16)
-            for i in range(SEG // rows):
-                at = j * (SEG // rows) + i
-                mixed[(at % 2) ^ core, at // 2, :, k * cols : (k + 1) * cols] = out[
-                    i * rows : (i + 1) * rows
-                ]
-
-
-def first_kernel(dp, core, *refs):
+def down_columns(hidden, downs, mixed):
+    lines, rows, cols = mixed.shape
+    cols //= len(downs)
+    for k, down in enumerate(downs):
+        out = lax.dot_general(
+            hidden, down[0], (((0,), (0,)), ((), ())), preferred_element_type=F32
+        ).astype(BF16)
+        mixed[:, :, k * cols : (k + 1) * cols] = out.reshape(lines, rows, cols)
+
+
+def hidden_kernel(dp, *refs):
     parts, downs, hidden, mixed = refs[:dp], refs[dp:-2], refs[-2], refs[-1]
-    half = hidden.shape[1]
-    kept = []
-    for j in range(hidden.shape[0]):
-        total = parts[0][j].astype(F32)
-        for part in parts[1:]:
-            total += part[j].astype(F32)
-        gate, up = total[:half], total[half:]
-        kept.append((gate / (1.0 + jnp.exp(-gate)) * up).astype(BF16))
-        hidden[j] = kept[j]
-    down_columns(core[0], kept, downs, mixed)
-
-
-def second_kernel(count, core, hidden, *refs):
-    kept = [hidden[j] for j in range(hidden.shape[0])]
-    down_columns(core[0], kept, refs[:count], refs[-1])
+    half = hidden.shape[0]
+    total = parts[0][0].astype(F32)
+    for part in parts[1:]:
+        total += part[0].astype(F32)
+    gate, up = total[:half], total[half:]
+    value = (gate / (1.0 + jnp.exp(-gate)) * up).astype(BF16)
+    hidden[...] = value
+    down_columns(value[:, value.shape[1] // 2 :], downs, mixed)
+
+
+def product_kernel(count, near, hidden, *refs):
+    half = hidden.shape[1] // 2
+    part = hidden[:, :half] if near else hidden[:, half:]
+    down_columns(part, refs[:count], refs[-1])
 
 
 def finish_kernel(groups, lines, my_dp, *refs):
@@ -284,12 +281,25 @@
             out[:, pl.ds(at, cols)] = total[:, k * cols : (k + 1) * cols]
 
 
-def tensor_sum_pieces(mixed, lines):
+def product(near, hidden, downs, lines, flops, after=()):
+    (mixed,) = call(
+        functools.partial(product_kernel, len(downs), near),
+        [((lines, hidden.shape[1] // 2 // lines, len(downs) * downs[0].shape[2]), BF16)],
+        [VMEM] * (1 + len(downs)) + [ANY] * len(after),
+        (hidden, *downs, *after),
+        flops,
+        2 * len(downs) * downs[0].size,
+    )
+    return mixed
+
+
+def tensor_sum_pieces(mine, theirs):
+    lines = mine.shape[0]
     my_line = lax.axis_index("tensor") // 2
-    pair = mixed[0].astype(F32) + swap(mixed[1], "tensor", 1).astype(F32)
+    pair = mine.astype(F32) + swap(theirs, "tensor", 1).astype(F32)
     pair = pair.astype(BF16)
     pieces = [lax.dynamic_index_in_dim(pair, my_line ^ k, 0, keepdims=False) for k in range(lines)]
-    return [swap(pieces[k], "tensor", 2 * k) for k in range(lines - 1, 0, -1)] + [pieces[0]]
+    return [pieces[0]] + [swap(pieces[k], "tensor", 2 * k) for k in range(1, lines)]
 
 
 def on_device(tokens, gate_weight, up_weight, down_weight, router_weight, carry_mean):
@@ -300,6 +310,8 @@
     core = (lax.axis_index("tensor") % 2).reshape(1)
     own_rows, width = tokens.shape
     own_segs = own_rows // SEG
+    assert own_segs == 1
+    rows = own_rows // tensor
     experts, depth, hidden_count = gate_weight.shape
     cols = down_weight.shape[2]
     segs = dp * own_segs
@@ -307,7 +319,7 @@
     extra = -(-(own_segs + 1) // 16) * 16
     quarter = own_rows // 4
     own, *sends = call(
-        functools.partial(prepare_kernel, dp, own_segs),
+        functools.partial(prepare_kernel, dp, own_segs, rows),
         [((own_rows, depth), BF16)]
         + [((quarter + extra, depth), BF16)] * (dp - 1)
         + [((quarter, depth), BF16)] * (dp - 1),
@@ -316,7 +328,7 @@
         2 * extra * own_rows * width,
         4 * own_rows * width,
         [
-            pltpu.VMEM((dp - 1, own_rows, depth), BF16),
+            pltpu.VMEM((dp, own_rows, depth), BF16),
             pltpu.VMEM((experts, width), F32),
             pltpu.VMEM((1, width), F32),
             pltpu.SemaphoreType.DMA((dp + 2,)),
@@ -334,7 +346,7 @@
         0,
         2 * own_rows * depth,
     )
-    merged_down = merge(mix, dp, own_segs, (down,))
+    merged_down = merge(mix, dp, own_segs, (down,), 2 * mix.size * down.size // experts // block)
     downs = [block if k == 0 else swap(block, "dp", k) for k, block in enumerate(merged_down)]
     gate_t, up_t = load(
         (jnp.swapaxes(gate_weight, 1, 2), jnp.swapaxes(up_weight, 1, 2)), merged_down[0]
@@ -348,31 +360,26 @@
         2 * own_rows * width,
     )
     other = swap(stacked, "tensor", 1)
-    merged = merge(mix, dp, own_segs, (gate_t, up_t))
-    partial_pre = preact(core, own, stacked, other, merged)
+    merged = merge(mix, dp, own_segs, (gate_t, up_t), BESIDE)
+    partial_pre = preact(own, stacked, other, merged)
     parts = [partial_pre[0]] + [swap(partial_pre[k], "dp", k) for k in range(1, dp)]
 
-    rows = own_rows // tensor
     early, late = tuple(range(dp - 1)), (dp - 1,)
-    flops = 2 * own_rows * hidden_count * cols
-    hidden, mixed = call(
-        functools.partial(first_kernel, dp),
-        [((own_segs, hidden_count, SEG), BF16), ((2, lines, rows, len(early) * cols), BF16)],
-        [SMEM] + [VMEM] * (dp + len(early)),
-        (core, *parts, *[downs[k] for k in early]),
-        flops * len(early),
+    downs_early, downs_late = [downs[k] for k in early], [downs[k] for k in late]
+    hidden, theirs = call(
+        functools.partial(hidden_kernel, dp),
+        [((hidden_count, SEG), BF16), ((lines, rows, len(early) * cols), BF16)],
+        [VMEM] * (dp + len(early)),
+        (*parts, *downs_early),
+        own_rows * hidden_count * cols * len(early),
         2 * (own_rows * hidden_count * dp * 2 + hidden_count * cols * len(early)),
     )
-    early_pieces = tensor_sum_pieces(mixed, lines)
-    (mixed,) = call(
-        functools.partial(second_kernel, len(late)),
-        [((2, lines, rows, len(late) * cols), BF16)],
-        [SMEM] + [VMEM] * (1 + len(late)) + [ANY] * lines,
-        (core, hidden, *[downs[k] for k in late], *early_pieces),
-        flops * len(late),
-        2 * (own_rows * hidden_count + hidden_count * cols * len(late)),
-    )
-    late_pieces = tensor_sum_pieces(mixed, lines)
+    mine = product(True, hidden, downs_early, lines, BESIDE)
+    early_pieces = tensor_sum_pieces(mine, theirs)
+    flops = own_rows * hidden_count * cols
+    theirs = product(False, hidden, downs_late, lines, flops, early_pieces[1:])
+    mine = product(True, hidden, downs_late, lines, BESIDE)
+    late_pieces = tensor_sum_pieces(mine, theirs)
     (out,) = call(
         functools.partial(finish_kernel, (early, late), lines),
         [((rows, width), BF16)],

time: 70.1 us -> 74.1 us (1.057)
  Pallas kernels: 10.9 us -> 12.7 us
  waiting for transfers between devices: 33.2 us -> 34.6 us
  starting transfers between devices: 25.5 us -> 26.3 us
    pallas_call x11 -> x13, Pallas kernels: 10.9 us -> 12.7 us  [call(): pl.pallas_call(kernel, out_shape=[jax.ShapeDtypeStruct(shape, dtype) for...]
    ppermute x21, waiting for transfers between devices: 33.2 us -> 34.6 us  [swap(): return lax.ppermute(value, axis, [(i, i ^ step) for i in range(count)])]
    ppermute x21, starting transfers between devices: 25.5 us -> 26.3 us  [swap(): return lax.ppermute(value, axis, [(i, i ^ step) for i in range(count)])]
  transfers between devices with their start and end apart: 21 -> 21, of which waited for: 10 -> 9; matrix products, arithmetic and copies ran while one was open for 0% -> 0% of each run, Pallas kernels for 10% -> 14%
where the time goes in v8:
time: 74.1 us; the launch traced here: 73.9 us
  waiting for transfers between devices  34.6 us (47%)
  starting transfers between devices  26.3 us (35%)
  Pallas kernels  12.7 us (17%)
    ppermute x21, waiting for transfers between devices, swap(): return lax.ppermute(value, axis, [(i, i ^ step) for i in range(count)])  34.6 us
    ppermute x21, starting transfers between devices, swap(): return lax.ppermute(value, axis, [(i, i ^ step) for i in range(count)])  26.3 us
    pallas_call x13, Pallas kernels, call(): pl.pallas_call(kernel, out_shape=[jax.ShapeDtypeStruct(shape, dtype) for...  12.7 us
  transfers between devices with their start and end apart: 21, of which 9 were waited for; matrix products, arithmetic and copies ran while one was open for 0% of the time, Pallas kernels for 14%

profile of v8, /device:TPU:0, one launch (start us, length us, event | category | flops | bytes accessed | tf_op | source)
XLA Modules:
  0.0 73.9 jit_solution(1967456921653612369)
XLA Ops:
  0.0 1.7 %shard_map.64 = (bf16[256,512]{1,0:T(8,128)(2,1)S(1)}, bf16[80,512]{1,0:T(8,128)(2,1)S(1)}, bf16[80,512]{1,0:T(8,128)(2,1)S(1)}, bf16[80,512]{1,0:T(8,128)(2,1)S...) custom-call(s32[1]{0:T(128)} %bitcast.my_dp, s32[1]{0:T(128)} %bitcast.1.core, ...), custom_call_target="tpu_custom_call" | custom-call | flops 16777216 | bytes 2097152 | tf_op jit(solution)/shard_map/pallas_call | solution.py:32
  1.7 3.0 %collective-permute-start.1 = (bf16[80,512]{1,0:T(8,128)(2,1)S(1)}, bf16[80,512]{1,0:T(8,128)(2,1)S(1)}, u32[]{:S(2)}, u32[]{:S(2)}) collective-permute-start(bf16[80,512]{1,0:T(8,128)(2,1)S(1)} %get-tuple-element.30), channel_id=1, source_target_pairs={{0,16},{8,24},{16,0},{24,8},{1,17},{9,25},{17,1},{25,9},{2,18},{10... | collective-permute-start | bytes 245768 | tf_op jit(solution)/shard_map/ppermute | solution.py:24
  4.7 1.4 %collective-permute-start.2 = (bf16[80,512]{1,0:T(8,128)(2,1)S(1)}, bf16[80,512]{1,0:T(8,128)(2,1)S(1)}, u32[]{:S(2)}, u32[]{:S(2)}) collective-permute-start(bf16[80,512]{1,0:T(8,128)(2,1)S(1)} %get-tuple-element.31), channel_id=1, source_target_pairs={{0,24},{8,16},{16,8},{24,0},{1,25},{9,17},{17,9},{25,1},{2,26},{10... | collective-permute-start | bytes 245768 | tf_op jit(solution)/shard_map/ppermute | solution.py:24
  6.2 0.1 collective-permute-start
  6.3 1.9 %collective-permute-start.3 = (bf16[64,512]{1,0:T(8,128)(2,1)S(1)}, bf16[64,512]{1,0:T(8,128)(2,1)S(1)}, u32[]{:S(2)}, u32[]{:S(2)}) collective-permute-start(bf16[64,512]{1,0:T(8,128)(2,1)S(1)} %get-tuple-element.32), channel_id=1, source_target_pairs={{0,8},{8,0},{16,24},{24,16},{1,9},{9,1},{17,25},{25,17},{2,10},{10... | collective-permute-start | bytes 196616 | tf_op jit(solution)/shard_map/ppermute | solution.py:24
  8.2 1.5 %collective-permute-start.4 = (bf16[64,512]{1,0:T(8,128)(2,1)S(1)}, bf16[64,512]{1,0:T(8,128)(2,1)S(1)}, u32[]{:S(2)}, u32[]{:S(2)}) collective-permute-start(bf16[64,512]{1,0:T(8,128)(2,1)S(1)} %get-tuple-element.33), channel_id=1, source_target_pairs={{0,16},{8,24},{16,0},{24,8},{1,17},{9,25},{17,1},{25,9},{2,18},{10... | collective-permute-start | bytes 196616 | tf_op jit(solution)/shard_map/ppermute | solution.py:24
  9.7 0.0 collective-permute-done.1.refs_2_.refs_1_
  9.7 1.7 %collective-permute-start.5 = (bf16[64,512]{1,0:T(8,128)(2,1)S(1)}, bf16[64,512]{1,0:T(8,128)(2,1)S(1)}, u32[]{:S(2)}, u32[]{:S(2)}) collective-permute-start(bf16[64,512]{1,0:T(8,128)(2,1)S(1)} %get-tuple-element.34), channel_id=1, source_target_pairs={{0,24},{8,16},{16,8},{24,0},{1,25},{9,17},{17,9},{25,1},{2,26},{10... | collective-permute-start | bytes 196616 | tf_op jit(solution)/shard_map/ppermute | solution.py:24
  11.4 1.8 %shard_map.65.refs_4_.refs_0_ = bf16[8,352,512]{2,1,0:T(8,128)(2,1)S(1)} custom-call(bf16[8,352,512]{2,1,0:T(8,128)(2,1)} %refs_0_.1, bf16[256,512]{1,0:T(8,128)(2,1)S(1)} %get-tuple-element.28.refs_1_.own), custom_call_target="tpu_custom_call" | custom-call | bytes 5767168 | tf_op jit(solution)/shard_map/pallas_call | solution.py:32
  13.2 0.0 collective-permute-done.2.refs_3_.refs_2_
  13.2 0.0 collective-permute-done.refs_1_.refs_0_
  13.2 0.4 shard_map.66.mix_ref
  13.6 1.3 %shard_map.67 = (bf16[1,352,512]{2,1,0:T(8,128)(2,1)S(1)}, bf16[1,352,512]{2,1,0:T(8,128)(2,1)}, bf16[1,352,512]{2,1,0:T(8,128)(2,1)S(1)}, bf16[1,352,512]{2,1,0:T(8,128)(2,1)S(1)}) custom-call(bf16[128,256]{1,0:T(8,128)(2,1)S(1)} %shard_map.66.mix_ref, bf16[8,352,512]{2,1,0:T(8,128)(2,1)S(1)} %shard_map.65.refs_4_.refs_0_), custom_call_target="tpu_custom_call" | custom-call | flops 369098752 | bytes 4325376 | tf_op jit(solution)/shard_map/pallas_call | solution.py:32
  14.9 0.8 %collective-permute-start.10 = (bf16[1,352,512]{2,1,0:T(8,128)(2,1)}, bf16[1,352,512]{2,1,0:T(8,128)(2,1)S(1)}, u32[]{:S(2)}, u32[]{:S(2)}) collective-permute-start(bf16[1,352,512]{2,1,0:T(8,128)(2,1)} %get-tuple-element.46), channel_id=1, source_target_pairs={{0,8},{8,0},{16,24},{24,16},{1,9},{9,1},{17,25},{25,17},{2,10},{10... | collective-permute-start | bytes 1081352 | tf_op jit(solution)/shard_map/ppermute | solution.py:24
  15.7 1.0 %collective-permute-start.11 = (bf16[1,352,512]{2,1,0:T(8,128)(2,1)S(1)}, bf16[1,352,512]{2,1,0:T(8,128)(2,1)S(1)}, u32[]{:S(2)}, u32[]{:S(2)}) collective-permute-start(bf16[1,352,512]{2,1,0:T(8,128)(2,1)S(1)} %get-tuple-element.47), channel_id=1, source_target_pairs={{0,16},{8,24},{16,0},{24,8},{1,17},{9,25},{17,1},{25,9},{2,18},{10... | collective-permute-start | bytes 1081352 | tf_op jit(solution)/shard_map/ppermute | solution.py:24
  16.7 2.7 %shard_map.68 = (bf16[8,352,512]{2,1,0:T(8,128)(2,1)S(1)}, bf16[8,352,512]{2,1,0:T(8,128)(2,1)S(1)}) custom-call(bf16[8,352,512]{2,1,0:T(8,128)(2,1)} %bitcast.22, bf16[8,352,512]{2,1,0:T(8,128)(2,1)} %bitcast.23, bf16[1,352,512]{2,1,0:T(8,128)(2,1)S(1)} %get-tuple-element.35.refs_2_.refs_4_.refs_0_), custom_call_target="tpu_custom_call" | custom-call | bytes 11534336 | tf_op jit(solution)/shard_map/pallas_call | solution.py:32
  19.4 0.0 collective-permute-done.3.refs_3_
  19.4 0.0 collective-permute-done.5.refs_5_
  19.5 0.1 collective-permute-start.6
  19.6 0.9 %shard_map.70 = (bf16[1,704,512]{2,1,0:T(8,128)(2,1)S(1)}, bf16[1,704,512]{2,1,0:T(8,128)(2,1)S(1)}, bf16[1,704,512]{2,1,0:T(8,128)(2,1)S(1)}, bf16[1,704,512]{2,1,0:T(8,128)(2,1)S(1)}) custom-call(bf16[128,256]{1,0:T(8,128)(2,1)S(1)} %shard_map.66.mix_ref, bf16[8,352,512]{2,1,0:T(8,128)(2,1)S(1)} %get-tuple-element.37.refs_0_, ...), custom_call_target="tpu_custom_call" | custom-call | flops 10000000000 | bytes 8650752 | tf_op jit(solution)/shard_map/pallas_call | solution.py:32
  20.5 0.8 %collective-permute-done.6.other = bf16[3,128,512]{2,1,0:T(8,128)(2,1)S(1)} collective-permute-done((bf16[3,128,512]{2,1,0:T(8,128)(2,1)S(1)}, bf16[3,128,512]{2,1,0:T(8,128)(2,1)S(1)}, u32[]{:S(2)}, u32[]{:S(2)}) %collective-permute-start.6) | collective-permute-done | bytes 393248 | tf_op jit(solution)/shard_map/ppermute | solution.py:24
  21.3 1.7 %shard_map.71 = (bf16[1,704,256]{2,1,0:T(8,128)(2,1)S(1)}, bf16[1,704,256]{2,1,0:T(8,128)(2,1)}, bf16[1,704,256]{2,1,0:T(8,128)(2,1)}, bf16[1,704,256]{2,1,0:T(8,128)(2,1)}) custom-call(bf16[256,512]{1,0:T(8,128)(2,1)S(1)} %get-tuple-element.28.refs_1_.own, bf16[3,128,512]{2,1,0:T(8,128)(2,1)S(1)} %shard_map.69.brought, ...), custom_call_target="tpu_custom_call" | custom-call | flops 738197504 | bytes 5373952 | tf_op jit(solution)/shard_map/pallas_call | solution.py:32
  22.9 0.5 collective-permute-start.7
  23.5 1.7 %collective-permute-start.8 = (bf16[1,704,256]{2,1,0:T(8,128)(2,1)}, bf16[1,704,256]{2,1,0:T(8,128)(2,1)S(1)}, u32[]{:S(2)}, u32[]{:S(2)}) collective-permute-start(bf16[1,704,256]{2,1,0:T(8,128)(2,1)} %get-tuple-element.44), channel_id=1, source_target_pairs={{0,16},{8,24},{16,0},{24,8},{1,17},{9,25},{17,1},{25,9},{2,18},{10... | collective-permute-start | bytes 1081352 | tf_op jit(solution)/shard_map/ppermute | solution.py:24
  25.2 1.3 %collective-permute-start.9 = (bf16[1,704,256]{2,1,0:T(8,128)(2,1)}, bf16[1,704,256]{2,1,0:T(8,128)(2,1)S(1)}, u32[]{:S(2)}, u32[]{:S(2)}) collective-permute-start(bf16[1,704,256]{2,1,0:T(8,128)(2,1)} %get-tuple-element.45), channel_id=1, source_target_pairs={{0,24},{8,16},{16,8},{24,0},{1,25},{9,17},{17,9},{25,1},{2,26},{10... | collective-permute-start | bytes 1081352 | tf_op jit(solution)/shard_map/ppermute | solution.py:24
  26.4 1.7 %collective-permute-start.16 = (bf16[1,352,512]{2,1,0:T(8,128)(2,1)S(1)}, bf16[1,352,512]{2,1,0:T(8,128)(2,1)S(1)}, u32[]{:S(2)}, u32[]{:S(2)}) collective-permute-start(bf16[1,352,512]{2,1,0:T(8,128)(2,1)S(1)} %get-tuple-element.50), channel_id=1, source_target_pairs={{0,24},{8,16},{16,8},{24,0},{1,25},{9,17},{17,9},{25,1},{2,26},{10... | collective-permute-start | bytes 1081352 | tf_op jit(solution)/shard_map/ppermute | solution.py:24
  28.1 6.3 %collective-permute-done.7.refs_1_ = bf16[1,704,256]{2,1,0:T(8,128)(2,1)S(1)} collective-permute-done((bf16[1,704,256]{2,1,0:T(8,128)(2,1)}, bf16[1,704,256]{2,1,0:T(8,128)(2,1)S(1)}, u32[]{:S(2)}, u32[]{:S(2)}) %collective-permute-start.7) | collective-permute-done | bytes 360480 | tf_op jit(solution)/shard_map/ppermute | solution.py:24
  34.4 14.3 %collective-permute-done.8.refs_2_ = bf16[1,704,256]{2,1,0:T(8,128)(2,1)S(1)} collective-permute-done((bf16[1,704,256]{2,1,0:T(8,128)(2,1)}, bf16[1,704,256]{2,1,0:T(8,128)(2,1)S(1)}, u32[]{:S(2)}, u32[]{:S(2)}) %collective-permute-start.8) | collective-permute-done | bytes 360480 | tf_op jit(solution)/shard_map/ppermute | solution.py:24
  48.7 0.6 shard_map.72
  49.3 0.1 collective-permute-start.12
  49.4 0.4 shard_map.73
  49.8 1.3 %collective-permute-done.12 = bf16[4,32,1536]{2,1,0:T(8,128)(2,1)S(1)} collective-permute-done((bf16[4,32,1536]{2,1,0:T(8,128)(2,1)S(1)}, bf16[4,32,1536]{2,1,0:T(8,128)(2,1)S(1)}, u32[]{:S(2)}, u32[]{:S(2)}) %collective-permute-start.12) | collective-permute-done | bytes 393248 | tf_op jit(solution)/shard_map/ppermute | solution.py:24
  51.1 0.1 add_convert_fusion
  51.2 4.3 %collective-permute-start.15 = (bf16[32,1536]{1,0:T(8,128)(2,1)S(1)}, bf16[32,1536]{1,0:T(8,128)(2,1)S(1)}, u32[]{:S(2)}, u32[]{:S(2)}) collective-permute-start(bf16[32,1536]{1,0:T(8,128)(2,1)S(1)} %get-tuple-element.51), channel_id=1, source_target_pairs={{0,6},{1,7},{2,4},{3,5},{4,2},{5,3},{6,0},{7,1},{8,14},{9,15},{10,... | collective-permute-start | bytes 294920 | tf_op jit(solution)/shard_map/ppermute | solution.py:24
  55.5 0.0 collective-permute-start.14
  55.5 0.6 collective-permute-start.13
  56.2 3.0 %collective-permute-done.15.refs_3_ = bf16[32,1536]{1,0:T(8,128)(2,1)S(1)} collective-permute-done((bf16[32,1536]{1,0:T(8,128)(2,1)S(1)}, bf16[32,1536]{1,0:T(8,128)(2,1)S(1)}, u32[]{:S(2)}, u32[]{:S(2)}) %collective-permute-start.15) | collective-permute-done | bytes 98336 | tf_op jit(solution)/shard_map/ppermute | solution.py:24
  59.2 4.9 %collective-permute-done.14.refs_2_ = bf16[32,1536]{1,0:T(8,128)(2,1)S(1)} collective-permute-done((bf16[32,1536]{1,0:T(8,128)(2,1)S(1)}, bf16[32,1536]{1,0:T(8,128)(2,1)S(1)}, u32[]{:S(2)}, u32[]{:S(2)}) %collective-permute-start.14) | collective-permute-done | bytes 98336 | tf_op jit(solution)/shard_map/ppermute | solution.py:24
  64.1 0.0 collective-permute-done.13.refs_1_
  64.1 0.2 shard_map.75
  64.4 0.1 collective-permute-start.17
  64.4 0.2 shard_map.74
  64.7 1.1 %collective-permute-done.17 = bf16[4,32,512]{2,1,0:T(8,128)(2,1)S(1)} collective-permute-done((bf16[4,32,512]{2,1,0:T(8,128)(2,1)S(1)}, bf16[4,32,512]{2,1,0:T(8,128)(2,1)S(1)}, u32[]{:S(2)}, u32[]{:S(2)}) %collective-permute-start.17) | collective-permute-done | bytes 131104 | tf_op jit(solution)/shard_map/ppermute | solution.py:24
  65.8 2.5 %collective-permute-start.20 = (bf16[32,512]{1,0:T(8,128)(2,1)S(1)}, bf16[32,512]{1,0:T(8,128)(2,1)S(1)}, u32[]{:S(2)}, u32[]{:S(2)}) collective-permute-start(bf16[32,512]{1,0:T(8,128)(2,1)S(1)} %get-tuple-element.55), channel_id=1, source_target_pairs={{0,6},{1,7},{2,4},{3,5},{4,2},{5,3},{6,0},{7,1},{8,14},{9,15},{10,... | collective-permute-start | bytes 98312 | tf_op jit(solution)/shard_map/ppermute | solution.py:24
  68.4 1.9 %collective-permute-start.18 = (bf16[32,512]{1,0:T(8,128)(2,1)S(1)}, bf16[32,512]{1,0:T(8,128)(2,1)S(1)}, u32[]{:S(2)}, u32[]{:S(2)}) collective-permute-start(bf16[32,512]{1,0:T(8,128)(2,1)S(1)} %get-tuple-element.57), channel_id=1, source_target_pairs={{0,2},{1,3},{2,0},{3,1},{4,6},{5,7},{6,4},{7,5},{8,10},{9,11},{10,... | collective-permute-start | bytes 98312 | tf_op jit(solution)/shard_map/ppermute | solution.py:24
  70.3 1.3 %collective-permute-done.20.refs_7_ = bf16[32,512]{1,0:T(8,128)(2,1)S(1)} collective-permute-done((bf16[32,512]{1,0:T(8,128)(2,1)S(1)}, bf16[32,512]{1,0:T(8,128)(2,1)S(1)}, u32[]{:S(2)}, u32[]{:S(2)}) %collective-permute-start.20) | collective-permute-done | bytes 32800 | tf_op jit(solution)/shard_map/ppermute | solution.py:24
  71.6 1.6 %collective-permute-done.19.refs_6_ = bf16[32,512]{1,0:T(8,128)(2,1)S(1)} collective-permute-done((bf16[32,512]{1,0:T(8,128)(2,1)S(1)}, bf16[32,512]{1,0:T(8,128)(2,1)S(1)}, u32[]{:S(2)}, u32[]{:S(2)}) %collective-permute-start.19) | collective-permute-done | bytes 32800 | tf_op jit(solution)/shard_map/ppermute | solution.py:24
  73.2 0.7 shard_map.76
  (11 shorter events, 0.1 us)
Async XLA Ops:
  1.7 8.0 %collective-permute-start.1 = (bf16[80,512]{1,0:T(8,128)(2,1)S(1)}, bf16[80,512]{1,0:T(8,128)(2,1)S(1)}, u32[]{:S(2)}, u32[]{:S(2)}) collective-permute-start(bf16[80,512]{1,0:T(8,128)(2,1)S(1)} %get-tuple-element.30), channel_id=1, source_target_pairs={{0,16},{8,24},{16,0},{24,8},{1,17},{9,25},{17,1},{25,9},{2,18},{10... | collective-permute-start | bytes 245768 | tf_op jit(solution)/shard_map/ppermute | solution.py:24
  4.7 8.5 %collective-permute-start.2 = (bf16[80,512]{1,0:T(8,128)(2,1)S(1)}, bf16[80,512]{1,0:T(8,128)(2,1)S(1)}, u32[]{:S(2)}, u32[]{:S(2)}) collective-permute-start(bf16[80,512]{1,0:T(8,128)(2,1)S(1)} %get-tuple-element.31), channel_id=1, source_target_pairs={{0,24},{8,16},{16,8},{24,0},{1,25},{9,17},{17,9},{25,1},{2,26},{10... | collective-permute-start | bytes 245768 | tf_op jit(solution)/shard_map/ppermute | solution.py:24
  6.2 7.1 %collective-permute-start = (bf16[80,512]{1,0:T(8,128)(2,1)S(1)}, bf16[80,512]{1,0:T(8,128)(2,1)S(1)}, u32[]{:S(2)}, u32[]{:S(2)}) collective-permute-start(bf16[80,512]{1,0:T(8,128)(2,1)S(1)} %get-tuple-element.29.refs_0_), channel_id=1, source_target_pairs={{0,8},{8,0},{16,24},{24,16},{1,9},{9,1},{17,25},{25,17},{2,10},{10... | collective-permute-start | bytes 245768 | tf_op jit(solution)/shard_map/ppermute | solution.py:24
  6.3 13.1 %collective-permute-start.3 = (bf16[64,512]{1,0:T(8,128)(2,1)S(1)}, bf16[64,512]{1,0:T(8,128)(2,1)S(1)}, u32[]{:S(2)}, u32[]{:S(2)}) collective-permute-start(bf16[64,512]{1,0:T(8,128)(2,1)S(1)} %get-tuple-element.32), channel_id=1, source_target_pairs={{0,8},{8,0},{16,24},{24,16},{1,9},{9,1},{17,25},{25,17},{2,10},{10... | collective-permute-start | bytes 196616 | tf_op jit(solution)/shard_map/ppermute | solution.py:24
  8.2 11.2 %collective-permute-start.4 = (bf16[64,512]{1,0:T(8,128)(2,1)S(1)}, bf16[64,512]{1,0:T(8,128)(2,1)S(1)}, u32[]{:S(2)}, u32[]{:S(2)}) collective-permute-start(bf16[64,512]{1,0:T(8,128)(2,1)S(1)} %get-tuple-element.33), channel_id=1, source_target_pairs={{0,16},{8,24},{16,0},{24,8},{1,17},{9,25},{17,1},{25,9},{2,18},{10... | collective-permute-start | bytes 196616 | tf_op jit(solution)/shard_map/ppermute | solution.py:24
  9.7 9.7 %collective-permute-start.5 = (bf16[64,512]{1,0:T(8,128)(2,1)S(1)}, bf16[64,512]{1,0:T(8,128)(2,1)S(1)}, u32[]{:S(2)}, u32[]{:S(2)}) collective-permute-start(bf16[64,512]{1,0:T(8,128)(2,1)S(1)} %get-tuple-element.34), channel_id=1, source_target_pairs={{0,24},{8,16},{16,8},{24,0},{1,25},{9,17},{17,9},{25,1},{2,26},{10... | collective-permute-start | bytes 196616 | tf_op jit(solution)/shard_map/ppermute | solution.py:24
  14.9 11.6 %collective-permute-start.10 = (bf16[1,352,512]{2,1,0:T(8,128)(2,1)}, bf16[1,352,512]{2,1,0:T(8,128)(2,1)S(1)}, u32[]{:S(2)}, u32[]{:S(2)}) collective-permute-start(bf16[1,352,512]{2,1,0:T(8,128)(2,1)} %get-tuple-element.46), channel_id=1, source_target_pairs={{0,8},{8,0},{16,24},{24,16},{1,9},{9,1},{17,25},{25,17},{2,10},{10... | collective-permute-start | bytes 1081352 | tf_op jit(solution)/shard_map/ppermute | solution.py:24
  15.7 12.4 %collective-permute-start.11 = (bf16[1,352,512]{2,1,0:T(8,128)(2,1)S(1)}, bf16[1,352,512]{2,1,0:T(8,128)(2,1)S(1)}, u32[]{:S(2)}, u32[]{:S(2)}) collective-permute-start(bf16[1,352,512]{2,1,0:T(8,128)(2,1)S(1)} %get-tuple-element.47), channel_id=1, source_target_pairs={{0,16},{8,24},{16,0},{24,8},{1,17},{9,25},{17,1},{25,9},{2,18},{10... | collective-permute-start | bytes 1081352 | tf_op jit(solution)/shard_map/ppermute | solution.py:24
  19.5 1.8 %collective-permute-start.6 = (bf16[3,128,512]{2,1,0:T(8,128)(2,1)S(1)}, bf16[3,128,512]{2,1,0:T(8,128)(2,1)S(1)}, u32[]{:S(2)}, u32[]{:S(2)}) collective-permute-start(bf16[3,128,512]{2,1,0:T(8,128)(2,1)S(1)} %shard_map.69.brought), channel_id=1, source_target_pairs={{0,1},{1,0},{2,3},{3,2},{4,5},{5,4},{6,7},{7,6},{8,9},{9,8},{10,11... | collective-permute-start | bytes 1179656 | tf_op jit(solution)/shard_map/ppermute | solution.py:24
  22.9 11.5 %collective-permute-start.7 = (bf16[1,704,256]{2,1,0:T(8,128)(2,1)}, bf16[1,704,256]{2,1,0:T(8,128)(2,1)S(1)}, u32[]{:S(2)}, u32[]{:S(2)}) collective-permute-start(bf16[1,704,256]{2,1,0:T(8,128)(2,1)} %get-tuple-element.43), channel_id=1, source_target_pairs={{0,8},{8,0},{16,24},{24,16},{1,9},{9,1},{17,25},{25,17},{2,10},{10... | collective-permute-start | bytes 1081352 | tf_op jit(solution)/shard_map/ppermute | solution.py:24
  23.5 25.2 %collective-permute-start.8 = (bf16[1,704,256]{2,1,0:T(8,128)(2,1)}, bf16[1,704,256]{2,1,0:T(8,128)(2,1)S(1)}, u32[]{:S(2)}, u32[]{:S(2)}) collective-permute-start(bf16[1,704,256]{2,1,0:T(8,128)(2,1)} %get-tuple-element.44), channel_id=1, source_target_pairs={{0,16},{8,24},{16,0},{24,8},{1,17},{9,25},{17,1},{25,9},{2,18},{10... | collective-permute-start | bytes 1081352 | tf_op jit(solution)/shard_map/ppermute | solution.py:24
  25.2 23.5 %collective-permute-start.9 = (bf16[1,704,256]{2,1,0:T(8,128)(2,1)}, bf16[1,704,256]{2,1,0:T(8,128)(2,1)S(1)}, u32[]{:S(2)}, u32[]{:S(2)}) collective-permute-start(bf16[1,704,256]{2,1,0:T(8,128)(2,1)} %get-tuple-element.45), channel_id=1, source_target_pairs={{0,24},{8,16},{16,8},{24,0},{1,25},{9,17},{17,9},{25,1},{2,26},{10... | collective-permute-start | bytes 1081352 | tf_op jit(solution)/shard_map/ppermute | solution.py:24
  26.4 29.7 %collective-permute-start.16 = (bf16[1,352,512]{2,1,0:T(8,128)(2,1)S(1)}, bf16[1,352,512]{2,1,0:T(8,128)(2,1)S(1)}, u32[]{:S(2)}, u32[]{:S(2)}) collective-permute-start(bf16[1,352,512]{2,1,0:T(8,128)(2,1)S(1)} %get-tuple-element.50), channel_id=1, source_target_pairs={{0,24},{8,16},{16,8},{24,0},{1,25},{9,17},{17,9},{25,1},{2,26},{10... | collective-permute-start | bytes 1081352 | tf_op jit(solution)/shard_map/ppermute | solution.py:24
  49.3 1.8 %collective-permute-start.12 = (bf16[4,32,1536]{2,1,0:T(8,128)(2,1)S(1)}, bf16[4,32,1536]{2,1,0:T(8,128)(2,1)S(1)}, u32[]{:S(2)}, u32[]{:S(2)}) collective-permute-start(bf16[4,32,1536]{2,1,0:T(8,128)(2,1)S(1)} %get-tuple-element.49), channel_id=1, source_target_pairs={{0,1},{1,0},{2,3},{3,2},{4,5},{5,4},{6,7},{7,6},{8,9},{9,8},{10,11... | collective-permute-start | bytes 1179656 | tf_op jit(solution)/shard_map/ppermute | solution.py:24
  51.2 8.0 %collective-permute-start.15 = (bf16[32,1536]{1,0:T(8,128)(2,1)S(1)}, bf16[32,1536]{1,0:T(8,128)(2,1)S(1)}, u32[]{:S(2)}, u32[]{:S(2)}) collective-permute-start(bf16[32,1536]{1,0:T(8,128)(2,1)S(1)} %get-tuple-element.51), channel_id=1, source_target_pairs={{0,6},{1,7},{2,4},{3,5},{4,2},{5,3},{6,0},{7,1},{8,14},{9,15},{10,... | collective-permute-start | bytes 294920 | tf_op jit(solution)/shard_map/ppermute | solution.py:24
  55.5 8.6 %collective-permute-start.14 = (bf16[32,1536]{1,0:T(8,128)(2,1)S(1)}, bf16[32,1536]{1,0:T(8,128)(2,1)S(1)}, u32[]{:S(2)}, u32[]{:S(2)}) collective-permute-start(bf16[32,1536]{1,0:T(8,128)(2,1)S(1)} %get-tuple-element.52), channel_id=1, source_target_pairs={{0,4},{1,5},{2,6},{3,7},{4,0},{5,1},{6,2},{7,3},{8,12},{9,13},{10,... | collective-permute-start | bytes 294920 | tf_op jit(solution)/shard_map/ppermute | solution.py:24
  55.5 8.6 %collective-permute-start.13 = (bf16[32,1536]{1,0:T(8,128)(2,1)S(1)}, bf16[32,1536]{1,0:T(8,128)(2,1)S(1)}, u32[]{:S(2)}, u32[]{:S(2)}) collective-permute-start(bf16[32,1536]{1,0:T(8,128)(2,1)S(1)} %get-tuple-element.53), channel_id=1, source_target_pairs={{0,2},{1,3},{2,0},{3,1},{4,6},{5,7},{6,4},{7,5},{8,10},{9,11},{10,... | collective-permute-start | bytes 294920 | tf_op jit(solution)/shard_map/ppermute | solution.py:24
  64.4 1.4 %collective-permute-start.17 = (bf16[4,32,512]{2,1,0:T(8,128)(2,1)S(1)}, bf16[4,32,512]{2,1,0:T(8,128)(2,1)S(1)}, u32[]{:S(2)}, u32[]{:S(2)}) collective-permute-start(bf16[4,32,512]{2,1,0:T(8,128)(2,1)S(1)} %shard_map.75), channel_id=1, source_target_pairs={{0,1},{1,0},{2,3},{3,2},{4,5},{5,4},{6,7},{7,6},{8,9},{9,8},{10,11... | collective-permute-start | bytes 393224 | tf_op jit(solution)/shard_map/ppermute | solution.py:24
  65.8 5.8 %collective-permute-start.20 = (bf16[32,512]{1,0:T(8,128)(2,1)S(1)}, bf16[32,512]{1,0:T(8,128)(2,1)S(1)}, u32[]{:S(2)}, u32[]{:S(2)}) collective-permute-start(bf16[32,512]{1,0:T(8,128)(2,1)S(1)} %get-tuple-element.55), channel_id=1, source_target_pairs={{0,6},{1,7},{2,4},{3,5},{4,2},{5,3},{6,0},{7,1},{8,14},{9,15},{10,... | collective-permute-start | bytes 98312 | tf_op jit(solution)/shard_map/ppermute | solution.py:24
  68.4 4.8 %collective-permute-start.19 = (bf16[32,512]{1,0:T(8,128)(2,1)S(1)}, bf16[32,512]{1,0:T(8,128)(2,1)S(1)}, u32[]{:S(2)}, u32[]{:S(2)}) collective-permute-start(bf16[32,512]{1,0:T(8,128)(2,1)S(1)} %get-tuple-element.56), channel_id=1, source_target_pairs={{0,4},{1,5},{2,6},{3,7},{4,0},{5,1},{6,2},{7,3},{8,12},{9,13},{10,... | collective-permute-start | bytes 98312 | tf_op jit(solution)/shard_map/ppermute | solution.py:24
  68.4 4.8 %collective-permute-start.18 = (bf16[32,512]{1,0:T(8,128)(2,1)S(1)}, bf16[32,512]{1,0:T(8,128)(2,1)S(1)}, u32[]{:S(2)}, u32[]{:S(2)}) collective-permute-start(bf16[32,512]{1,0:T(8,128)(2,1)S(1)} %get-tuple-element.57), channel_id=1, source_target_pairs={{0,2},{1,3},{2,0},{3,1},{4,6},{5,7},{6,4},{7,5},{8,10},{9,11},{10,... | collective-permute-start | bytes 98312 | tf_op jit(solution)/shard_map/ppermute | solution.py:24

commit v9 on v7

--- a/solution.py
+++ b/solution.py
@@ -14,6 +14,7 @@
 F32 = jnp.float32
 BF16 = jnp.bfloat16
 LANES = 128
+BESIDE = 10**10
 HBM = pl.BlockSpec(memory_space=pltpu.HBM)
 ANY = pl.BlockSpec(memory_space=pl.ANY)
 
@@ -184,7 +185,7 @@
                 outs[k][:, at : at + block, :] = out[k]
 
 
-def merge(mix, dp, own_segs, weights):
+def merge(mix, dp, own_segs, weights, flops):
     experts, rows, cols = weights[0].shape
     total = rows * len(weights)
     count = len(weights)
@@ -197,7 +198,7 @@
         [((own_segs, total, cols), BF16)] * dp,
         [VMEM] * (1 + count),
         (mix, *weights),
-        2 * mix.size * total * cols // rows,
+        flops,
         2 * total * cols * (experts + dp * own_segs),
     )
 
@@ -334,21 +335,19 @@
         0,
         2 * own_rows * depth,
     )
-    merged_down = merge(mix, dp, own_segs, (down,))
+    merged_down = merge(mix, dp, own_segs, (down,), 2 * mix.size * down.size // experts // block)
     downs = [block if k == 0 else swap(block, "dp", k) for k, block in enumerate(merged_down)]
-    gate_t, up_t = load(
-        (jnp.swapaxes(gate_weight, 1, 2), jnp.swapaxes(up_weight, 1, 2)), merged_down[0]
-    )
+    gate_up = (jnp.swapaxes(gate_weight, 1, 2), jnp.swapaxes(up_weight, 1, 2))
     (stacked,) = call(
         functools.partial(stack_kernel, dp),
         [((dp - 1, own_rows // 2, depth), BF16)],
         [VMEM] * (2 * dp - 2) + [ANY],
-        (*firsts, *seconds, up_t),
+        (*firsts, *seconds, merged_down[0]),
         0,
         2 * own_rows * width,
     )
     other = swap(stacked, "tensor", 1)
-    merged = merge(mix, dp, own_segs, (gate_t, up_t))
+    merged = merge(mix, dp, own_segs, gate_up, BESIDE)
     partial_pre = preact(core, own, stacked, other, merged)
     parts = [partial_pre[0]] + [swap(partial_pre[k], "dp", k) for k in range(1, dp)]
 

time: 70.1 us -> 65 us (0.927)
  waiting for transfers between devices: 33.2 us -> 30.2 us
  Pallas kernels: 10.9 us -> 8.15 us
    ppermute x21, waiting for transfers between devices: 33.2 us -> 30.2 us  [swap(): return lax.ppermute(value, axis, [(i, i ^ step) for i in range(count)])]
    pallas_call x11 -> x10, Pallas kernels: 10.9 us -> 8.15 us  [call(): pl.pallas_call(kernel, out_shape=[jax.ShapeDtypeStruct(shape, dtype) for...]
  transfers between devices with their start and end apart: 21 -> 21, of which waited for: 10 -> 10; matrix products, arithmetic and copies ran while one was open for 0% -> 0% of each run, Pallas kernels for 10% -> 7%
where the time goes in v9:
time: 65 us; the launch traced here: 64.8 us
  waiting for transfers between devices  30.2 us (46%)
  starting transfers between devices  26 us (40%)
  Pallas kernels  8.15 us (13%)
    ppermute x21, waiting for transfers between devices, swap(): return lax.ppermute(value, axis, [(i, i ^ step) for i in range(count)])  30.2 us
    ppermute x21, starting transfers between devices, swap(): return lax.ppermute(value, axis, [(i, i ^ step) for i in range(count)])  26 us
    pallas_call x10, Pallas kernels, call(): pl.pallas_call(kernel, out_shape=[jax.ShapeDtypeStruct(shape, dtype) for...  8.15 us
  transfers between devices with their start and end apart: 21, of which 10 were waited for; matrix products, arithmetic and copies ran while one was open for 0% of the time, Pallas kernels for 7%

profile of v9, /device:TPU:0, one launch (start us, length us, event | category | flops | bytes accessed | tf_op | source)
XLA Modules:
  0.0 64.8 jit_solution(974724015595320485)
XLA Ops:
  0.0 1.7 %shard_map.64 = (bf16[256,512]{1,0:T(8,128)(2,1)S(1)}, bf16[80,512]{1,0:T(8,128)(2,1)S(1)}, bf16[80,512]{1,0:T(8,128)(2,1)S(1)}, bf16[80,512]{1,0:T(8,128)(2,1)S...) custom-call(s32[1]{0:T(128)} %bitcast.my_dp, s32[1]{0:T(128)} %bitcast.1.core, ...), custom_call_target="tpu_custom_call" | custom-call | flops 16777216 | bytes 2097152 | tf_op jit(solution)/shard_map/pallas_call | solution.py:32
  1.7 3.0 %collective-permute-start.1 = (bf16[80,512]{1,0:T(8,128)(2,1)S(1)}, bf16[80,512]{1,0:T(8,128)(2,1)S(1)}, u32[]{:S(2)}, u32[]{:S(2)}) collective-permute-start(bf16[80,512]{1,0:T(8,128)(2,1)S(1)} %get-tuple-element.28), channel_id=1, source_target_pairs={{0,16},{8,24},{16,0},{24,8},{1,17},{9,25},{17,1},{25,9},{2,18},{10... | collective-permute-start | bytes 245768 | tf_op jit(solution)/shard_map/ppermute | solution.py:24
  4.7 1.4 %collective-permute-start.2 = (bf16[80,512]{1,0:T(8,128)(2,1)S(1)}, bf16[80,512]{1,0:T(8,128)(2,1)S(1)}, u32[]{:S(2)}, u32[]{:S(2)}) collective-permute-start(bf16[80,512]{1,0:T(8,128)(2,1)S(1)} %get-tuple-element.29), channel_id=1, source_target_pairs={{0,24},{8,16},{16,8},{24,0},{1,25},{9,17},{17,9},{25,1},{2,26},{10... | collective-permute-start | bytes 245768 | tf_op jit(solution)/shard_map/ppermute | solution.py:24
  6.2 0.1 collective-permute-start
  6.3 1.9 %collective-permute-start.3 = (bf16[64,512]{1,0:T(8,128)(2,1)S(1)}, bf16[64,512]{1,0:T(8,128)(2,1)S(1)}, u32[]{:S(2)}, u32[]{:S(2)}) collective-permute-start(bf16[64,512]{1,0:T(8,128)(2,1)S(1)} %get-tuple-element.30), channel_id=1, source_target_pairs={{0,8},{8,0},{16,24},{24,16},{1,9},{9,1},{17,25},{25,17},{2,10},{10... | collective-permute-start | bytes 196616 | tf_op jit(solution)/shard_map/ppermute | solution.py:24
  8.2 1.5 %collective-permute-start.4 = (bf16[64,512]{1,0:T(8,128)(2,1)S(1)}, bf16[64,512]{1,0:T(8,128)(2,1)S(1)}, u32[]{:S(2)}, u32[]{:S(2)}) collective-permute-start(bf16[64,512]{1,0:T(8,128)(2,1)S(1)} %get-tuple-element.31), channel_id=1, source_target_pairs={{0,16},{8,24},{16,0},{24,8},{1,17},{9,25},{17,1},{25,9},{2,18},{10... | collective-permute-start | bytes 196616 | tf_op jit(solution)/shard_map/ppermute | solution.py:24
  9.7 1.7 %collective-permute-start.5 = (bf16[64,512]{1,0:T(8,128)(2,1)S(1)}, bf16[64,512]{1,0:T(8,128)(2,1)S(1)}, u32[]{:S(2)}, u32[]{:S(2)}) collective-permute-start(bf16[64,512]{1,0:T(8,128)(2,1)S(1)} %get-tuple-element.32), channel_id=1, source_target_pairs={{0,24},{8,16},{16,8},{24,0},{1,25},{9,17},{17,9},{25,1},{2,26},{10... | collective-permute-start | bytes 196616 | tf_op jit(solution)/shard_map/ppermute | solution.py:24
  11.4 1.8 %shard_map.65.refs_4_.refs_0_ = bf16[8,352,512]{2,1,0:T(8,128)(2,1)S(1)} custom-call(bf16[8,352,512]{2,1,0:T(8,128)(2,1)} %refs_0_.1, bf16[256,512]{1,0:T(8,128)(2,1)S(1)} %get-tuple-element.26.refs_1_.own), custom_call_target="tpu_custom_call" | custom-call | bytes 5767168 | tf_op jit(solution)/shard_map/pallas_call | solution.py:32
  13.2 0.0 collective-permute-done.refs_1_.refs_0_
  13.2 0.0 copy-start.1
  13.2 0.4 shard_map.66.mix_ref
  13.6 0.0 copy-start
  13.6 0.5 shard_map.67
  14.2 0.9 %collective-permute-start.10 = (bf16[1,352,512]{2,1,0:T(8,128)(2,1)S(1)}, bf16[1,352,512]{2,1,0:T(8,128)(2,1)S(1)}, u32[]{:S(2)}, u32[]{:S(2)}) collective-permute-start(bf16[1,352,512]{2,1,0:T(8,128)(2,1)S(1)} %get-tuple-element.42), channel_id=1, source_target_pairs={{0,8},{8,0},{16,24},{24,16},{1,9},{9,1},{17,25},{25,17},{2,10},{10... | collective-permute-start | bytes 1081352 | tf_op jit(solution)/shard_map/ppermute | solution.py:24
  15.0 1.0 %collective-permute-start.11 = (bf16[1,352,512]{2,1,0:T(8,128)(2,1)S(1)}, bf16[1,352,512]{2,1,0:T(8,128)(2,1)S(1)}, u32[]{:S(2)}, u32[]{:S(2)}) collective-permute-start(bf16[1,352,512]{2,1,0:T(8,128)(2,1)S(1)} %get-tuple-element.43), channel_id=1, source_target_pairs={{0,16},{8,24},{16,0},{24,8},{1,17},{9,25},{17,1},{25,9},{2,18},{10... | collective-permute-start | bytes 1081352 | tf_op jit(solution)/shard_map/ppermute | solution.py:24
  16.0 0.0 collective-permute-done.4.refs_4_
  16.0 0.0 collective-permute-done.5.refs_5_
  16.1 0.1 collective-permute-start.6
  16.2 0.9 %shard_map.69 = (bf16[1,704,512]{2,1,0:T(8,128)(2,1)S(1)}, bf16[1,704,512]{2,1,0:T(8,128)(2,1)S(1)}, bf16[1,704,512]{2,1,0:T(8,128)(2,1)S(1)}, bf16[1,704,512]{2,1,0:T(8,128)(2,1)S(1)}) custom-call(bf16[128,256]{1,0:T(8,128)(2,1)S(1)} %shard_map.66.mix_ref, bf16[8,352,512]{2,1,0:T(8,128)(2,1)S(1)} %bitcast.34, bf16[8,352,512]{2,1,0:T(8,128)(2,1)S(1)} %bitcast.35), custom_call_target="tpu_custom_call" | custom-call | flops 10000000000 | bytes 8650752 | tf_op jit(solution)/shard_map/pallas_call | solution.py:32
  17.1 0.8 %collective-permute-done.6.other = bf16[3,128,512]{2,1,0:T(8,128)(2,1)S(1)} collective-permute-done((bf16[3,128,512]{2,1,0:T(8,128)(2,1)S(1)}, bf16[3,128,512]{2,1,0:T(8,128)(2,1)S(1)}, u32[]{:S(2)}, u32[]{:S(2)}) %collective-permute-start.6) | collective-permute-done | bytes 393248 | tf_op jit(solution)/shard_map/ppermute | solution.py:24
  17.9 1.0 %shard_map.70 = (bf16[1,704,256]{2,1,0:T(8,128)(2,1)S(1)}, bf16[1,704,256]{2,1,0:T(8,128)(2,1)S(1)}, bf16[1,704,256]{2,1,0:T(8,128)(2,1)S(1)}, bf16[1,704,256]{2,1,0:T(8,128)(2,1)S(1)}) custom-call(s32[1]{0:T(128)} %bitcast.1.core, bf16[256,512]{1,0:T(8,128)(2,1)S(1)} %get-tuple-element.26.refs_1_.own, bf16[3,128,512]{2,1,0:T(8,128)(2,1)S(1)} %shard_map.68.brought, ...), custom_call_target="tpu_custom_call" | custom-call | flops 738197504 | bytes 5373952 | tf_op jit(solution)/shard_map/pallas_call | solution.py:32
  18.9 0.6 collective-permute-start.7
  19.5 1.7 %collective-permute-start.8 = (bf16[1,704,256]{2,1,0:T(8,128)(2,1)S(1)}, bf16[1,704,256]{2,1,0:T(8,128)(2,1)S(1)}, u32[]{:S(2)}, u32[]{:S(2)}) collective-permute-start(bf16[1,704,256]{2,1,0:T(8,128)(2,1)S(1)} %get-tuple-element.40), channel_id=1, source_target_pairs={{0,16},{8,24},{16,0},{24,8},{1,17},{9,25},{17,1},{25,9},{2,18},{10... | collective-permute-start | bytes 1081352 | tf_op jit(solution)/shard_map/ppermute | solution.py:24
  21.2 1.3 %collective-permute-start.9 = (bf16[1,704,256]{2,1,0:T(8,128)(2,1)S(1)}, bf16[1,704,256]{2,1,0:T(8,128)(2,1)S(1)}, u32[]{:S(2)}, u32[]{:S(2)}) collective-permute-start(bf16[1,704,256]{2,1,0:T(8,128)(2,1)S(1)} %get-tuple-element.41), channel_id=1, source_target_pairs={{0,24},{8,16},{16,8},{24,0},{1,25},{9,17},{17,9},{25,1},{2,26},{10... | collective-permute-start | bytes 1081352 | tf_op jit(solution)/shard_map/ppermute | solution.py:24
  22.4 0.2 collective-permute-done.10.refs_5_
  22.6 0.9 %collective-permute-done.11.refs_6_ = bf16[1,352,512]{2,1,0:T(8,128)(2,1)S(1)} collective-permute-done((bf16[1,352,512]{2,1,0:T(8,128)(2,1)S(1)}, bf16[1,352,512]{2,1,0:T(8,128)(2,1)S(1)}, u32[]{:S(2)}, u32[]{:S(2)}) %collective-permute-start.11) | collective-permute-done | bytes 360480 | tf_op jit(solution)/shard_map/ppermute | solution.py:24
  23.5 6.8 %collective-permute-done.7.refs_1_ = bf16[1,704,256]{2,1,0:T(8,128)(2,1)S(1)} collective-permute-done((bf16[1,704,256]{2,1,0:T(8,128)(2,1)S(1)}, bf16[1,704,256]{2,1,0:T(8,128)(2,1)S(1)}, u32[]{:S(2)}, u32[]{:S(2)}) %collective-permute-start.7) | collective-permute-done | bytes 360480 | tf_op jit(solution)/shard_map/ppermute | solution.py:24
  30.3 7.9 %collective-permute-done.8.refs_2_ = bf16[1,704,256]{2,1,0:T(8,128)(2,1)S(1)} collective-permute-done((bf16[1,704,256]{2,1,0:T(8,128)(2,1)S(1)}, bf16[1,704,256]{2,1,0:T(8,128)(2,1)S(1)}, u32[]{:S(2)}, u32[]{:S(2)}) %collective-permute-start.8) | collective-permute-done | bytes 360480 | tf_op jit(solution)/shard_map/ppermute | solution.py:24
  38.2 0.8 %shard_map.71 = (bf16[1,352,256]{2,1,0:T(8,128)(2,1)S(1)}, bf16[2,4,32,1536]{3,2,1,0:T(8,128)(2,1)S(1)}) custom-call(s32[1]{0:T(128)} %bitcast.1.core, bf16[1,704,256]{2,1,0:T(8,128)(2,1)S(1)} %get-tuple-element.38.refs_0_, bf16[1,704,256]{2,1,0:T(8,128)(2,1)S(1)} %collective-permute-done.7.refs_1_, bf16[1,704,256]{2,1,0:T(8,128)(2,1)S(1)} %collective-permute-done.8.refs_2_, ...), custom_call_target="tpu_custom_call" | custom-call | flops 276824064 | bytes 2523136 | tf_op jit(solution)/shard_map/pallas_call | solution.py:32
  39.0 0.1 collective-permute-start.12
  39.2 1.7 %collective-permute-start.16 = (bf16[1,352,512]{2,1,0:T(8,128)(2,1)S(1)}, bf16[1,352,512]{2,1,0:T(8,128)(2,1)S(1)}, u32[]{:S(2)}, u32[]{:S(2)}) collective-permute-start(bf16[1,352,512]{2,1,0:T(8,128)(2,1)S(1)} %get-tuple-element.46), channel_id=1, source_target_pairs={{0,24},{8,16},{16,8},{24,0},{1,25},{9,17},{17,9},{25,1},{2,26},{10... | collective-permute-start | bytes 1081352 | tf_op jit(solution)/shard_map/ppermute | solution.py:24
  40.9 0.0 collective-permute-done.12
  40.9 0.1 fusion
  41.0 1.6 %collective-permute-start.15 = (bf16[32,1536]{1,0:T(8,128)(2,1)S(1)}, bf16[32,1536]{1,0:T(8,128)(2,1)S(1)}, u32[]{:S(2)}, u32[]{:S(2)}) collective-permute-start(bf16[32,1536]{1,0:T(8,128)(2,1)S(1)} %get-tuple-element.48), channel_id=1, source_target_pairs={{0,2},{1,3},{2,0},{3,1},{4,6},{5,7},{6,4},{7,5},{8,10},{9,11},{10,... | collective-permute-start | bytes 294920 | tf_op jit(solution)/shard_map/ppermute | solution.py:24
  42.7 2.6 %collective-permute-start.14 = (bf16[32,1536]{1,0:T(8,128)(2,1)S(1)}, bf16[32,1536]{1,0:T(8,128)(2,1)S(1)}, u32[]{:S(2)}, u32[]{:S(2)}) collective-permute-start(bf16[32,1536]{1,0:T(8,128)(2,1)S(1)} %get-tuple-element.49), channel_id=1, source_target_pairs={{0,4},{1,5},{2,6},{3,7},{4,0},{5,1},{6,2},{7,3},{8,12},{9,13},{10,... | collective-permute-start | bytes 294920 | tf_op jit(solution)/shard_map/ppermute | solution.py:24
  45.3 0.2 collective-permute-start.13
  45.5 5.4 %collective-permute-done.16.refs_0_ = bf16[1,352,512]{2,1,0:T(8,128)(2,1)S(1)} collective-permute-done((bf16[1,352,512]{2,1,0:T(8,128)(2,1)S(1)}, bf16[1,352,512]{2,1,0:T(8,128)(2,1)S(1)}, u32[]{:S(2)}, u32[]{:S(2)}) %collective-permute-start.16) | collective-permute-done | bytes 360480 | tf_op jit(solution)/shard_map/ppermute | solution.py:24
  50.9 0.0 collective-permute-done.15.refs_3_.refs_2_
  50.9 2.5 %collective-permute-done.14.refs_2_.refs_1_ = bf16[32,1536]{1,0:T(8,128)(2,1)S(1)} collective-permute-done((bf16[32,1536]{1,0:T(8,128)(2,1)S(1)}, bf16[32,1536]{1,0:T(8,128)(2,1)S(1)}, u32[]{:S(2)}, u32[]{:S(2)}) %collective-permute-start.14) | collective-permute-done | bytes 98336 | tf_op jit(solution)/shard_map/ppermute | solution.py:24
  53.3 0.3 shard_map.72
  53.7 0.1 collective-permute-start.17
  53.8 1.3 %collective-permute-done.17 = bf16[4,32,512]{2,1,0:T(8,128)(2,1)S(1)} collective-permute-done((bf16[4,32,512]{2,1,0:T(8,128)(2,1)S(1)}, bf16[4,32,512]{2,1,0:T(8,128)(2,1)S(1)}, u32[]{:S(2)}, u32[]{:S(2)}) %collective-permute-start.17) | collective-permute-done | bytes 131104 | tf_op jit(solution)/shard_map/ppermute | solution.py:24
  55.2 1.8 %collective-permute-start.20 = (bf16[32,512]{1,0:T(8,128)(2,1)S(1)}, bf16[32,512]{1,0:T(8,128)(2,1)S(1)}, u32[]{:S(2)}, u32[]{:S(2)}) collective-permute-start(bf16[32,512]{1,0:T(8,128)(2,1)S(1)} %get-tuple-element.52), channel_id=1, source_target_pairs={{0,2},{1,3},{2,0},{3,1},{4,6},{5,7},{6,4},{7,5},{8,10},{9,11},{10,... | collective-permute-start | bytes 98312 | tf_op jit(solution)/shard_map/ppermute | solution.py:24
  57.0 1.4 %collective-permute-start.19 = (bf16[32,512]{1,0:T(8,128)(2,1)S(1)}, bf16[32,512]{1,0:T(8,128)(2,1)S(1)}, u32[]{:S(2)}, u32[]{:S(2)}) collective-permute-start(bf16[32,512]{1,0:T(8,128)(2,1)S(1)} %get-tuple-element.53), channel_id=1, source_target_pairs={{0,4},{1,5},{2,6},{3,7},{4,0},{5,1},{6,2},{7,3},{8,12},{9,13},{10,... | collective-permute-start | bytes 98312 | tf_op jit(solution)/shard_map/ppermute | solution.py:24
  58.4 1.2 %collective-permute-start.18 = (bf16[32,512]{1,0:T(8,128)(2,1)S(1)}, bf16[32,512]{1,0:T(8,128)(2,1)S(1)}, u32[]{:S(2)}, u32[]{:S(2)}) collective-permute-start(bf16[32,512]{1,0:T(8,128)(2,1)S(1)} %get-tuple-element.54), channel_id=1, source_target_pairs={{0,6},{1,7},{2,4},{3,5},{4,2},{5,3},{6,0},{7,1},{8,14},{9,15},{10,... | collective-permute-start | bytes 98312 | tf_op jit(solution)/shard_map/ppermute | solution.py:24
  59.6 2.7 %collective-permute-done.19.refs_5_ = bf16[32,512]{1,0:T(8,128)(2,1)S(1)} collective-permute-done((bf16[32,512]{1,0:T(8,128)(2,1)S(1)}, bf16[32,512]{1,0:T(8,128)(2,1)S(1)}, u32[]{:S(2)}, u32[]{:S(2)}) %collective-permute-start.19) | collective-permute-done | bytes 32800 | tf_op jit(solution)/shard_map/ppermute | solution.py:24
  62.4 1.7 %collective-permute-done.18.refs_4_ = bf16[32,512]{1,0:T(8,128)(2,1)S(1)} collective-permute-done((bf16[32,512]{1,0:T(8,128)(2,1)S(1)}, bf16[32,512]{1,0:T(8,128)(2,1)S(1)}, u32[]{:S(2)}, u32[]{:S(2)}) %collective-permute-start.18) | collective-permute-done | bytes 32800 | tf_op jit(solution)/shard_map/ppermute | solution.py:24
  64.1 0.7 %shard_map.73 = bf16[32,2048]{1,0:T(8,128)(2,1)} custom-call(s32[1]{0:T(128)} %bitcast.my_dp, bf16[32,1536]{1,0:T(8,128)(2,1)S(1)} %collective-permute-done.13.refs_1_.refs_0_, bf16[32,1536]{1,0:T(8,128)(2,1)S(1)} %collective-permute-done.14.refs_2_.refs_1_, bf16[32,1536]{1,0:T(8,128)(2,1)S(1)} %collective-permute-done.15.refs_3_.refs_2_, ...), custom_call_target="tpu_custom_call" | custom-call | flops 262144 | bytes 655360 | tf_op jit(solution)/shard_map/pallas_call | solution.py:32
  (14 shorter events, 0.2 us)
Async XLA Ops:
  1.7 8.0 %collective-permute-start.1 = (bf16[80,512]{1,0:T(8,128)(2,1)S(1)}, bf16[80,512]{1,0:T(8,128)(2,1)S(1)}, u32[]{:S(2)}, u32[]{:S(2)}) collective-permute-start(bf16[80,512]{1,0:T(8,128)(2,1)S(1)} %get-tuple-element.28), channel_id=1, source_target_pairs={{0,16},{8,24},{16,0},{24,8},{1,17},{9,25},{17,1},{25,9},{2,18},{10... | collective-permute-start | bytes 245768 | tf_op jit(solution)/shard_map/ppermute | solution.py:24
  4.7 8.5 %collective-permute-start.2 = (bf16[80,512]{1,0:T(8,128)(2,1)S(1)}, bf16[80,512]{1,0:T(8,128)(2,1)S(1)}, u32[]{:S(2)}, u32[]{:S(2)}) collective-permute-start(bf16[80,512]{1,0:T(8,128)(2,1)S(1)} %get-tuple-element.29), channel_id=1, source_target_pairs={{0,24},{8,16},{16,8},{24,0},{1,25},{9,17},{17,9},{25,1},{2,26},{10... | collective-permute-start | bytes 245768 | tf_op jit(solution)/shard_map/ppermute | solution.py:24
  6.2 7.1 %collective-permute-start = (bf16[80,512]{1,0:T(8,128)(2,1)S(1)}, bf16[80,512]{1,0:T(8,128)(2,1)S(1)}, u32[]{:S(2)}, u32[]{:S(2)}) collective-permute-start(bf16[80,512]{1,0:T(8,128)(2,1)S(1)} %get-tuple-element.27.refs_0_), channel_id=1, source_target_pairs={{0,8},{8,0},{16,24},{24,16},{1,9},{9,1},{17,25},{25,17},{2,10},{10... | collective-permute-start | bytes 245768 | tf_op jit(solution)/shard_map/ppermute | solution.py:24
  6.3 9.8 %collective-permute-start.3 = (bf16[64,512]{1,0:T(8,128)(2,1)S(1)}, bf16[64,512]{1,0:T(8,128)(2,1)S(1)}, u32[]{:S(2)}, u32[]{:S(2)}) collective-permute-start(bf16[64,512]{1,0:T(8,128)(2,1)S(1)} %get-tuple-element.30), channel_id=1, source_target_pairs={{0,8},{8,0},{16,24},{24,16},{1,9},{9,1},{17,25},{25,17},{2,10},{10... | collective-permute-start | bytes 196616 | tf_op jit(solution)/shard_map/ppermute | solution.py:24
  8.2 7.9 %collective-permute-start.4 = (bf16[64,512]{1,0:T(8,128)(2,1)S(1)}, bf16[64,512]{1,0:T(8,128)(2,1)S(1)}, u32[]{:S(2)}, u32[]{:S(2)}) collective-permute-start(bf16[64,512]{1,0:T(8,128)(2,1)S(1)} %get-tuple-element.31), channel_id=1, source_target_pairs={{0,16},{8,24},{16,0},{24,8},{1,17},{9,25},{17,1},{25,9},{2,18},{10... | collective-permute-start | bytes 196616 | tf_op jit(solution)/shard_map/ppermute | solution.py:24
  9.7 6.3 %collective-permute-start.5 = (bf16[64,512]{1,0:T(8,128)(2,1)S(1)}, bf16[64,512]{1,0:T(8,128)(2,1)S(1)}, u32[]{:S(2)}, u32[]{:S(2)}) collective-permute-start(bf16[64,512]{1,0:T(8,128)(2,1)S(1)} %get-tuple-element.32), channel_id=1, source_target_pairs={{0,24},{8,16},{16,8},{24,0},{1,25},{9,17},{17,9},{25,1},{2,26},{10... | collective-permute-start | bytes 196616 | tf_op jit(solution)/shard_map/ppermute | solution.py:24
  13.2 2.9 %copy-start.1 = (bf16[8,512,352]{1,2,0:T(8,128)(2,1)S(1)}, bf16[8,512,352]{1,2,0:T(8,128)(2,1)}, u32[]{:S(2)}) copy-start(bf16[8,512,352]{1,2,0:T(8,128)(2,1)} %param.8) | copy-start | bytes 8650756
  13.6 2.6 %copy-start = (bf16[8,512,352]{1,2,0:T(8,128)(2,1)S(1)}, bf16[8,512,352]{1,2,0:T(8,128)(2,1)}, u32[]{:S(2)}) copy-start(bf16[8,512,352]{1,2,0:T(8,128)(2,1)} %param.7) | copy-start | bytes 8650756
  14.2 8.4 %collective-permute-start.10 = (bf16[1,352,512]{2,1,0:T(8,128)(2,1)S(1)}, bf16[1,352,512]{2,1,0:T(8,128)(2,1)S(1)}, u32[]{:S(2)}, u32[]{:S(2)}) collective-permute-start(bf16[1,352,512]{2,1,0:T(8,128)(2,1)S(1)} %get-tuple-element.42), channel_id=1, source_target_pairs={{0,8},{8,0},{16,24},{24,16},{1,9},{9,1},{17,25},{25,17},{2,10},{10... | collective-permute-start | bytes 1081352 | tf_op jit(solution)/shard_map/ppermute | solution.py:24
  15.0 8.5 %collective-permute-start.11 = (bf16[1,352,512]{2,1,0:T(8,128)(2,1)S(1)}, bf16[1,352,512]{2,1,0:T(8,128)(2,1)S(1)}, u32[]{:S(2)}, u32[]{:S(2)}) collective-permute-start(bf16[1,352,512]{2,1,0:T(8,128)(2,1)S(1)} %get-tuple-element.43), channel_id=1, source_target_pairs={{0,16},{8,24},{16,0},{24,8},{1,17},{9,25},{17,1},{25,9},{2,18},{10... | collective-permute-start | bytes 1081352 | tf_op jit(solution)/shard_map/ppermute | solution.py:24
  16.1 1.8 %collective-permute-start.6 = (bf16[3,128,512]{2,1,0:T(8,128)(2,1)S(1)}, bf16[3,128,512]{2,1,0:T(8,128)(2,1)S(1)}, u32[]{:S(2)}, u32[]{:S(2)}) collective-permute-start(bf16[3,128,512]{2,1,0:T(8,128)(2,1)S(1)} %shard_map.68.brought), channel_id=1, source_target_pairs={{0,1},{1,0},{2,3},{3,2},{4,5},{5,4},{6,7},{7,6},{8,9},{9,8},{10,11... | collective-permute-start | bytes 1179656 | tf_op jit(solution)/shard_map/ppermute | solution.py:24
  18.9 11.4 %collective-permute-start.7 = (bf16[1,704,256]{2,1,0:T(8,128)(2,1)S(1)}, bf16[1,704,256]{2,1,0:T(8,128)(2,1)S(1)}, u32[]{:S(2)}, u32[]{:S(2)}) collective-permute-start(bf16[1,704,256]{2,1,0:T(8,128)(2,1)S(1)} %get-tuple-element.39), channel_id=1, source_target_pairs={{0,8},{8,0},{16,24},{24,16},{1,9},{9,1},{17,25},{25,17},{2,10},{10... | collective-permute-start | bytes 1081352 | tf_op jit(solution)/shard_map/ppermute | solution.py:24
  19.5 18.7 %collective-permute-start.8 = (bf16[1,704,256]{2,1,0:T(8,128)(2,1)S(1)}, bf16[1,704,256]{2,1,0:T(8,128)(2,1)S(1)}, u32[]{:S(2)}, u32[]{:S(2)}) collective-permute-start(bf16[1,704,256]{2,1,0:T(8,128)(2,1)S(1)} %get-tuple-element.40), channel_id=1, source_target_pairs={{0,16},{8,24},{16,0},{24,8},{1,17},{9,25},{17,1},{25,9},{2,18},{10... | collective-permute-start | bytes 1081352 | tf_op jit(solution)/shard_map/ppermute | solution.py:24
  21.2 17.0 %collective-permute-start.9 = (bf16[1,704,256]{2,1,0:T(8,128)(2,1)S(1)}, bf16[1,704,256]{2,1,0:T(8,128)(2,1)S(1)}, u32[]{:S(2)}, u32[]{:S(2)}) collective-permute-start(bf16[1,704,256]{2,1,0:T(8,128)(2,1)S(1)} %get-tuple-element.41), channel_id=1, source_target_pairs={{0,24},{8,16},{16,8},{24,0},{1,25},{9,17},{17,9},{25,1},{2,26},{10... | collective-permute-start | bytes 1081352 | tf_op jit(solution)/shard_map/ppermute | solution.py:24
  39.0 1.8 %collective-permute-start.12 = (bf16[4,32,1536]{2,1,0:T(8,128)(2,1)S(1)}, bf16[4,32,1536]{2,1,0:T(8,128)(2,1)S(1)}, u32[]{:S(2)}, u32[]{:S(2)}) collective-permute-start(bf16[4,32,1536]{2,1,0:T(8,128)(2,1)S(1)} %slice_bitcast_fusion), channel_id=1, source_target_pairs={{0,1},{1,0},{2,3},{3,2},{4,5},{5,4},{6,7},{7,6},{8,9},{9,8},{10,11... | collective-permute-start | bytes 1179656 | tf_op jit(solution)/shard_map/ppermute | solution.py:24
  39.2 11.7 %collective-permute-start.16 = (bf16[1,352,512]{2,1,0:T(8,128)(2,1)S(1)}, bf16[1,352,512]{2,1,0:T(8,128)(2,1)S(1)}, u32[]{:S(2)}, u32[]{:S(2)}) collective-permute-start(bf16[1,352,512]{2,1,0:T(8,128)(2,1)S(1)} %get-tuple-element.46), channel_id=1, source_target_pairs={{0,24},{8,16},{16,8},{24,0},{1,25},{9,17},{17,9},{25,1},{2,26},{10... | collective-permute-start | bytes 1081352 | tf_op jit(solution)/shard_map/ppermute | solution.py:24
  41.0 9.8 %collective-permute-start.15 = (bf16[32,1536]{1,0:T(8,128)(2,1)S(1)}, bf16[32,1536]{1,0:T(8,128)(2,1)S(1)}, u32[]{:S(2)}, u32[]{:S(2)}) collective-permute-start(bf16[32,1536]{1,0:T(8,128)(2,1)S(1)} %get-tuple-element.48), channel_id=1, source_target_pairs={{0,2},{1,3},{2,0},{3,1},{4,6},{5,7},{6,4},{7,5},{8,10},{9,11},{10,... | collective-permute-start | bytes 294920 | tf_op jit(solution)/shard_map/ppermute | solution.py:24
  42.7 10.7 %collective-permute-start.14 = (bf16[32,1536]{1,0:T(8,128)(2,1)S(1)}, bf16[32,1536]{1,0:T(8,128)(2,1)S(1)}, u32[]{:S(2)}, u32[]{:S(2)}) collective-permute-start(bf16[32,1536]{1,0:T(8,128)(2,1)S(1)} %get-tuple-element.49), channel_id=1, source_target_pairs={{0,4},{1,5},{2,6},{3,7},{4,0},{5,1},{6,2},{7,3},{8,12},{9,13},{10,... | collective-permute-start | bytes 294920 | tf_op jit(solution)/shard_map/ppermute | solution.py:24
  45.3 8.1 %collective-permute-start.13 = (bf16[32,1536]{1,0:T(8,128)(2,1)S(1)}, bf16[32,1536]{1,0:T(8,128)(2,1)S(1)}, u32[]{:S(2)}, u32[]{:S(2)}) collective-permute-start(bf16[32,1536]{1,0:T(8,128)(2,1)S(1)} %get-tuple-element.50), channel_id=1, source_target_pairs={{0,6},{1,7},{2,4},{3,5},{4,2},{5,3},{6,0},{7,1},{8,14},{9,15},{10,... | collective-permute-start | bytes 294920 | tf_op jit(solution)/shard_map/ppermute | solution.py:24
  53.7 1.4 %collective-permute-start.17 = (bf16[4,32,512]{2,1,0:T(8,128)(2,1)S(1)}, bf16[4,32,512]{2,1,0:T(8,128)(2,1)S(1)}, u32[]{:S(2)}, u32[]{:S(2)}) collective-permute-start(bf16[4,32,512]{2,1,0:T(8,128)(2,1)S(1)} %slice_bitcast_fusion.1), channel_id=1, source_target_pairs={{0,1},{1,0},{2,3},{3,2},{4,5},{5,4},{6,7},{7,6},{8,9},{9,8},{10,11... | collective-permute-start | bytes 393224 | tf_op jit(solution)/shard_map/ppermute | solution.py:24
  55.2 4.5 %collective-permute-start.20 = (bf16[32,512]{1,0:T(8,128)(2,1)S(1)}, bf16[32,512]{1,0:T(8,128)(2,1)S(1)}, u32[]{:S(2)}, u32[]{:S(2)}) collective-permute-start(bf16[32,512]{1,0:T(8,128)(2,1)S(1)} %get-tuple-element.52), channel_id=1, source_target_pairs={{0,2},{1,3},{2,0},{3,1},{4,6},{5,7},{6,4},{7,5},{8,10},{9,11},{10,... | collective-permute-start | bytes 98312 | tf_op jit(solution)/shard_map/ppermute | solution.py:24
  57.0 5.4 %collective-permute-start.19 = (bf16[32,512]{1,0:T(8,128)(2,1)S(1)}, bf16[32,512]{1,0:T(8,128)(2,1)S(1)}, u32[]{:S(2)}, u32[]{:S(2)}) collective-permute-start(bf16[32,512]{1,0:T(8,128)(2,1)S(1)} %get-tuple-element.53), channel_id=1, source_target_pairs={{0,4},{1,5},{2,6},{3,7},{4,0},{5,1},{6,2},{7,3},{8,12},{9,13},{10,... | collective-permute-start | bytes 98312 | tf_op jit(solution)/shard_map/ppermute | solution.py:24
  58.4 5.7 %collective-permute-start.18 = (bf16[32,512]{1,0:T(8,128)(2,1)S(1)}, bf16[32,512]{1,0:T(8,128)(2,1)S(1)}, u32[]{:S(2)}, u32[]{:S(2)}) collective-permute-start(bf16[32,512]{1,0:T(8,128)(2,1)S(1)} %get-tuple-element.54), channel_id=1, source_target_pairs={{0,6},{1,7},{2,4},{3,5},{4,2},{5,3},{6,0},{7,1},{8,14},{9,15},{10,... | collective-permute-start | bytes 98312 | tf_op jit(solution)/shard_map/ppermute | solution.py:24

commit v10 on v9

--- a/solution.py
+++ b/solution.py
@@ -97,36 +97,11 @@
         first[quarter:, :LANES] = terms
 
 
-def load_kernel(count, *refs):
-    sources, targets, sems = refs[:count], refs[-count - 1 : -1], refs[-1]
-    copies = [
-        pltpu.make_async_copy(source, target, sems.at[i])
-        for i, (source, target) in enumerate(zip(sources, targets))
-    ]
-    for copy in copies:
-        copy.start()
-    for copy in copies:
-        copy.wait()
-
-
 def read_table(piece, tokens, experts):
     lane = lax.broadcasted_iota(jnp.int32, (LANES, experts), 0)
     summed = lane % experts == lax.broadcasted_iota(jnp.int32, (LANES, experts), 1)
     summed = jnp.where(summed & (lane < 3 * experts), 1.0, 0.0).astype(BF16)
     return jnp.dot(piece[tokens:, :LANES], summed, preferred_element_type=F32)
-
-
-def load(weights, after):
-    count = len(weights)
-    return call(
-        functools.partial(load_kernel, count),
-        [(weight.shape, BF16) for weight in weights],
-        [HBM] * count + [ANY],
-        (*map(in_hbm, weights), after),
-        0,
-        4 * count * weights[0].size,
-        [pltpu.SemaphoreType.DMA((count,))],
-    )
 
 
 def spread_probs(my_dp, tables, own_segs, experts, steps, block):
@@ -314,7 +289,7 @@
         + [((quarter, depth), BF16)] * (dp - 1),
         [SMEM, SMEM, HBM, HBM, HBM],
         (my_dp, core, *map(in_hbm, (tokens, router_weight.T, carry_mean.reshape(1, width)))),
-        2 * extra * own_rows * width,
+        BESIDE,
         4 * own_rows * width,
         [
             pltpu.VMEM((dp - 1, own_rows, depth), BF16),
@@ -325,17 +300,16 @@
     )
     firsts = [swap(sends[k - 1], "dp", k) for k in range(1, dp)]
     seconds = [swap(sends[dp + k - 2], "dp", k) for k in range(1, dp)]
-    (down,) = load((down_weight,), own)
     block = 32 if hidden_count % 32 == 0 else 16
     (mix,) = call(
         functools.partial(route_kernel, dp, own_segs, block),
         [((segs * block, experts * block), BF16)],
-        [SMEM] + [VMEM] * dp + [ANY],
-        (my_dp, sends[0], *firsts, down),
+        [SMEM] + [VMEM] * dp,
+        (my_dp, sends[0], *firsts),
         0,
         2 * own_rows * depth,
     )
-    merged_down = merge(mix, dp, own_segs, (down,), 2 * mix.size * down.size // experts // block)
+    merged_down = merge(mix, dp, own_segs, (down_weight,), 2 * mix.size * down_weight.size // experts // block)
     downs = [block if k == 0 else swap(block, "dp", k) for k, block in enumerate(merged_down)]
     gate_up = (jnp.swapaxes(gate_weight, 1, 2), jnp.swapaxes(up_weight, 1, 2))
     (stacked,) = call(

time: 65 us -> 65 us (level)
  Pallas kernels: 8.15 us -> 6.46 us
  starting transfers between devices: 26 us -> 27.5 us
    pallas_call x10 -> x9, Pallas kernels: 8.15 us -> 6.46 us  [call(): pl.pallas_call(kernel, out_shape=[jax.ShapeDtypeStruct(shape, dtype) for...]
    ppermute x21, starting transfers between devices: 26 us -> 27.5 us  [swap(): return lax.ppermute(value, axis, [(i, i ^ step) for i in range(count)])]
  transfers between devices with their start and end apart: 21 -> 21, of which waited for: 10 -> 11; matrix products, arithmetic and copies ran while one was open for 0% -> 0% of each run, Pallas kernels for 7% -> 4%
where the time goes in v10:
time: 65 us; the launch traced here: 64.9 us
  waiting for transfers between devices  30.5 us (47%)
  starting transfers between devices  27.5 us (42%)
  Pallas kernels  6.46 us (10%)
    ppermute x21, waiting for transfers between devices, swap(): return lax.ppermute(value, axis, [(i, i ^ step) for i in range(count)])  30.5 us
    ppermute x21, starting transfers between devices, swap(): return lax.ppermute(value, axis, [(i, i ^ step) for i in range(count)])  27.5 us
    pallas_call x9, Pallas kernels, call(): pl.pallas_call(kernel, out_shape=[jax.ShapeDtypeStruct(shape, dtype) for...  6.46 us
  transfers between devices with their start and end apart: 21, of which 11 were waited for; matrix products, arithmetic and copies ran while one was open for 0% of the time, Pallas kernels for 4%

profile of v10, /device:TPU:0, one launch (start us, length us, event | category | flops | bytes accessed | tf_op | source)
XLA Modules:
  0.0 64.9 jit_solution(5658628676265971521)
XLA Ops:
  0.0 1.8 %shard_map.64 = (bf16[256,512]{1,0:T(8,128)(2,1)S(1)}, bf16[80,512]{1,0:T(8,128)(2,1)S(1)}, bf16[80,512]{1,0:T(8,128)(2,1)S(1)}, bf16[80,512]{1,0:T(8,128)(2,1)S...) custom-call(s32[1]{0:T(128)} %bitcast.my_dp, s32[1]{0:T(128)} %bitcast.1.core, ...), custom_call_target="tpu_custom_call" | custom-call | flops 10000000000 | bytes 2097152 | tf_op jit(solution)/shard_map/pallas_call | solution.py:32
  1.8 0.0 copy-start.1
  1.8 3.0 %collective-permute-start.1 = (bf16[80,512]{1,0:T(8,128)(2,1)S(1)}, bf16[80,512]{1,0:T(8,128)(2,1)S(1)}, u32[]{:S(2)}, u32[]{:S(2)}) collective-permute-start(bf16[80,512]{1,0:T(8,128)(2,1)S(1)} %get-tuple-element.28), channel_id=1, source_target_pairs={{0,16},{8,24},{16,0},{24,8},{1,17},{9,25},{17,1},{25,9},{2,18},{10... | collective-permute-start | bytes 245768 | tf_op jit(solution)/shard_map/ppermute | solution.py:24
  4.9 1.4 %collective-permute-start.2 = (bf16[80,512]{1,0:T(8,128)(2,1)S(1)}, bf16[80,512]{1,0:T(8,128)(2,1)S(1)}, u32[]{:S(2)}, u32[]{:S(2)}) collective-permute-start(bf16[80,512]{1,0:T(8,128)(2,1)S(1)} %get-tuple-element.29), channel_id=1, source_target_pairs={{0,24},{8,16},{16,8},{24,0},{1,25},{9,17},{17,9},{25,1},{2,26},{10... | collective-permute-start | bytes 245768 | tf_op jit(solution)/shard_map/ppermute | solution.py:24
  6.3 0.1 collective-permute-start
  6.4 1.9 %collective-permute-start.3 = (bf16[64,512]{1,0:T(8,128)(2,1)S(1)}, bf16[64,512]{1,0:T(8,128)(2,1)S(1)}, u32[]{:S(2)}, u32[]{:S(2)}) collective-permute-start(bf16[64,512]{1,0:T(8,128)(2,1)S(1)} %get-tuple-element.30), channel_id=1, source_target_pairs={{0,8},{8,0},{16,24},{24,16},{1,9},{9,1},{17,25},{25,17},{2,10},{10... | collective-permute-start | bytes 196616 | tf_op jit(solution)/shard_map/ppermute | solution.py:24
  8.3 1.5 %collective-permute-start.4 = (bf16[64,512]{1,0:T(8,128)(2,1)S(1)}, bf16[64,512]{1,0:T(8,128)(2,1)S(1)}, u32[]{:S(2)}, u32[]{:S(2)}) collective-permute-start(bf16[64,512]{1,0:T(8,128)(2,1)S(1)} %get-tuple-element.31), channel_id=1, source_target_pairs={{0,16},{8,24},{16,0},{24,8},{1,17},{9,25},{17,1},{25,9},{2,18},{10... | collective-permute-start | bytes 196616 | tf_op jit(solution)/shard_map/ppermute | solution.py:24
  9.9 0.0 collective-permute-done.1.refs_2_.refs_1_
  9.9 1.7 %collective-permute-start.5 = (bf16[64,512]{1,0:T(8,128)(2,1)S(1)}, bf16[64,512]{1,0:T(8,128)(2,1)S(1)}, u32[]{:S(2)}, u32[]{:S(2)}) collective-permute-start(bf16[64,512]{1,0:T(8,128)(2,1)S(1)} %get-tuple-element.32), channel_id=1, source_target_pairs={{0,24},{8,16},{16,8},{24,0},{1,25},{9,17},{17,9},{25,1},{2,26},{10... | collective-permute-start | bytes 196616 | tf_op jit(solution)/shard_map/ppermute | solution.py:24
  11.5 0.0 collective-permute-done.2.refs_3_.refs_2_
  11.5 0.2 collective-permute-done.refs_1_.refs_0_
  11.7 0.3 shard_map.65.mix_ref
  12.1 0.5 shard_map.66
  12.6 1.7 %collective-permute-start.10 = (bf16[1,352,512]{2,1,0:T(8,128)(2,1)S(1)}, bf16[1,352,512]{2,1,0:T(8,128)(2,1)S(1)}, u32[]{:S(2)}, u32[]{:S(2)}) collective-permute-start(bf16[1,352,512]{2,1,0:T(8,128)(2,1)S(1)} %get-tuple-element.42), channel_id=1, source_target_pairs={{0,8},{8,0},{16,24},{24,16},{1,9},{9,1},{17,25},{25,17},{2,10},{10... | collective-permute-start | bytes 1081352 | tf_op jit(solution)/shard_map/ppermute | solution.py:24
  14.4 1.5 %collective-permute-start.11 = (bf16[1,352,512]{2,1,0:T(8,128)(2,1)S(1)}, bf16[1,352,512]{2,1,0:T(8,128)(2,1)S(1)}, u32[]{:S(2)}, u32[]{:S(2)}) collective-permute-start(bf16[1,352,512]{2,1,0:T(8,128)(2,1)S(1)} %get-tuple-element.43), channel_id=1, source_target_pairs={{0,16},{8,24},{16,0},{24,8},{1,17},{9,25},{17,1},{25,9},{2,18},{10... | collective-permute-start | bytes 1081352 | tf_op jit(solution)/shard_map/ppermute | solution.py:24
  15.9 0.0 collective-permute-done.3.refs_3_
  15.9 0.0 collective-permute-done.4.refs_4_
  15.9 0.0 collective-permute-done.5.refs_5_
  15.9 0.1 collective-permute-start.6
  16.0 0.9 %shard_map.68 = (bf16[1,704,512]{2,1,0:T(8,128)(2,1)S(1)}, bf16[1,704,512]{2,1,0:T(8,128)(2,1)S(1)}, bf16[1,704,512]{2,1,0:T(8,128)(2,1)S(1)}, bf16[1,704,512]{2,1,0:T(8,128)(2,1)S(1)}) custom-call(bf16[128,256]{1,0:T(8,128)(2,1)S(1)} %shard_map.65.mix_ref, bf16[8,352,512]{2,1,0:T(8,128)(2,1)S(1)} %bitcast.34, bf16[8,352,512]{2,1,0:T(8,128)(2,1)S(1)} %bitcast.35), custom_call_target="tpu_custom_call" | custom-call | flops 10000000000 | bytes 8650752 | tf_op jit(solution)/shard_map/pallas_call | solution.py:32
  16.9 0.8 %collective-permute-done.6.other = bf16[3,128,512]{2,1,0:T(8,128)(2,1)S(1)} collective-permute-done((bf16[3,128,512]{2,1,0:T(8,128)(2,1)S(1)}, bf16[3,128,512]{2,1,0:T(8,128)(2,1)S(1)}, u32[]{:S(2)}, u32[]{:S(2)}) %collective-permute-start.6) | collective-permute-done | bytes 393248 | tf_op jit(solution)/shard_map/ppermute | solution.py:24
  17.7 1.0 %shard_map.69 = (bf16[1,704,256]{2,1,0:T(8,128)(2,1)S(1)}, bf16[1,704,256]{2,1,0:T(8,128)(2,1)S(1)}, bf16[1,704,256]{2,1,0:T(8,128)(2,1)S(1)}, bf16[1,704,256]{2,1,0:T(8,128)(2,1)S(1)}) custom-call(s32[1]{0:T(128)} %bitcast.1.core, bf16[256,512]{1,0:T(8,128)(2,1)S(1)} %get-tuple-element.26.own, bf16[3,128,512]{2,1,0:T(8,128)(2,1)S(1)} %shard_map.67.brought, ...), custom_call_target="tpu_custom_call" | custom-call | flops 738197504 | bytes 5373952 | tf_op jit(solution)/shard_map/pallas_call | solution.py:32
  18.7 0.6 collective-permute-start.7
  19.3 1.6 %collective-permute-start.8 = (bf16[1,704,256]{2,1,0:T(8,128)(2,1)S(1)}, bf16[1,704,256]{2,1,0:T(8,128)(2,1)S(1)}, u32[]{:S(2)}, u32[]{:S(2)}) collective-permute-start(bf16[1,704,256]{2,1,0:T(8,128)(2,1)S(1)} %get-tuple-element.40), channel_id=1, source_target_pairs={{0,16},{8,24},{16,0},{24,8},{1,17},{9,25},{17,1},{25,9},{2,18},{10... | collective-permute-start | bytes 1081352 | tf_op jit(solution)/shard_map/ppermute | solution.py:24
  20.9 1.4 %collective-permute-start.9 = (bf16[1,704,256]{2,1,0:T(8,128)(2,1)S(1)}, bf16[1,704,256]{2,1,0:T(8,128)(2,1)S(1)}, u32[]{:S(2)}, u32[]{:S(2)}) collective-permute-start(bf16[1,704,256]{2,1,0:T(8,128)(2,1)S(1)} %get-tuple-element.41), channel_id=1, source_target_pairs={{0,24},{8,16},{16,8},{24,0},{1,25},{9,17},{17,9},{25,1},{2,26},{10... | collective-permute-start | bytes 1081352 | tf_op jit(solution)/shard_map/ppermute | solution.py:24
  22.3 0.2 collective-permute-done.11.refs_6_
  22.4 7.6 %collective-permute-done.7.refs_1_ = bf16[1,704,256]{2,1,0:T(8,128)(2,1)S(1)} collective-permute-done((bf16[1,704,256]{2,1,0:T(8,128)(2,1)S(1)}, bf16[1,704,256]{2,1,0:T(8,128)(2,1)S(1)}, u32[]{:S(2)}, u32[]{:S(2)}) %collective-permute-start.7) | collective-permute-done | bytes 360480 | tf_op jit(solution)/shard_map/ppermute | solution.py:24
  30.0 6.8 %collective-permute-done.8.refs_2_ = bf16[1,704,256]{2,1,0:T(8,128)(2,1)S(1)} collective-permute-done((bf16[1,704,256]{2,1,0:T(8,128)(2,1)S(1)}, bf16[1,704,256]{2,1,0:T(8,128)(2,1)S(1)}, u32[]{:S(2)}, u32[]{:S(2)}) %collective-permute-start.8) | collective-permute-done | bytes 360480 | tf_op jit(solution)/shard_map/ppermute | solution.py:24
  36.8 1.2 %collective-permute-done.9.refs_3_ = bf16[1,704,256]{2,1,0:T(8,128)(2,1)S(1)} collective-permute-done((bf16[1,704,256]{2,1,0:T(8,128)(2,1)S(1)}, bf16[1,704,256]{2,1,0:T(8,128)(2,1)S(1)}, u32[]{:S(2)}, u32[]{:S(2)}) %collective-permute-start.9) | collective-permute-done | bytes 360480 | tf_op jit(solution)/shard_map/ppermute | solution.py:24
  38.0 0.8 %shard_map.70 = (bf16[1,352,256]{2,1,0:T(8,128)(2,1)S(1)}, bf16[2,4,32,1536]{3,2,1,0:T(8,128)(2,1)S(1)}) custom-call(s32[1]{0:T(128)} %bitcast.1.core, bf16[1,704,256]{2,1,0:T(8,128)(2,1)S(1)} %get-tuple-element.38.refs_0_, bf16[1,704,256]{2,1,0:T(8,128)(2,1)S(1)} %collective-permute-done.7.refs_1_, bf16[1,704,256]{2,1,0:T(8,128)(2,1)S(1)} %collective-permute-done.8.refs_2_, ...), custom_call_target="tpu_custom_call" | custom-call | flops 276824064 | bytes 2523136 | tf_op jit(solution)/shard_map/pallas_call | solution.py:32
  38.8 0.1 collective-permute-start.12
  38.9 1.8 %collective-permute-start.16 = (bf16[1,352,512]{2,1,0:T(8,128)(2,1)S(1)}, bf16[1,352,512]{2,1,0:T(8,128)(2,1)S(1)}, u32[]{:S(2)}, u32[]{:S(2)}) collective-permute-start(bf16[1,352,512]{2,1,0:T(8,128)(2,1)S(1)} %get-tuple-element.46), channel_id=1, source_target_pairs={{0,24},{8,16},{16,8},{24,0},{1,25},{9,17},{17,9},{25,1},{2,26},{10... | collective-permute-start | bytes 1081352 | tf_op jit(solution)/shard_map/ppermute | solution.py:24
  40.7 0.0 collective-permute-done.12
  40.7 0.1 fusion
  40.9 1.9 %collective-permute-start.15 = (bf16[32,1536]{1,0:T(8,128)(2,1)S(1)}, bf16[32,1536]{1,0:T(8,128)(2,1)S(1)}, u32[]{:S(2)}, u32[]{:S(2)}) collective-permute-start(bf16[32,1536]{1,0:T(8,128)(2,1)S(1)} %get-tuple-element.48), channel_id=1, source_target_pairs={{0,2},{1,3},{2,0},{3,1},{4,6},{5,7},{6,4},{7,5},{8,10},{9,11},{10,... | collective-permute-start | bytes 294920 | tf_op jit(solution)/shard_map/ppermute | solution.py:24
  42.7 2.6 %collective-permute-start.14 = (bf16[32,1536]{1,0:T(8,128)(2,1)S(1)}, bf16[32,1536]{1,0:T(8,128)(2,1)S(1)}, u32[]{:S(2)}, u32[]{:S(2)}) collective-permute-start(bf16[32,1536]{1,0:T(8,128)(2,1)S(1)} %get-tuple-element.49), channel_id=1, source_target_pairs={{0,4},{1,5},{2,6},{3,7},{4,0},{5,1},{6,2},{7,3},{8,12},{9,13},{10,... | collective-permute-start | bytes 294920 | tf_op jit(solution)/shard_map/ppermute | solution.py:24
  45.3 0.0 collective-permute-start.13
  45.3 5.3 %collective-permute-done.16.refs_0_ = bf16[1,352,512]{2,1,0:T(8,128)(2,1)S(1)} collective-permute-done((bf16[1,352,512]{2,1,0:T(8,128)(2,1)S(1)}, bf16[1,352,512]{2,1,0:T(8,128)(2,1)S(1)}, u32[]{:S(2)}, u32[]{:S(2)}) %collective-permute-start.16) | collective-permute-done | bytes 360480 | tf_op jit(solution)/shard_map/ppermute | solution.py:24
  50.6 2.8 %collective-permute-done.14.refs_2_.refs_1_ = bf16[32,1536]{1,0:T(8,128)(2,1)S(1)} collective-permute-done((bf16[32,1536]{1,0:T(8,128)(2,1)S(1)}, bf16[32,1536]{1,0:T(8,128)(2,1)S(1)}, u32[]{:S(2)}, u32[]{:S(2)}) %collective-permute-start.14) | collective-permute-done | bytes 98336 | tf_op jit(solution)/shard_map/ppermute | solution.py:24
  53.4 0.3 shard_map.71
  53.7 0.1 collective-permute-start.17
  53.8 1.3 %collective-permute-done.17 = bf16[4,32,512]{2,1,0:T(8,128)(2,1)S(1)} collective-permute-done((bf16[4,32,512]{2,1,0:T(8,128)(2,1)S(1)}, bf16[4,32,512]{2,1,0:T(8,128)(2,1)S(1)}, u32[]{:S(2)}, u32[]{:S(2)}) %collective-permute-start.17) | collective-permute-done | bytes 131104 | tf_op jit(solution)/shard_map/ppermute | solution.py:24
  55.2 1.8 %collective-permute-start.20 = (bf16[32,512]{1,0:T(8,128)(2,1)S(1)}, bf16[32,512]{1,0:T(8,128)(2,1)S(1)}, u32[]{:S(2)}, u32[]{:S(2)}) collective-permute-start(bf16[32,512]{1,0:T(8,128)(2,1)S(1)} %get-tuple-element.52), channel_id=1, source_target_pairs={{0,2},{1,3},{2,0},{3,1},{4,6},{5,7},{6,4},{7,5},{8,10},{9,11},{10,... | collective-permute-start | bytes 98312 | tf_op jit(solution)/shard_map/ppermute | solution.py:24
  57.0 1.4 %collective-permute-start.19 = (bf16[32,512]{1,0:T(8,128)(2,1)S(1)}, bf16[32,512]{1,0:T(8,128)(2,1)S(1)}, u32[]{:S(2)}, u32[]{:S(2)}) collective-permute-start(bf16[32,512]{1,0:T(8,128)(2,1)S(1)} %get-tuple-element.53), channel_id=1, source_target_pairs={{0,4},{1,5},{2,6},{3,7},{4,0},{5,1},{6,2},{7,3},{8,12},{9,13},{10,... | collective-permute-start | bytes 98312 | tf_op jit(solution)/shard_map/ppermute | solution.py:24
  58.5 1.2 %collective-permute-start.18 = (bf16[32,512]{1,0:T(8,128)(2,1)S(1)}, bf16[32,512]{1,0:T(8,128)(2,1)S(1)}, u32[]{:S(2)}, u32[]{:S(2)}) collective-permute-start(bf16[32,512]{1,0:T(8,128)(2,1)S(1)} %get-tuple-element.54), channel_id=1, source_target_pairs={{0,6},{1,7},{2,4},{3,5},{4,2},{5,3},{6,0},{7,1},{8,14},{9,15},{10,... | collective-permute-start | bytes 98312 | tf_op jit(solution)/shard_map/ppermute | solution.py:24
  59.7 2.8 %collective-permute-done.19.refs_5_ = bf16[32,512]{1,0:T(8,128)(2,1)S(1)} collective-permute-done((bf16[32,512]{1,0:T(8,128)(2,1)S(1)}, bf16[32,512]{1,0:T(8,128)(2,1)S(1)}, u32[]{:S(2)}, u32[]{:S(2)}) %collective-permute-start.19) | collective-permute-done | bytes 32800 | tf_op jit(solution)/shard_map/ppermute | solution.py:24
  62.4 1.7 %collective-permute-done.18.refs_4_ = bf16[32,512]{1,0:T(8,128)(2,1)S(1)} collective-permute-done((bf16[32,512]{1,0:T(8,128)(2,1)S(1)}, bf16[32,512]{1,0:T(8,128)(2,1)S(1)}, u32[]{:S(2)}, u32[]{:S(2)}) %collective-permute-start.18) | collective-permute-done | bytes 32800 | tf_op jit(solution)/shard_map/ppermute | solution.py:24
  64.2 0.7 %shard_map.72 = bf16[32,2048]{1,0:T(8,128)(2,1)} custom-call(s32[1]{0:T(128)} %bitcast.my_dp, bf16[32,1536]{1,0:T(8,128)(2,1)S(1)} %collective-permute-done.13.refs_1_.refs_0_, bf16[32,1536]{1,0:T(8,128)(2,1)S(1)} %collective-permute-done.14.refs_2_.refs_1_, bf16[32,1536]{1,0:T(8,128)(2,1)S(1)} %collective-permute-done.15.refs_3_.refs_2_, ...), custom_call_target="tpu_custom_call" | custom-call | flops 262144 | bytes 655360 | tf_op jit(solution)/shard_map/pallas_call | solution.py:32
  (15 shorter events, 0.2 us)
Async XLA Ops:
  0.0 12.0 %copy-start = (bf16[8,352,512]{2,1,0:T(8,128)(2,1)S(1)}, bf16[8,352,512]{2,1,0:T(8,128)(2,1)}, u32[]{:S(2)}) copy-start(bf16[8,352,512]{2,1,0:T(8,128)(2,1)} %refs_0_.1) | copy-start | bytes 8650756
  0.0 16.0 %copy-start.2 = (bf16[8,512,352]{1,2,0:T(8,128)(2,1)S(1)}, bf16[8,512,352]{1,2,0:T(8,128)(2,1)}, u32[]{:S(2)}) copy-start(bf16[8,512,352]{1,2,0:T(8,128)(2,1)} %param.8) | copy-start | bytes 8650756
  1.8 14.2 %copy-start.1 = (bf16[8,512,352]{1,2,0:T(8,128)(2,1)S(1)}, bf16[8,512,352]{1,2,0:T(8,128)(2,1)}, u32[]{:S(2)}) copy-start(bf16[8,512,352]{1,2,0:T(8,128)(2,1)} %param.7) | copy-start | bytes 8650756
  1.8 8.0 %collective-permute-start.1 = (bf16[80,512]{1,0:T(8,128)(2,1)S(1)}, bf16[80,512]{1,0:T(8,128)(2,1)S(1)}, u32[]{:S(2)}, u32[]{:S(2)}) collective-permute-start(bf16[80,512]{1,0:T(8,128)(2,1)S(1)} %get-tuple-element.28), channel_id=1, source_target_pairs={{0,16},{8,24},{16,0},{24,8},{1,17},{9,25},{17,1},{25,9},{2,18},{10... | collective-permute-start | bytes 245768 | tf_op jit(solution)/shard_map/ppermute | solution.py:24
  4.9 6.7 %collective-permute-start.2 = (bf16[80,512]{1,0:T(8,128)(2,1)S(1)}, bf16[80,512]{1,0:T(8,128)(2,1)S(1)}, u32[]{:S(2)}, u32[]{:S(2)}) collective-permute-start(bf16[80,512]{1,0:T(8,128)(2,1)S(1)} %get-tuple-element.29), channel_id=1, source_target_pairs={{0,24},{8,16},{16,8},{24,0},{1,25},{9,17},{17,9},{25,1},{2,26},{10... | collective-permute-start | bytes 245768 | tf_op jit(solution)/shard_map/ppermute | solution.py:24
  6.3 5.4 %collective-permute-start = (bf16[80,512]{1,0:T(8,128)(2,1)S(1)}, bf16[80,512]{1,0:T(8,128)(2,1)S(1)}, u32[]{:S(2)}, u32[]{:S(2)}) collective-permute-start(bf16[80,512]{1,0:T(8,128)(2,1)S(1)} %get-tuple-element.27.refs_0_), channel_id=1, source_target_pairs={{0,8},{8,0},{16,24},{24,16},{1,9},{9,1},{17,25},{25,17},{2,10},{10... | collective-permute-start | bytes 245768 | tf_op jit(solution)/shard_map/ppermute | solution.py:24
  6.4 9.5 %collective-permute-start.3 = (bf16[64,512]{1,0:T(8,128)(2,1)S(1)}, bf16[64,512]{1,0:T(8,128)(2,1)S(1)}, u32[]{:S(2)}, u32[]{:S(2)}) collective-permute-start(bf16[64,512]{1,0:T(8,128)(2,1)S(1)} %get-tuple-element.30), channel_id=1, source_target_pairs={{0,8},{8,0},{16,24},{24,16},{1,9},{9,1},{17,25},{25,17},{2,10},{10... | collective-permute-start | bytes 196616 | tf_op jit(solution)/shard_map/ppermute | solution.py:24
  8.3 7.5 %collective-permute-start.4 = (bf16[64,512]{1,0:T(8,128)(2,1)S(1)}, bf16[64,512]{1,0:T(8,128)(2,1)S(1)}, u32[]{:S(2)}, u32[]{:S(2)}) collective-permute-start(bf16[64,512]{1,0:T(8,128)(2,1)S(1)} %get-tuple-element.31), channel_id=1, source_target_pairs={{0,16},{8,24},{16,0},{24,8},{1,17},{9,25},{17,1},{25,9},{2,18},{10... | collective-permute-start | bytes 196616 | tf_op jit(solution)/shard_map/ppermute | solution.py:24
  9.9 6.0 %collective-permute-start.5 = (bf16[64,512]{1,0:T(8,128)(2,1)S(1)}, bf16[64,512]{1,0:T(8,128)(2,1)S(1)}, u32[]{:S(2)}, u32[]{:S(2)}) collective-permute-start(bf16[64,512]{1,0:T(8,128)(2,1)S(1)} %get-tuple-element.32), channel_id=1, source_target_pairs={{0,24},{8,16},{16,8},{24,0},{1,25},{9,17},{17,9},{25,1},{2,26},{10... | collective-permute-start | bytes 196616 | tf_op jit(solution)/shard_map/ppermute | solution.py:24
  12.6 9.6 %collective-permute-start.10 = (bf16[1,352,512]{2,1,0:T(8,128)(2,1)S(1)}, bf16[1,352,512]{2,1,0:T(8,128)(2,1)S(1)}, u32[]{:S(2)}, u32[]{:S(2)}) collective-permute-start(bf16[1,352,512]{2,1,0:T(8,128)(2,1)S(1)} %get-tuple-element.42), channel_id=1, source_target_pairs={{0,8},{8,0},{16,24},{24,16},{1,9},{9,1},{17,25},{25,17},{2,10},{10... | collective-permute-start | bytes 1081352 | tf_op jit(solution)/shard_map/ppermute | solution.py:24
  14.4 8.1 %collective-permute-start.11 = (bf16[1,352,512]{2,1,0:T(8,128)(2,1)S(1)}, bf16[1,352,512]{2,1,0:T(8,128)(2,1)S(1)}, u32[]{:S(2)}, u32[]{:S(2)}) collective-permute-start(bf16[1,352,512]{2,1,0:T(8,128)(2,1)S(1)} %get-tuple-element.43), channel_id=1, source_target_pairs={{0,16},{8,24},{16,0},{24,8},{1,17},{9,25},{17,1},{25,9},{2,18},{10... | collective-permute-start | bytes 1081352 | tf_op jit(solution)/shard_map/ppermute | solution.py:24
  15.9 1.8 %collective-permute-start.6 = (bf16[3,128,512]{2,1,0:T(8,128)(2,1)S(1)}, bf16[3,128,512]{2,1,0:T(8,128)(2,1)S(1)}, u32[]{:S(2)}, u32[]{:S(2)}) collective-permute-start(bf16[3,128,512]{2,1,0:T(8,128)(2,1)S(1)} %shard_map.67.brought), channel_id=1, source_target_pairs={{0,1},{1,0},{2,3},{3,2},{4,5},{5,4},{6,7},{7,6},{8,9},{9,8},{10,11... | collective-permute-start | bytes 1179656 | tf_op jit(solution)/shard_map/ppermute | solution.py:24
  18.7 11.3 %collective-permute-start.7 = (bf16[1,704,256]{2,1,0:T(8,128)(2,1)S(1)}, bf16[1,704,256]{2,1,0:T(8,128)(2,1)S(1)}, u32[]{:S(2)}, u32[]{:S(2)}) collective-permute-start(bf16[1,704,256]{2,1,0:T(8,128)(2,1)S(1)} %get-tuple-element.39), channel_id=1, source_target_pairs={{0,8},{8,0},{16,24},{24,16},{1,9},{9,1},{17,25},{25,17},{2,10},{10... | collective-permute-start | bytes 1081352 | tf_op jit(solution)/shard_map/ppermute | solution.py:24
  19.3 17.5 %collective-permute-start.8 = (bf16[1,704,256]{2,1,0:T(8,128)(2,1)S(1)}, bf16[1,704,256]{2,1,0:T(8,128)(2,1)S(1)}, u32[]{:S(2)}, u32[]{:S(2)}) collective-permute-start(bf16[1,704,256]{2,1,0:T(8,128)(2,1)S(1)} %get-tuple-element.40), channel_id=1, source_target_pairs={{0,16},{8,24},{16,0},{24,8},{1,17},{9,25},{17,1},{25,9},{2,18},{10... | collective-permute-start | bytes 1081352 | tf_op jit(solution)/shard_map/ppermute | solution.py:24
  20.9 17.1 %collective-permute-start.9 = (bf16[1,704,256]{2,1,0:T(8,128)(2,1)S(1)}, bf16[1,704,256]{2,1,0:T(8,128)(2,1)S(1)}, u32[]{:S(2)}, u32[]{:S(2)}) collective-permute-start(bf16[1,704,256]{2,1,0:T(8,128)(2,1)S(1)} %get-tuple-element.41), channel_id=1, source_target_pairs={{0,24},{8,16},{16,8},{24,0},{1,25},{9,17},{17,9},{25,1},{2,26},{10... | collective-permute-start | bytes 1081352 | tf_op jit(solution)/shard_map/ppermute | solution.py:24
  38.8 1.9 %collective-permute-start.12 = (bf16[4,32,1536]{2,1,0:T(8,128)(2,1)S(1)}, bf16[4,32,1536]{2,1,0:T(8,128)(2,1)S(1)}, u32[]{:S(2)}, u32[]{:S(2)}) collective-permute-start(bf16[4,32,1536]{2,1,0:T(8,128)(2,1)S(1)} %slice_bitcast_fusion), channel_id=1, source_target_pairs={{0,1},{1,0},{2,3},{3,2},{4,5},{5,4},{6,7},{7,6},{8,9},{9,8},{10,11... | collective-permute-start | bytes 1179656 | tf_op jit(solution)/shard_map/ppermute | solution.py:24
  38.9 11.7 %collective-permute-start.16 = (bf16[1,352,512]{2,1,0:T(8,128)(2,1)S(1)}, bf16[1,352,512]{2,1,0:T(8,128)(2,1)S(1)}, u32[]{:S(2)}, u32[]{:S(2)}) collective-permute-start(bf16[1,352,512]{2,1,0:T(8,128)(2,1)S(1)} %get-tuple-element.46), channel_id=1, source_target_pairs={{0,24},{8,16},{16,8},{24,0},{1,25},{9,17},{17,9},{25,1},{2,26},{10... | collective-permute-start | bytes 1081352 | tf_op jit(solution)/shard_map/ppermute | solution.py:24
  40.9 9.8 %collective-permute-start.15 = (bf16[32,1536]{1,0:T(8,128)(2,1)S(1)}, bf16[32,1536]{1,0:T(8,128)(2,1)S(1)}, u32[]{:S(2)}, u32[]{:S(2)}) collective-permute-start(bf16[32,1536]{1,0:T(8,128)(2,1)S(1)} %get-tuple-element.48), channel_id=1, source_target_pairs={{0,2},{1,3},{2,0},{3,1},{4,6},{5,7},{6,4},{7,5},{8,10},{9,11},{10,... | collective-permute-start | bytes 294920 | tf_op jit(solution)/shard_map/ppermute | solution.py:24
  42.7 10.7 %collective-permute-start.14 = (bf16[32,1536]{1,0:T(8,128)(2,1)S(1)}, bf16[32,1536]{1,0:T(8,128)(2,1)S(1)}, u32[]{:S(2)}, u32[]{:S(2)}) collective-permute-start(bf16[32,1536]{1,0:T(8,128)(2,1)S(1)} %get-tuple-element.49), channel_id=1, source_target_pairs={{0,4},{1,5},{2,6},{3,7},{4,0},{5,1},{6,2},{7,3},{8,12},{9,13},{10,... | collective-permute-start | bytes 294920 | tf_op jit(solution)/shard_map/ppermute | solution.py:24
  45.3 8.1 %collective-permute-start.13 = (bf16[32,1536]{1,0:T(8,128)(2,1)S(1)}, bf16[32,1536]{1,0:T(8,128)(2,1)S(1)}, u32[]{:S(2)}, u32[]{:S(2)}) collective-permute-start(bf16[32,1536]{1,0:T(8,128)(2,1)S(1)} %get-tuple-element.50), channel_id=1, source_target_pairs={{0,6},{1,7},{2,4},{3,5},{4,2},{5,3},{6,0},{7,1},{8,14},{9,15},{10,... | collective-permute-start | bytes 294920 | tf_op jit(solution)/shard_map/ppermute | solution.py:24
  53.7 1.4 %collective-permute-start.17 = (bf16[4,32,512]{2,1,0:T(8,128)(2,1)S(1)}, bf16[4,32,512]{2,1,0:T(8,128)(2,1)S(1)}, u32[]{:S(2)}, u32[]{:S(2)}) collective-permute-start(bf16[4,32,512]{2,1,0:T(8,128)(2,1)S(1)} %slice_bitcast_fusion.1), channel_id=1, source_target_pairs={{0,1},{1,0},{2,3},{3,2},{4,5},{5,4},{6,7},{7,6},{8,9},{9,8},{10,11... | collective-permute-start | bytes 393224 | tf_op jit(solution)/shard_map/ppermute | solution.py:24
  55.2 4.5 %collective-permute-start.20 = (bf16[32,512]{1,0:T(8,128)(2,1)S(1)}, bf16[32,512]{1,0:T(8,128)(2,1)S(1)}, u32[]{:S(2)}, u32[]{:S(2)}) collective-permute-start(bf16[32,512]{1,0:T(8,128)(2,1)S(1)} %get-tuple-element.52), channel_id=1, source_target_pairs={{0,2},{1,3},{2,0},{3,1},{4,6},{5,7},{6,4},{7,5},{8,10},{9,11},{10,... | collective-permute-start | bytes 98312 | tf_op jit(solution)/shard_map/ppermute | solution.py:24
  57.0 5.4 %collective-permute-start.19 = (bf16[32,512]{1,0:T(8,128)(2,1)S(1)}, bf16[32,512]{1,0:T(8,128)(2,1)S(1)}, u32[]{:S(2)}, u32[]{:S(2)}) collective-permute-start(bf16[32,512]{1,0:T(8,128)(2,1)S(1)} %get-tuple-element.53), channel_id=1, source_target_pairs={{0,4},{1,5},{2,6},{3,7},{4,0},{5,1},{6,2},{7,3},{8,12},{9,13},{10,... | collective-permute-start | bytes 98312 | tf_op jit(solution)/shard_map/ppermute | solution.py:24
  58.5 5.7 %collective-permute-start.18 = (bf16[32,512]{1,0:T(8,128)(2,1)S(1)}, bf16[32,512]{1,0:T(8,128)(2,1)S(1)}, u32[]{:S(2)}, u32[]{:S(2)}) collective-permute-start(bf16[32,512]{1,0:T(8,128)(2,1)S(1)} %get-tuple-element.54), channel_id=1, source_target_pairs={{0,6},{1,7},{2,4},{3,5},{4,2},{5,3},{6,0},{7,1},{8,14},{9,15},{10,... | collective-permute-start | bytes 98312 | tf_op jit(solution)/shard_map/ppermute | solution.py:24

commit v11 on v10

--- a/solution.py
+++ b/solution.py
@@ -246,23 +246,35 @@
     down_columns(core[0], kept, refs[:count], refs[-1])
 
 
-def finish_kernel(groups, lines, my_dp, *refs):
+def sum_kernel(*refs):
+    total = refs[0][...].astype(F32)
+    for piece in refs[1:-1]:
+        total += piece[...].astype(F32)
+    refs[-1][...] = total.astype(BF16)
+
+
+def copy_kernel(source, target):
+    target[...] = source[0]
+
+
+def finish_kernel(groups, my_dp, early, *refs):
     out = refs[-1]
-    for g, steps in enumerate(groups):
-        pieces = refs[g * lines : (g + 1) * lines]
-        cols = pieces[0].shape[1] // len(steps)
-        total = pieces[0][...].astype(F32)
-        for piece in pieces[1:]:
-            total += piece[...].astype(F32)
-        total = total.astype(BF16)
+    total = refs[0][...].astype(F32)
+    for piece in refs[1:-1]:
+        total += piece[...].astype(F32)
+    for value, steps in zip((early[...], total.astype(BF16)), groups):
+        cols = value.shape[1] // len(steps)
         for k, step in enumerate(steps):
             at = pl.multiple_of((my_dp[0] ^ step) * cols, cols)
-            out[:, pl.ds(at, cols)] = total[:, k * cols : (k + 1) * cols]
-
-
-def tensor_sum_pieces(mixed, lines):
+            out[:, pl.ds(at, cols)] = value[:, k * cols : (k + 1) * cols]
+
+
+def tensor_sum_pieces(mixed, lines, beside):
     my_line = lax.axis_index("tensor") // 2
-    pair = mixed[0].astype(F32) + swap(mixed[1], "tensor", 1).astype(F32)
+    mine = mixed[0]
+    if beside:
+        (mine,) = call(copy_kernel, [(mine.shape, BF16)], [VMEM], (mixed,), BESIDE, 0)
+    pair = mine.astype(F32) + swap(mixed[1], "tensor", 1).astype(F32)
     pair = pair.astype(BF16)
     pieces = [lax.dynamic_index_in_dim(pair, my_line ^ k, 0, keepdims=False) for k in range(lines)]
     return [swap(pieces[k], "tensor", 2 * k) for k in range(lines - 1, 0, -1)] + [pieces[0]]
@@ -336,21 +348,29 @@
         flops * len(early),
         2 * (own_rows * hidden_count * dp * 2 + hidden_count * cols * len(early)),
     )
-    early_pieces = tensor_sum_pieces(mixed, lines)
+    early_pieces = tensor_sum_pieces(mixed, lines, False)
     (mixed,) = call(
         functools.partial(second_kernel, len(late)),
         [((2, lines, rows, len(late) * cols), BF16)],
-        [SMEM] + [VMEM] * (1 + len(late)) + [ANY] * lines,
-        (core, hidden, *[downs[k] for k in late], *early_pieces),
+        [SMEM] + [VMEM] * (1 + len(late)) + [ANY],
+        (core, hidden, *[downs[k] for k in late], early_pieces[0]),
         flops * len(late),
         2 * (own_rows * hidden_count + hidden_count * cols * len(late)),
     )
-    late_pieces = tensor_sum_pieces(mixed, lines)
+    late_pieces = tensor_sum_pieces(mixed, lines, True)
+    (early_sum,) = call(
+        sum_kernel,
+        [(early_pieces[0].shape, BF16)],
+        [VMEM] * lines,
+        early_pieces,
+        BESIDE,
+        2 * rows * width * lines,
+    )
     (out,) = call(
-        functools.partial(finish_kernel, (early, late), lines),
+        functools.partial(finish_kernel, (early, late)),
         [((rows, width), BF16)],
-        [SMEM] + [VMEM] * (2 * lines),
-        (my_dp, *early_pieces, *late_pieces),
+        [SMEM] + [VMEM] * (1 + lines),
+        (my_dp, early_sum, *late_pieces),
         rows * width * lines,
         2 * rows * width * (lines + 1),
     )

time: 65 us -> 63.5 us (0.977)
  waiting for transfers between devices: 30.5 us -> 28.8 us
    ppermute x21, waiting for transfers between devices: 30.5 us -> 28.8 us  [swap(): return lax.ppermute(value, axis, [(i, i ^ step) for i in range(count)])]
    pallas_call x9 -> x11, Pallas kernels: 6.46 us -> 6.48 us  [call(): pl.pallas_call(kernel, out_shape=[jax.ShapeDtypeStruct(shape, dtype) for...]
  transfers between devices with their start and end apart: 21 -> 21, of which waited for: 11 -> 10; matrix products, arithmetic and copies ran while one was open for 0% -> 0% of each run, Pallas kernels for 4% -> 5%
where the time goes in v11:
time: 63.5 us; the launch traced here: 63.3 us
  waiting for transfers between devices  28.8 us (45%)
  starting transfers between devices  27.6 us (43%)
  Pallas kernels  6.48 us (10%)
    ppermute x21, waiting for transfers between devices, swap(): return lax.ppermute(value, axis, [(i, i ^ step) for i in range(count)])  28.8 us
    ppermute x21, starting transfers between devices, swap(): return lax.ppermute(value, axis, [(i, i ^ step) for i in range(count)])  27.6 us
    pallas_call x11, Pallas kernels, call(): pl.pallas_call(kernel, out_shape=[jax.ShapeDtypeStruct(shape, dtype) for...  6.48 us
  transfers between devices with their start and end apart: 21, of which 10 were waited for; matrix products, arithmetic and copies ran while one was open for 0% of the time, Pallas kernels for 5%

profile of v11, /device:TPU:0, one launch (start us, length us, event | category | flops | bytes accessed | tf_op | source)
XLA Modules:
  0.0 63.3 jit_solution(14459443937299773894)
XLA Ops:
  0.0 1.8 %shard_map.64 = (bf16[256,512]{1,0:T(8,128)(2,1)S(1)}, bf16[80,512]{1,0:T(8,128)(2,1)S(1)}, bf16[80,512]{1,0:T(8,128)(2,1)S(1)}, bf16[80,512]{1,0:T(8,128)(2,1)S...) custom-call(s32[1]{0:T(128)} %bitcast.my_dp, s32[1]{0:T(128)} %bitcast.1.core, ...), custom_call_target="tpu_custom_call" | custom-call | flops 10000000000 | bytes 2097152 | tf_op jit(solution)/shard_map/pallas_call | solution.py:32
  1.8 0.0 copy-start.1
  1.8 3.0 %collective-permute-start.1 = (bf16[80,512]{1,0:T(8,128)(2,1)S(1)}, bf16[80,512]{1,0:T(8,128)(2,1)S(1)}, u32[]{:S(2)}, u32[]{:S(2)}) collective-permute-start(bf16[80,512]{1,0:T(8,128)(2,1)S(1)} %get-tuple-element.28), channel_id=1, source_target_pairs={{0,16},{8,24},{16,0},{24,8},{1,17},{9,25},{17,1},{25,9},{2,18},{10... | collective-permute-start | bytes 245768 | tf_op jit(solution)/shard_map/ppermute | solution.py:24
  4.9 1.4 %collective-permute-start.2 = (bf16[80,512]{1,0:T(8,128)(2,1)S(1)}, bf16[80,512]{1,0:T(8,128)(2,1)S(1)}, u32[]{:S(2)}, u32[]{:S(2)}) collective-permute-start(bf16[80,512]{1,0:T(8,128)(2,1)S(1)} %get-tuple-element.29), channel_id=1, source_target_pairs={{0,24},{8,16},{16,8},{24,0},{1,25},{9,17},{17,9},{25,1},{2,26},{10... | collective-permute-start | bytes 245768 | tf_op jit(solution)/shard_map/ppermute | solution.py:24
  6.3 0.1 collective-permute-start
  6.4 1.9 %collective-permute-start.3 = (bf16[64,512]{1,0:T(8,128)(2,1)S(1)}, bf16[64,512]{1,0:T(8,128)(2,1)S(1)}, u32[]{:S(2)}, u32[]{:S(2)}) collective-permute-start(bf16[64,512]{1,0:T(8,128)(2,1)S(1)} %get-tuple-element.30), channel_id=1, source_target_pairs={{0,8},{8,0},{16,24},{24,16},{1,9},{9,1},{17,25},{25,17},{2,10},{10... | collective-permute-start | bytes 196616 | tf_op jit(solution)/shard_map/ppermute | solution.py:24
  8.3 1.5 %collective-permute-start.4 = (bf16[64,512]{1,0:T(8,128)(2,1)S(1)}, bf16[64,512]{1,0:T(8,128)(2,1)S(1)}, u32[]{:S(2)}, u32[]{:S(2)}) collective-permute-start(bf16[64,512]{1,0:T(8,128)(2,1)S(1)} %get-tuple-element.31), channel_id=1, source_target_pairs={{0,16},{8,24},{16,0},{24,8},{1,17},{9,25},{17,1},{25,9},{2,18},{10... | collective-permute-start | bytes 196616 | tf_op jit(solution)/shard_map/ppermute | solution.py:24
  9.9 0.0 collective-permute-done.1.refs_2_.refs_1_
  9.9 1.7 %collective-permute-start.5 = (bf16[64,512]{1,0:T(8,128)(2,1)S(1)}, bf16[64,512]{1,0:T(8,128)(2,1)S(1)}, u32[]{:S(2)}, u32[]{:S(2)}) collective-permute-start(bf16[64,512]{1,0:T(8,128)(2,1)S(1)} %get-tuple-element.32), channel_id=1, source_target_pairs={{0,24},{8,16},{16,8},{24,0},{1,25},{9,17},{17,9},{25,1},{2,26},{10... | collective-permute-start | bytes 196616 | tf_op jit(solution)/shard_map/ppermute | solution.py:24
  11.5 0.0 collective-permute-done.2.refs_3_.refs_2_
  11.5 0.2 collective-permute-done.refs_1_.refs_0_
  11.7 0.3 shard_map.65.mix_ref
  12.1 0.5 shard_map.66
  12.6 1.7 %collective-permute-start.10 = (bf16[1,352,512]{2,1,0:T(8,128)(2,1)S(1)}, bf16[1,352,512]{2,1,0:T(8,128)(2,1)S(1)}, u32[]{:S(2)}, u32[]{:S(2)}) collective-permute-start(bf16[1,352,512]{2,1,0:T(8,128)(2,1)S(1)} %get-tuple-element.42), channel_id=1, source_target_pairs={{0,8},{8,0},{16,24},{24,16},{1,9},{9,1},{17,25},{25,17},{2,10},{10... | collective-permute-start | bytes 1081352 | tf_op jit(solution)/shard_map/ppermute | solution.py:24
  14.4 1.5 %collective-permute-start.11 = (bf16[1,352,512]{2,1,0:T(8,128)(2,1)S(1)}, bf16[1,352,512]{2,1,0:T(8,128)(2,1)S(1)}, u32[]{:S(2)}, u32[]{:S(2)}) collective-permute-start(bf16[1,352,512]{2,1,0:T(8,128)(2,1)S(1)} %get-tuple-element.43), channel_id=1, source_target_pairs={{0,16},{8,24},{16,0},{24,8},{1,17},{9,25},{17,1},{25,9},{2,18},{10... | collective-permute-start | bytes 1081352 | tf_op jit(solution)/shard_map/ppermute | solution.py:24
  15.9 0.0 collective-permute-done.4.refs_4_
  15.9 0.0 collective-permute-done.5.refs_5_
  15.9 0.1 collective-permute-start.6
  16.0 0.9 %shard_map.68 = (bf16[1,704,512]{2,1,0:T(8,128)(2,1)S(1)}, bf16[1,704,512]{2,1,0:T(8,128)(2,1)S(1)}, bf16[1,704,512]{2,1,0:T(8,128)(2,1)S(1)}, bf16[1,704,512]{2,1,0:T(8,128)(2,1)S(1)}) custom-call(bf16[128,256]{1,0:T(8,128)(2,1)S(1)} %shard_map.65.mix_ref, bf16[8,352,512]{2,1,0:T(8,128)(2,1)S(1)} %bitcast.29, bf16[8,352,512]{2,1,0:T(8,128)(2,1)S(1)} %bitcast.30), custom_call_target="tpu_custom_call" | custom-call | flops 10000000000 | bytes 8650752 | tf_op jit(solution)/shard_map/pallas_call | solution.py:32
  16.9 0.8 %collective-permute-done.6.other = bf16[3,128,512]{2,1,0:T(8,128)(2,1)S(1)} collective-permute-done((bf16[3,128,512]{2,1,0:T(8,128)(2,1)S(1)}, bf16[3,128,512]{2,1,0:T(8,128)(2,1)S(1)}, u32[]{:S(2)}, u32[]{:S(2)}) %collective-permute-start.6) | collective-permute-done | bytes 393248 | tf_op jit(solution)/shard_map/ppermute | solution.py:24
  17.7 1.0 %shard_map.69 = (bf16[1,704,256]{2,1,0:T(8,128)(2,1)S(1)}, bf16[1,704,256]{2,1,0:T(8,128)(2,1)S(1)}, bf16[1,704,256]{2,1,0:T(8,128)(2,1)S(1)}, bf16[1,704,256]{2,1,0:T(8,128)(2,1)S(1)}) custom-call(s32[1]{0:T(128)} %bitcast.1.core, bf16[256,512]{1,0:T(8,128)(2,1)S(1)} %get-tuple-element.26.own, bf16[3,128,512]{2,1,0:T(8,128)(2,1)S(1)} %shard_map.67.brought, ...), custom_call_target="tpu_custom_call" | custom-call | flops 738197504 | bytes 5373952 | tf_op jit(solution)/shard_map/pallas_call | solution.py:32
  18.7 0.6 collective-permute-start.7
  19.3 1.6 %collective-permute-start.8 = (bf16[1,704,256]{2,1,0:T(8,128)(2,1)S(1)}, bf16[1,704,256]{2,1,0:T(8,128)(2,1)S(1)}, u32[]{:S(2)}, u32[]{:S(2)}) collective-permute-start(bf16[1,704,256]{2,1,0:T(8,128)(2,1)S(1)} %get-tuple-element.40), channel_id=1, source_target_pairs={{0,16},{8,24},{16,0},{24,8},{1,17},{9,25},{17,1},{25,9},{2,18},{10... | collective-permute-start | bytes 1081352 | tf_op jit(solution)/shard_map/ppermute | solution.py:24
  20.9 1.4 %collective-permute-start.9 = (bf16[1,704,256]{2,1,0:T(8,128)(2,1)S(1)}, bf16[1,704,256]{2,1,0:T(8,128)(2,1)S(1)}, u32[]{:S(2)}, u32[]{:S(2)}) collective-permute-start(bf16[1,704,256]{2,1,0:T(8,128)(2,1)S(1)} %get-tuple-element.41), channel_id=1, source_target_pairs={{0,24},{8,16},{16,8},{24,0},{1,25},{9,17},{17,9},{25,1},{2,26},{10... | collective-permute-start | bytes 1081352 | tf_op jit(solution)/shard_map/ppermute | solution.py:24
  22.2 0.0 collective-permute-done.10.refs_5_
  22.3 0.2 collective-permute-done.11.refs_6_
  22.4 7.6 %collective-permute-done.7.refs_1_ = bf16[1,704,256]{2,1,0:T(8,128)(2,1)S(1)} collective-permute-done((bf16[1,704,256]{2,1,0:T(8,128)(2,1)S(1)}, bf16[1,704,256]{2,1,0:T(8,128)(2,1)S(1)}, u32[]{:S(2)}, u32[]{:S(2)}) %collective-permute-start.7) | collective-permute-done | bytes 360480 | tf_op jit(solution)/shard_map/ppermute | solution.py:24
  30.0 6.8 %collective-permute-done.8.refs_2_ = bf16[1,704,256]{2,1,0:T(8,128)(2,1)S(1)} collective-permute-done((bf16[1,704,256]{2,1,0:T(8,128)(2,1)S(1)}, bf16[1,704,256]{2,1,0:T(8,128)(2,1)S(1)}, u32[]{:S(2)}, u32[]{:S(2)}) %collective-permute-start.8) | collective-permute-done | bytes 360480 | tf_op jit(solution)/shard_map/ppermute | solution.py:24
  36.8 1.2 %collective-permute-done.9.refs_3_ = bf16[1,704,256]{2,1,0:T(8,128)(2,1)S(1)} collective-permute-done((bf16[1,704,256]{2,1,0:T(8,128)(2,1)S(1)}, bf16[1,704,256]{2,1,0:T(8,128)(2,1)S(1)}, u32[]{:S(2)}, u32[]{:S(2)}) %collective-permute-start.9) | collective-permute-done | bytes 360480 | tf_op jit(solution)/shard_map/ppermute | solution.py:24
  38.0 0.8 %shard_map.70 = (bf16[1,352,256]{2,1,0:T(8,128)(2,1)S(1)}, bf16[2,4,32,1536]{3,2,1,0:T(8,128)(2,1)S(1)}) custom-call(s32[1]{0:T(128)} %bitcast.1.core, bf16[1,704,256]{2,1,0:T(8,128)(2,1)S(1)} %get-tuple-element.38.refs_0_, bf16[1,704,256]{2,1,0:T(8,128)(2,1)S(1)} %collective-permute-done.7.refs_1_, bf16[1,704,256]{2,1,0:T(8,128)(2,1)S(1)} %collective-permute-done.8.refs_2_, ...), custom_call_target="tpu_custom_call" | custom-call | flops 276824064 | bytes 2523136 | tf_op jit(solution)/shard_map/pallas_call | solution.py:32
  38.8 0.1 collective-permute-start.12
  38.9 1.8 %collective-permute-start.16 = (bf16[1,352,512]{2,1,0:T(8,128)(2,1)S(1)}, bf16[1,352,512]{2,1,0:T(8,128)(2,1)S(1)}, u32[]{:S(2)}, u32[]{:S(2)}) collective-permute-start(bf16[1,352,512]{2,1,0:T(8,128)(2,1)S(1)} %get-tuple-element.46), channel_id=1, source_target_pairs={{0,24},{8,16},{16,8},{24,0},{1,25},{9,17},{17,9},{25,1},{2,26},{10... | collective-permute-start | bytes 1081352 | tf_op jit(solution)/shard_map/ppermute | solution.py:24
  40.7 0.0 collective-permute-done.12
  40.7 0.1 fusion
  40.9 3.9 %collective-permute-start.13 = (bf16[32,1536]{1,0:T(8,128)(2,1)S(1)}, bf16[32,1536]{1,0:T(8,128)(2,1)S(1)}, u32[]{:S(2)}, u32[]{:S(2)}) collective-permute-start(bf16[32,1536]{1,0:T(8,128)(2,1)S(1)} %get-tuple-element.50), channel_id=1, source_target_pairs={{0,6},{1,7},{2,4},{3,5},{4,2},{5,3},{6,0},{7,1},{8,14},{9,15},{10,... | collective-permute-start | bytes 294920 | tf_op jit(solution)/shard_map/ppermute | solution.py:24
  44.8 0.0 collective-permute-start.15
  44.8 0.6 %collective-permute-start.14 = (bf16[32,1536]{1,0:T(8,128)(2,1)S(1)}, bf16[32,1536]{1,0:T(8,128)(2,1)S(1)}, u32[]{:S(2)}, u32[]{:S(2)}) collective-permute-start(bf16[32,1536]{1,0:T(8,128)(2,1)S(1)} %get-tuple-element.49), channel_id=1, source_target_pairs={{0,4},{1,5},{2,6},{3,7},{4,0},{5,1},{6,2},{7,3},{8,12},{9,13},{10,... | collective-permute-start | bytes 294920 | tf_op jit(solution)/shard_map/ppermute | solution.py:24
  45.4 5.2 %collective-permute-done.16.refs_0_ = bf16[1,352,512]{2,1,0:T(8,128)(2,1)S(1)} collective-permute-done((bf16[1,352,512]{2,1,0:T(8,128)(2,1)S(1)}, bf16[1,352,512]{2,1,0:T(8,128)(2,1)S(1)}, u32[]{:S(2)}, u32[]{:S(2)}) %collective-permute-start.16) | collective-permute-done | bytes 360480 | tf_op jit(solution)/shard_map/ppermute | solution.py:24
  50.6 0.0 collective-permute-done.13.refs_0_.refs_1_
  50.6 0.3 shard_map.72.source
  51.0 0.1 collective-permute-start.17
  51.1 1.3 %collective-permute-done.17 = bf16[4,32,512]{2,1,0:T(8,128)(2,1)S(1)} collective-permute-done((bf16[4,32,512]{2,1,0:T(8,128)(2,1)S(1)}, bf16[4,32,512]{2,1,0:T(8,128)(2,1)S(1)}, u32[]{:S(2)}, u32[]{:S(2)}) %collective-permute-start.17) | collective-permute-done | bytes 131104 | tf_op jit(solution)/shard_map/ppermute | solution.py:24
  52.4 1.9 %collective-permute-start.20 = (bf16[32,512]{1,0:T(8,128)(2,1)S(1)}, bf16[32,512]{1,0:T(8,128)(2,1)S(1)}, u32[]{:S(2)}, u32[]{:S(2)}) collective-permute-start(bf16[32,512]{1,0:T(8,128)(2,1)S(1)} %get-tuple-element.52), channel_id=1, source_target_pairs={{0,2},{1,3},{2,0},{3,1},{4,6},{5,7},{6,4},{7,5},{8,10},{9,11},{10,... | collective-permute-start | bytes 98312 | tf_op jit(solution)/shard_map/ppermute | solution.py:24
  54.3 2.6 %collective-permute-start.19 = (bf16[32,512]{1,0:T(8,128)(2,1)S(1)}, bf16[32,512]{1,0:T(8,128)(2,1)S(1)}, u32[]{:S(2)}, u32[]{:S(2)}) collective-permute-start(bf16[32,512]{1,0:T(8,128)(2,1)S(1)} %get-tuple-element.53), channel_id=1, source_target_pairs={{0,4},{1,5},{2,6},{3,7},{4,0},{5,1},{6,2},{7,3},{8,12},{9,13},{10,... | collective-permute-start | bytes 98312 | tf_op jit(solution)/shard_map/ppermute | solution.py:24
  56.9 0.1 shard_map.71.early
  57.0 2.7 %collective-permute-done.19.refs_1_ = bf16[32,512]{1,0:T(8,128)(2,1)S(1)} collective-permute-done((bf16[32,512]{1,0:T(8,128)(2,1)S(1)}, bf16[32,512]{1,0:T(8,128)(2,1)S(1)}, u32[]{:S(2)}, u32[]{:S(2)}) %collective-permute-start.19) | collective-permute-done | bytes 32800 | tf_op jit(solution)/shard_map/ppermute | solution.py:24
  59.7 2.9 %collective-permute-done.18.refs_0_ = bf16[32,512]{1,0:T(8,128)(2,1)S(1)} collective-permute-done((bf16[32,512]{1,0:T(8,128)(2,1)S(1)}, bf16[32,512]{1,0:T(8,128)(2,1)S(1)}, u32[]{:S(2)}, u32[]{:S(2)}) %collective-permute-start.18) | collective-permute-done | bytes 32800 | tf_op jit(solution)/shard_map/ppermute | solution.py:24
  62.6 0.7 %shard_map.74 = bf16[32,2048]{1,0:T(8,128)(2,1)} custom-call(s32[1]{0:T(128)} %bitcast.my_dp, bf16[32,1536]{1,0:T(8,128)(2,1)S(1)} %shard_map.71.early, bf16[32,512]{1,0:T(8,128)(2,1)S(1)} %collective-permute-done.18.refs_0_, bf16[32,512]{1,0:T(8,128)(2,1)S(1)} %collective-permute-done.19.refs_1_, bf16[32,512]{1,0:T(8,128)(2,1)S(1)} %collective-permute-done.20.refs_2_, ...), custom_call_target="tpu_custom_call" | custom-call | flops 262144 | bytes 655360 | tf_op jit(solution)/shard_map/pallas_call | solution.py:32
  (17 shorter events, 0.2 us)
Async XLA Ops:
  0.0 12.0 %copy-start = (bf16[8,352,512]{2,1,0:T(8,128)(2,1)S(1)}, bf16[8,352,512]{2,1,0:T(8,128)(2,1)}, u32[]{:S(2)}) copy-start(bf16[8,352,512]{2,1,0:T(8,128)(2,1)} %refs_0_.1) | copy-start | bytes 8650756
  0.0 16.0 %copy-start.2 = (bf16[8,512,352]{1,2,0:T(8,128)(2,1)S(1)}, bf16[8,512,352]{1,2,0:T(8,128)(2,1)}, u32[]{:S(2)}) copy-start(bf16[8,512,352]{1,2,0:T(8,128)(2,1)} %param.8) | copy-start | bytes 8650756
  1.8 14.2 %copy-start.1 = (bf16[8,512,352]{1,2,0:T(8,128)(2,1)S(1)}, bf16[8,512,352]{1,2,0:T(8,128)(2,1)}, u32[]{:S(2)}) copy-start(bf16[8,512,352]{1,2,0:T(8,128)(2,1)} %param.7) | copy-start | bytes 8650756
  1.8 8.0 %collective-permute-start.1 = (bf16[80,512]{1,0:T(8,128)(2,1)S(1)}, bf16[80,512]{1,0:T(8,128)(2,1)S(1)}, u32[]{:S(2)}, u32[]{:S(2)}) collective-permute-start(bf16[80,512]{1,0:T(8,128)(2,1)S(1)} %get-tuple-element.28), channel_id=1, source_target_pairs={{0,16},{8,24},{16,0},{24,8},{1,17},{9,25},{17,1},{25,9},{2,18},{10... | collective-permute-start | bytes 245768 | tf_op jit(solution)/shard_map/ppermute | solution.py:24
  4.9 6.7 %collective-permute-start.2 = (bf16[80,512]{1,0:T(8,128)(2,1)S(1)}, bf16[80,512]{1,0:T(8,128)(2,1)S(1)}, u32[]{:S(2)}, u32[]{:S(2)}) collective-permute-start(bf16[80,512]{1,0:T(8,128)(2,1)S(1)} %get-tuple-element.29), channel_id=1, source_target_pairs={{0,24},{8,16},{16,8},{24,0},{1,25},{9,17},{17,9},{25,1},{2,26},{10... | collective-permute-start | bytes 245768 | tf_op jit(solution)/shard_map/ppermute | solution.py:24
  6.3 5.4 %collective-permute-start = (bf16[80,512]{1,0:T(8,128)(2,1)S(1)}, bf16[80,512]{1,0:T(8,128)(2,1)S(1)}, u32[]{:S(2)}, u32[]{:S(2)}) collective-permute-start(bf16[80,512]{1,0:T(8,128)(2,1)S(1)} %get-tuple-element.27.refs_0_), channel_id=1, source_target_pairs={{0,8},{8,0},{16,24},{24,16},{1,9},{9,1},{17,25},{25,17},{2,10},{10... | collective-permute-start | bytes 245768 | tf_op jit(solution)/shard_map/ppermute | solution.py:24
  6.4 9.5 %collective-permute-start.3 = (bf16[64,512]{1,0:T(8,128)(2,1)S(1)}, bf16[64,512]{1,0:T(8,128)(2,1)S(1)}, u32[]{:S(2)}, u32[]{:S(2)}) collective-permute-start(bf16[64,512]{1,0:T(8,128)(2,1)S(1)} %get-tuple-element.30), channel_id=1, source_target_pairs={{0,8},{8,0},{16,24},{24,16},{1,9},{9,1},{17,25},{25,17},{2,10},{10... | collective-permute-start | bytes 196616 | tf_op jit(solution)/shard_map/ppermute | solution.py:24
  8.3 7.5 %collective-permute-start.4 = (bf16[64,512]{1,0:T(8,128)(2,1)S(1)}, bf16[64,512]{1,0:T(8,128)(2,1)S(1)}, u32[]{:S(2)}, u32[]{:S(2)}) collective-permute-start(bf16[64,512]{1,0:T(8,128)(2,1)S(1)} %get-tuple-element.31), channel_id=1, source_target_pairs={{0,16},{8,24},{16,0},{24,8},{1,17},{9,25},{17,1},{25,9},{2,18},{10... | collective-permute-start | bytes 196616 | tf_op jit(solution)/shard_map/ppermute | solution.py:24
  9.9 6.0 %collective-permute-start.5 = (bf16[64,512]{1,0:T(8,128)(2,1)S(1)}, bf16[64,512]{1,0:T(8,128)(2,1)S(1)}, u32[]{:S(2)}, u32[]{:S(2)}) collective-permute-start(bf16[64,512]{1,0:T(8,128)(2,1)S(1)} %get-tuple-element.32), channel_id=1, source_target_pairs={{0,24},{8,16},{16,8},{24,0},{1,25},{9,17},{17,9},{25,1},{2,26},{10... | collective-permute-start | bytes 196616 | tf_op jit(solution)/shard_map/ppermute | solution.py:24
  12.6 9.6 %collective-permute-start.10 = (bf16[1,352,512]{2,1,0:T(8,128)(2,1)S(1)}, bf16[1,352,512]{2,1,0:T(8,128)(2,1)S(1)}, u32[]{:S(2)}, u32[]{:S(2)}) collective-permute-start(bf16[1,352,512]{2,1,0:T(8,128)(2,1)S(1)} %get-tuple-element.42), channel_id=1, source_target_pairs={{0,8},{8,0},{16,24},{24,16},{1,9},{9,1},{17,25},{25,17},{2,10},{10... | collective-permute-start | bytes 1081352 | tf_op jit(solution)/shard_map/ppermute | solution.py:24
  14.4 8.1 %collective-permute-start.11 = (bf16[1,352,512]{2,1,0:T(8,128)(2,1)S(1)}, bf16[1,352,512]{2,1,0:T(8,128)(2,1)S(1)}, u32[]{:S(2)}, u32[]{:S(2)}) collective-permute-start(bf16[1,352,512]{2,1,0:T(8,128)(2,1)S(1)} %get-tuple-element.43), channel_id=1, source_target_pairs={{0,16},{8,24},{16,0},{24,8},{1,17},{9,25},{17,1},{25,9},{2,18},{10... | collective-permute-start | bytes 1081352 | tf_op jit(solution)/shard_map/ppermute | solution.py:24
  15.9 1.8 %collective-permute-start.6 = (bf16[3,128,512]{2,1,0:T(8,128)(2,1)S(1)}, bf16[3,128,512]{2,1,0:T(8,128)(2,1)S(1)}, u32[]{:S(2)}, u32[]{:S(2)}) collective-permute-start(bf16[3,128,512]{2,1,0:T(8,128)(2,1)S(1)} %shard_map.67.brought), channel_id=1, source_target_pairs={{0,1},{1,0},{2,3},{3,2},{4,5},{5,4},{6,7},{7,6},{8,9},{9,8},{10,11... | collective-permute-start | bytes 1179656 | tf_op jit(solution)/shard_map/ppermute | solution.py:24
  18.7 11.3 %collective-permute-start.7 = (bf16[1,704,256]{2,1,0:T(8,128)(2,1)S(1)}, bf16[1,704,256]{2,1,0:T(8,128)(2,1)S(1)}, u32[]{:S(2)}, u32[]{:S(2)}) collective-permute-start(bf16[1,704,256]{2,1,0:T(8,128)(2,1)S(1)} %get-tuple-element.39), channel_id=1, source_target_pairs={{0,8},{8,0},{16,24},{24,16},{1,9},{9,1},{17,25},{25,17},{2,10},{10... | collective-permute-start | bytes 1081352 | tf_op jit(solution)/shard_map/ppermute | solution.py:24
  19.3 17.5 %collective-permute-start.8 = (bf16[1,704,256]{2,1,0:T(8,128)(2,1)S(1)}, bf16[1,704,256]{2,1,0:T(8,128)(2,1)S(1)}, u32[]{:S(2)}, u32[]{:S(2)}) collective-permute-start(bf16[1,704,256]{2,1,0:T(8,128)(2,1)S(1)} %get-tuple-element.40), channel_id=1, source_target_pairs={{0,16},{8,24},{16,0},{24,8},{1,17},{9,25},{17,1},{25,9},{2,18},{10... | collective-permute-start | bytes 1081352 | tf_op jit(solution)/shard_map/ppermute | solution.py:24
  20.9 17.1 %collective-permute-start.9 = (bf16[1,704,256]{2,1,0:T(8,128)(2,1)S(1)}, bf16[1,704,256]{2,1,0:T(8,128)(2,1)S(1)}, u32[]{:S(2)}, u32[]{:S(2)}) collective-permute-start(bf16[1,704,256]{2,1,0:T(8,128)(2,1)S(1)} %get-tuple-element.41), channel_id=1, source_target_pairs={{0,24},{8,16},{16,8},{24,0},{1,25},{9,17},{17,9},{25,1},{2,26},{10... | collective-permute-start | bytes 1081352 | tf_op jit(solution)/shard_map/ppermute | solution.py:24
  38.8 1.9 %collective-permute-start.12 = (bf16[4,32,1536]{2,1,0:T(8,128)(2,1)S(1)}, bf16[4,32,1536]{2,1,0:T(8,128)(2,1)S(1)}, u32[]{:S(2)}, u32[]{:S(2)}) collective-permute-start(bf16[4,32,1536]{2,1,0:T(8,128)(2,1)S(1)} %slice_bitcast_fusion), channel_id=1, source_target_pairs={{0,1},{1,0},{2,3},{3,2},{4,5},{5,4},{6,7},{7,6},{8,9},{9,8},{10,11... | collective-permute-start | bytes 1179656 | tf_op jit(solution)/shard_map/ppermute | solution.py:24
  38.9 11.7 %collective-permute-start.16 = (bf16[1,352,512]{2,1,0:T(8,128)(2,1)S(1)}, bf16[1,352,512]{2,1,0:T(8,128)(2,1)S(1)}, u32[]{:S(2)}, u32[]{:S(2)}) collective-permute-start(bf16[1,352,512]{2,1,0:T(8,128)(2,1)S(1)} %get-tuple-element.46), channel_id=1, source_target_pairs={{0,24},{8,16},{16,8},{24,0},{1,25},{9,17},{17,9},{25,1},{2,26},{10... | collective-permute-start | bytes 1081352 | tf_op jit(solution)/shard_map/ppermute | solution.py:24
  40.9 9.8 %collective-permute-start.13 = (bf16[32,1536]{1,0:T(8,128)(2,1)S(1)}, bf16[32,1536]{1,0:T(8,128)(2,1)S(1)}, u32[]{:S(2)}, u32[]{:S(2)}) collective-permute-start(bf16[32,1536]{1,0:T(8,128)(2,1)S(1)} %get-tuple-element.50), channel_id=1, source_target_pairs={{0,6},{1,7},{2,4},{3,5},{4,2},{5,3},{6,0},{7,1},{8,14},{9,15},{10,... | collective-permute-start | bytes 294920 | tf_op jit(solution)/shard_map/ppermute | solution.py:24
  44.8 12.2 %collective-permute-start.15 = (bf16[32,1536]{1,0:T(8,128)(2,1)S(1)}, bf16[32,1536]{1,0:T(8,128)(2,1)S(1)}, u32[]{:S(2)}, u32[]{:S(2)}) collective-permute-start(bf16[32,1536]{1,0:T(8,128)(2,1)S(1)} %get-tuple-element.48), channel_id=1, source_target_pairs={{0,2},{1,3},{2,0},{3,1},{4,6},{5,7},{6,4},{7,5},{8,10},{9,11},{10,... | collective-permute-start | bytes 294920 | tf_op jit(solution)/shard_map/ppermute | solution.py:24
  44.8 12.2 %collective-permute-start.14 = (bf16[32,1536]{1,0:T(8,128)(2,1)S(1)}, bf16[32,1536]{1,0:T(8,128)(2,1)S(1)}, u32[]{:S(2)}, u32[]{:S(2)}) collective-permute-start(bf16[32,1536]{1,0:T(8,128)(2,1)S(1)} %get-tuple-element.49), channel_id=1, source_target_pairs={{0,4},{1,5},{2,6},{3,7},{4,0},{5,1},{6,2},{7,3},{8,12},{9,13},{10,... | collective-permute-start | bytes 294920 | tf_op jit(solution)/shard_map/ppermute | solution.py:24
  51.0 1.4 %collective-permute-start.17 = (bf16[4,32,512]{2,1,0:T(8,128)(2,1)S(1)}, bf16[4,32,512]{2,1,0:T(8,128)(2,1)S(1)}, u32[]{:S(2)}, u32[]{:S(2)}) collective-permute-start(bf16[4,32,512]{2,1,0:T(8,128)(2,1)S(1)} %slice_bitcast_fusion.1), channel_id=1, source_target_pairs={{0,1},{1,0},{2,3},{3,2},{4,5},{5,4},{6,7},{7,6},{8,9},{9,8},{10,11... | collective-permute-start | bytes 393224 | tf_op jit(solution)/shard_map/ppermute | solution.py:24
  52.4 4.5 %collective-permute-start.20 = (bf16[32,512]{1,0:T(8,128)(2,1)S(1)}, bf16[32,512]{1,0:T(8,128)(2,1)S(1)}, u32[]{:S(2)}, u32[]{:S(2)}) collective-permute-start(bf16[32,512]{1,0:T(8,128)(2,1)S(1)} %get-tuple-element.52), channel_id=1, source_target_pairs={{0,2},{1,3},{2,0},{3,1},{4,6},{5,7},{6,4},{7,5},{8,10},{9,11},{10,... | collective-permute-start | bytes 98312 | tf_op jit(solution)/shard_map/ppermute | solution.py:24
  54.3 5.4 %collective-permute-start.19 = (bf16[32,512]{1,0:T(8,128)(2,1)S(1)}, bf16[32,512]{1,0:T(8,128)(2,1)S(1)}, u32[]{:S(2)}, u32[]{:S(2)}) collective-permute-start(bf16[32,512]{1,0:T(8,128)(2,1)S(1)} %get-tuple-element.53), channel_id=1, source_target_pairs={{0,4},{1,5},{2,6},{3,7},{4,0},{5,1},{6,2},{7,3},{8,12},{9,13},{10,... | collective-permute-start | bytes 98312 | tf_op jit(solution)/shard_map/ppermute | solution.py:24
  56.9 5.7 %collective-permute-start.18 = (bf16[32,512]{1,0:T(8,128)(2,1)S(1)}, bf16[32,512]{1,0:T(8,128)(2,1)S(1)}, u32[]{:S(2)}, u32[]{:S(2)}) collective-permute-start(bf16[32,512]{1,0:T(8,128)(2,1)S(1)} %get-tuple-element.54), channel_id=1, source_target_pairs={{0,6},{1,7},{2,4},{3,5},{4,2},{5,3},{6,0},{7,1},{8,14},{9,15},{10,... | collective-permute-start | bytes 98312 | tf_op jit(solution)/shard_map/ppermute | solution.py:24

commit v12 on v11

--- a/solution.py
+++ b/solution.py
@@ -146,35 +146,38 @@
         stacked[k, quarter:] = seconds[k][...]
 
 
-def merge_kernel(own_segs, mix, *refs):
+def merge_kernel(own_segs, steps, mix, *refs):
     weights, outs = refs
     experts, rows, cols = weights[0].shape
     block = mix.shape[1] // experts
+    size = own_segs * block
+    rows_of = mix[steps[0] * size : (steps[-1] + 1) * size, :]
     for w, weight in enumerate(weights):
         for start in range(0, rows, block):
             tile = weight[:, start : start + block, :].reshape(experts * block, cols)
-            out = jnp.dot(mix[...], tile, preferred_element_type=F32).astype(BF16)
+            out = jnp.dot(rows_of, tile, preferred_element_type=F32).astype(BF16)
             out = out.reshape(len(outs), own_segs, block, cols)
             at = w * rows + start
             for k in range(len(outs)):
                 outs[k][:, at : at + block, :] = out[k]
 
 
-def merge(mix, dp, own_segs, weights, flops):
+def merge(mix, steps, own_segs, weights, flops, after=()):
     experts, rows, cols = weights[0].shape
     total = rows * len(weights)
     count = len(weights)
 
     def kernel(mix_ref, *refs):
-        merge_kernel(own_segs, mix_ref, refs[:count], refs[-dp:])
+        outs = refs[-len(steps) :]
+        merge_kernel(own_segs, steps, mix_ref, refs[:count], outs)
 
     return call(
         kernel,
-        [((own_segs, total, cols), BF16)] * dp,
-        [VMEM] * (1 + count),
-        (mix, *weights),
+        [((own_segs, total, cols), BF16)] * len(steps),
+        [VMEM] * (1 + count) + [ANY] * len(after),
+        (mix, *weights, *after),
         flops,
-        2 * total * cols * (experts + dp * own_segs),
+        2 * total * cols * (experts + len(steps) * own_segs),
     )
 
 
@@ -228,7 +231,7 @@
 
 
 def first_kernel(dp, core, *refs):
-    parts, downs, hidden, mixed = refs[:dp], refs[dp:-2], refs[-2], refs[-1]
+    parts, downs, hidden, mixed = refs[:dp], refs[dp:-3], refs[-2], refs[-1]
     half = hidden.shape[1]
     kept = []
     for j in range(hidden.shape[0]):
@@ -321,8 +324,9 @@
         0,
         2 * own_rows * depth,
     )
-    merged_down = merge(mix, dp, own_segs, (down_weight,), 2 * mix.size * down_weight.size // experts // block)
-    downs = [block if k == 0 else swap(block, "dp", k) for k, block in enumerate(merged_down)]
+    flops = 2 * mix.size * down_weight.size // experts // block
+    merged_down = merge(mix, tuple(range(dp - 1)), own_segs, (down_weight,), flops)
+    downs = [down if k == 0 else swap(down, "dp", k) for k, down in enumerate(merged_down)]
     gate_up = (jnp.swapaxes(gate_weight, 1, 2), jnp.swapaxes(up_weight, 1, 2))
     (stacked,) = call(
         functools.partial(stack_kernel, dp),
@@ -333,22 +337,25 @@
         2 * own_rows * width,
     )
     other = swap(stacked, "tensor", 1)
-    merged = merge(mix, dp, own_segs, gate_up, BESIDE)
+    merged = merge(mix, tuple(range(dp)), own_segs, gate_up, BESIDE)
     partial_pre = preact(core, own, stacked, other, merged)
     parts = [partial_pre[0]] + [swap(partial_pre[k], "dp", k) for k in range(1, dp)]
 
     rows = own_rows // tensor
+    last = (dp - 1,)
+    (down,) = merge(mix, last, own_segs, (down_weight,), flops // dp, (parts[1], *downs[1:]))
+    downs.append(swap(down, "dp", dp - 1))
     early, late = tuple(range(dp - 1)), (dp - 1,)
     flops = 2 * own_rows * hidden_count * cols
     hidden, mixed = call(
         functools.partial(first_kernel, dp),
         [((own_segs, hidden_count, SEG), BF16), ((2, lines, rows, len(early) * cols), BF16)],
-        [SMEM] + [VMEM] * (dp + len(early)),
-        (core, *parts, *[downs[k] for k in early]),
+        [SMEM] + [VMEM] * (dp + len(early)) + [ANY],
+        (core, *parts, *[downs[k] for k in early], down),
         flops * len(early),
         2 * (own_rows * hidden_count * dp * 2 + hidden_count * cols * len(early)),
     )
-    early_pieces = tensor_sum_pieces(mixed, lines, False)
+    early_pieces = tensor_sum_pieces(mixed, lines, True)
     (mixed,) = call(
         functools.partial(second_kernel, len(late)),
         [((2, lines, rows, len(late) * cols), BF16)],

time: 63.5 us -> 71.9 us (1.13)
  waiting for transfers between devices: 28.8 us -> 33.9 us
  Pallas kernels: 6.48 us -> 10.2 us
  starting transfers between devices: 27.6 us -> 26.5 us
  local copies, waits for them, and re-layouts: 0.11 us -> 0.85 us
    ppermute x21, waiting for transfers between devices: 28.8 us -> 33.9 us  [swap(): return lax.ppermute(value, axis, [(i, i ^ step) for i in range(count)])]
    pallas_call x11 -> x13, Pallas kernels: 6.48 us -> 10.2 us  [call(): pl.pallas_call(kernel, out_shape=[jax.ShapeDtypeStruct(shape, dtype) for...]
    ppermute x21, starting transfers between devices: 27.6 us -> 26.5 us  [swap(): return lax.ppermute(value, axis, [(i, i ^ step) for i in range(count)])]
    unnamed x6 -> x10, local copies, waits for them, and re-layouts: 0.01 us -> 0.75 us
  transfers between devices with their start and end apart: 21 -> 21, of which waited for: 10 -> 9; matrix products, arithmetic and copies ran while one was open for 0% -> 0% of each run, Pallas kernels for 5% -> 11%
where the time goes in v12:
time: 71.9 us; the launch traced here: 71.8 us
  waiting for transfers between devices  33.9 us (47%)
  starting transfers between devices  26.5 us (37%)
  Pallas kernels  10.2 us (14%)
  local copies, waits for them, and re-layouts  0.85 us (1%)
    ppermute x21, waiting for transfers between devices, swap(): return lax.ppermute(value, axis, [(i, i ^ step) for i in range(count)])  33.9 us
    ppermute x21, starting transfers between devices, swap(): return lax.ppermute(value, axis, [(i, i ^ step) for i in range(count)])  26.5 us
    pallas_call x13, Pallas kernels, call(): pl.pallas_call(kernel, out_shape=[jax.ShapeDtypeStruct(shape, dtype) for...  10.2 us
  transfers between devices with their start and end apart: 21, of which 9 were waited for; matrix products, arithmetic and copies ran while one was open for 0% of the time, Pallas kernels for 11%

profile of v12, /device:TPU:0, one launch (start us, length us, event | category | flops | bytes accessed | tf_op | source)
XLA Modules:
  0.0 71.8 jit_solution(14706564513661982718)
XLA Ops:
  0.0 1.8 %shard_map.64 = (bf16[256,512]{1,0:T(8,128)(2,1)S(1)}, bf16[80,512]{1,0:T(8,128)(2,1)S(1)}, bf16[80,512]{1,0:T(8,128)(2,1)S(1)}, bf16[80,512]{1,0:T(8,128)(2,1)S...) custom-call(s32[1]{0:T(128)} %bitcast.my_dp, s32[1]{0:T(128)} %bitcast.1.core, ...), custom_call_target="tpu_custom_call" | custom-call | flops 10000000000 | bytes 2097152 | tf_op jit(solution)/shard_map/pallas_call | solution.py:32
  1.8 0.0 copy-start.3
  1.8 3.0 %collective-permute-start.1 = (bf16[80,512]{1,0:T(8,128)(2,1)S(1)}, bf16[80,512]{1,0:T(8,128)(2,1)S(1)}, u32[]{:S(2)}, u32[]{:S(2)}) collective-permute-start(bf16[80,512]{1,0:T(8,128)(2,1)S(1)} %get-tuple-element.27), channel_id=1, source_target_pairs={{0,16},{8,24},{16,0},{24,8},{1,17},{9,25},{17,1},{25,9},{2,18},{10... | collective-permute-start | bytes 245768 | tf_op jit(solution)/shard_map/ppermute | solution.py:24
  4.9 1.4 %collective-permute-start.2 = (bf16[80,512]{1,0:T(8,128)(2,1)S(1)}, bf16[80,512]{1,0:T(8,128)(2,1)S(1)}, u32[]{:S(2)}, u32[]{:S(2)}) collective-permute-start(bf16[80,512]{1,0:T(8,128)(2,1)S(1)} %get-tuple-element.28), channel_id=1, source_target_pairs={{0,24},{8,16},{16,8},{24,0},{1,25},{9,17},{17,9},{25,1},{2,26},{10... | collective-permute-start | bytes 245768 | tf_op jit(solution)/shard_map/ppermute | solution.py:24
  6.3 0.1 collective-permute-start
  6.4 1.9 %collective-permute-start.3 = (bf16[64,512]{1,0:T(8,128)(2,1)S(1)}, bf16[64,512]{1,0:T(8,128)(2,1)S(1)}, u32[]{:S(2)}, u32[]{:S(2)}) collective-permute-start(bf16[64,512]{1,0:T(8,128)(2,1)S(1)} %get-tuple-element.29), channel_id=1, source_target_pairs={{0,8},{8,0},{16,24},{24,16},{1,9},{9,1},{17,25},{25,17},{2,10},{10... | collective-permute-start | bytes 196616 | tf_op jit(solution)/shard_map/ppermute | solution.py:24
  8.3 1.5 %collective-permute-start.4 = (bf16[64,512]{1,0:T(8,128)(2,1)S(1)}, bf16[64,512]{1,0:T(8,128)(2,1)S(1)}, u32[]{:S(2)}, u32[]{:S(2)}) collective-permute-start(bf16[64,512]{1,0:T(8,128)(2,1)S(1)} %get-tuple-element.30), channel_id=1, source_target_pairs={{0,16},{8,24},{16,0},{24,8},{1,17},{9,25},{17,1},{25,9},{2,18},{10... | collective-permute-start | bytes 196616 | tf_op jit(solution)/shard_map/ppermute | solution.py:24
  9.9 0.0 collective-permute-done.1.refs_2_.refs_1_
  9.9 1.7 %collective-permute-start.5 = (bf16[64,512]{1,0:T(8,128)(2,1)S(1)}, bf16[64,512]{1,0:T(8,128)(2,1)S(1)}, u32[]{:S(2)}, u32[]{:S(2)}) collective-permute-start(bf16[64,512]{1,0:T(8,128)(2,1)S(1)} %get-tuple-element.31), channel_id=1, source_target_pairs={{0,24},{8,16},{16,8},{24,0},{1,25},{9,17},{17,9},{25,1},{2,26},{10... | collective-permute-start | bytes 196616 | tf_op jit(solution)/shard_map/ppermute | solution.py:24
  11.5 0.2 collective-permute-done.refs_1_.refs_0_
  11.7 0.3 shard_map.65.mix_ref
  12.1 1.5 %shard_map.66 = (bf16[1,352,512]{2,1,0:T(8,128)(2,1)S(1)}, bf16[1,352,512]{2,1,0:T(8,128)(2,1)}, bf16[1,352,512]{2,1,0:T(8,128)(2,1)}) custom-call(bf16[128,256]{1,0:T(8,128)(2,1)S(1)} %shard_map.65.mix_ref, bf16[8,352,512]{2,1,0:T(8,128)(2,1)S(1)} %copy-done), custom_call_target="tpu_custom_call" | custom-call | flops 369098752 | bytes 3964928 | tf_op jit(solution)/shard_map/pallas_call | solution.py:32
  13.5 1.7 %collective-permute-start.10 = (bf16[1,352,512]{2,1,0:T(8,128)(2,1)}, bf16[1,352,512]{2,1,0:T(8,128)(2,1)}, u32[]{:S(2)}, u32[]{:S(2)}) collective-permute-start(bf16[1,352,512]{2,1,0:T(8,128)(2,1)} %get-tuple-element.41), channel_id=1, source_target_pairs={{0,8},{8,0},{16,24},{24,16},{1,9},{9,1},{17,25},{25,17},{2,10},{10... | collective-permute-start | bytes 1081352 | tf_op jit(solution)/shard_map/ppermute | solution.py:24
  15.2 1.5 %collective-permute-start.11 = (bf16[1,352,512]{2,1,0:T(8,128)(2,1)}, bf16[1,352,512]{2,1,0:T(8,128)(2,1)}, u32[]{:S(2)}, u32[]{:S(2)}) collective-permute-start(bf16[1,352,512]{2,1,0:T(8,128)(2,1)} %get-tuple-element.42), channel_id=1, source_target_pairs={{0,16},{8,24},{16,0},{24,8},{1,17},{9,25},{17,1},{25,9},{2,18},{10... | collective-permute-start | bytes 1081352 | tf_op jit(solution)/shard_map/ppermute | solution.py:24
  16.8 0.1 collective-permute-start.6
  16.9 0.9 %shard_map.68 = (bf16[1,704,512]{2,1,0:T(8,128)(2,1)S(1)}, bf16[1,704,512]{2,1,0:T(8,128)(2,1)S(1)}, bf16[1,704,512]{2,1,0:T(8,128)(2,1)S(1)}, bf16[1,704,512]{2,1,0:T(8,128)(2,1)S(1)}) custom-call(bf16[128,256]{1,0:T(8,128)(2,1)S(1)} %shard_map.65.mix_ref, bf16[8,352,512]{2,1,0:T(8,128)(2,1)S(1)} %bitcast.26, bf16[8,352,512]{2,1,0:T(8,128)(2,1)S(1)} %bitcast.27), custom_call_target="tpu_custom_call" | custom-call | flops 10000000000 | bytes 8650752 | tf_op jit(solution)/shard_map/pallas_call | solution.py:32
  17.8 0.8 %collective-permute-done.6.other = bf16[3,128,512]{2,1,0:T(8,128)(2,1)S(1)} collective-permute-done((bf16[3,128,512]{2,1,0:T(8,128)(2,1)S(1)}, bf16[3,128,512]{2,1,0:T(8,128)(2,1)S(1)}, u32[]{:S(2)}, u32[]{:S(2)}) %collective-permute-start.6) | collective-permute-done | bytes 393248 | tf_op jit(solution)/shard_map/ppermute | solution.py:24
  18.6 1.7 %shard_map.69 = (bf16[1,704,256]{2,1,0:T(8,128)(2,1)S(1)}, bf16[1,704,256]{2,1,0:T(8,128)(2,1)}, bf16[1,704,256]{2,1,0:T(8,128)(2,1)}, bf16[1,704,256]{2,1,0:T(8,128)(2,1)}) custom-call(s32[1]{0:T(128)} %bitcast.1.core, bf16[256,512]{1,0:T(8,128)(2,1)S(1)} %get-tuple-element.25.own, bf16[3,128,512]{2,1,0:T(8,128)(2,1)S(1)} %shard_map.67.brought, ...), custom_call_target="tpu_custom_call" | custom-call | flops 738197504 | bytes 5373952 | tf_op jit(solution)/shard_map/pallas_call | solution.py:32
  20.3 0.7 %copy-done.1 = bf16[1,704,256]{2,1,0:T(8,128)(2,1)} copy-done((bf16[1,704,256]{2,1,0:T(8,128)(2,1)}, bf16[1,704,256]{2,1,0:T(8,128)(2,1)S(1)}, u32[]{:S(2)}) %copy-start.1) | copy-done | bytes 360472
  21.0 0.5 collective-permute-start.7
  21.6 0.7 collective-permute-start.8
  22.2 2.3 %collective-permute-start.9 = (bf16[1,704,256]{2,1,0:T(8,128)(2,1)}, bf16[1,704,256]{2,1,0:T(8,128)(2,1)}, u32[]{:S(2)}, u32[]{:S(2)}) collective-permute-start(bf16[1,704,256]{2,1,0:T(8,128)(2,1)} %get-tuple-element.40), channel_id=1, source_target_pairs={{0,24},{8,16},{16,8},{24,0},{1,25},{9,17},{17,9},{25,1},{2,26},{10... | collective-permute-start | bytes 1081352 | tf_op jit(solution)/shard_map/ppermute | solution.py:24
  24.5 0.0 collective-permute-done.10.refs_2_.refs_5_
  24.5 0.0 collective-permute-done.11.refs_3_.refs_6_
  24.5 8.1 %collective-permute-done.7.refs_1_ = bf16[1,704,256]{2,1,0:T(8,128)(2,1)} collective-permute-done((bf16[1,704,256]{2,1,0:T(8,128)(2,1)}, bf16[1,704,256]{2,1,0:T(8,128)(2,1)}, u32[]{:S(2)}, u32[]{:S(2)}) %collective-permute-start.7) | collective-permute-done | bytes 360480 | tf_op jit(solution)/shard_map/ppermute | solution.py:24
  32.6 0.6 shard_map.70.refs_7_
  33.2 0.7 collective-permute-start.16
  33.9 13.6 %collective-permute-done.8.refs_2_ = bf16[1,704,256]{2,1,0:T(8,128)(2,1)} collective-permute-done((bf16[1,704,256]{2,1,0:T(8,128)(2,1)}, bf16[1,704,256]{2,1,0:T(8,128)(2,1)}, u32[]{:S(2)}, u32[]{:S(2)}) %collective-permute-start.8) | collective-permute-done | bytes 360480 | tf_op jit(solution)/shard_map/ppermute | solution.py:24
  47.5 0.0 collective-permute-done.9.refs_3_
  47.5 2.2 %shard_map.71 = (bf16[1,352,256]{2,1,0:T(8,128)(2,1)S(1)}, bf16[2,4,32,1536]{3,2,1,0:T(8,128)(2,1)S(1)}) custom-call(s32[1]{0:T(128)} %bitcast.1.core, bf16[1,704,256]{2,1,0:T(8,128)(2,1)S(1)} %copy-done.2, bf16[1,704,256]{2,1,0:T(8,128)(2,1)} %collective-permute-done.7.refs_1_, bf16[1,704,256]{2,1,0:T(8,128)(2,1)} %collective-permute-done.8.refs_2_, ...), custom_call_target="tpu_custom_call" | custom-call | flops 276824064 | bytes 2523136 | tf_op jit(solution)/shard_map/pallas_call | solution.py:32
  49.8 0.1 collective-permute-start.12
  49.9 1.7 %collective-permute-done.12 = bf16[4,32,1536]{2,1,0:T(8,128)(2,1)S(1)} collective-permute-done((bf16[4,32,1536]{2,1,0:T(8,128)(2,1)S(1)}, bf16[4,32,1536]{2,1,0:T(8,128)(2,1)S(1)}, u32[]{:S(2)}, u32[]{:S(2)}) %collective-permute-start.12) | collective-permute-done | bytes 393248 | tf_op jit(solution)/shard_map/ppermute | solution.py:24
  51.6 0.1 add_convert_fusion
  51.7 3.7 %collective-permute-start.13 = (bf16[32,1536]{1,0:T(8,128)(2,1)S(1)}, bf16[32,1536]{1,0:T(8,128)(2,1)S(1)}, u32[]{:S(2)}, u32[]{:S(2)}) collective-permute-start(bf16[32,1536]{1,0:T(8,128)(2,1)S(1)} %get-tuple-element.48), channel_id=1, source_target_pairs={{0,6},{1,7},{2,4},{3,5},{4,2},{5,3},{6,0},{7,1},{8,14},{9,15},{10,... | collective-permute-start | bytes 294920 | tf_op jit(solution)/shard_map/ppermute | solution.py:24
  55.4 0.0 collective-permute-start.15
  55.4 0.8 %collective-permute-start.14 = (bf16[32,1536]{1,0:T(8,128)(2,1)S(1)}, bf16[32,1536]{1,0:T(8,128)(2,1)S(1)}, u32[]{:S(2)}, u32[]{:S(2)}) collective-permute-start(bf16[32,1536]{1,0:T(8,128)(2,1)S(1)} %get-tuple-element.47), channel_id=1, source_target_pairs={{0,4},{1,5},{2,6},{3,7},{4,0},{5,1},{6,2},{7,3},{8,12},{9,13},{10,... | collective-permute-start | bytes 294920 | tf_op jit(solution)/shard_map/ppermute | solution.py:24
  56.2 0.0 collective-permute-done.16.refs_0_
  56.2 3.1 %collective-permute-done.13.refs_0_.refs_1_ = bf16[32,1536]{1,0:T(8,128)(2,1)S(1)} collective-permute-done((bf16[32,1536]{1,0:T(8,128)(2,1)S(1)}, bf16[32,1536]{1,0:T(8,128)(2,1)S(1)}, u32[]{:S(2)}, u32[]{:S(2)}) %collective-permute-start.13) | collective-permute-done | bytes 98336 | tf_op jit(solution)/shard_map/ppermute | solution.py:24
  59.2 0.3 shard_map.74.source
  59.6 0.1 collective-permute-start.17
  59.7 1.3 %collective-permute-done.17 = bf16[4,32,512]{2,1,0:T(8,128)(2,1)S(1)} collective-permute-done((bf16[4,32,512]{2,1,0:T(8,128)(2,1)S(1)}, bf16[4,32,512]{2,1,0:T(8,128)(2,1)S(1)}, u32[]{:S(2)}, u32[]{:S(2)}) %collective-permute-start.17) | collective-permute-done | bytes 131104 | tf_op jit(solution)/shard_map/ppermute | solution.py:24
  61.1 2.3 %collective-permute-start.20 = (bf16[32,512]{1,0:T(8,128)(2,1)S(1)}, bf16[32,512]{1,0:T(8,128)(2,1)S(1)}, u32[]{:S(2)}, u32[]{:S(2)}) collective-permute-start(bf16[32,512]{1,0:T(8,128)(2,1)S(1)} %get-tuple-element.50), channel_id=1, source_target_pairs={{0,2},{1,3},{2,0},{3,1},{4,6},{5,7},{6,4},{7,5},{8,10},{9,11},{10,... | collective-permute-start | bytes 98312 | tf_op jit(solution)/shard_map/ppermute | solution.py:24
  63.4 2.0 %collective-permute-start.19 = (bf16[32,512]{1,0:T(8,128)(2,1)S(1)}, bf16[32,512]{1,0:T(8,128)(2,1)S(1)}, u32[]{:S(2)}, u32[]{:S(2)}) collective-permute-start(bf16[32,512]{1,0:T(8,128)(2,1)S(1)} %get-tuple-element.51), channel_id=1, source_target_pairs={{0,4},{1,5},{2,6},{3,7},{4,0},{5,1},{6,2},{7,3},{8,12},{9,13},{10,... | collective-permute-start | bytes 98312 | tf_op jit(solution)/shard_map/ppermute | solution.py:24
  65.4 0.4 collective-permute-start.18
  65.8 0.1 shard_map.73.early
  65.9 2.5 %collective-permute-done.19.refs_1_ = bf16[32,512]{1,0:T(8,128)(2,1)S(1)} collective-permute-done((bf16[32,512]{1,0:T(8,128)(2,1)S(1)}, bf16[32,512]{1,0:T(8,128)(2,1)S(1)}, u32[]{:S(2)}, u32[]{:S(2)}) %collective-permute-start.19) | collective-permute-done | bytes 32800 | tf_op jit(solution)/shard_map/ppermute | solution.py:24
  68.4 2.7 %collective-permute-done.18.refs_0_ = bf16[32,512]{1,0:T(8,128)(2,1)S(1)} collective-permute-done((bf16[32,512]{1,0:T(8,128)(2,1)S(1)}, bf16[32,512]{1,0:T(8,128)(2,1)S(1)}, u32[]{:S(2)}, u32[]{:S(2)}) %collective-permute-start.18) | collective-permute-done | bytes 32800 | tf_op jit(solution)/shard_map/ppermute | solution.py:24
  71.1 0.7 shard_map.76
  (23 shorter events, 0.2 us)
Async XLA Ops:
  0.0 12.0 %copy-start = (bf16[8,352,512]{2,1,0:T(8,128)(2,1)S(1)}, bf16[8,352,512]{2,1,0:T(8,128)(2,1)}, u32[]{:S(2)}) copy-start(bf16[8,352,512]{2,1,0:T(8,128)(2,1)} %refs_0_.3) | copy-start | bytes 8650756
  0.0 16.9 %copy-start.4 = (bf16[8,512,352]{1,2,0:T(8,128)(2,1)S(1)}, bf16[8,512,352]{1,2,0:T(8,128)(2,1)}, u32[]{:S(2)}) copy-start(bf16[8,512,352]{1,2,0:T(8,128)(2,1)} %param.8) | copy-start | bytes 8650756
  1.8 15.0 %copy-start.3 = (bf16[8,512,352]{1,2,0:T(8,128)(2,1)S(1)}, bf16[8,512,352]{1,2,0:T(8,128)(2,1)}, u32[]{:S(2)}) copy-start(bf16[8,512,352]{1,2,0:T(8,128)(2,1)} %param.7) | copy-start | bytes 8650756
  1.8 8.0 %collective-permute-start.1 = (bf16[80,512]{1,0:T(8,128)(2,1)S(1)}, bf16[80,512]{1,0:T(8,128)(2,1)S(1)}, u32[]{:S(2)}, u32[]{:S(2)}) collective-permute-start(bf16[80,512]{1,0:T(8,128)(2,1)S(1)} %get-tuple-element.27), channel_id=1, source_target_pairs={{0,16},{8,24},{16,0},{24,8},{1,17},{9,25},{17,1},{25,9},{2,18},{10... | collective-permute-start | bytes 245768 | tf_op jit(solution)/shard_map/ppermute | solution.py:24
  4.9 6.7 %collective-permute-start.2 = (bf16[80,512]{1,0:T(8,128)(2,1)S(1)}, bf16[80,512]{1,0:T(8,128)(2,1)S(1)}, u32[]{:S(2)}, u32[]{:S(2)}) collective-permute-start(bf16[80,512]{1,0:T(8,128)(2,1)S(1)} %get-tuple-element.28), channel_id=1, source_target_pairs={{0,24},{8,16},{16,8},{24,0},{1,25},{9,17},{17,9},{25,1},{2,26},{10... | collective-permute-start | bytes 245768 | tf_op jit(solution)/shard_map/ppermute | solution.py:24
  6.3 5.4 %collective-permute-start = (bf16[80,512]{1,0:T(8,128)(2,1)S(1)}, bf16[80,512]{1,0:T(8,128)(2,1)S(1)}, u32[]{:S(2)}, u32[]{:S(2)}) collective-permute-start(bf16[80,512]{1,0:T(8,128)(2,1)S(1)} %get-tuple-element.26.refs_0_), channel_id=1, source_target_pairs={{0,8},{8,0},{16,24},{24,16},{1,9},{9,1},{17,25},{25,17},{2,10},{10... | collective-permute-start | bytes 245768 | tf_op jit(solution)/shard_map/ppermute | solution.py:24
  6.4 10.3 %collective-permute-start.3 = (bf16[64,512]{1,0:T(8,128)(2,1)S(1)}, bf16[64,512]{1,0:T(8,128)(2,1)S(1)}, u32[]{:S(2)}, u32[]{:S(2)}) collective-permute-start(bf16[64,512]{1,0:T(8,128)(2,1)S(1)} %get-tuple-element.29), channel_id=1, source_target_pairs={{0,8},{8,0},{16,24},{24,16},{1,9},{9,1},{17,25},{25,17},{2,10},{10... | collective-permute-start | bytes 196616 | tf_op jit(solution)/shard_map/ppermute | solution.py:24
  8.3 8.4 %collective-permute-start.4 = (bf16[64,512]{1,0:T(8,128)(2,1)S(1)}, bf16[64,512]{1,0:T(8,128)(2,1)S(1)}, u32[]{:S(2)}, u32[]{:S(2)}) collective-permute-start(bf16[64,512]{1,0:T(8,128)(2,1)S(1)} %get-tuple-element.30), channel_id=1, source_target_pairs={{0,16},{8,24},{16,0},{24,8},{1,17},{9,25},{17,1},{25,9},{2,18},{10... | collective-permute-start | bytes 196616 | tf_op jit(solution)/shard_map/ppermute | solution.py:24
  9.9 6.9 %collective-permute-start.5 = (bf16[64,512]{1,0:T(8,128)(2,1)S(1)}, bf16[64,512]{1,0:T(8,128)(2,1)S(1)}, u32[]{:S(2)}, u32[]{:S(2)}) collective-permute-start(bf16[64,512]{1,0:T(8,128)(2,1)S(1)} %get-tuple-element.31), channel_id=1, source_target_pairs={{0,24},{8,16},{16,8},{24,0},{1,25},{9,17},{17,9},{25,1},{2,26},{10... | collective-permute-start | bytes 196616 | tf_op jit(solution)/shard_map/ppermute | solution.py:24
  13.5 11.0 %collective-permute-start.10 = (bf16[1,352,512]{2,1,0:T(8,128)(2,1)}, bf16[1,352,512]{2,1,0:T(8,128)(2,1)}, u32[]{:S(2)}, u32[]{:S(2)}) collective-permute-start(bf16[1,352,512]{2,1,0:T(8,128)(2,1)} %get-tuple-element.41), channel_id=1, source_target_pairs={{0,8},{8,0},{16,24},{24,16},{1,9},{9,1},{17,25},{25,17},{2,10},{10... | collective-permute-start | bytes 1081352 | tf_op jit(solution)/shard_map/ppermute | solution.py:24
  15.2 9.3 %collective-permute-start.11 = (bf16[1,352,512]{2,1,0:T(8,128)(2,1)}, bf16[1,352,512]{2,1,0:T(8,128)(2,1)}, u32[]{:S(2)}, u32[]{:S(2)}) collective-permute-start(bf16[1,352,512]{2,1,0:T(8,128)(2,1)} %get-tuple-element.42), channel_id=1, source_target_pairs={{0,16},{8,24},{16,0},{24,8},{1,17},{9,25},{17,1},{25,9},{2,18},{10... | collective-permute-start | bytes 1081352 | tf_op jit(solution)/shard_map/ppermute | solution.py:24
  16.8 1.8 %collective-permute-start.6 = (bf16[3,128,512]{2,1,0:T(8,128)(2,1)S(1)}, bf16[3,128,512]{2,1,0:T(8,128)(2,1)S(1)}, u32[]{:S(2)}, u32[]{:S(2)}) collective-permute-start(bf16[3,128,512]{2,1,0:T(8,128)(2,1)S(1)} %shard_map.67.brought), channel_id=1, source_target_pairs={{0,1},{1,0},{2,3},{3,2},{4,5},{5,4},{6,7},{7,6},{8,9},{9,8},{10,11... | collective-permute-start | bytes 1179656 | tf_op jit(solution)/shard_map/ppermute | solution.py:24
  20.3 0.7 %copy-start.1 = (bf16[1,704,256]{2,1,0:T(8,128)(2,1)}, bf16[1,704,256]{2,1,0:T(8,128)(2,1)S(1)}, u32[]{:S(2)}) copy-start(bf16[1,704,256]{2,1,0:T(8,128)(2,1)S(1)} %get-tuple-element.37.refs_0_) | copy-start | bytes 1081348
  21.0 11.6 %collective-permute-start.7 = (bf16[1,704,256]{2,1,0:T(8,128)(2,1)}, bf16[1,704,256]{2,1,0:T(8,128)(2,1)}, u32[]{:S(2)}, u32[]{:S(2)}) collective-permute-start(bf16[1,704,256]{2,1,0:T(8,128)(2,1)} %get-tuple-element.38), channel_id=1, source_target_pairs={{0,8},{8,0},{16,24},{24,16},{1,9},{9,1},{17,25},{25,17},{2,10},{10... | collective-permute-start | bytes 1081352 | tf_op jit(solution)/shard_map/ppermute | solution.py:24
  21.6 25.9 %collective-permute-start.8 = (bf16[1,704,256]{2,1,0:T(8,128)(2,1)}, bf16[1,704,256]{2,1,0:T(8,128)(2,1)}, u32[]{:S(2)}, u32[]{:S(2)}) collective-permute-start(bf16[1,704,256]{2,1,0:T(8,128)(2,1)} %get-tuple-element.39), channel_id=1, source_target_pairs={{0,16},{8,24},{16,0},{24,8},{1,17},{9,25},{17,1},{25,9},{2,18},{10... | collective-permute-start | bytes 1081352 | tf_op jit(solution)/shard_map/ppermute | solution.py:24
  22.2 25.3 %collective-permute-start.9 = (bf16[1,704,256]{2,1,0:T(8,128)(2,1)}, bf16[1,704,256]{2,1,0:T(8,128)(2,1)}, u32[]{:S(2)}, u32[]{:S(2)}) collective-permute-start(bf16[1,704,256]{2,1,0:T(8,128)(2,1)} %get-tuple-element.40), channel_id=1, source_target_pairs={{0,24},{8,16},{16,8},{24,0},{1,25},{9,17},{17,9},{25,1},{2,26},{10... | collective-permute-start | bytes 1081352 | tf_op jit(solution)/shard_map/ppermute | solution.py:24
  24.5 23.0 %copy-start.2 = (bf16[1,704,256]{2,1,0:T(8,128)(2,1)S(1)}, bf16[1,704,256]{2,1,0:T(8,128)(2,1)}, u32[]{:S(2)}) copy-start(bf16[1,704,256]{2,1,0:T(8,128)(2,1)} %copy-done.1) | copy-start | bytes 1081348
  33.2 23.0 %collective-permute-start.16 = (bf16[1,352,512]{2,1,0:T(8,128)(2,1)S(1)}, bf16[1,352,512]{2,1,0:T(8,128)(2,1)S(1)}, u32[]{:S(2)}, u32[]{:S(2)}) collective-permute-start(bf16[1,352,512]{2,1,0:T(8,128)(2,1)S(1)} %shard_map.70.refs_7_), channel_id=1, source_target_pairs={{0,24},{8,16},{16,8},{24,0},{1,25},{9,17},{17,9},{25,1},{2,26},{10... | collective-permute-start | bytes 1081352 | tf_op jit(solution)/shard_map/ppermute | solution.py:24
  49.8 1.8 %collective-permute-start.12 = (bf16[4,32,1536]{2,1,0:T(8,128)(2,1)S(1)}, bf16[4,32,1536]{2,1,0:T(8,128)(2,1)S(1)}, u32[]{:S(2)}, u32[]{:S(2)}) collective-permute-start(bf16[4,32,1536]{2,1,0:T(8,128)(2,1)S(1)} %slice_bitcast_fusion), channel_id=1, source_target_pairs={{0,1},{1,0},{2,3},{3,2},{4,5},{5,4},{6,7},{7,6},{8,9},{9,8},{10,11... | collective-permute-start | bytes 1179656 | tf_op jit(solution)/shard_map/ppermute | solution.py:24
  51.7 7.5 %collective-permute-start.13 = (bf16[32,1536]{1,0:T(8,128)(2,1)S(1)}, bf16[32,1536]{1,0:T(8,128)(2,1)S(1)}, u32[]{:S(2)}, u32[]{:S(2)}) collective-permute-start(bf16[32,1536]{1,0:T(8,128)(2,1)S(1)} %get-tuple-element.48), channel_id=1, source_target_pairs={{0,6},{1,7},{2,4},{3,5},{4,2},{5,3},{6,0},{7,1},{8,14},{9,15},{10,... | collective-permute-start | bytes 294920 | tf_op jit(solution)/shard_map/ppermute | solution.py:24
  55.4 10.4 %collective-permute-start.15 = (bf16[32,1536]{1,0:T(8,128)(2,1)S(1)}, bf16[32,1536]{1,0:T(8,128)(2,1)S(1)}, u32[]{:S(2)}, u32[]{:S(2)}) collective-permute-start(bf16[32,1536]{1,0:T(8,128)(2,1)S(1)} %get-tuple-element.46), channel_id=1, source_target_pairs={{0,2},{1,3},{2,0},{3,1},{4,6},{5,7},{6,4},{7,5},{8,10},{9,11},{10,... | collective-permute-start | bytes 294920 | tf_op jit(solution)/shard_map/ppermute | solution.py:24
  55.4 10.4 %collective-permute-start.14 = (bf16[32,1536]{1,0:T(8,128)(2,1)S(1)}, bf16[32,1536]{1,0:T(8,128)(2,1)S(1)}, u32[]{:S(2)}, u32[]{:S(2)}) collective-permute-start(bf16[32,1536]{1,0:T(8,128)(2,1)S(1)} %get-tuple-element.47), channel_id=1, source_target_pairs={{0,4},{1,5},{2,6},{3,7},{4,0},{5,1},{6,2},{7,3},{8,12},{9,13},{10,... | collective-permute-start | bytes 294920 | tf_op jit(solution)/shard_map/ppermute | solution.py:24
  59.6 1.4 %collective-permute-start.17 = (bf16[4,32,512]{2,1,0:T(8,128)(2,1)S(1)}, bf16[4,32,512]{2,1,0:T(8,128)(2,1)S(1)}, u32[]{:S(2)}, u32[]{:S(2)}) collective-permute-start(bf16[4,32,512]{2,1,0:T(8,128)(2,1)S(1)} %slice_bitcast_fusion.1), channel_id=1, source_target_pairs={{0,1},{1,0},{2,3},{3,2},{4,5},{5,4},{6,7},{7,6},{8,9},{9,8},{10,11... | collective-permute-start | bytes 393224 | tf_op jit(solution)/shard_map/ppermute | solution.py:24
  61.1 4.8 %collective-permute-start.20 = (bf16[32,512]{1,0:T(8,128)(2,1)S(1)}, bf16[32,512]{1,0:T(8,128)(2,1)S(1)}, u32[]{:S(2)}, u32[]{:S(2)}) collective-permute-start(bf16[32,512]{1,0:T(8,128)(2,1)S(1)} %get-tuple-element.50), channel_id=1, source_target_pairs={{0,2},{1,3},{2,0},{3,1},{4,6},{5,7},{6,4},{7,5},{8,10},{9,11},{10,... | collective-permute-start | bytes 98312 | tf_op jit(solution)/shard_map/ppermute | solution.py:24
  63.4 5.0 %collective-permute-start.19 = (bf16[32,512]{1,0:T(8,128)(2,1)S(1)}, bf16[32,512]{1,0:T(8,128)(2,1)S(1)}, u32[]{:S(2)}, u32[]{:S(2)}) collective-permute-start(bf16[32,512]{1,0:T(8,128)(2,1)S(1)} %get-tuple-element.51), channel_id=1, source_target_pairs={{0,4},{1,5},{2,6},{3,7},{4,0},{5,1},{6,2},{7,3},{8,12},{9,13},{10,... | collective-permute-start | bytes 98312 | tf_op jit(solution)/shard_map/ppermute | solution.py:24
  65.4 5.7 %collective-permute-start.18 = (bf16[32,512]{1,0:T(8,128)(2,1)S(1)}, bf16[32,512]{1,0:T(8,128)(2,1)S(1)}, u32[]{:S(2)}, u32[]{:S(2)}) collective-permute-start(bf16[32,512]{1,0:T(8,128)(2,1)S(1)} %get-tuple-element.52), channel_id=1, source_target_pairs={{0,6},{1,7},{2,4},{3,5},{4,2},{5,3},{6,0},{7,1},{8,14},{9,15},{10,... | collective-permute-start | bytes 98312 | tf_op jit(solution)/shard_map/ppermute | solution.py:24

commit v13 on v11

--- a/solution.py
+++ b/solution.py
@@ -353,7 +353,7 @@
         functools.partial(second_kernel, len(late)),
         [((2, lines, rows, len(late) * cols), BF16)],
         [SMEM] + [VMEM] * (1 + len(late)) + [ANY],
-        (core, hidden, *[downs[k] for k in late], early_pieces[0]),
+        (core, hidden, *[downs[k] for k in late], early_pieces[-2]),
         flops * len(late),
         2 * (own_rows * hidden_count + hidden_count * cols * len(late)),
     )

time: 63.5 us -> 63.5 us (level)
  no operation moved by 1% of the time
where the time goes in v13:
time: 63.5 us; the launch traced here: 63.3 us
  waiting for transfers between devices  28.9 us (46%)
  starting transfers between devices  27.5 us (43%)
  Pallas kernels  6.48 us (10%)
    ppermute x21, waiting for transfers between devices, swap(): return lax.ppermute(value, axis, [(i, i ^ step) for i in range(count)])  28.9 us
    ppermute x21, starting transfers between devices, swap(): return lax.ppermute(value, axis, [(i, i ^ step) for i in range(count)])  27.5 us
    pallas_call x11, Pallas kernels, call(): pl.pallas_call(kernel, out_shape=[jax.ShapeDtypeStruct(shape, dtype) for...  6.48 us
  transfers between devices with their start and end apart: 21, of which 10 were waited for; matrix products, arithmetic and copies ran while one was open for 0% of the time, Pallas kernels for 5%

profile of v13, /device:TPU:0, one launch (start us, length us, event | category | flops | bytes accessed | tf_op | source)
XLA Modules:
  0.0 63.3 jit_solution(2984151996418527631)
XLA Ops:
  0.0 1.8 %shard_map.64 = (bf16[256,512]{1,0:T(8,128)(2,1)S(1)}, bf16[80,512]{1,0:T(8,128)(2,1)S(1)}, bf16[80,512]{1,0:T(8,128)(2,1)S(1)}, bf16[80,512]{1,0:T(8,128)(2,1)S...) custom-call(s32[1]{0:T(128)} %bitcast.my_dp, s32[1]{0:T(128)} %bitcast.1.core, ...), custom_call_target="tpu_custom_call" | custom-call | flops 10000000000 | bytes 2097152 | tf_op jit(solution)/shard_map/pallas_call | solution.py:32
  1.8 0.0 copy-start.1
  1.8 3.0 %collective-permute-start.1 = (bf16[80,512]{1,0:T(8,128)(2,1)S(1)}, bf16[80,512]{1,0:T(8,128)(2,1)S(1)}, u32[]{:S(2)}, u32[]{:S(2)}) collective-permute-start(bf16[80,512]{1,0:T(8,128)(2,1)S(1)} %get-tuple-element.28), channel_id=1, source_target_pairs={{0,16},{8,24},{16,0},{24,8},{1,17},{9,25},{17,1},{25,9},{2,18},{10... | collective-permute-start | bytes 245768 | tf_op jit(solution)/shard_map/ppermute | solution.py:24
  4.9 1.4 %collective-permute-start.2 = (bf16[80,512]{1,0:T(8,128)(2,1)S(1)}, bf16[80,512]{1,0:T(8,128)(2,1)S(1)}, u32[]{:S(2)}, u32[]{:S(2)}) collective-permute-start(bf16[80,512]{1,0:T(8,128)(2,1)S(1)} %get-tuple-element.29), channel_id=1, source_target_pairs={{0,24},{8,16},{16,8},{24,0},{1,25},{9,17},{17,9},{25,1},{2,26},{10... | collective-permute-start | bytes 245768 | tf_op jit(solution)/shard_map/ppermute | solution.py:24
  6.3 0.1 collective-permute-start
  6.4 1.9 %collective-permute-start.3 = (bf16[64,512]{1,0:T(8,128)(2,1)S(1)}, bf16[64,512]{1,0:T(8,128)(2,1)S(1)}, u32[]{:S(2)}, u32[]{:S(2)}) collective-permute-start(bf16[64,512]{1,0:T(8,128)(2,1)S(1)} %get-tuple-element.30), channel_id=1, source_target_pairs={{0,8},{8,0},{16,24},{24,16},{1,9},{9,1},{17,25},{25,17},{2,10},{10... | collective-permute-start | bytes 196616 | tf_op jit(solution)/shard_map/ppermute | solution.py:24
  8.3 1.5 %collective-permute-start.4 = (bf16[64,512]{1,0:T(8,128)(2,1)S(1)}, bf16[64,512]{1,0:T(8,128)(2,1)S(1)}, u32[]{:S(2)}, u32[]{:S(2)}) collective-permute-start(bf16[64,512]{1,0:T(8,128)(2,1)S(1)} %get-tuple-element.31), channel_id=1, source_target_pairs={{0,16},{8,24},{16,0},{24,8},{1,17},{9,25},{17,1},{25,9},{2,18},{10... | collective-permute-start | bytes 196616 | tf_op jit(solution)/shard_map/ppermute | solution.py:24
  9.9 0.0 collective-permute-done.1.refs_2_.refs_1_
  9.9 1.7 %collective-permute-start.5 = (bf16[64,512]{1,0:T(8,128)(2,1)S(1)}, bf16[64,512]{1,0:T(8,128)(2,1)S(1)}, u32[]{:S(2)}, u32[]{:S(2)}) collective-permute-start(bf16[64,512]{1,0:T(8,128)(2,1)S(1)} %get-tuple-element.32), channel_id=1, source_target_pairs={{0,24},{8,16},{16,8},{24,0},{1,25},{9,17},{17,9},{25,1},{2,26},{10... | collective-permute-start | bytes 196616 | tf_op jit(solution)/shard_map/ppermute | solution.py:24
  11.5 0.0 collective-permute-done.2.refs_3_.refs_2_
  11.5 0.2 collective-permute-done.refs_1_.refs_0_
  11.7 0.3 shard_map.65.mix_ref
  12.1 0.5 shard_map.66
  12.6 1.7 %collective-permute-start.10 = (bf16[1,352,512]{2,1,0:T(8,128)(2,1)S(1)}, bf16[1,352,512]{2,1,0:T(8,128)(2,1)S(1)}, u32[]{:S(2)}, u32[]{:S(2)}) collective-permute-start(bf16[1,352,512]{2,1,0:T(8,128)(2,1)S(1)} %get-tuple-element.42), channel_id=1, source_target_pairs={{0,8},{8,0},{16,24},{24,16},{1,9},{9,1},{17,25},{25,17},{2,10},{10... | collective-permute-start | bytes 1081352 | tf_op jit(solution)/shard_map/ppermute | solution.py:24
  14.4 1.5 %collective-permute-start.11 = (bf16[1,352,512]{2,1,0:T(8,128)(2,1)S(1)}, bf16[1,352,512]{2,1,0:T(8,128)(2,1)S(1)}, u32[]{:S(2)}, u32[]{:S(2)}) collective-permute-start(bf16[1,352,512]{2,1,0:T(8,128)(2,1)S(1)} %get-tuple-element.43), channel_id=1, source_target_pairs={{0,16},{8,24},{16,0},{24,8},{1,17},{9,25},{17,1},{25,9},{2,18},{10... | collective-permute-start | bytes 1081352 | tf_op jit(solution)/shard_map/ppermute | solution.py:24
  15.9 0.0 collective-permute-done.4.refs_4_
  15.9 0.0 collective-permute-done.5.refs_5_
  15.9 0.1 collective-permute-start.6
  16.0 0.9 %shard_map.68 = (bf16[1,704,512]{2,1,0:T(8,128)(2,1)S(1)}, bf16[1,704,512]{2,1,0:T(8,128)(2,1)S(1)}, bf16[1,704,512]{2,1,0:T(8,128)(2,1)S(1)}, bf16[1,704,512]{2,1,0:T(8,128)(2,1)S(1)}) custom-call(bf16[128,256]{1,0:T(8,128)(2,1)S(1)} %shard_map.65.mix_ref, bf16[8,352,512]{2,1,0:T(8,128)(2,1)S(1)} %bitcast.29, bf16[8,352,512]{2,1,0:T(8,128)(2,1)S(1)} %bitcast.30), custom_call_target="tpu_custom_call" | custom-call | flops 10000000000 | bytes 8650752 | tf_op jit(solution)/shard_map/pallas_call | solution.py:32
  16.9 0.8 %collective-permute-done.6.other = bf16[3,128,512]{2,1,0:T(8,128)(2,1)S(1)} collective-permute-done((bf16[3,128,512]{2,1,0:T(8,128)(2,1)S(1)}, bf16[3,128,512]{2,1,0:T(8,128)(2,1)S(1)}, u32[]{:S(2)}, u32[]{:S(2)}) %collective-permute-start.6) | collective-permute-done | bytes 393248 | tf_op jit(solution)/shard_map/ppermute | solution.py:24
  17.7 1.0 %shard_map.69 = (bf16[1,704,256]{2,1,0:T(8,128)(2,1)S(1)}, bf16[1,704,256]{2,1,0:T(8,128)(2,1)S(1)}, bf16[1,704,256]{2,1,0:T(8,128)(2,1)S(1)}, bf16[1,704,256]{2,1,0:T(8,128)(2,1)S(1)}) custom-call(s32[1]{0:T(128)} %bitcast.1.core, bf16[256,512]{1,0:T(8,128)(2,1)S(1)} %get-tuple-element.26.own, bf16[3,128,512]{2,1,0:T(8,128)(2,1)S(1)} %shard_map.67.brought, ...), custom_call_target="tpu_custom_call" | custom-call | flops 738197504 | bytes 5373952 | tf_op jit(solution)/shard_map/pallas_call | solution.py:32
  18.7 0.6 collective-permute-start.7
  19.3 1.6 %collective-permute-start.8 = (bf16[1,704,256]{2,1,0:T(8,128)(2,1)S(1)}, bf16[1,704,256]{2,1,0:T(8,128)(2,1)S(1)}, u32[]{:S(2)}, u32[]{:S(2)}) collective-permute-start(bf16[1,704,256]{2,1,0:T(8,128)(2,1)S(1)} %get-tuple-element.40), channel_id=1, source_target_pairs={{0,16},{8,24},{16,0},{24,8},{1,17},{9,25},{17,1},{25,9},{2,18},{10... | collective-permute-start | bytes 1081352 | tf_op jit(solution)/shard_map/ppermute | solution.py:24
  20.9 1.4 %collective-permute-start.9 = (bf16[1,704,256]{2,1,0:T(8,128)(2,1)S(1)}, bf16[1,704,256]{2,1,0:T(8,128)(2,1)S(1)}, u32[]{:S(2)}, u32[]{:S(2)}) collective-permute-start(bf16[1,704,256]{2,1,0:T(8,128)(2,1)S(1)} %get-tuple-element.41), channel_id=1, source_target_pairs={{0,24},{8,16},{16,8},{24,0},{1,25},{9,17},{17,9},{25,1},{2,26},{10... | collective-permute-start | bytes 1081352 | tf_op jit(solution)/shard_map/ppermute | solution.py:24
  22.2 0.0 collective-permute-done.10.refs_5_
  22.3 0.2 collective-permute-done.11.refs_6_
  22.4 7.6 %collective-permute-done.7.refs_1_ = bf16[1,704,256]{2,1,0:T(8,128)(2,1)S(1)} collective-permute-done((bf16[1,704,256]{2,1,0:T(8,128)(2,1)S(1)}, bf16[1,704,256]{2,1,0:T(8,128)(2,1)S(1)}, u32[]{:S(2)}, u32[]{:S(2)}) %collective-permute-start.7) | collective-permute-done | bytes 360480 | tf_op jit(solution)/shard_map/ppermute | solution.py:24
  30.0 6.8 %collective-permute-done.8.refs_2_ = bf16[1,704,256]{2,1,0:T(8,128)(2,1)S(1)} collective-permute-done((bf16[1,704,256]{2,1,0:T(8,128)(2,1)S(1)}, bf16[1,704,256]{2,1,0:T(8,128)(2,1)S(1)}, u32[]{:S(2)}, u32[]{:S(2)}) %collective-permute-start.8) | collective-permute-done | bytes 360480 | tf_op jit(solution)/shard_map/ppermute | solution.py:24
  36.8 1.2 %collective-permute-done.9.refs_3_ = bf16[1,704,256]{2,1,0:T(8,128)(2,1)S(1)} collective-permute-done((bf16[1,704,256]{2,1,0:T(8,128)(2,1)S(1)}, bf16[1,704,256]{2,1,0:T(8,128)(2,1)S(1)}, u32[]{:S(2)}, u32[]{:S(2)}) %collective-permute-start.9) | collective-permute-done | bytes 360480 | tf_op jit(solution)/shard_map/ppermute | solution.py:24
  38.0 0.8 %shard_map.70 = (bf16[1,352,256]{2,1,0:T(8,128)(2,1)S(1)}, bf16[2,4,32,1536]{3,2,1,0:T(8,128)(2,1)S(1)}) custom-call(s32[1]{0:T(128)} %bitcast.1.core, bf16[1,704,256]{2,1,0:T(8,128)(2,1)S(1)} %get-tuple-element.38.refs_0_, bf16[1,704,256]{2,1,0:T(8,128)(2,1)S(1)} %collective-permute-done.7.refs_1_, bf16[1,704,256]{2,1,0:T(8,128)(2,1)S(1)} %collective-permute-done.8.refs_2_, ...), custom_call_target="tpu_custom_call" | custom-call | flops 276824064 | bytes 2523136 | tf_op jit(solution)/shard_map/pallas_call | solution.py:32
  38.8 0.1 collective-permute-start.12
  38.9 1.8 %collective-permute-start.16 = (bf16[1,352,512]{2,1,0:T(8,128)(2,1)S(1)}, bf16[1,352,512]{2,1,0:T(8,128)(2,1)S(1)}, u32[]{:S(2)}, u32[]{:S(2)}) collective-permute-start(bf16[1,352,512]{2,1,0:T(8,128)(2,1)S(1)} %get-tuple-element.46), channel_id=1, source_target_pairs={{0,24},{8,16},{16,8},{24,0},{1,25},{9,17},{17,9},{25,1},{2,26},{10... | collective-permute-start | bytes 1081352 | tf_op jit(solution)/shard_map/ppermute | solution.py:24
  40.7 0.0 collective-permute-done.12
  40.7 0.1 fusion
  40.9 1.9 %collective-permute-start.15 = (bf16[32,1536]{1,0:T(8,128)(2,1)S(1)}, bf16[32,1536]{1,0:T(8,128)(2,1)S(1)}, u32[]{:S(2)}, u32[]{:S(2)}) collective-permute-start(bf16[32,1536]{1,0:T(8,128)(2,1)S(1)} %get-tuple-element.48), channel_id=1, source_target_pairs={{0,2},{1,3},{2,0},{3,1},{4,6},{5,7},{6,4},{7,5},{8,10},{9,11},{10,... | collective-permute-start | bytes 294920 | tf_op jit(solution)/shard_map/ppermute | solution.py:24
  42.7 2.6 %collective-permute-start.14 = (bf16[32,1536]{1,0:T(8,128)(2,1)S(1)}, bf16[32,1536]{1,0:T(8,128)(2,1)S(1)}, u32[]{:S(2)}, u32[]{:S(2)}) collective-permute-start(bf16[32,1536]{1,0:T(8,128)(2,1)S(1)} %get-tuple-element.49), channel_id=1, source_target_pairs={{0,4},{1,5},{2,6},{3,7},{4,0},{5,1},{6,2},{7,3},{8,12},{9,13},{10,... | collective-permute-start | bytes 294920 | tf_op jit(solution)/shard_map/ppermute | solution.py:24
  45.3 5.3 %collective-permute-done.16.refs_0_ = bf16[1,352,512]{2,1,0:T(8,128)(2,1)S(1)} collective-permute-done((bf16[1,352,512]{2,1,0:T(8,128)(2,1)S(1)}, bf16[1,352,512]{2,1,0:T(8,128)(2,1)S(1)}, u32[]{:S(2)}, u32[]{:S(2)}) %collective-permute-start.16) | collective-permute-done | bytes 360480 | tf_op jit(solution)/shard_map/ppermute | solution.py:24
  50.6 0.0 collective-permute-done.15.refs_2_.refs_1_
  50.6 0.3 shard_map.72.source
  51.0 0.1 collective-permute-start.17
  51.1 1.3 %collective-permute-done.17 = bf16[4,32,512]{2,1,0:T(8,128)(2,1)S(1)} collective-permute-done((bf16[4,32,512]{2,1,0:T(8,128)(2,1)S(1)}, bf16[4,32,512]{2,1,0:T(8,128)(2,1)S(1)}, u32[]{:S(2)}, u32[]{:S(2)}) %collective-permute-start.17) | collective-permute-done | bytes 131104 | tf_op jit(solution)/shard_map/ppermute | solution.py:24
  52.4 1.9 %collective-permute-start.20 = (bf16[32,512]{1,0:T(8,128)(2,1)S(1)}, bf16[32,512]{1,0:T(8,128)(2,1)S(1)}, u32[]{:S(2)}, u32[]{:S(2)}) collective-permute-start(bf16[32,512]{1,0:T(8,128)(2,1)S(1)} %get-tuple-element.52), channel_id=1, source_target_pairs={{0,2},{1,3},{2,0},{3,1},{4,6},{5,7},{6,4},{7,5},{8,10},{9,11},{10,... | collective-permute-start | bytes 98312 | tf_op jit(solution)/shard_map/ppermute | solution.py:24
  54.3 2.6 %collective-permute-start.19 = (bf16[32,512]{1,0:T(8,128)(2,1)S(1)}, bf16[32,512]{1,0:T(8,128)(2,1)S(1)}, u32[]{:S(2)}, u32[]{:S(2)}) collective-permute-start(bf16[32,512]{1,0:T(8,128)(2,1)S(1)} %get-tuple-element.53), channel_id=1, source_target_pairs={{0,4},{1,5},{2,6},{3,7},{4,0},{5,1},{6,2},{7,3},{8,12},{9,13},{10,... | collective-permute-start | bytes 98312 | tf_op jit(solution)/shard_map/ppermute | solution.py:24
  56.9 0.0 collective-permute-done.14.refs_1_
  56.9 0.1 shard_map.71.early
  57.0 2.7 %collective-permute-done.19.refs_1_ = bf16[32,512]{1,0:T(8,128)(2,1)S(1)} collective-permute-done((bf16[32,512]{1,0:T(8,128)(2,1)S(1)}, bf16[32,512]{1,0:T(8,128)(2,1)S(1)}, u32[]{:S(2)}, u32[]{:S(2)}) %collective-permute-start.19) | collective-permute-done | bytes 32800 | tf_op jit(solution)/shard_map/ppermute | solution.py:24
  59.7 2.9 %collective-permute-done.18.refs_0_ = bf16[32,512]{1,0:T(8,128)(2,1)S(1)} collective-permute-done((bf16[32,512]{1,0:T(8,128)(2,1)S(1)}, bf16[32,512]{1,0:T(8,128)(2,1)S(1)}, u32[]{:S(2)}, u32[]{:S(2)}) %collective-permute-start.18) | collective-permute-done | bytes 32800 | tf_op jit(solution)/shard_map/ppermute | solution.py:24
  62.6 0.7 %shard_map.74 = bf16[32,2048]{1,0:T(8,128)(2,1)} custom-call(s32[1]{0:T(128)} %bitcast.my_dp, bf16[32,1536]{1,0:T(8,128)(2,1)S(1)} %shard_map.71.early, bf16[32,512]{1,0:T(8,128)(2,1)S(1)} %collective-permute-done.18.refs_0_, bf16[32,512]{1,0:T(8,128)(2,1)S(1)} %collective-permute-done.19.refs_1_, bf16[32,512]{1,0:T(8,128)(2,1)S(1)} %collective-permute-done.20.refs_2_, ...), custom_call_target="tpu_custom_call" | custom-call | flops 262144 | bytes 655360 | tf_op jit(solution)/shard_map/pallas_call | solution.py:32
  (17 shorter events, 0.2 us)
Async XLA Ops:
  0.0 12.0 %copy-start = (bf16[8,352,512]{2,1,0:T(8,128)(2,1)S(1)}, bf16[8,352,512]{2,1,0:T(8,128)(2,1)}, u32[]{:S(2)}) copy-start(bf16[8,352,512]{2,1,0:T(8,128)(2,1)} %refs_0_.1) | copy-start | bytes 8650756
  0.0 16.0 %copy-start.2 = (bf16[8,512,352]{1,2,0:T(8,128)(2,1)S(1)}, bf16[8,512,352]{1,2,0:T(8,128)(2,1)}, u32[]{:S(2)}) copy-start(bf16[8,512,352]{1,2,0:T(8,128)(2,1)} %param.8) | copy-start | bytes 8650756
  1.8 14.2 %copy-start.1 = (bf16[8,512,352]{1,2,0:T(8,128)(2,1)S(1)}, bf16[8,512,352]{1,2,0:T(8,128)(2,1)}, u32[]{:S(2)}) copy-start(bf16[8,512,352]{1,2,0:T(8,128)(2,1)} %param.7) | copy-start | bytes 8650756
  1.8 8.0 %collective-permute-start.1 = (bf16[80,512]{1,0:T(8,128)(2,1)S(1)}, bf16[80,512]{1,0:T(8,128)(2,1)S(1)}, u32[]{:S(2)}, u32[]{:S(2)}) collective-permute-start(bf16[80,512]{1,0:T(8,128)(2,1)S(1)} %get-tuple-element.28), channel_id=1, source_target_pairs={{0,16},{8,24},{16,0},{24,8},{1,17},{9,25},{17,1},{25,9},{2,18},{10... | collective-permute-start | bytes 245768 | tf_op jit(solution)/shard_map/ppermute | solution.py:24
  4.9 6.7 %collective-permute-start.2 = (bf16[80,512]{1,0:T(8,128)(2,1)S(1)}, bf16[80,512]{1,0:T(8,128)(2,1)S(1)}, u32[]{:S(2)}, u32[]{:S(2)}) collective-permute-start(bf16[80,512]{1,0:T(8,128)(2,1)S(1)} %get-tuple-element.29), channel_id=1, source_target_pairs={{0,24},{8,16},{16,8},{24,0},{1,25},{9,17},{17,9},{25,1},{2,26},{10... | collective-permute-start | bytes 245768 | tf_op jit(solution)/shard_map/ppermute | solution.py:24
  6.3 5.4 %collective-permute-start = (bf16[80,512]{1,0:T(8,128)(2,1)S(1)}, bf16[80,512]{1,0:T(8,128)(2,1)S(1)}, u32[]{:S(2)}, u32[]{:S(2)}) collective-permute-start(bf16[80,512]{1,0:T(8,128)(2,1)S(1)} %get-tuple-element.27.refs_0_), channel_id=1, source_target_pairs={{0,8},{8,0},{16,24},{24,16},{1,9},{9,1},{17,25},{25,17},{2,10},{10... | collective-permute-start | bytes 245768 | tf_op jit(solution)/shard_map/ppermute | solution.py:24
  6.4 9.5 %collective-permute-start.3 = (bf16[64,512]{1,0:T(8,128)(2,1)S(1)}, bf16[64,512]{1,0:T(8,128)(2,1)S(1)}, u32[]{:S(2)}, u32[]{:S(2)}) collective-permute-start(bf16[64,512]{1,0:T(8,128)(2,1)S(1)} %get-tuple-element.30), channel_id=1, source_target_pairs={{0,8},{8,0},{16,24},{24,16},{1,9},{9,1},{17,25},{25,17},{2,10},{10... | collective-permute-start | bytes 196616 | tf_op jit(solution)/shard_map/ppermute | solution.py:24
  8.3 7.5 %collective-permute-start.4 = (bf16[64,512]{1,0:T(8,128)(2,1)S(1)}, bf16[64,512]{1,0:T(8,128)(2,1)S(1)}, u32[]{:S(2)}, u32[]{:S(2)}) collective-permute-start(bf16[64,512]{1,0:T(8,128)(2,1)S(1)} %get-tuple-element.31), channel_id=1, source_target_pairs={{0,16},{8,24},{16,0},{24,8},{1,17},{9,25},{17,1},{25,9},{2,18},{10... | collective-permute-start | bytes 196616 | tf_op jit(solution)/shard_map/ppermute | solution.py:24
  9.9 6.0 %collective-permute-start.5 = (bf16[64,512]{1,0:T(8,128)(2,1)S(1)}, bf16[64,512]{1,0:T(8,128)(2,1)S(1)}, u32[]{:S(2)}, u32[]{:S(2)}) collective-permute-start(bf16[64,512]{1,0:T(8,128)(2,1)S(1)} %get-tuple-element.32), channel_id=1, source_target_pairs={{0,24},{8,16},{16,8},{24,0},{1,25},{9,17},{17,9},{25,1},{2,26},{10... | collective-permute-start | bytes 196616 | tf_op jit(solution)/shard_map/ppermute | solution.py:24
  12.6 9.6 %collective-permute-start.10 = (bf16[1,352,512]{2,1,0:T(8,128)(2,1)S(1)}, bf16[1,352,512]{2,1,0:T(8,128)(2,1)S(1)}, u32[]{:S(2)}, u32[]{:S(2)}) collective-permute-start(bf16[1,352,512]{2,1,0:T(8,128)(2,1)S(1)} %get-tuple-element.42), channel_id=1, source_target_pairs={{0,8},{8,0},{16,24},{24,16},{1,9},{9,1},{17,25},{25,17},{2,10},{10... | collective-permute-start | bytes 1081352 | tf_op jit(solution)/shard_map/ppermute | solution.py:24
  14.4 8.1 %collective-permute-start.11 = (bf16[1,352,512]{2,1,0:T(8,128)(2,1)S(1)}, bf16[1,352,512]{2,1,0:T(8,128)(2,1)S(1)}, u32[]{:S(2)}, u32[]{:S(2)}) collective-permute-start(bf16[1,352,512]{2,1,0:T(8,128)(2,1)S(1)} %get-tuple-element.43), channel_id=1, source_target_pairs={{0,16},{8,24},{16,0},{24,8},{1,17},{9,25},{17,1},{25,9},{2,18},{10... | collective-permute-start | bytes 1081352 | tf_op jit(solution)/shard_map/ppermute | solution.py:24
  15.9 1.8 %collective-permute-start.6 = (bf16[3,128,512]{2,1,0:T(8,128)(2,1)S(1)}, bf16[3,128,512]{2,1,0:T(8,128)(2,1)S(1)}, u32[]{:S(2)}, u32[]{:S(2)}) collective-permute-start(bf16[3,128,512]{2,1,0:T(8,128)(2,1)S(1)} %shard_map.67.brought), channel_id=1, source_target_pairs={{0,1},{1,0},{2,3},{3,2},{4,5},{5,4},{6,7},{7,6},{8,9},{9,8},{10,11... | collective-permute-start | bytes 1179656 | tf_op jit(solution)/shard_map/ppermute | solution.py:24
  18.7 11.3 %collective-permute-start.7 = (bf16[1,704,256]{2,1,0:T(8,128)(2,1)S(1)}, bf16[1,704,256]{2,1,0:T(8,128)(2,1)S(1)}, u32[]{:S(2)}, u32[]{:S(2)}) collective-permute-start(bf16[1,704,256]{2,1,0:T(8,128)(2,1)S(1)} %get-tuple-element.39), channel_id=1, source_target_pairs={{0,8},{8,0},{16,24},{24,16},{1,9},{9,1},{17,25},{25,17},{2,10},{10... | collective-permute-start | bytes 1081352 | tf_op jit(solution)/shard_map/ppermute | solution.py:24
  19.3 17.5 %collective-permute-start.8 = (bf16[1,704,256]{2,1,0:T(8,128)(2,1)S(1)}, bf16[1,704,256]{2,1,0:T(8,128)(2,1)S(1)}, u32[]{:S(2)}, u32[]{:S(2)}) collective-permute-start(bf16[1,704,256]{2,1,0:T(8,128)(2,1)S(1)} %get-tuple-element.40), channel_id=1, source_target_pairs={{0,16},{8,24},{16,0},{24,8},{1,17},{9,25},{17,1},{25,9},{2,18},{10... | collective-permute-start | bytes 1081352 | tf_op jit(solution)/shard_map/ppermute | solution.py:24
  20.9 17.1 %collective-permute-start.9 = (bf16[1,704,256]{2,1,0:T(8,128)(2,1)S(1)}, bf16[1,704,256]{2,1,0:T(8,128)(2,1)S(1)}, u32[]{:S(2)}, u32[]{:S(2)}) collective-permute-start(bf16[1,704,256]{2,1,0:T(8,128)(2,1)S(1)} %get-tuple-element.41), channel_id=1, source_target_pairs={{0,24},{8,16},{16,8},{24,0},{1,25},{9,17},{17,9},{25,1},{2,26},{10... | collective-permute-start | bytes 1081352 | tf_op jit(solution)/shard_map/ppermute | solution.py:24
  38.8 1.9 %collective-permute-start.12 = (bf16[4,32,1536]{2,1,0:T(8,128)(2,1)S(1)}, bf16[4,32,1536]{2,1,0:T(8,128)(2,1)S(1)}, u32[]{:S(2)}, u32[]{:S(2)}) collective-permute-start(bf16[4,32,1536]{2,1,0:T(8,128)(2,1)S(1)} %slice_bitcast_fusion), channel_id=1, source_target_pairs={{0,1},{1,0},{2,3},{3,2},{4,5},{5,4},{6,7},{7,6},{8,9},{9,8},{10,11... | collective-permute-start | bytes 1179656 | tf_op jit(solution)/shard_map/ppermute | solution.py:24
  38.9 11.7 %collective-permute-start.16 = (bf16[1,352,512]{2,1,0:T(8,128)(2,1)S(1)}, bf16[1,352,512]{2,1,0:T(8,128)(2,1)S(1)}, u32[]{:S(2)}, u32[]{:S(2)}) collective-permute-start(bf16[1,352,512]{2,1,0:T(8,128)(2,1)S(1)} %get-tuple-element.46), channel_id=1, source_target_pairs={{0,24},{8,16},{16,8},{24,0},{1,25},{9,17},{17,9},{25,1},{2,26},{10... | collective-permute-start | bytes 1081352 | tf_op jit(solution)/shard_map/ppermute | solution.py:24
  40.9 9.8 %collective-permute-start.15 = (bf16[32,1536]{1,0:T(8,128)(2,1)S(1)}, bf16[32,1536]{1,0:T(8,128)(2,1)S(1)}, u32[]{:S(2)}, u32[]{:S(2)}) collective-permute-start(bf16[32,1536]{1,0:T(8,128)(2,1)S(1)} %get-tuple-element.48), channel_id=1, source_target_pairs={{0,2},{1,3},{2,0},{3,1},{4,6},{5,7},{6,4},{7,5},{8,10},{9,11},{10,... | collective-permute-start | bytes 294920 | tf_op jit(solution)/shard_map/ppermute | solution.py:24
  42.7 14.2 %collective-permute-start.14 = (bf16[32,1536]{1,0:T(8,128)(2,1)S(1)}, bf16[32,1536]{1,0:T(8,128)(2,1)S(1)}, u32[]{:S(2)}, u32[]{:S(2)}) collective-permute-start(bf16[32,1536]{1,0:T(8,128)(2,1)S(1)} %get-tuple-element.49), channel_id=1, source_target_pairs={{0,4},{1,5},{2,6},{3,7},{4,0},{5,1},{6,2},{7,3},{8,12},{9,13},{10,... | collective-permute-start | bytes 294920 | tf_op jit(solution)/shard_map/ppermute | solution.py:24
  45.3 11.6 %collective-permute-start.13 = (bf16[32,1536]{1,0:T(8,128)(2,1)S(1)}, bf16[32,1536]{1,0:T(8,128)(2,1)S(1)}, u32[]{:S(2)}, u32[]{:S(2)}) collective-permute-start(bf16[32,1536]{1,0:T(8,128)(2,1)S(1)} %get-tuple-element.50), channel_id=1, source_target_pairs={{0,6},{1,7},{2,4},{3,5},{4,2},{5,3},{6,0},{7,1},{8,14},{9,15},{10,... | collective-permute-start | bytes 294920 | tf_op jit(solution)/shard_map/ppermute | solution.py:24
  51.0 1.4 %collective-permute-start.17 = (bf16[4,32,512]{2,1,0:T(8,128)(2,1)S(1)}, bf16[4,32,512]{2,1,0:T(8,128)(2,1)S(1)}, u32[]{:S(2)}, u32[]{:S(2)}) collective-permute-start(bf16[4,32,512]{2,1,0:T(8,128)(2,1)S(1)} %slice_bitcast_fusion.1), channel_id=1, source_target_pairs={{0,1},{1,0},{2,3},{3,2},{4,5},{5,4},{6,7},{7,6},{8,9},{9,8},{10,11... | collective-permute-start | bytes 393224 | tf_op jit(solution)/shard_map/ppermute | solution.py:24
  52.4 4.5 %collective-permute-start.20 = (bf16[32,512]{1,0:T(8,128)(2,1)S(1)}, bf16[32,512]{1,0:T(8,128)(2,1)S(1)}, u32[]{:S(2)}, u32[]{:S(2)}) collective-permute-start(bf16[32,512]{1,0:T(8,128)(2,1)S(1)} %get-tuple-element.52), channel_id=1, source_target_pairs={{0,2},{1,3},{2,0},{3,1},{4,6},{5,7},{6,4},{7,5},{8,10},{9,11},{10,... | collective-permute-start | bytes 98312 | tf_op jit(solution)/shard_map/ppermute | solution.py:24
  54.3 5.4 %collective-permute-start.19 = (bf16[32,512]{1,0:T(8,128)(2,1)S(1)}, bf16[32,512]{1,0:T(8,128)(2,1)S(1)}, u32[]{:S(2)}, u32[]{:S(2)}) collective-permute-start(bf16[32,512]{1,0:T(8,128)(2,1)S(1)} %get-tuple-element.53), channel_id=1, source_target_pairs={{0,4},{1,5},{2,6},{3,7},{4,0},{5,1},{6,2},{7,3},{8,12},{9,13},{10,... | collective-permute-start | bytes 98312 | tf_op jit(solution)/shard_map/ppermute | solution.py:24
  56.9 5.7 %collective-permute-start.18 = (bf16[32,512]{1,0:T(8,128)(2,1)S(1)}, bf16[32,512]{1,0:T(8,128)(2,1)S(1)}, u32[]{:S(2)}, u32[]{:S(2)}) collective-permute-start(bf16[32,512]{1,0:T(8,128)(2,1)S(1)} %get-tuple-element.54), channel_id=1, source_target_pairs={{0,6},{1,7},{2,4},{3,5},{4,2},{5,3},{6,0},{7,1},{8,14},{9,15},{10,... | collective-permute-start | bytes 98312 | tf_op jit(solution)/shard_map/ppermute | solution.py:24

commit v14 on v11

--- a/solution.py
+++ b/solution.py
@@ -254,7 +254,7 @@
 
 
 def copy_kernel(source, target):
-    target[...] = source[0]
+    target[...] = source[...]
 
 
 def finish_kernel(groups, my_dp, early, *refs):
@@ -269,15 +269,30 @@
             out[:, pl.ds(at, cols)] = value[:, k * cols : (k + 1) * cols]
 
 
-def tensor_sum_pieces(mixed, lines, beside):
+def tensor_sum_pieces(mixed, lines):
     my_line = lax.axis_index("tensor") // 2
-    mine = mixed[0]
-    if beside:
-        (mine,) = call(copy_kernel, [(mine.shape, BF16)], [VMEM], (mixed,), BESIDE, 0)
-    pair = mine.astype(F32) + swap(mixed[1], "tensor", 1).astype(F32)
+    pair = mixed[0].astype(F32) + swap(mixed[1], "tensor", 1).astype(F32)
     pair = pair.astype(BF16)
     pieces = [lax.dynamic_index_in_dim(pair, my_line ^ k, 0, keepdims=False) for k in range(lines)]
     return [swap(pieces[k], "tensor", 2 * k) for k in range(lines - 1, 0, -1)] + [pieces[0]]
+
+
+def keep(value):
+    return call(copy_kernel, [(value.shape, BF16)], [VMEM], (value,), BESIDE, 0)[0]
+
+
+def tensor_halve(mixed):
+    mine, theirs = keep(mixed[0]), mixed[1]
+    step, my_line = 1, lax.axis_index("tensor") // 2
+    while mine.shape[0] > 1:
+        total = mine.astype(F32) + swap(theirs, "tensor", step).astype(F32)
+        total = total.astype(BF16).reshape(-1, 2, *mine.shape[1:])
+        side = my_line % 2
+        mine = lax.dynamic_index_in_dim(total, side, 1, keepdims=False)
+        mine = keep(mine) if mine.shape[0] > 1 else mine
+        theirs = lax.dynamic_index_in_dim(total, 1 - side, 1, keepdims=False)
+        step, my_line = 2 * step, my_line // 2
+    return [mine[0], swap(theirs[0], "tensor", step)]
 
 
 def on_device(tokens, gate_weight, up_weight, down_weight, router_weight, carry_mean):
@@ -348,7 +363,7 @@
         flops * len(early),
         2 * (own_rows * hidden_count * dp * 2 + hidden_count * cols * len(early)),
     )
-    early_pieces = tensor_sum_pieces(mixed, lines, False)
+    early_pieces = tensor_sum_pieces(mixed, lines)
     (mixed,) = call(
         functools.partial(second_kernel, len(late)),
         [((2, lines, rows, len(late) * cols), BF16)],
@@ -357,7 +372,7 @@
         flops * len(late),
         2 * (own_rows * hidden_count + hidden_count * cols * len(late)),
     )
-    late_pieces = tensor_sum_pieces(mixed, lines, True)
+    late_pieces = tensor_halve(mixed)
     (early_sum,) = call(
         sum_kernel,
         [(early_pieces[0].shape, BF16)],
@@ -369,7 +384,7 @@
     (out,) = call(
         functools.partial(finish_kernel, (early, late)),
         [((rows, width), BF16)],
-        [SMEM] + [VMEM] * (1 + lines),
+        [SMEM] + [VMEM] * (1 + len(late_pieces)),
         (my_dp, early_sum, *late_pieces),
         rows * width * lines,
         2 * rows * width * (lines + 1),

time: 63.5 us -> 66.2 us (1.043)
  waiting for transfers between devices: 28.8 us -> 34.4 us
  starting transfers between devices: 27.6 us -> 24.7 us
    ppermute x21 -> x20, waiting for transfers between devices: 28.8 us -> 34.4 us  [swap(): return lax.ppermute(value, axis, [(i, i ^ step) for i in range(count)])]
    ppermute x21 -> x20, starting transfers between devices: 27.6 us -> 24.7 us  [swap(): return lax.ppermute(value, axis, [(i, i ^ step) for i in range(count)])]
    pallas_call x11 -> x12, Pallas kernels: 6.48 us -> 6.48 us  [call(): pl.pallas_call(kernel, out_shape=[jax.ShapeDtypeStruct(shape, dtype) for...]
  transfers between devices with their start and end apart: 21 -> 20, of which waited for: 10 -> 12; matrix products, arithmetic and copies ran while one was open for 0% -> 0% of each run, Pallas kernels for 5% -> 5%
where the time goes in v14:
time: 66.2 us; the launch traced here: 66.1 us
  waiting for transfers between devices  34.4 us (52%)
  starting transfers between devices  24.7 us (37%)
  Pallas kernels  6.48 us (10%)
    ppermute x20, waiting for transfers between devices, swap(): return lax.ppermute(value, axis, [(i, i ^ step) for i in range(count)])  34.4 us
    ppermute x20, starting transfers between devices, swap(): return lax.ppermute(value, axis, [(i, i ^ step) for i in range(count)])  24.7 us
    pallas_call x12, Pallas kernels, call(): pl.pallas_call(kernel, out_shape=[jax.ShapeDtypeStruct(shape, dtype) for...  6.48 us
  transfers between devices with their start and end apart: 20, of which 12 were waited for; matrix products, arithmetic and copies ran while one was open for 0% of the time, Pallas kernels for 5%

profile of v14, /device:TPU:0, one launch (start us, length us, event | category | flops | bytes accessed | tf_op | source)
XLA Modules:
  0.0 66.1 jit_solution(6649274169646758368)
XLA Ops:
  0.0 1.8 %shard_map.64 = (bf16[256,512]{1,0:T(8,128)(2,1)S(1)}, bf16[80,512]{1,0:T(8,128)(2,1)S(1)}, bf16[80,512]{1,0:T(8,128)(2,1)S(1)}, bf16[80,512]{1,0:T(8,128)(2,1)S...) custom-call(s32[1]{0:T(128)} %bitcast.my_dp, s32[1]{0:T(128)} %bitcast.1.core, ...), custom_call_target="tpu_custom_call" | custom-call | flops 10000000000 | bytes 2097152 | tf_op jit(solution)/shard_map/pallas_call | solution.py:32
  1.8 0.0 copy-start.1
  1.8 3.0 %collective-permute-start = (bf16[80,512]{1,0:T(8,128)(2,1)S(1)}, bf16[80,512]{1,0:T(8,128)(2,1)S(1)}, u32[]{:S(2)}, u32[]{:S(2)}) collective-permute-start(bf16[80,512]{1,0:T(8,128)(2,1)S(1)} %get-tuple-element.27.refs_0_), channel_id=1, source_target_pairs={{0,8},{8,0},{16,24},{24,16},{1,9},{9,1},{17,25},{25,17},{2,10},{10... | collective-permute-start | bytes 245768 | tf_op jit(solution)/shard_map/ppermute | solution.py:24
  4.8 1.5 %collective-permute-start.1 = (bf16[80,512]{1,0:T(8,128)(2,1)S(1)}, bf16[80,512]{1,0:T(8,128)(2,1)S(1)}, u32[]{:S(2)}, u32[]{:S(2)}) collective-permute-start(bf16[80,512]{1,0:T(8,128)(2,1)S(1)} %get-tuple-element.28), channel_id=1, source_target_pairs={{0,16},{8,24},{16,0},{24,8},{1,17},{9,25},{17,1},{25,9},{2,18},{10... | collective-permute-start | bytes 245768 | tf_op jit(solution)/shard_map/ppermute | solution.py:24
  6.4 0.0 collective-permute-start.2
  6.4 1.9 %collective-permute-start.3 = (bf16[64,512]{1,0:T(8,128)(2,1)S(1)}, bf16[64,512]{1,0:T(8,128)(2,1)S(1)}, u32[]{:S(2)}, u32[]{:S(2)}) collective-permute-start(bf16[64,512]{1,0:T(8,128)(2,1)S(1)} %get-tuple-element.30), channel_id=1, source_target_pairs={{0,8},{8,0},{16,24},{24,16},{1,9},{9,1},{17,25},{25,17},{2,10},{10... | collective-permute-start | bytes 196616 | tf_op jit(solution)/shard_map/ppermute | solution.py:24
  8.3 1.5 %collective-permute-start.4 = (bf16[64,512]{1,0:T(8,128)(2,1)S(1)}, bf16[64,512]{1,0:T(8,128)(2,1)S(1)}, u32[]{:S(2)}, u32[]{:S(2)}) collective-permute-start(bf16[64,512]{1,0:T(8,128)(2,1)S(1)} %get-tuple-element.31), channel_id=1, source_target_pairs={{0,16},{8,24},{16,0},{24,8},{1,17},{9,25},{17,1},{25,9},{2,18},{10... | collective-permute-start | bytes 196616 | tf_op jit(solution)/shard_map/ppermute | solution.py:24
  9.9 1.0 %collective-permute-start.5 = (bf16[64,512]{1,0:T(8,128)(2,1)S(1)}, bf16[64,512]{1,0:T(8,128)(2,1)S(1)}, u32[]{:S(2)}, u32[]{:S(2)}) collective-permute-start(bf16[64,512]{1,0:T(8,128)(2,1)S(1)} %get-tuple-element.32), channel_id=1, source_target_pairs={{0,24},{8,16},{16,8},{24,0},{1,25},{9,17},{17,9},{25,1},{2,26},{10... | collective-permute-start | bytes 196616 | tf_op jit(solution)/shard_map/ppermute | solution.py:24
  10.8 0.0 collective-permute-done.1.refs_2_.refs_1_
  10.8 0.9 %collective-permute-done.2.refs_3_.refs_2_ = bf16[80,512]{1,0:T(8,128)(2,1)S(1)} collective-permute-done((bf16[80,512]{1,0:T(8,128)(2,1)S(1)}, bf16[80,512]{1,0:T(8,128)(2,1)S(1)}, u32[]{:S(2)}, u32[]{:S(2)}) %collective-permute-start.2) | collective-permute-done | bytes 81952 | tf_op jit(solution)/shard_map/ppermute | solution.py:24
  11.7 0.3 shard_map.65.mix_ref
  12.1 0.5 shard_map.66
  12.7 0.6 collective-permute-done.4.refs_4_
  13.2 1.8 %collective-permute-done.5.refs_5_ = bf16[64,512]{1,0:T(8,128)(2,1)S(1)} collective-permute-done((bf16[64,512]{1,0:T(8,128)(2,1)S(1)}, bf16[64,512]{1,0:T(8,128)(2,1)S(1)}, u32[]{:S(2)}, u32[]{:S(2)}) %collective-permute-start.5) | collective-permute-done | bytes 65568 | tf_op jit(solution)/shard_map/ppermute | solution.py:24
  15.1 0.1 collective-permute-start.6
  15.1 0.6 collective-permute-start.10
  15.7 1.0 %collective-permute-start.11 = (bf16[1,352,512]{2,1,0:T(8,128)(2,1)S(1)}, bf16[1,352,512]{2,1,0:T(8,128)(2,1)S(1)}, u32[]{:S(2)}, u32[]{:S(2)}) collective-permute-start(bf16[1,352,512]{2,1,0:T(8,128)(2,1)S(1)} %get-tuple-element.43), channel_id=1, source_target_pairs={{0,16},{8,24},{16,0},{24,8},{1,17},{9,25},{17,1},{25,9},{2,18},{10... | collective-permute-start | bytes 1081352 | tf_op jit(solution)/shard_map/ppermute | solution.py:24
  16.7 0.9 %shard_map.68 = (bf16[1,704,512]{2,1,0:T(8,128)(2,1)S(1)}, bf16[1,704,512]{2,1,0:T(8,128)(2,1)S(1)}, bf16[1,704,512]{2,1,0:T(8,128)(2,1)S(1)}, bf16[1,704,512]{2,1,0:T(8,128)(2,1)S(1)}) custom-call(bf16[128,256]{1,0:T(8,128)(2,1)S(1)} %shard_map.65.mix_ref, bf16[8,352,512]{2,1,0:T(8,128)(2,1)S(1)} %bitcast.36, bf16[8,352,512]{2,1,0:T(8,128)(2,1)S(1)} %bitcast.37), custom_call_target="tpu_custom_call" | custom-call | flops 10000000000 | bytes 8650752 | tf_op jit(solution)/shard_map/pallas_call | solution.py:32
  17.7 1.0 %shard_map.69 = (bf16[1,704,256]{2,1,0:T(8,128)(2,1)S(1)}, bf16[1,704,256]{2,1,0:T(8,128)(2,1)S(1)}, bf16[1,704,256]{2,1,0:T(8,128)(2,1)S(1)}, bf16[1,704,256]{2,1,0:T(8,128)(2,1)S(1)}) custom-call(s32[1]{0:T(128)} %bitcast.1.core, bf16[256,512]{1,0:T(8,128)(2,1)S(1)} %get-tuple-element.26.own, bf16[3,128,512]{2,1,0:T(8,128)(2,1)S(1)} %shard_map.67.brought, ...), custom_call_target="tpu_custom_call" | custom-call | flops 738197504 | bytes 5373952 | tf_op jit(solution)/shard_map/pallas_call | solution.py:32
  18.6 1.1 %collective-permute-start.7 = (bf16[1,704,256]{2,1,0:T(8,128)(2,1)S(1)}, bf16[1,704,256]{2,1,0:T(8,128)(2,1)S(1)}, u32[]{:S(2)}, u32[]{:S(2)}) collective-permute-start(bf16[1,704,256]{2,1,0:T(8,128)(2,1)S(1)} %get-tuple-element.39), channel_id=1, source_target_pairs={{0,8},{8,0},{16,24},{24,16},{1,9},{9,1},{17,25},{25,17},{2,10},{10... | collective-permute-start | bytes 1081352 | tf_op jit(solution)/shard_map/ppermute | solution.py:24
  19.7 1.5 %collective-permute-start.8 = (bf16[1,704,256]{2,1,0:T(8,128)(2,1)S(1)}, bf16[1,704,256]{2,1,0:T(8,128)(2,1)S(1)}, u32[]{:S(2)}, u32[]{:S(2)}) collective-permute-start(bf16[1,704,256]{2,1,0:T(8,128)(2,1)S(1)} %get-tuple-element.40), channel_id=1, source_target_pairs={{0,16},{8,24},{16,0},{24,8},{1,17},{9,25},{17,1},{25,9},{2,18},{10... | collective-permute-start | bytes 1081352 | tf_op jit(solution)/shard_map/ppermute | solution.py:24
  21.2 1.0 %collective-permute-start.9 = (bf16[1,704,256]{2,1,0:T(8,128)(2,1)S(1)}, bf16[1,704,256]{2,1,0:T(8,128)(2,1)S(1)}, u32[]{:S(2)}, u32[]{:S(2)}) collective-permute-start(bf16[1,704,256]{2,1,0:T(8,128)(2,1)S(1)} %get-tuple-element.41), channel_id=1, source_target_pairs={{0,24},{8,16},{16,8},{24,0},{1,25},{9,17},{17,9},{25,1},{2,26},{10... | collective-permute-start | bytes 1081352 | tf_op jit(solution)/shard_map/ppermute | solution.py:24
  22.2 4.2 %collective-permute-done.10.refs_5_ = bf16[1,352,512]{2,1,0:T(8,128)(2,1)S(1)} collective-permute-done((bf16[1,352,512]{2,1,0:T(8,128)(2,1)S(1)}, bf16[1,352,512]{2,1,0:T(8,128)(2,1)S(1)}, u32[]{:S(2)}, u32[]{:S(2)}) %collective-permute-start.10) | collective-permute-done | bytes 360480 | tf_op jit(solution)/shard_map/ppermute | solution.py:24
  26.4 0.6 collective-permute-done.11.refs_6_
  27.0 7.1 %collective-permute-done.7.refs_1_ = bf16[1,704,256]{2,1,0:T(8,128)(2,1)S(1)} collective-permute-done((bf16[1,704,256]{2,1,0:T(8,128)(2,1)S(1)}, bf16[1,704,256]{2,1,0:T(8,128)(2,1)S(1)}, u32[]{:S(2)}, u32[]{:S(2)}) %collective-permute-start.7) | collective-permute-done | bytes 360480 | tf_op jit(solution)/shard_map/ppermute | solution.py:24
  34.1 7.5 %collective-permute-done.8.refs_2_ = bf16[1,704,256]{2,1,0:T(8,128)(2,1)S(1)} collective-permute-done((bf16[1,704,256]{2,1,0:T(8,128)(2,1)S(1)}, bf16[1,704,256]{2,1,0:T(8,128)(2,1)S(1)}, u32[]{:S(2)}, u32[]{:S(2)}) %collective-permute-start.8) | collective-permute-done | bytes 360480 | tf_op jit(solution)/shard_map/ppermute | solution.py:24
  41.7 0.0 collective-permute-done.9.refs_3_
  41.7 0.8 %shard_map.70 = (bf16[1,352,256]{2,1,0:T(8,128)(2,1)S(1)}, bf16[2,4,32,1536]{3,2,1,0:T(8,128)(2,1)S(1)}) custom-call(s32[1]{0:T(128)} %bitcast.1.core, bf16[1,704,256]{2,1,0:T(8,128)(2,1)S(1)} %get-tuple-element.38.refs_0_, bf16[1,704,256]{2,1,0:T(8,128)(2,1)S(1)} %collective-permute-done.7.refs_1_, bf16[1,704,256]{2,1,0:T(8,128)(2,1)S(1)} %collective-permute-done.8.refs_2_, ...), custom_call_target="tpu_custom_call" | custom-call | flops 276824064 | bytes 2523136 | tf_op jit(solution)/shard_map/pallas_call | solution.py:32
  42.5 0.1 collective-permute-start.12
  42.6 1.5 %collective-permute-start.16 = (bf16[1,352,512]{2,1,0:T(8,128)(2,1)S(1)}, bf16[1,352,512]{2,1,0:T(8,128)(2,1)S(1)}, u32[]{:S(2)}, u32[]{:S(2)}) collective-permute-start(bf16[1,352,512]{2,1,0:T(8,128)(2,1)S(1)} %get-tuple-element.46), channel_id=1, source_target_pairs={{0,24},{8,16},{16,8},{24,0},{1,25},{9,17},{17,9},{25,1},{2,26},{10... | collective-permute-start | bytes 1081352 | tf_op jit(solution)/shard_map/ppermute | solution.py:24
  44.2 0.1 collective-permute-done.12
  44.3 0.1 fusion
  44.4 3.7 %collective-permute-start.13 = (bf16[32,1536]{1,0:T(8,128)(2,1)S(1)}, bf16[32,1536]{1,0:T(8,128)(2,1)S(1)}, u32[]{:S(2)}, u32[]{:S(2)}) collective-permute-start(bf16[32,1536]{1,0:T(8,128)(2,1)S(1)} %get-tuple-element.50), channel_id=1, source_target_pairs={{0,6},{1,7},{2,4},{3,5},{4,2},{5,3},{6,0},{7,1},{8,14},{9,15},{10,... | collective-permute-start | bytes 294920 | tf_op jit(solution)/shard_map/ppermute | solution.py:24
  48.1 0.0 collective-permute-start.14
  48.1 0.8 %collective-permute-start.15 = (bf16[32,1536]{1,0:T(8,128)(2,1)S(1)}, bf16[32,1536]{1,0:T(8,128)(2,1)S(1)}, u32[]{:S(2)}, u32[]{:S(2)}) collective-permute-start(bf16[32,1536]{1,0:T(8,128)(2,1)S(1)} %get-tuple-element.48), channel_id=1, source_target_pairs={{0,2},{1,3},{2,0},{3,1},{4,6},{5,7},{6,4},{7,5},{8,10},{9,11},{10,... | collective-permute-start | bytes 294920 | tf_op jit(solution)/shard_map/ppermute | solution.py:24
  48.9 5.4 %collective-permute-done.16.refs_0_ = bf16[1,352,512]{2,1,0:T(8,128)(2,1)S(1)} collective-permute-done((bf16[1,352,512]{2,1,0:T(8,128)(2,1)S(1)}, bf16[1,352,512]{2,1,0:T(8,128)(2,1)S(1)}, u32[]{:S(2)}, u32[]{:S(2)}) %collective-permute-start.16) | collective-permute-done | bytes 360480 | tf_op jit(solution)/shard_map/ppermute | solution.py:24
  54.3 0.0 collective-permute-done.13.refs_0_.refs_1_
  54.3 0.3 shard_map.72
  54.7 0.1 collective-permute-start.17
  54.8 1.3 %collective-permute-done.17 = bf16[4,32,512]{2,1,0:T(8,128)(2,1)S(1)} collective-permute-done((bf16[4,32,512]{2,1,0:T(8,128)(2,1)S(1)}, bf16[4,32,512]{2,1,0:T(8,128)(2,1)S(1)}, u32[]{:S(2)}, u32[]{:S(2)}) %collective-permute-start.17) | collective-permute-done | bytes 131104 | tf_op jit(solution)/shard_map/ppermute | solution.py:24
  56.1 1.7 %collective-permute-start.18 = (bf16[2,32,512]{2,1,0:T(8,128)(2,1)S(1)}, bf16[2,32,512]{2,1,0:T(8,128)(2,1)S(1)}, u32[]{:S(2)}, u32[]{:S(2)}) collective-permute-start(bf16[2,32,512]{2,1,0:T(8,128)(2,1)S(1)} %get-tuple-element.54), channel_id=1, source_target_pairs={{0,2},{1,3},{2,0},{3,1},{4,6},{5,7},{6,4},{7,5},{8,10},{9,11},{10,... | collective-permute-start | bytes 196616 | tf_op jit(solution)/shard_map/ppermute | solution.py:24
  57.8 2.6 %collective-permute-done.18 = bf16[2,32,512]{2,1,0:T(8,128)(2,1)S(1)} collective-permute-done((bf16[2,32,512]{2,1,0:T(8,128)(2,1)S(1)}, bf16[2,32,512]{2,1,0:T(8,128)(2,1)S(1)}, u32[]{:S(2)}, u32[]{:S(2)}) %collective-permute-start.18) | collective-permute-done | bytes 65568 | tf_op jit(solution)/shard_map/ppermute | solution.py:24
  60.5 2.7 %collective-permute-start.19 = (bf16[32,512]{1,0:T(8,128)(2,1)S(1)}, bf16[32,512]{1,0:T(8,128)(2,1)S(1)}, u32[]{:S(2)}, u32[]{:S(2)}) collective-permute-start(bf16[32,512]{1,0:T(8,128)(2,1)S(1)} %get-tuple-element.55), channel_id=1, source_target_pairs={{0,4},{1,5},{2,6},{3,7},{4,0},{5,1},{6,2},{7,3},{8,12},{9,13},{10,... | collective-permute-start | bytes 98312 | tf_op jit(solution)/shard_map/ppermute | solution.py:24
  63.2 0.0 collective-permute-done.14.refs_1_
  63.2 0.0 collective-permute-done.15.refs_2_
  63.2 0.1 shard_map.71.early
  63.3 2.1 %collective-permute-done.19.refs_1_ = bf16[32,512]{1,0:T(8,128)(2,1)S(1)} collective-permute-done((bf16[32,512]{1,0:T(8,128)(2,1)S(1)}, bf16[32,512]{1,0:T(8,128)(2,1)S(1)}, u32[]{:S(2)}, u32[]{:S(2)}) %collective-permute-start.19) | collective-permute-done | bytes 32800 | tf_op jit(solution)/shard_map/ppermute | solution.py:24
  65.4 0.7 %shard_map.75 = bf16[32,2048]{1,0:T(8,128)(2,1)} custom-call(s32[1]{0:T(128)} %bitcast.my_dp, bf16[32,1536]{1,0:T(8,128)(2,1)S(1)} %shard_map.71.early, bf16[32,512]{1,0:T(8,128)(2,1)S(1)} %get-tuple-element.56.refs_0_, bf16[32,512]{1,0:T(8,128)(2,1)S(1)} %collective-permute-done.19.refs_1_), custom_call_target="tpu_custom_call" | custom-call | flops 262144 | bytes 655360 | tf_op jit(solution)/shard_map/pallas_call | solution.py:32
  (18 shorter events, 0.2 us)
Async XLA Ops:
  0.0 12.1 %copy-start = (bf16[8,352,512]{2,1,0:T(8,128)(2,1)S(1)}, bf16[8,352,512]{2,1,0:T(8,128)(2,1)}, u32[]{:S(2)}) copy-start(bf16[8,352,512]{2,1,0:T(8,128)(2,1)} %refs_0_.1) | copy-start | bytes 8650756
  0.0 16.7 %copy-start.2 = (bf16[8,512,352]{1,2,0:T(8,128)(2,1)S(1)}, bf16[8,512,352]{1,2,0:T(8,128)(2,1)}, u32[]{:S(2)}) copy-start(bf16[8,512,352]{1,2,0:T(8,128)(2,1)} %param.8) | copy-start | bytes 8650756
  1.8 14.9 %copy-start.1 = (bf16[8,512,352]{1,2,0:T(8,128)(2,1)S(1)}, bf16[8,512,352]{1,2,0:T(8,128)(2,1)}, u32[]{:S(2)}) copy-start(bf16[8,512,352]{1,2,0:T(8,128)(2,1)} %param.7) | copy-start | bytes 8650756
  1.8 8.0 %collective-permute-start = (bf16[80,512]{1,0:T(8,128)(2,1)S(1)}, bf16[80,512]{1,0:T(8,128)(2,1)S(1)}, u32[]{:S(2)}, u32[]{:S(2)}) collective-permute-start(bf16[80,512]{1,0:T(8,128)(2,1)S(1)} %get-tuple-element.27.refs_0_), channel_id=1, source_target_pairs={{0,8},{8,0},{16,24},{24,16},{1,9},{9,1},{17,25},{25,17},{2,10},{10... | collective-permute-start | bytes 245768 | tf_op jit(solution)/shard_map/ppermute | solution.py:24
  4.8 6.0 %collective-permute-start.1 = (bf16[80,512]{1,0:T(8,128)(2,1)S(1)}, bf16[80,512]{1,0:T(8,128)(2,1)S(1)}, u32[]{:S(2)}, u32[]{:S(2)}) collective-permute-start(bf16[80,512]{1,0:T(8,128)(2,1)S(1)} %get-tuple-element.28), channel_id=1, source_target_pairs={{0,16},{8,24},{16,0},{24,8},{1,17},{9,25},{17,1},{25,9},{2,18},{10... | collective-permute-start | bytes 245768 | tf_op jit(solution)/shard_map/ppermute | solution.py:24
  6.4 5.4 %collective-permute-start.2 = (bf16[80,512]{1,0:T(8,128)(2,1)S(1)}, bf16[80,512]{1,0:T(8,128)(2,1)S(1)}, u32[]{:S(2)}, u32[]{:S(2)}) collective-permute-start(bf16[80,512]{1,0:T(8,128)(2,1)S(1)} %get-tuple-element.29), channel_id=1, source_target_pairs={{0,24},{8,16},{16,8},{24,0},{1,25},{9,17},{17,9},{25,1},{2,26},{10... | collective-permute-start | bytes 245768 | tf_op jit(solution)/shard_map/ppermute | solution.py:24
  6.4 6.3 %collective-permute-start.3 = (bf16[64,512]{1,0:T(8,128)(2,1)S(1)}, bf16[64,512]{1,0:T(8,128)(2,1)S(1)}, u32[]{:S(2)}, u32[]{:S(2)}) collective-permute-start(bf16[64,512]{1,0:T(8,128)(2,1)S(1)} %get-tuple-element.30), channel_id=1, source_target_pairs={{0,8},{8,0},{16,24},{24,16},{1,9},{9,1},{17,25},{25,17},{2,10},{10... | collective-permute-start | bytes 196616 | tf_op jit(solution)/shard_map/ppermute | solution.py:24
  8.3 4.9 %collective-permute-start.4 = (bf16[64,512]{1,0:T(8,128)(2,1)S(1)}, bf16[64,512]{1,0:T(8,128)(2,1)S(1)}, u32[]{:S(2)}, u32[]{:S(2)}) collective-permute-start(bf16[64,512]{1,0:T(8,128)(2,1)S(1)} %get-tuple-element.31), channel_id=1, source_target_pairs={{0,16},{8,24},{16,0},{24,8},{1,17},{9,25},{17,1},{25,9},{2,18},{10... | collective-permute-start | bytes 196616 | tf_op jit(solution)/shard_map/ppermute | solution.py:24
  9.9 5.2 %collective-permute-start.5 = (bf16[64,512]{1,0:T(8,128)(2,1)S(1)}, bf16[64,512]{1,0:T(8,128)(2,1)S(1)}, u32[]{:S(2)}, u32[]{:S(2)}) collective-permute-start(bf16[64,512]{1,0:T(8,128)(2,1)S(1)} %get-tuple-element.32), channel_id=1, source_target_pairs={{0,24},{8,16},{16,8},{24,0},{1,25},{9,17},{17,9},{25,1},{2,26},{10... | collective-permute-start | bytes 196616 | tf_op jit(solution)/shard_map/ppermute | solution.py:24
  15.1 2.6 %collective-permute-start.6 = (bf16[3,128,512]{2,1,0:T(8,128)(2,1)S(1)}, bf16[3,128,512]{2,1,0:T(8,128)(2,1)S(1)}, u32[]{:S(2)}, u32[]{:S(2)}) collective-permute-start(bf16[3,128,512]{2,1,0:T(8,128)(2,1)S(1)} %shard_map.67.brought), channel_id=1, source_target_pairs={{0,1},{1,0},{2,3},{3,2},{4,5},{5,4},{6,7},{7,6},{8,9},{9,8},{10,11... | collective-permute-start | bytes 1179656 | tf_op jit(solution)/shard_map/ppermute | solution.py:24
  15.1 11.3 %collective-permute-start.10 = (bf16[1,352,512]{2,1,0:T(8,128)(2,1)S(1)}, bf16[1,352,512]{2,1,0:T(8,128)(2,1)S(1)}, u32[]{:S(2)}, u32[]{:S(2)}) collective-permute-start(bf16[1,352,512]{2,1,0:T(8,128)(2,1)S(1)} %get-tuple-element.42), channel_id=1, source_target_pairs={{0,8},{8,0},{16,24},{24,16},{1,9},{9,1},{17,25},{25,17},{2,10},{10... | collective-permute-start | bytes 1081352 | tf_op jit(solution)/shard_map/ppermute | solution.py:24
  15.7 11.3 %collective-permute-start.11 = (bf16[1,352,512]{2,1,0:T(8,128)(2,1)S(1)}, bf16[1,352,512]{2,1,0:T(8,128)(2,1)S(1)}, u32[]{:S(2)}, u32[]{:S(2)}) collective-permute-start(bf16[1,352,512]{2,1,0:T(8,128)(2,1)S(1)} %get-tuple-element.43), channel_id=1, source_target_pairs={{0,16},{8,24},{16,0},{24,8},{1,17},{9,25},{17,1},{25,9},{2,18},{10... | collective-permute-start | bytes 1081352 | tf_op jit(solution)/shard_map/ppermute | solution.py:24
  18.6 15.5 %collective-permute-start.7 = (bf16[1,704,256]{2,1,0:T(8,128)(2,1)S(1)}, bf16[1,704,256]{2,1,0:T(8,128)(2,1)S(1)}, u32[]{:S(2)}, u32[]{:S(2)}) collective-permute-start(bf16[1,704,256]{2,1,0:T(8,128)(2,1)S(1)} %get-tuple-element.39), channel_id=1, source_target_pairs={{0,8},{8,0},{16,24},{24,16},{1,9},{9,1},{17,25},{25,17},{2,10},{10... | collective-permute-start | bytes 1081352 | tf_op jit(solution)/shard_map/ppermute | solution.py:24
  19.7 21.9 %collective-permute-start.8 = (bf16[1,704,256]{2,1,0:T(8,128)(2,1)S(1)}, bf16[1,704,256]{2,1,0:T(8,128)(2,1)S(1)}, u32[]{:S(2)}, u32[]{:S(2)}) collective-permute-start(bf16[1,704,256]{2,1,0:T(8,128)(2,1)S(1)} %get-tuple-element.40), channel_id=1, source_target_pairs={{0,16},{8,24},{16,0},{24,8},{1,17},{9,25},{17,1},{25,9},{2,18},{10... | collective-permute-start | bytes 1081352 | tf_op jit(solution)/shard_map/ppermute | solution.py:24
  21.2 20.4 %collective-permute-start.9 = (bf16[1,704,256]{2,1,0:T(8,128)(2,1)S(1)}, bf16[1,704,256]{2,1,0:T(8,128)(2,1)S(1)}, u32[]{:S(2)}, u32[]{:S(2)}) collective-permute-start(bf16[1,704,256]{2,1,0:T(8,128)(2,1)S(1)} %get-tuple-element.41), channel_id=1, source_target_pairs={{0,24},{8,16},{16,8},{24,0},{1,25},{9,17},{17,9},{25,1},{2,26},{10... | collective-permute-start | bytes 1081352 | tf_op jit(solution)/shard_map/ppermute | solution.py:24
  42.5 1.8 %collective-permute-start.12 = (bf16[4,32,1536]{2,1,0:T(8,128)(2,1)S(1)}, bf16[4,32,1536]{2,1,0:T(8,128)(2,1)S(1)}, u32[]{:S(2)}, u32[]{:S(2)}) collective-permute-start(bf16[4,32,1536]{2,1,0:T(8,128)(2,1)S(1)} %slice_bitcast_fusion), channel_id=1, source_target_pairs={{0,1},{1,0},{2,3},{3,2},{4,5},{5,4},{6,7},{7,6},{8,9},{9,8},{10,11... | collective-permute-start | bytes 1179656 | tf_op jit(solution)/shard_map/ppermute | solution.py:24
  42.6 11.7 %collective-permute-start.16 = (bf16[1,352,512]{2,1,0:T(8,128)(2,1)S(1)}, bf16[1,352,512]{2,1,0:T(8,128)(2,1)S(1)}, u32[]{:S(2)}, u32[]{:S(2)}) collective-permute-start(bf16[1,352,512]{2,1,0:T(8,128)(2,1)S(1)} %get-tuple-element.46), channel_id=1, source_target_pairs={{0,24},{8,16},{16,8},{24,0},{1,25},{9,17},{17,9},{25,1},{2,26},{10... | collective-permute-start | bytes 1081352 | tf_op jit(solution)/shard_map/ppermute | solution.py:24
  44.4 9.9 %collective-permute-start.13 = (bf16[32,1536]{1,0:T(8,128)(2,1)S(1)}, bf16[32,1536]{1,0:T(8,128)(2,1)S(1)}, u32[]{:S(2)}, u32[]{:S(2)}) collective-permute-start(bf16[32,1536]{1,0:T(8,128)(2,1)S(1)} %get-tuple-element.50), channel_id=1, source_target_pairs={{0,6},{1,7},{2,4},{3,5},{4,2},{5,3},{6,0},{7,1},{8,14},{9,15},{10,... | collective-permute-start | bytes 294920 | tf_op jit(solution)/shard_map/ppermute | solution.py:24
  48.1 15.1 %collective-permute-start.14 = (bf16[32,1536]{1,0:T(8,128)(2,1)S(1)}, bf16[32,1536]{1,0:T(8,128)(2,1)S(1)}, u32[]{:S(2)}, u32[]{:S(2)}) collective-permute-start(bf16[32,1536]{1,0:T(8,128)(2,1)S(1)} %get-tuple-element.49), channel_id=1, source_target_pairs={{0,4},{1,5},{2,6},{3,7},{4,0},{5,1},{6,2},{7,3},{8,12},{9,13},{10,... | collective-permute-start | bytes 294920 | tf_op jit(solution)/shard_map/ppermute | solution.py:24
  48.1 15.1 %collective-permute-start.15 = (bf16[32,1536]{1,0:T(8,128)(2,1)S(1)}, bf16[32,1536]{1,0:T(8,128)(2,1)S(1)}, u32[]{:S(2)}, u32[]{:S(2)}) collective-permute-start(bf16[32,1536]{1,0:T(8,128)(2,1)S(1)} %get-tuple-element.48), channel_id=1, source_target_pairs={{0,2},{1,3},{2,0},{3,1},{4,6},{5,7},{6,4},{7,5},{8,10},{9,11},{10,... | collective-permute-start | bytes 294920 | tf_op jit(solution)/shard_map/ppermute | solution.py:24
  54.7 1.4 %collective-permute-start.17 = (bf16[4,32,512]{2,1,0:T(8,128)(2,1)S(1)}, bf16[4,32,512]{2,1,0:T(8,128)(2,1)S(1)}, u32[]{:S(2)}, u32[]{:S(2)}) collective-permute-start(bf16[4,32,512]{2,1,0:T(8,128)(2,1)S(1)} %get-tuple-element.52), channel_id=1, source_target_pairs={{0,1},{1,0},{2,3},{3,2},{4,5},{5,4},{6,7},{7,6},{8,9},{9,8},{10,11... | collective-permute-start | bytes 393224 | tf_op jit(solution)/shard_map/ppermute | solution.py:24
  56.1 4.3 %collective-permute-start.18 = (bf16[2,32,512]{2,1,0:T(8,128)(2,1)S(1)}, bf16[2,32,512]{2,1,0:T(8,128)(2,1)S(1)}, u32[]{:S(2)}, u32[]{:S(2)}) collective-permute-start(bf16[2,32,512]{2,1,0:T(8,128)(2,1)S(1)} %get-tuple-element.54), channel_id=1, source_target_pairs={{0,2},{1,3},{2,0},{3,1},{4,6},{5,7},{6,4},{7,5},{8,10},{9,11},{10,... | collective-permute-start | bytes 196616 | tf_op jit(solution)/shard_map/ppermute | solution.py:24
  60.5 4.9 %collective-permute-start.19 = (bf16[32,512]{1,0:T(8,128)(2,1)S(1)}, bf16[32,512]{1,0:T(8,128)(2,1)S(1)}, u32[]{:S(2)}, u32[]{:S(2)}) collective-permute-start(bf16[32,512]{1,0:T(8,128)(2,1)S(1)} %get-tuple-element.55), channel_id=1, source_target_pairs={{0,4},{1,5},{2,6},{3,7},{4,0},{5,1},{6,2},{7,3},{8,12},{9,13},{10,... | collective-permute-start | bytes 98312 | tf_op jit(solution)/shard_map/ppermute | solution.py:24

commit v15 on v14

--- a/solution.py
+++ b/solution.py
@@ -343,7 +343,7 @@
         functools.partial(stack_kernel, dp),
         [((dp - 1, own_rows // 2, depth), BF16)],
         [VMEM] * (2 * dp - 2) + [ANY],
-        (*firsts, *seconds, merged_down[0]),
+        (*firsts, *seconds, merged_down[1]),
         0,
         2 * own_rows * width,
     )

time: 66.2 us -> 66.6 us (level)
  waiting for transfers between devices: 34.4 us -> 35.2 us
    ppermute x20, waiting for transfers between devices: 34.4 us -> 35.2 us  [swap(): return lax.ppermute(value, axis, [(i, i ^ step) for i in range(count)])]
where the time goes in v15:
time: 66.6 us; the launch traced here: 66.5 us
  waiting for transfers between devices  35.2 us (53%)
  starting transfers between devices  24.3 us (36%)
  Pallas kernels  6.46 us (10%)
    ppermute x20, waiting for transfers between devices, swap(): return lax.ppermute(value, axis, [(i, i ^ step) for i in range(count)])  35.2 us
    ppermute x20, starting transfers between devices, swap(): return lax.ppermute(value, axis, [(i, i ^ step) for i in range(count)])  24.3 us
    pallas_call x12, Pallas kernels, call(): pl.pallas_call(kernel, out_shape=[jax.ShapeDtypeStruct(shape, dtype) for...  6.46 us
  transfers between devices with their start and end apart: 20, of which 12 were waited for; matrix products, arithmetic and copies ran while one was open for 0% of the time, Pallas kernels for 5%

profile of v15, /device:TPU:0, one launch (start us, length us, event | category | flops | bytes accessed | tf_op | source)
XLA Modules:
  0.0 66.5 jit_solution(12531233295208659130)
XLA Ops:
  0.0 1.8 %shard_map.64 = (bf16[256,512]{1,0:T(8,128)(2,1)S(1)}, bf16[80,512]{1,0:T(8,128)(2,1)S(1)}, bf16[80,512]{1,0:T(8,128)(2,1)S(1)}, bf16[80,512]{1,0:T(8,128)(2,1)S...) custom-call(s32[1]{0:T(128)} %bitcast.my_dp, s32[1]{0:T(128)} %bitcast.1.core, ...), custom_call_target="tpu_custom_call" | custom-call | flops 10000000000 | bytes 2097152 | tf_op jit(solution)/shard_map/pallas_call | solution.py:32
  1.8 0.0 copy-start.1
  1.8 3.0 %collective-permute-start = (bf16[80,512]{1,0:T(8,128)(2,1)S(1)}, bf16[80,512]{1,0:T(8,128)(2,1)S(1)}, u32[]{:S(2)}, u32[]{:S(2)}) collective-permute-start(bf16[80,512]{1,0:T(8,128)(2,1)S(1)} %get-tuple-element.27.refs_0_), channel_id=1, source_target_pairs={{0,8},{8,0},{16,24},{24,16},{1,9},{9,1},{17,25},{25,17},{2,10},{10... | collective-permute-start | bytes 245768 | tf_op jit(solution)/shard_map/ppermute | solution.py:24
  4.8 1.5 %collective-permute-start.1 = (bf16[80,512]{1,0:T(8,128)(2,1)S(1)}, bf16[80,512]{1,0:T(8,128)(2,1)S(1)}, u32[]{:S(2)}, u32[]{:S(2)}) collective-permute-start(bf16[80,512]{1,0:T(8,128)(2,1)S(1)} %get-tuple-element.28), channel_id=1, source_target_pairs={{0,16},{8,24},{16,0},{24,8},{1,17},{9,25},{17,1},{25,9},{2,18},{10... | collective-permute-start | bytes 245768 | tf_op jit(solution)/shard_map/ppermute | solution.py:24
  6.4 0.0 collective-permute-start.2
  6.4 1.9 %collective-permute-start.3 = (bf16[64,512]{1,0:T(8,128)(2,1)S(1)}, bf16[64,512]{1,0:T(8,128)(2,1)S(1)}, u32[]{:S(2)}, u32[]{:S(2)}) collective-permute-start(bf16[64,512]{1,0:T(8,128)(2,1)S(1)} %get-tuple-element.30), channel_id=1, source_target_pairs={{0,8},{8,0},{16,24},{24,16},{1,9},{9,1},{17,25},{25,17},{2,10},{10... | collective-permute-start | bytes 196616 | tf_op jit(solution)/shard_map/ppermute | solution.py:24
  8.3 1.5 %collective-permute-start.4 = (bf16[64,512]{1,0:T(8,128)(2,1)S(1)}, bf16[64,512]{1,0:T(8,128)(2,1)S(1)}, u32[]{:S(2)}, u32[]{:S(2)}) collective-permute-start(bf16[64,512]{1,0:T(8,128)(2,1)S(1)} %get-tuple-element.31), channel_id=1, source_target_pairs={{0,16},{8,24},{16,0},{24,8},{1,17},{9,25},{17,1},{25,9},{2,18},{10... | collective-permute-start | bytes 196616 | tf_op jit(solution)/shard_map/ppermute | solution.py:24
  9.9 0.0 collective-permute-done.refs_1_.refs_0_
  9.9 1.0 %collective-permute-start.5 = (bf16[64,512]{1,0:T(8,128)(2,1)S(1)}, bf16[64,512]{1,0:T(8,128)(2,1)S(1)}, u32[]{:S(2)}, u32[]{:S(2)}) collective-permute-start(bf16[64,512]{1,0:T(8,128)(2,1)S(1)} %get-tuple-element.32), channel_id=1, source_target_pairs={{0,24},{8,16},{16,8},{24,0},{1,25},{9,17},{17,9},{25,1},{2,26},{10... | collective-permute-start | bytes 196616 | tf_op jit(solution)/shard_map/ppermute | solution.py:24
  10.8 0.9 %collective-permute-done.2.refs_3_.refs_2_ = bf16[80,512]{1,0:T(8,128)(2,1)S(1)} collective-permute-done((bf16[80,512]{1,0:T(8,128)(2,1)S(1)}, bf16[80,512]{1,0:T(8,128)(2,1)S(1)}, u32[]{:S(2)}, u32[]{:S(2)}) %collective-permute-start.2) | collective-permute-done | bytes 81952 | tf_op jit(solution)/shard_map/ppermute | solution.py:24
  11.7 0.3 shard_map.65.mix_ref
  12.1 0.5 shard_map.66
  12.7 1.5 %collective-permute-start.10 = (bf16[1,352,512]{2,1,0:T(8,128)(2,1)S(1)}, bf16[1,352,512]{2,1,0:T(8,128)(2,1)S(1)}, u32[]{:S(2)}, u32[]{:S(2)}) collective-permute-start(bf16[1,352,512]{2,1,0:T(8,128)(2,1)S(1)} %get-tuple-element.33.refs_6_), channel_id=1, source_target_pairs={{0,8},{8,0},{16,24},{24,16},{1,9},{9,1},{17,25},{25,17},{2,10},{10... | collective-permute-start | bytes 1081352 | tf_op jit(solution)/shard_map/ppermute | solution.py:24
  14.1 0.0 collective-permute-done.3.refs_3_
  14.1 0.0 collective-permute-done.4.refs_4_
  14.1 1.6 %collective-permute-done.5.refs_5_ = bf16[64,512]{1,0:T(8,128)(2,1)S(1)} collective-permute-done((bf16[64,512]{1,0:T(8,128)(2,1)S(1)}, bf16[64,512]{1,0:T(8,128)(2,1)S(1)}, u32[]{:S(2)}, u32[]{:S(2)}) %collective-permute-start.5) | collective-permute-done | bytes 65568 | tf_op jit(solution)/shard_map/ppermute | solution.py:24
  15.7 0.1 collective-permute-start.6
  15.8 0.4 collective-permute-start.11
  16.3 0.9 %shard_map.68 = (bf16[1,704,512]{2,1,0:T(8,128)(2,1)S(1)}, bf16[1,704,512]{2,1,0:T(8,128)(2,1)S(1)}, bf16[1,704,512]{2,1,0:T(8,128)(2,1)S(1)}, bf16[1,704,512]{2,1,0:T(8,128)(2,1)S(1)}) custom-call(bf16[128,256]{1,0:T(8,128)(2,1)S(1)} %shard_map.65.mix_ref, bf16[8,352,512]{2,1,0:T(8,128)(2,1)S(1)} %bitcast.36, bf16[8,352,512]{2,1,0:T(8,128)(2,1)S(1)} %bitcast.37), custom_call_target="tpu_custom_call" | custom-call | flops 10000000000 | bytes 8650752 | tf_op jit(solution)/shard_map/pallas_call | solution.py:32
  17.2 0.3 collective-permute-done.6.other
  17.5 1.0 %shard_map.69 = (bf16[1,704,256]{2,1,0:T(8,128)(2,1)S(1)}, bf16[1,704,256]{2,1,0:T(8,128)(2,1)S(1)}, bf16[1,704,256]{2,1,0:T(8,128)(2,1)S(1)}, bf16[1,704,256]{2,1,0:T(8,128)(2,1)S(1)}) custom-call(s32[1]{0:T(128)} %bitcast.1.core, bf16[256,512]{1,0:T(8,128)(2,1)S(1)} %get-tuple-element.26.own, bf16[3,128,512]{2,1,0:T(8,128)(2,1)S(1)} %shard_map.67.brought, ...), custom_call_target="tpu_custom_call" | custom-call | flops 738197504 | bytes 5373952 | tf_op jit(solution)/shard_map/pallas_call | solution.py:32
  18.5 0.7 collective-permute-start.7
  19.2 1.3 %collective-permute-start.8 = (bf16[1,704,256]{2,1,0:T(8,128)(2,1)S(1)}, bf16[1,704,256]{2,1,0:T(8,128)(2,1)S(1)}, u32[]{:S(2)}, u32[]{:S(2)}) collective-permute-start(bf16[1,704,256]{2,1,0:T(8,128)(2,1)S(1)} %get-tuple-element.40), channel_id=1, source_target_pairs={{0,16},{8,24},{16,0},{24,8},{1,17},{9,25},{17,1},{25,9},{2,18},{10... | collective-permute-start | bytes 1081352 | tf_op jit(solution)/shard_map/ppermute | solution.py:24
  20.4 1.6 %collective-permute-start.9 = (bf16[1,704,256]{2,1,0:T(8,128)(2,1)S(1)}, bf16[1,704,256]{2,1,0:T(8,128)(2,1)S(1)}, u32[]{:S(2)}, u32[]{:S(2)}) collective-permute-start(bf16[1,704,256]{2,1,0:T(8,128)(2,1)S(1)} %get-tuple-element.41), channel_id=1, source_target_pairs={{0,24},{8,16},{16,8},{24,0},{1,25},{9,17},{17,9},{25,1},{2,26},{10... | collective-permute-start | bytes 1081352 | tf_op jit(solution)/shard_map/ppermute | solution.py:24
  22.1 0.2 collective-permute-done.10.refs_5_
  22.2 4.9 %collective-permute-done.11.refs_6_ = bf16[1,352,512]{2,1,0:T(8,128)(2,1)S(1)} collective-permute-done((bf16[1,352,512]{2,1,0:T(8,128)(2,1)S(1)}, bf16[1,352,512]{2,1,0:T(8,128)(2,1)S(1)}, u32[]{:S(2)}, u32[]{:S(2)}) %collective-permute-start.11) | collective-permute-done | bytes 360480 | tf_op jit(solution)/shard_map/ppermute | solution.py:24
  27.1 2.8 %collective-permute-done.7.refs_1_ = bf16[1,704,256]{2,1,0:T(8,128)(2,1)S(1)} collective-permute-done((bf16[1,704,256]{2,1,0:T(8,128)(2,1)S(1)}, bf16[1,704,256]{2,1,0:T(8,128)(2,1)S(1)}, u32[]{:S(2)}, u32[]{:S(2)}) %collective-permute-start.7) | collective-permute-done | bytes 360480 | tf_op jit(solution)/shard_map/ppermute | solution.py:24
  29.9 12.2 %collective-permute-done.8.refs_2_ = bf16[1,704,256]{2,1,0:T(8,128)(2,1)S(1)} collective-permute-done((bf16[1,704,256]{2,1,0:T(8,128)(2,1)S(1)}, bf16[1,704,256]{2,1,0:T(8,128)(2,1)S(1)}, u32[]{:S(2)}, u32[]{:S(2)}) %collective-permute-start.8) | collective-permute-done | bytes 360480 | tf_op jit(solution)/shard_map/ppermute | solution.py:24
  42.1 0.0 collective-permute-done.9.refs_3_
  42.1 0.8 %shard_map.70 = (bf16[1,352,256]{2,1,0:T(8,128)(2,1)S(1)}, bf16[2,4,32,1536]{3,2,1,0:T(8,128)(2,1)S(1)}) custom-call(s32[1]{0:T(128)} %bitcast.1.core, bf16[1,704,256]{2,1,0:T(8,128)(2,1)S(1)} %get-tuple-element.38.refs_0_, bf16[1,704,256]{2,1,0:T(8,128)(2,1)S(1)} %collective-permute-done.7.refs_1_, bf16[1,704,256]{2,1,0:T(8,128)(2,1)S(1)} %collective-permute-done.8.refs_2_, ...), custom_call_target="tpu_custom_call" | custom-call | flops 276824064 | bytes 2523136 | tf_op jit(solution)/shard_map/pallas_call | solution.py:32
  42.9 0.1 collective-permute-start.12
  43.0 0.8 %collective-permute-start.16 = (bf16[1,352,512]{2,1,0:T(8,128)(2,1)S(1)}, bf16[1,352,512]{2,1,0:T(8,128)(2,1)S(1)}, u32[]{:S(2)}, u32[]{:S(2)}) collective-permute-start(bf16[1,352,512]{2,1,0:T(8,128)(2,1)S(1)} %get-tuple-element.46), channel_id=1, source_target_pairs={{0,24},{8,16},{16,8},{24,0},{1,25},{9,17},{17,9},{25,1},{2,26},{10... | collective-permute-start | bytes 1081352 | tf_op jit(solution)/shard_map/ppermute | solution.py:24
  43.9 0.8 %collective-permute-done.12 = bf16[4,32,1536]{2,1,0:T(8,128)(2,1)S(1)} collective-permute-done((bf16[4,32,1536]{2,1,0:T(8,128)(2,1)S(1)}, bf16[4,32,1536]{2,1,0:T(8,128)(2,1)S(1)}, u32[]{:S(2)}, u32[]{:S(2)}) %collective-permute-start.12) | collective-permute-done | bytes 393248 | tf_op jit(solution)/shard_map/ppermute | solution.py:24
  44.7 0.1 fusion
  44.9 3.7 %collective-permute-start.13 = (bf16[32,1536]{1,0:T(8,128)(2,1)S(1)}, bf16[32,1536]{1,0:T(8,128)(2,1)S(1)}, u32[]{:S(2)}, u32[]{:S(2)}) collective-permute-start(bf16[32,1536]{1,0:T(8,128)(2,1)S(1)} %get-tuple-element.50), channel_id=1, source_target_pairs={{0,6},{1,7},{2,4},{3,5},{4,2},{5,3},{6,0},{7,1},{8,14},{9,15},{10,... | collective-permute-start | bytes 294920 | tf_op jit(solution)/shard_map/ppermute | solution.py:24
  48.5 0.8 %collective-permute-start.15 = (bf16[32,1536]{1,0:T(8,128)(2,1)S(1)}, bf16[32,1536]{1,0:T(8,128)(2,1)S(1)}, u32[]{:S(2)}, u32[]{:S(2)}) collective-permute-start(bf16[32,1536]{1,0:T(8,128)(2,1)S(1)} %get-tuple-element.48), channel_id=1, source_target_pairs={{0,2},{1,3},{2,0},{3,1},{4,6},{5,7},{6,4},{7,5},{8,10},{9,11},{10,... | collective-permute-start | bytes 294920 | tf_op jit(solution)/shard_map/ppermute | solution.py:24
  49.3 5.4 %collective-permute-done.16.refs_0_ = bf16[1,352,512]{2,1,0:T(8,128)(2,1)S(1)} collective-permute-done((bf16[1,352,512]{2,1,0:T(8,128)(2,1)S(1)}, bf16[1,352,512]{2,1,0:T(8,128)(2,1)S(1)}, u32[]{:S(2)}, u32[]{:S(2)}) %collective-permute-start.16) | collective-permute-done | bytes 360480 | tf_op jit(solution)/shard_map/ppermute | solution.py:24
  54.7 0.3 shard_map.72
  55.1 0.1 collective-permute-start.17
  55.2 1.3 %collective-permute-done.17 = bf16[4,32,512]{2,1,0:T(8,128)(2,1)S(1)} collective-permute-done((bf16[4,32,512]{2,1,0:T(8,128)(2,1)S(1)}, bf16[4,32,512]{2,1,0:T(8,128)(2,1)S(1)}, u32[]{:S(2)}, u32[]{:S(2)}) %collective-permute-start.17) | collective-permute-done | bytes 131104 | tf_op jit(solution)/shard_map/ppermute | solution.py:24
  56.5 1.7 %collective-permute-start.18 = (bf16[2,32,512]{2,1,0:T(8,128)(2,1)S(1)}, bf16[2,32,512]{2,1,0:T(8,128)(2,1)S(1)}, u32[]{:S(2)}, u32[]{:S(2)}) collective-permute-start(bf16[2,32,512]{2,1,0:T(8,128)(2,1)S(1)} %get-tuple-element.54), channel_id=1, source_target_pairs={{0,2},{1,3},{2,0},{3,1},{4,6},{5,7},{6,4},{7,5},{8,10},{9,11},{10,... | collective-permute-start | bytes 196616 | tf_op jit(solution)/shard_map/ppermute | solution.py:24
  58.2 2.6 %collective-permute-done.18 = bf16[2,32,512]{2,1,0:T(8,128)(2,1)S(1)} collective-permute-done((bf16[2,32,512]{2,1,0:T(8,128)(2,1)S(1)}, bf16[2,32,512]{2,1,0:T(8,128)(2,1)S(1)}, u32[]{:S(2)}, u32[]{:S(2)}) %collective-permute-start.18) | collective-permute-done | bytes 65568 | tf_op jit(solution)/shard_map/ppermute | solution.py:24
  60.9 2.7 %collective-permute-start.19 = (bf16[32,512]{1,0:T(8,128)(2,1)S(1)}, bf16[32,512]{1,0:T(8,128)(2,1)S(1)}, u32[]{:S(2)}, u32[]{:S(2)}) collective-permute-start(bf16[32,512]{1,0:T(8,128)(2,1)S(1)} %get-tuple-element.55), channel_id=1, source_target_pairs={{0,4},{1,5},{2,6},{3,7},{4,0},{5,1},{6,2},{7,3},{8,12},{9,13},{10,... | collective-permute-start | bytes 98312 | tf_op jit(solution)/shard_map/ppermute | solution.py:24
  63.6 0.0 collective-permute-done.14.refs_1_
  63.6 0.0 collective-permute-done.15.refs_2_
  63.6 0.1 shard_map.71.early
  63.7 2.1 %collective-permute-done.19.refs_1_ = bf16[32,512]{1,0:T(8,128)(2,1)S(1)} collective-permute-done((bf16[32,512]{1,0:T(8,128)(2,1)S(1)}, bf16[32,512]{1,0:T(8,128)(2,1)S(1)}, u32[]{:S(2)}, u32[]{:S(2)}) %collective-permute-start.19) | collective-permute-done | bytes 32800 | tf_op jit(solution)/shard_map/ppermute | solution.py:24
  65.8 0.7 %shard_map.75 = bf16[32,2048]{1,0:T(8,128)(2,1)} custom-call(s32[1]{0:T(128)} %bitcast.my_dp, bf16[32,1536]{1,0:T(8,128)(2,1)S(1)} %shard_map.71.early, bf16[32,512]{1,0:T(8,128)(2,1)S(1)} %get-tuple-element.56.refs_0_, bf16[32,512]{1,0:T(8,128)(2,1)S(1)} %collective-permute-done.19.refs_1_), custom_call_target="tpu_custom_call" | custom-call | flops 262144 | bytes 655360 | tf_op jit(solution)/shard_map/pallas_call | solution.py:32
  (18 shorter events, 0.2 us)
Async XLA Ops:
  0.0 12.1 %copy-start = (bf16[8,352,512]{2,1,0:T(8,128)(2,1)S(1)}, bf16[8,352,512]{2,1,0:T(8,128)(2,1)}, u32[]{:S(2)}) copy-start(bf16[8,352,512]{2,1,0:T(8,128)(2,1)} %refs_0_.1) | copy-start | bytes 8650756
  0.0 16.3 %copy-start.2 = (bf16[8,512,352]{1,2,0:T(8,128)(2,1)S(1)}, bf16[8,512,352]{1,2,0:T(8,128)(2,1)}, u32[]{:S(2)}) copy-start(bf16[8,512,352]{1,2,0:T(8,128)(2,1)} %param.8) | copy-start | bytes 8650756
  1.8 14.4 %copy-start.1 = (bf16[8,512,352]{1,2,0:T(8,128)(2,1)S(1)}, bf16[8,512,352]{1,2,0:T(8,128)(2,1)}, u32[]{:S(2)}) copy-start(bf16[8,512,352]{1,2,0:T(8,128)(2,1)} %param.7) | copy-start | bytes 8650756
  1.8 8.0 %collective-permute-start = (bf16[80,512]{1,0:T(8,128)(2,1)S(1)}, bf16[80,512]{1,0:T(8,128)(2,1)S(1)}, u32[]{:S(2)}, u32[]{:S(2)}) collective-permute-start(bf16[80,512]{1,0:T(8,128)(2,1)S(1)} %get-tuple-element.27.refs_0_), channel_id=1, source_target_pairs={{0,8},{8,0},{16,24},{24,16},{1,9},{9,1},{17,25},{25,17},{2,10},{10... | collective-permute-start | bytes 245768 | tf_op jit(solution)/shard_map/ppermute | solution.py:24
  4.8 6.0 %collective-permute-start.1 = (bf16[80,512]{1,0:T(8,128)(2,1)S(1)}, bf16[80,512]{1,0:T(8,128)(2,1)S(1)}, u32[]{:S(2)}, u32[]{:S(2)}) collective-permute-start(bf16[80,512]{1,0:T(8,128)(2,1)S(1)} %get-tuple-element.28), channel_id=1, source_target_pairs={{0,16},{8,24},{16,0},{24,8},{1,17},{9,25},{17,1},{25,9},{2,18},{10... | collective-permute-start | bytes 245768 | tf_op jit(solution)/shard_map/ppermute | solution.py:24
  6.4 5.4 %collective-permute-start.2 = (bf16[80,512]{1,0:T(8,128)(2,1)S(1)}, bf16[80,512]{1,0:T(8,128)(2,1)S(1)}, u32[]{:S(2)}, u32[]{:S(2)}) collective-permute-start(bf16[80,512]{1,0:T(8,128)(2,1)S(1)} %get-tuple-element.29), channel_id=1, source_target_pairs={{0,24},{8,16},{16,8},{24,0},{1,25},{9,17},{17,9},{25,1},{2,26},{10... | collective-permute-start | bytes 245768 | tf_op jit(solution)/shard_map/ppermute | solution.py:24
  6.4 7.7 %collective-permute-start.3 = (bf16[64,512]{1,0:T(8,128)(2,1)S(1)}, bf16[64,512]{1,0:T(8,128)(2,1)S(1)}, u32[]{:S(2)}, u32[]{:S(2)}) collective-permute-start(bf16[64,512]{1,0:T(8,128)(2,1)S(1)} %get-tuple-element.30), channel_id=1, source_target_pairs={{0,8},{8,0},{16,24},{24,16},{1,9},{9,1},{17,25},{25,17},{2,10},{10... | collective-permute-start | bytes 196616 | tf_op jit(solution)/shard_map/ppermute | solution.py:24
  8.3 5.8 %collective-permute-start.4 = (bf16[64,512]{1,0:T(8,128)(2,1)S(1)}, bf16[64,512]{1,0:T(8,128)(2,1)S(1)}, u32[]{:S(2)}, u32[]{:S(2)}) collective-permute-start(bf16[64,512]{1,0:T(8,128)(2,1)S(1)} %get-tuple-element.31), channel_id=1, source_target_pairs={{0,16},{8,24},{16,0},{24,8},{1,17},{9,25},{17,1},{25,9},{2,18},{10... | collective-permute-start | bytes 196616 | tf_op jit(solution)/shard_map/ppermute | solution.py:24
  9.9 5.8 %collective-permute-start.5 = (bf16[64,512]{1,0:T(8,128)(2,1)S(1)}, bf16[64,512]{1,0:T(8,128)(2,1)S(1)}, u32[]{:S(2)}, u32[]{:S(2)}) collective-permute-start(bf16[64,512]{1,0:T(8,128)(2,1)S(1)} %get-tuple-element.32), channel_id=1, source_target_pairs={{0,24},{8,16},{16,8},{24,0},{1,25},{9,17},{17,9},{25,1},{2,26},{10... | collective-permute-start | bytes 196616 | tf_op jit(solution)/shard_map/ppermute | solution.py:24
  12.7 9.6 %collective-permute-start.10 = (bf16[1,352,512]{2,1,0:T(8,128)(2,1)S(1)}, bf16[1,352,512]{2,1,0:T(8,128)(2,1)S(1)}, u32[]{:S(2)}, u32[]{:S(2)}) collective-permute-start(bf16[1,352,512]{2,1,0:T(8,128)(2,1)S(1)} %get-tuple-element.33.refs_6_), channel_id=1, source_target_pairs={{0,8},{8,0},{16,24},{24,16},{1,9},{9,1},{17,25},{25,17},{2,10},{10... | collective-permute-start | bytes 1081352 | tf_op jit(solution)/shard_map/ppermute | solution.py:24
  15.7 1.8 %collective-permute-start.6 = (bf16[3,128,512]{2,1,0:T(8,128)(2,1)S(1)}, bf16[3,128,512]{2,1,0:T(8,128)(2,1)S(1)}, u32[]{:S(2)}, u32[]{:S(2)}) collective-permute-start(bf16[3,128,512]{2,1,0:T(8,128)(2,1)S(1)} %shard_map.67.brought), channel_id=1, source_target_pairs={{0,1},{1,0},{2,3},{3,2},{4,5},{5,4},{6,7},{7,6},{8,9},{9,8},{10,11... | collective-permute-start | bytes 1179656 | tf_op jit(solution)/shard_map/ppermute | solution.py:24
  15.8 11.3 %collective-permute-start.11 = (bf16[1,352,512]{2,1,0:T(8,128)(2,1)S(1)}, bf16[1,352,512]{2,1,0:T(8,128)(2,1)S(1)}, u32[]{:S(2)}, u32[]{:S(2)}) collective-permute-start(bf16[1,352,512]{2,1,0:T(8,128)(2,1)S(1)} %get-tuple-element.43), channel_id=1, source_target_pairs={{0,16},{8,24},{16,0},{24,8},{1,17},{9,25},{17,1},{25,9},{2,18},{10... | collective-permute-start | bytes 1081352 | tf_op jit(solution)/shard_map/ppermute | solution.py:24
  18.5 11.4 %collective-permute-start.7 = (bf16[1,704,256]{2,1,0:T(8,128)(2,1)S(1)}, bf16[1,704,256]{2,1,0:T(8,128)(2,1)S(1)}, u32[]{:S(2)}, u32[]{:S(2)}) collective-permute-start(bf16[1,704,256]{2,1,0:T(8,128)(2,1)S(1)} %get-tuple-element.39), channel_id=1, source_target_pairs={{0,8},{8,0},{16,24},{24,16},{1,9},{9,1},{17,25},{25,17},{2,10},{10... | collective-permute-start | bytes 1081352 | tf_op jit(solution)/shard_map/ppermute | solution.py:24
  19.2 22.9 %collective-permute-start.8 = (bf16[1,704,256]{2,1,0:T(8,128)(2,1)S(1)}, bf16[1,704,256]{2,1,0:T(8,128)(2,1)S(1)}, u32[]{:S(2)}, u32[]{:S(2)}) collective-permute-start(bf16[1,704,256]{2,1,0:T(8,128)(2,1)S(1)} %get-tuple-element.40), channel_id=1, source_target_pairs={{0,16},{8,24},{16,0},{24,8},{1,17},{9,25},{17,1},{25,9},{2,18},{10... | collective-permute-start | bytes 1081352 | tf_op jit(solution)/shard_map/ppermute | solution.py:24
  20.4 21.7 %collective-permute-start.9 = (bf16[1,704,256]{2,1,0:T(8,128)(2,1)S(1)}, bf16[1,704,256]{2,1,0:T(8,128)(2,1)S(1)}, u32[]{:S(2)}, u32[]{:S(2)}) collective-permute-start(bf16[1,704,256]{2,1,0:T(8,128)(2,1)S(1)} %get-tuple-element.41), channel_id=1, source_target_pairs={{0,24},{8,16},{16,8},{24,0},{1,25},{9,17},{17,9},{25,1},{2,26},{10... | collective-permute-start | bytes 1081352 | tf_op jit(solution)/shard_map/ppermute | solution.py:24
  42.9 1.8 %collective-permute-start.12 = (bf16[4,32,1536]{2,1,0:T(8,128)(2,1)S(1)}, bf16[4,32,1536]{2,1,0:T(8,128)(2,1)S(1)}, u32[]{:S(2)}, u32[]{:S(2)}) collective-permute-start(bf16[4,32,1536]{2,1,0:T(8,128)(2,1)S(1)} %slice_bitcast_fusion), channel_id=1, source_target_pairs={{0,1},{1,0},{2,3},{3,2},{4,5},{5,4},{6,7},{7,6},{8,9},{9,8},{10,11... | collective-permute-start | bytes 1179656 | tf_op jit(solution)/shard_map/ppermute | solution.py:24
  43.0 11.7 %collective-permute-start.16 = (bf16[1,352,512]{2,1,0:T(8,128)(2,1)S(1)}, bf16[1,352,512]{2,1,0:T(8,128)(2,1)S(1)}, u32[]{:S(2)}, u32[]{:S(2)}) collective-permute-start(bf16[1,352,512]{2,1,0:T(8,128)(2,1)S(1)} %get-tuple-element.46), channel_id=1, source_target_pairs={{0,24},{8,16},{16,8},{24,0},{1,25},{9,17},{17,9},{25,1},{2,26},{10... | collective-permute-start | bytes 1081352 | tf_op jit(solution)/shard_map/ppermute | solution.py:24
  44.9 9.9 %collective-permute-start.13 = (bf16[32,1536]{1,0:T(8,128)(2,1)S(1)}, bf16[32,1536]{1,0:T(8,128)(2,1)S(1)}, u32[]{:S(2)}, u32[]{:S(2)}) collective-permute-start(bf16[32,1536]{1,0:T(8,128)(2,1)S(1)} %get-tuple-element.50), channel_id=1, source_target_pairs={{0,6},{1,7},{2,4},{3,5},{4,2},{5,3},{6,0},{7,1},{8,14},{9,15},{10,... | collective-permute-start | bytes 294920 | tf_op jit(solution)/shard_map/ppermute | solution.py:24
  48.5 15.1 %collective-permute-start.14 = (bf16[32,1536]{1,0:T(8,128)(2,1)S(1)}, bf16[32,1536]{1,0:T(8,128)(2,1)S(1)}, u32[]{:S(2)}, u32[]{:S(2)}) collective-permute-start(bf16[32,1536]{1,0:T(8,128)(2,1)S(1)} %get-tuple-element.49), channel_id=1, source_target_pairs={{0,4},{1,5},{2,6},{3,7},{4,0},{5,1},{6,2},{7,3},{8,12},{9,13},{10,... | collective-permute-start | bytes 294920 | tf_op jit(solution)/shard_map/ppermute | solution.py:24
  48.5 15.1 %collective-permute-start.15 = (bf16[32,1536]{1,0:T(8,128)(2,1)S(1)}, bf16[32,1536]{1,0:T(8,128)(2,1)S(1)}, u32[]{:S(2)}, u32[]{:S(2)}) collective-permute-start(bf16[32,1536]{1,0:T(8,128)(2,1)S(1)} %get-tuple-element.48), channel_id=1, source_target_pairs={{0,2},{1,3},{2,0},{3,1},{4,6},{5,7},{6,4},{7,5},{8,10},{9,11},{10,... | collective-permute-start | bytes 294920 | tf_op jit(solution)/shard_map/ppermute | solution.py:24
  55.1 1.4 %collective-permute-start.17 = (bf16[4,32,512]{2,1,0:T(8,128)(2,1)S(1)}, bf16[4,32,512]{2,1,0:T(8,128)(2,1)S(1)}, u32[]{:S(2)}, u32[]{:S(2)}) collective-permute-start(bf16[4,32,512]{2,1,0:T(8,128)(2,1)S(1)} %get-tuple-element.52), channel_id=1, source_target_pairs={{0,1},{1,0},{2,3},{3,2},{4,5},{5,4},{6,7},{7,6},{8,9},{9,8},{10,11... | collective-permute-start | bytes 393224 | tf_op jit(solution)/shard_map/ppermute | solution.py:24
  56.5 4.3 %collective-permute-start.18 = (bf16[2,32,512]{2,1,0:T(8,128)(2,1)S(1)}, bf16[2,32,512]{2,1,0:T(8,128)(2,1)S(1)}, u32[]{:S(2)}, u32[]{:S(2)}) collective-permute-start(bf16[2,32,512]{2,1,0:T(8,128)(2,1)S(1)} %get-tuple-element.54), channel_id=1, source_target_pairs={{0,2},{1,3},{2,0},{3,1},{4,6},{5,7},{6,4},{7,5},{8,10},{9,11},{10,... | collective-permute-start | bytes 196616 | tf_op jit(solution)/shard_map/ppermute | solution.py:24
  60.9 4.9 %collective-permute-start.19 = (bf16[32,512]{1,0:T(8,128)(2,1)S(1)}, bf16[32,512]{1,0:T(8,128)(2,1)S(1)}, u32[]{:S(2)}, u32[]{:S(2)}) collective-permute-start(bf16[32,512]{1,0:T(8,128)(2,1)S(1)} %get-tuple-element.55), channel_id=1, source_target_pairs={{0,4},{1,5},{2,6},{3,7},{4,0},{5,1},{6,2},{7,3},{8,12},{9,13},{10,... | collective-permute-start | bytes 98312 | tf_op jit(solution)/shard_map/ppermute | solution.py:24

commit v16 on v15

--- a/solution.py
+++ b/solution.py
@@ -342,8 +342,8 @@
     (stacked,) = call(
         functools.partial(stack_kernel, dp),
         [((dp - 1, own_rows // 2, depth), BF16)],
-        [VMEM] * (2 * dp - 2) + [ANY],
-        (*firsts, *seconds, merged_down[1]),
+        [VMEM] * (2 * dp - 2) + [ANY] * (dp - 2),
+        (*firsts, *seconds, *merged_down[1:-1]),
         0,
         2 * own_rows * width,
     )

time: 66.6 us -> 62.7 us (0.941)
  waiting for transfers between devices: 35.2 us -> 31.3 us
    ppermute x20, waiting for transfers between devices: 35.2 us -> 31.3 us  [swap(): return lax.ppermute(value, axis, [(i, i ^ step) for i in range(count)])]
where the time goes in v16:
time: 62.7 us; the launch traced here: 62.6 us
  waiting for transfers between devices  31.3 us (50%)
  starting transfers between devices  24.3 us (39%)
  Pallas kernels  6.47 us (10%)
    ppermute x20, waiting for transfers between devices, swap(): return lax.ppermute(value, axis, [(i, i ^ step) for i in range(count)])  31.3 us
    ppermute x20, starting transfers between devices, swap(): return lax.ppermute(value, axis, [(i, i ^ step) for i in range(count)])  24.3 us
    pallas_call x12, Pallas kernels, call(): pl.pallas_call(kernel, out_shape=[jax.ShapeDtypeStruct(shape, dtype) for...  6.47 us
  transfers between devices with their start and end apart: 20, of which 12 were waited for; matrix products, arithmetic and copies ran while one was open for 0% of the time, Pallas kernels for 5%

profile of v16, /device:TPU:0, one launch (start us, length us, event | category | flops | bytes accessed | tf_op | source)
XLA Modules:
  0.0 62.6 jit_solution(11931529821205458810)
XLA Ops:
  0.0 1.8 %shard_map.64 = (bf16[256,512]{1,0:T(8,128)(2,1)S(1)}, bf16[80,512]{1,0:T(8,128)(2,1)S(1)}, bf16[80,512]{1,0:T(8,128)(2,1)S(1)}, bf16[80,512]{1,0:T(8,128)(2,1)S...) custom-call(s32[1]{0:T(128)} %bitcast.my_dp, s32[1]{0:T(128)} %bitcast.1.core, ...), custom_call_target="tpu_custom_call" | custom-call | flops 10000000000 | bytes 2097152 | tf_op jit(solution)/shard_map/pallas_call | solution.py:32
  1.8 0.0 copy-start.1
  1.8 3.0 %collective-permute-start = (bf16[80,512]{1,0:T(8,128)(2,1)S(1)}, bf16[80,512]{1,0:T(8,128)(2,1)S(1)}, u32[]{:S(2)}, u32[]{:S(2)}) collective-permute-start(bf16[80,512]{1,0:T(8,128)(2,1)S(1)} %get-tuple-element.27.refs_0_), channel_id=1, source_target_pairs={{0,8},{8,0},{16,24},{24,16},{1,9},{9,1},{17,25},{25,17},{2,10},{10... | collective-permute-start | bytes 245768 | tf_op jit(solution)/shard_map/ppermute | solution.py:24
  4.8 1.5 %collective-permute-start.1 = (bf16[80,512]{1,0:T(8,128)(2,1)S(1)}, bf16[80,512]{1,0:T(8,128)(2,1)S(1)}, u32[]{:S(2)}, u32[]{:S(2)}) collective-permute-start(bf16[80,512]{1,0:T(8,128)(2,1)S(1)} %get-tuple-element.28), channel_id=1, source_target_pairs={{0,16},{8,24},{16,0},{24,8},{1,17},{9,25},{17,1},{25,9},{2,18},{10... | collective-permute-start | bytes 245768 | tf_op jit(solution)/shard_map/ppermute | solution.py:24
  6.4 0.0 collective-permute-start.2
  6.4 1.9 %collective-permute-start.3 = (bf16[64,512]{1,0:T(8,128)(2,1)S(1)}, bf16[64,512]{1,0:T(8,128)(2,1)S(1)}, u32[]{:S(2)}, u32[]{:S(2)}) collective-permute-start(bf16[64,512]{1,0:T(8,128)(2,1)S(1)} %get-tuple-element.30), channel_id=1, source_target_pairs={{0,8},{8,0},{16,24},{24,16},{1,9},{9,1},{17,25},{25,17},{2,10},{10... | collective-permute-start | bytes 196616 | tf_op jit(solution)/shard_map/ppermute | solution.py:24
  8.3 1.5 %collective-permute-start.4 = (bf16[64,512]{1,0:T(8,128)(2,1)S(1)}, bf16[64,512]{1,0:T(8,128)(2,1)S(1)}, u32[]{:S(2)}, u32[]{:S(2)}) collective-permute-start(bf16[64,512]{1,0:T(8,128)(2,1)S(1)} %get-tuple-element.31), channel_id=1, source_target_pairs={{0,16},{8,24},{16,0},{24,8},{1,17},{9,25},{17,1},{25,9},{2,18},{10... | collective-permute-start | bytes 196616 | tf_op jit(solution)/shard_map/ppermute | solution.py:24
  9.9 0.0 collective-permute-done.refs_1_.refs_0_
  9.9 1.0 %collective-permute-start.5 = (bf16[64,512]{1,0:T(8,128)(2,1)S(1)}, bf16[64,512]{1,0:T(8,128)(2,1)S(1)}, u32[]{:S(2)}, u32[]{:S(2)}) collective-permute-start(bf16[64,512]{1,0:T(8,128)(2,1)S(1)} %get-tuple-element.32), channel_id=1, source_target_pairs={{0,24},{8,16},{16,8},{24,0},{1,25},{9,17},{17,9},{25,1},{2,26},{10... | collective-permute-start | bytes 196616 | tf_op jit(solution)/shard_map/ppermute | solution.py:24
  10.8 0.0 collective-permute-done.1.refs_2_.refs_1_
  10.8 0.9 %collective-permute-done.2.refs_3_.refs_2_ = bf16[80,512]{1,0:T(8,128)(2,1)S(1)} collective-permute-done((bf16[80,512]{1,0:T(8,128)(2,1)S(1)}, bf16[80,512]{1,0:T(8,128)(2,1)S(1)}, u32[]{:S(2)}, u32[]{:S(2)}) %collective-permute-start.2) | collective-permute-done | bytes 81952 | tf_op jit(solution)/shard_map/ppermute | solution.py:24
  11.7 0.3 shard_map.65.mix_ref
  12.1 0.5 shard_map.66
  12.7 1.5 %collective-permute-start.10 = (bf16[1,352,512]{2,1,0:T(8,128)(2,1)S(1)}, bf16[1,352,512]{2,1,0:T(8,128)(2,1)S(1)}, u32[]{:S(2)}, u32[]{:S(2)}) collective-permute-start(bf16[1,352,512]{2,1,0:T(8,128)(2,1)S(1)} %get-tuple-element.33.refs_6_), channel_id=1, source_target_pairs={{0,8},{8,0},{16,24},{24,16},{1,9},{9,1},{17,25},{25,17},{2,10},{10... | collective-permute-start | bytes 1081352 | tf_op jit(solution)/shard_map/ppermute | solution.py:24
  14.1 0.2 collective-permute-start.11
  14.3 0.0 collective-permute-done.3.refs_3_
  14.3 0.0 collective-permute-done.4.refs_4_
  14.3 1.4 %collective-permute-done.5.refs_5_ = bf16[64,512]{1,0:T(8,128)(2,1)S(1)} collective-permute-done((bf16[64,512]{1,0:T(8,128)(2,1)S(1)}, bf16[64,512]{1,0:T(8,128)(2,1)S(1)}, u32[]{:S(2)}, u32[]{:S(2)}) %collective-permute-start.5) | collective-permute-done | bytes 65568 | tf_op jit(solution)/shard_map/ppermute | solution.py:24
  15.7 0.1 collective-permute-start.6
  15.8 0.9 %shard_map.68 = (bf16[1,704,512]{2,1,0:T(8,128)(2,1)S(1)}, bf16[1,704,512]{2,1,0:T(8,128)(2,1)S(1)}, bf16[1,704,512]{2,1,0:T(8,128)(2,1)S(1)}, bf16[1,704,512]{2,1,0:T(8,128)(2,1)S(1)}) custom-call(bf16[128,256]{1,0:T(8,128)(2,1)S(1)} %shard_map.65.mix_ref, bf16[8,352,512]{2,1,0:T(8,128)(2,1)S(1)} %bitcast.36, bf16[8,352,512]{2,1,0:T(8,128)(2,1)S(1)} %bitcast.37), custom_call_target="tpu_custom_call" | custom-call | flops 10000000000 | bytes 8650752 | tf_op jit(solution)/shard_map/pallas_call | solution.py:32
  16.8 0.8 %collective-permute-done.6.other = bf16[3,128,512]{2,1,0:T(8,128)(2,1)S(1)} collective-permute-done((bf16[3,128,512]{2,1,0:T(8,128)(2,1)S(1)}, bf16[3,128,512]{2,1,0:T(8,128)(2,1)S(1)}, u32[]{:S(2)}, u32[]{:S(2)}) %collective-permute-start.6) | collective-permute-done | bytes 393248 | tf_op jit(solution)/shard_map/ppermute | solution.py:24
  17.5 1.0 %shard_map.69 = (bf16[1,704,256]{2,1,0:T(8,128)(2,1)S(1)}, bf16[1,704,256]{2,1,0:T(8,128)(2,1)S(1)}, bf16[1,704,256]{2,1,0:T(8,128)(2,1)S(1)}, bf16[1,704,256]{2,1,0:T(8,128)(2,1)S(1)}) custom-call(s32[1]{0:T(128)} %bitcast.1.core, bf16[256,512]{1,0:T(8,128)(2,1)S(1)} %get-tuple-element.26.own, bf16[3,128,512]{2,1,0:T(8,128)(2,1)S(1)} %shard_map.67.brought, ...), custom_call_target="tpu_custom_call" | custom-call | flops 738197504 | bytes 5373952 | tf_op jit(solution)/shard_map/pallas_call | solution.py:32
  18.5 0.6 collective-permute-start.7
  19.1 0.8 %collective-permute-start.8 = (bf16[1,704,256]{2,1,0:T(8,128)(2,1)S(1)}, bf16[1,704,256]{2,1,0:T(8,128)(2,1)S(1)}, u32[]{:S(2)}, u32[]{:S(2)}) collective-permute-start(bf16[1,704,256]{2,1,0:T(8,128)(2,1)S(1)} %get-tuple-element.41), channel_id=1, source_target_pairs={{0,16},{8,24},{16,0},{24,8},{1,17},{9,25},{17,1},{25,9},{2,18},{10... | collective-permute-start | bytes 1081352 | tf_op jit(solution)/shard_map/ppermute | solution.py:24
  19.9 2.2 %collective-permute-start.9 = (bf16[1,704,256]{2,1,0:T(8,128)(2,1)S(1)}, bf16[1,704,256]{2,1,0:T(8,128)(2,1)S(1)}, u32[]{:S(2)}, u32[]{:S(2)}) collective-permute-start(bf16[1,704,256]{2,1,0:T(8,128)(2,1)S(1)} %get-tuple-element.42), channel_id=1, source_target_pairs={{0,24},{8,16},{16,8},{24,0},{1,25},{9,17},{17,9},{25,1},{2,26},{10... | collective-permute-start | bytes 1081352 | tf_op jit(solution)/shard_map/ppermute | solution.py:24
  22.1 0.2 collective-permute-done.10.refs_5_
  22.2 1.7 %collective-permute-done.11.refs_6_ = bf16[1,352,512]{2,1,0:T(8,128)(2,1)S(1)} collective-permute-done((bf16[1,352,512]{2,1,0:T(8,128)(2,1)S(1)}, bf16[1,352,512]{2,1,0:T(8,128)(2,1)S(1)}, u32[]{:S(2)}, u32[]{:S(2)}) %collective-permute-start.11) | collective-permute-done | bytes 360480 | tf_op jit(solution)/shard_map/ppermute | solution.py:24
  23.9 6.1 %collective-permute-done.7.refs_1_ = bf16[1,704,256]{2,1,0:T(8,128)(2,1)S(1)} collective-permute-done((bf16[1,704,256]{2,1,0:T(8,128)(2,1)S(1)}, bf16[1,704,256]{2,1,0:T(8,128)(2,1)S(1)}, u32[]{:S(2)}, u32[]{:S(2)}) %collective-permute-start.7) | collective-permute-done | bytes 360480 | tf_op jit(solution)/shard_map/ppermute | solution.py:24
  29.9 8.3 %collective-permute-done.8.refs_2_ = bf16[1,704,256]{2,1,0:T(8,128)(2,1)S(1)} collective-permute-done((bf16[1,704,256]{2,1,0:T(8,128)(2,1)S(1)}, bf16[1,704,256]{2,1,0:T(8,128)(2,1)S(1)}, u32[]{:S(2)}, u32[]{:S(2)}) %collective-permute-start.8) | collective-permute-done | bytes 360480 | tf_op jit(solution)/shard_map/ppermute | solution.py:24
  38.2 0.0 collective-permute-done.9.refs_3_
  38.2 0.8 %shard_map.70 = (bf16[1,352,256]{2,1,0:T(8,128)(2,1)S(1)}, bf16[2,4,32,1536]{3,2,1,0:T(8,128)(2,1)S(1)}) custom-call(s32[1]{0:T(128)} %bitcast.1.core, bf16[1,704,256]{2,1,0:T(8,128)(2,1)S(1)} %get-tuple-element.39.refs_0_, bf16[1,704,256]{2,1,0:T(8,128)(2,1)S(1)} %collective-permute-done.7.refs_1_, bf16[1,704,256]{2,1,0:T(8,128)(2,1)S(1)} %collective-permute-done.8.refs_2_, ...), custom_call_target="tpu_custom_call" | custom-call | flops 276824064 | bytes 2523136 | tf_op jit(solution)/shard_map/pallas_call | solution.py:32
  39.0 0.1 collective-permute-start.12
  39.1 1.0 %collective-permute-start.16 = (bf16[1,352,512]{2,1,0:T(8,128)(2,1)S(1)}, bf16[1,352,512]{2,1,0:T(8,128)(2,1)S(1)}, u32[]{:S(2)}, u32[]{:S(2)}) collective-permute-start(bf16[1,352,512]{2,1,0:T(8,128)(2,1)S(1)} %get-tuple-element.46), channel_id=1, source_target_pairs={{0,24},{8,16},{16,8},{24,0},{1,25},{9,17},{17,9},{25,1},{2,26},{10... | collective-permute-start | bytes 1081352 | tf_op jit(solution)/shard_map/ppermute | solution.py:24
  40.2 0.6 %collective-permute-done.12 = bf16[4,32,1536]{2,1,0:T(8,128)(2,1)S(1)} collective-permute-done((bf16[4,32,1536]{2,1,0:T(8,128)(2,1)S(1)}, bf16[4,32,1536]{2,1,0:T(8,128)(2,1)S(1)}, u32[]{:S(2)}, u32[]{:S(2)}) %collective-permute-start.12) | collective-permute-done | bytes 393248 | tf_op jit(solution)/shard_map/ppermute | solution.py:24
  40.8 0.1 fusion
  41.0 3.7 %collective-permute-start.13 = (bf16[32,1536]{1,0:T(8,128)(2,1)S(1)}, bf16[32,1536]{1,0:T(8,128)(2,1)S(1)}, u32[]{:S(2)}, u32[]{:S(2)}) collective-permute-start(bf16[32,1536]{1,0:T(8,128)(2,1)S(1)} %get-tuple-element.50), channel_id=1, source_target_pairs={{0,6},{1,7},{2,4},{3,5},{4,2},{5,3},{6,0},{7,1},{8,14},{9,15},{10,... | collective-permute-start | bytes 294920 | tf_op jit(solution)/shard_map/ppermute | solution.py:24
  44.6 0.8 %collective-permute-start.15 = (bf16[32,1536]{1,0:T(8,128)(2,1)S(1)}, bf16[32,1536]{1,0:T(8,128)(2,1)S(1)}, u32[]{:S(2)}, u32[]{:S(2)}) collective-permute-start(bf16[32,1536]{1,0:T(8,128)(2,1)S(1)} %get-tuple-element.48), channel_id=1, source_target_pairs={{0,2},{1,3},{2,0},{3,1},{4,6},{5,7},{6,4},{7,5},{8,10},{9,11},{10,... | collective-permute-start | bytes 294920 | tf_op jit(solution)/shard_map/ppermute | solution.py:24
  45.4 5.4 %collective-permute-done.16.refs_0_ = bf16[1,352,512]{2,1,0:T(8,128)(2,1)S(1)} collective-permute-done((bf16[1,352,512]{2,1,0:T(8,128)(2,1)S(1)}, bf16[1,352,512]{2,1,0:T(8,128)(2,1)S(1)}, u32[]{:S(2)}, u32[]{:S(2)}) %collective-permute-start.16) | collective-permute-done | bytes 360480 | tf_op jit(solution)/shard_map/ppermute | solution.py:24
  50.8 0.3 shard_map.72
  51.2 0.1 collective-permute-start.17
  51.3 1.3 %collective-permute-done.17 = bf16[4,32,512]{2,1,0:T(8,128)(2,1)S(1)} collective-permute-done((bf16[4,32,512]{2,1,0:T(8,128)(2,1)S(1)}, bf16[4,32,512]{2,1,0:T(8,128)(2,1)S(1)}, u32[]{:S(2)}, u32[]{:S(2)}) %collective-permute-start.17) | collective-permute-done | bytes 131104 | tf_op jit(solution)/shard_map/ppermute | solution.py:24
  52.7 1.7 %collective-permute-start.18 = (bf16[2,32,512]{2,1,0:T(8,128)(2,1)S(1)}, bf16[2,32,512]{2,1,0:T(8,128)(2,1)S(1)}, u32[]{:S(2)}, u32[]{:S(2)}) collective-permute-start(bf16[2,32,512]{2,1,0:T(8,128)(2,1)S(1)} %get-tuple-element.54), channel_id=1, source_target_pairs={{0,2},{1,3},{2,0},{3,1},{4,6},{5,7},{6,4},{7,5},{8,10},{9,11},{10,... | collective-permute-start | bytes 196616 | tf_op jit(solution)/shard_map/ppermute | solution.py:24
  54.4 2.6 %collective-permute-done.18 = bf16[2,32,512]{2,1,0:T(8,128)(2,1)S(1)} collective-permute-done((bf16[2,32,512]{2,1,0:T(8,128)(2,1)S(1)}, bf16[2,32,512]{2,1,0:T(8,128)(2,1)S(1)}, u32[]{:S(2)}, u32[]{:S(2)}) %collective-permute-start.18) | collective-permute-done | bytes 65568 | tf_op jit(solution)/shard_map/ppermute | solution.py:24
  57.0 2.7 %collective-permute-start.19 = (bf16[32,512]{1,0:T(8,128)(2,1)S(1)}, bf16[32,512]{1,0:T(8,128)(2,1)S(1)}, u32[]{:S(2)}, u32[]{:S(2)}) collective-permute-start(bf16[32,512]{1,0:T(8,128)(2,1)S(1)} %get-tuple-element.55), channel_id=1, source_target_pairs={{0,4},{1,5},{2,6},{3,7},{4,0},{5,1},{6,2},{7,3},{8,12},{9,13},{10,... | collective-permute-start | bytes 98312 | tf_op jit(solution)/shard_map/ppermute | solution.py:24
  59.7 0.0 collective-permute-done.15.refs_2_
  59.7 0.1 shard_map.71.early
  59.8 2.1 %collective-permute-done.19.refs_1_ = bf16[32,512]{1,0:T(8,128)(2,1)S(1)} collective-permute-done((bf16[32,512]{1,0:T(8,128)(2,1)S(1)}, bf16[32,512]{1,0:T(8,128)(2,1)S(1)}, u32[]{:S(2)}, u32[]{:S(2)}) %collective-permute-start.19) | collective-permute-done | bytes 32800 | tf_op jit(solution)/shard_map/ppermute | solution.py:24
  61.9 0.7 %shard_map.75 = bf16[32,2048]{1,0:T(8,128)(2,1)} custom-call(s32[1]{0:T(128)} %bitcast.my_dp, bf16[32,1536]{1,0:T(8,128)(2,1)S(1)} %shard_map.71.early, bf16[32,512]{1,0:T(8,128)(2,1)S(1)} %get-tuple-element.56.refs_0_, bf16[32,512]{1,0:T(8,128)(2,1)S(1)} %collective-permute-done.19.refs_1_), custom_call_target="tpu_custom_call" | custom-call | flops 262144 | bytes 655360 | tf_op jit(solution)/shard_map/pallas_call | solution.py:32
  (18 shorter events, 0.2 us)
Async XLA Ops:
  0.0 12.1 %copy-start = (bf16[8,352,512]{2,1,0:T(8,128)(2,1)S(1)}, bf16[8,352,512]{2,1,0:T(8,128)(2,1)}, u32[]{:S(2)}) copy-start(bf16[8,352,512]{2,1,0:T(8,128)(2,1)} %refs_0_.1) | copy-start | bytes 8650756
  0.0 15.8 %copy-start.2 = (bf16[8,512,352]{1,2,0:T(8,128)(2,1)S(1)}, bf16[8,512,352]{1,2,0:T(8,128)(2,1)}, u32[]{:S(2)}) copy-start(bf16[8,512,352]{1,2,0:T(8,128)(2,1)} %param.8) | copy-start | bytes 8650756
  1.8 14.0 %copy-start.1 = (bf16[8,512,352]{1,2,0:T(8,128)(2,1)S(1)}, bf16[8,512,352]{1,2,0:T(8,128)(2,1)}, u32[]{:S(2)}) copy-start(bf16[8,512,352]{1,2,0:T(8,128)(2,1)} %param.7) | copy-start | bytes 8650756
  1.8 8.0 %collective-permute-start = (bf16[80,512]{1,0:T(8,128)(2,1)S(1)}, bf16[80,512]{1,0:T(8,128)(2,1)S(1)}, u32[]{:S(2)}, u32[]{:S(2)}) collective-permute-start(bf16[80,512]{1,0:T(8,128)(2,1)S(1)} %get-tuple-element.27.refs_0_), channel_id=1, source_target_pairs={{0,8},{8,0},{16,24},{24,16},{1,9},{9,1},{17,25},{25,17},{2,10},{10... | collective-permute-start | bytes 245768 | tf_op jit(solution)/shard_map/ppermute | solution.py:24
  4.8 6.0 %collective-permute-start.1 = (bf16[80,512]{1,0:T(8,128)(2,1)S(1)}, bf16[80,512]{1,0:T(8,128)(2,1)S(1)}, u32[]{:S(2)}, u32[]{:S(2)}) collective-permute-start(bf16[80,512]{1,0:T(8,128)(2,1)S(1)} %get-tuple-element.28), channel_id=1, source_target_pairs={{0,16},{8,24},{16,0},{24,8},{1,17},{9,25},{17,1},{25,9},{2,18},{10... | collective-permute-start | bytes 245768 | tf_op jit(solution)/shard_map/ppermute | solution.py:24
  6.4 5.4 %collective-permute-start.2 = (bf16[80,512]{1,0:T(8,128)(2,1)S(1)}, bf16[80,512]{1,0:T(8,128)(2,1)S(1)}, u32[]{:S(2)}, u32[]{:S(2)}) collective-permute-start(bf16[80,512]{1,0:T(8,128)(2,1)S(1)} %get-tuple-element.29), channel_id=1, source_target_pairs={{0,24},{8,16},{16,8},{24,0},{1,25},{9,17},{17,9},{25,1},{2,26},{10... | collective-permute-start | bytes 245768 | tf_op jit(solution)/shard_map/ppermute | solution.py:24
  6.4 8.0 %collective-permute-start.3 = (bf16[64,512]{1,0:T(8,128)(2,1)S(1)}, bf16[64,512]{1,0:T(8,128)(2,1)S(1)}, u32[]{:S(2)}, u32[]{:S(2)}) collective-permute-start(bf16[64,512]{1,0:T(8,128)(2,1)S(1)} %get-tuple-element.30), channel_id=1, source_target_pairs={{0,8},{8,0},{16,24},{24,16},{1,9},{9,1},{17,25},{25,17},{2,10},{10... | collective-permute-start | bytes 196616 | tf_op jit(solution)/shard_map/ppermute | solution.py:24
  8.3 6.0 %collective-permute-start.4 = (bf16[64,512]{1,0:T(8,128)(2,1)S(1)}, bf16[64,512]{1,0:T(8,128)(2,1)S(1)}, u32[]{:S(2)}, u32[]{:S(2)}) collective-permute-start(bf16[64,512]{1,0:T(8,128)(2,1)S(1)} %get-tuple-element.31), channel_id=1, source_target_pairs={{0,16},{8,24},{16,0},{24,8},{1,17},{9,25},{17,1},{25,9},{2,18},{10... | collective-permute-start | bytes 196616 | tf_op jit(solution)/shard_map/ppermute | solution.py:24
  9.9 5.8 %collective-permute-start.5 = (bf16[64,512]{1,0:T(8,128)(2,1)S(1)}, bf16[64,512]{1,0:T(8,128)(2,1)S(1)}, u32[]{:S(2)}, u32[]{:S(2)}) collective-permute-start(bf16[64,512]{1,0:T(8,128)(2,1)S(1)} %get-tuple-element.32), channel_id=1, source_target_pairs={{0,24},{8,16},{16,8},{24,0},{1,25},{9,17},{17,9},{25,1},{2,26},{10... | collective-permute-start | bytes 196616 | tf_op jit(solution)/shard_map/ppermute | solution.py:24
  12.7 9.6 %collective-permute-start.10 = (bf16[1,352,512]{2,1,0:T(8,128)(2,1)S(1)}, bf16[1,352,512]{2,1,0:T(8,128)(2,1)S(1)}, u32[]{:S(2)}, u32[]{:S(2)}) collective-permute-start(bf16[1,352,512]{2,1,0:T(8,128)(2,1)S(1)} %get-tuple-element.33.refs_6_), channel_id=1, source_target_pairs={{0,8},{8,0},{16,24},{24,16},{1,9},{9,1},{17,25},{25,17},{2,10},{10... | collective-permute-start | bytes 1081352 | tf_op jit(solution)/shard_map/ppermute | solution.py:24
  14.1 9.8 %collective-permute-start.11 = (bf16[1,352,512]{2,1,0:T(8,128)(2,1)S(1)}, bf16[1,352,512]{2,1,0:T(8,128)(2,1)S(1)}, u32[]{:S(2)}, u32[]{:S(2)}) collective-permute-start(bf16[1,352,512]{2,1,0:T(8,128)(2,1)S(1)} %get-tuple-element.34.refs_7_), channel_id=1, source_target_pairs={{0,16},{8,24},{16,0},{24,8},{1,17},{9,25},{17,1},{25,9},{2,18},{10... | collective-permute-start | bytes 1081352 | tf_op jit(solution)/shard_map/ppermute | solution.py:24
  15.7 1.8 %collective-permute-start.6 = (bf16[3,128,512]{2,1,0:T(8,128)(2,1)S(1)}, bf16[3,128,512]{2,1,0:T(8,128)(2,1)S(1)}, u32[]{:S(2)}, u32[]{:S(2)}) collective-permute-start(bf16[3,128,512]{2,1,0:T(8,128)(2,1)S(1)} %shard_map.67.brought), channel_id=1, source_target_pairs={{0,1},{1,0},{2,3},{3,2},{4,5},{5,4},{6,7},{7,6},{8,9},{9,8},{10,11... | collective-permute-start | bytes 1179656 | tf_op jit(solution)/shard_map/ppermute | solution.py:24
  18.5 11.4 %collective-permute-start.7 = (bf16[1,704,256]{2,1,0:T(8,128)(2,1)S(1)}, bf16[1,704,256]{2,1,0:T(8,128)(2,1)S(1)}, u32[]{:S(2)}, u32[]{:S(2)}) collective-permute-start(bf16[1,704,256]{2,1,0:T(8,128)(2,1)S(1)} %get-tuple-element.40), channel_id=1, source_target_pairs={{0,8},{8,0},{16,24},{24,16},{1,9},{9,1},{17,25},{25,17},{2,10},{10... | collective-permute-start | bytes 1081352 | tf_op jit(solution)/shard_map/ppermute | solution.py:24
  19.1 19.1 %collective-permute-start.8 = (bf16[1,704,256]{2,1,0:T(8,128)(2,1)S(1)}, bf16[1,704,256]{2,1,0:T(8,128)(2,1)S(1)}, u32[]{:S(2)}, u32[]{:S(2)}) collective-permute-start(bf16[1,704,256]{2,1,0:T(8,128)(2,1)S(1)} %get-tuple-element.41), channel_id=1, source_target_pairs={{0,16},{8,24},{16,0},{24,8},{1,17},{9,25},{17,1},{25,9},{2,18},{10... | collective-permute-start | bytes 1081352 | tf_op jit(solution)/shard_map/ppermute | solution.py:24
  19.9 18.3 %collective-permute-start.9 = (bf16[1,704,256]{2,1,0:T(8,128)(2,1)S(1)}, bf16[1,704,256]{2,1,0:T(8,128)(2,1)S(1)}, u32[]{:S(2)}, u32[]{:S(2)}) collective-permute-start(bf16[1,704,256]{2,1,0:T(8,128)(2,1)S(1)} %get-tuple-element.42), channel_id=1, source_target_pairs={{0,24},{8,16},{16,8},{24,0},{1,25},{9,17},{17,9},{25,1},{2,26},{10... | collective-permute-start | bytes 1081352 | tf_op jit(solution)/shard_map/ppermute | solution.py:24
  39.0 1.8 %collective-permute-start.12 = (bf16[4,32,1536]{2,1,0:T(8,128)(2,1)S(1)}, bf16[4,32,1536]{2,1,0:T(8,128)(2,1)S(1)}, u32[]{:S(2)}, u32[]{:S(2)}) collective-permute-start(bf16[4,32,1536]{2,1,0:T(8,128)(2,1)S(1)} %slice_bitcast_fusion), channel_id=1, source_target_pairs={{0,1},{1,0},{2,3},{3,2},{4,5},{5,4},{6,7},{7,6},{8,9},{9,8},{10,11... | collective-permute-start | bytes 1179656 | tf_op jit(solution)/shard_map/ppermute | solution.py:24
  39.1 11.7 %collective-permute-start.16 = (bf16[1,352,512]{2,1,0:T(8,128)(2,1)S(1)}, bf16[1,352,512]{2,1,0:T(8,128)(2,1)S(1)}, u32[]{:S(2)}, u32[]{:S(2)}) collective-permute-start(bf16[1,352,512]{2,1,0:T(8,128)(2,1)S(1)} %get-tuple-element.46), channel_id=1, source_target_pairs={{0,24},{8,16},{16,8},{24,0},{1,25},{9,17},{17,9},{25,1},{2,26},{10... | collective-permute-start | bytes 1081352 | tf_op jit(solution)/shard_map/ppermute | solution.py:24
  41.0 9.9 %collective-permute-start.13 = (bf16[32,1536]{1,0:T(8,128)(2,1)S(1)}, bf16[32,1536]{1,0:T(8,128)(2,1)S(1)}, u32[]{:S(2)}, u32[]{:S(2)}) collective-permute-start(bf16[32,1536]{1,0:T(8,128)(2,1)S(1)} %get-tuple-element.50), channel_id=1, source_target_pairs={{0,6},{1,7},{2,4},{3,5},{4,2},{5,3},{6,0},{7,1},{8,14},{9,15},{10,... | collective-permute-start | bytes 294920 | tf_op jit(solution)/shard_map/ppermute | solution.py:24
  44.6 15.1 %collective-permute-start.14 = (bf16[32,1536]{1,0:T(8,128)(2,1)S(1)}, bf16[32,1536]{1,0:T(8,128)(2,1)S(1)}, u32[]{:S(2)}, u32[]{:S(2)}) collective-permute-start(bf16[32,1536]{1,0:T(8,128)(2,1)S(1)} %get-tuple-element.49), channel_id=1, source_target_pairs={{0,4},{1,5},{2,6},{3,7},{4,0},{5,1},{6,2},{7,3},{8,12},{9,13},{10,... | collective-permute-start | bytes 294920 | tf_op jit(solution)/shard_map/ppermute | solution.py:24
  44.6 15.1 %collective-permute-start.15 = (bf16[32,1536]{1,0:T(8,128)(2,1)S(1)}, bf16[32,1536]{1,0:T(8,128)(2,1)S(1)}, u32[]{:S(2)}, u32[]{:S(2)}) collective-permute-start(bf16[32,1536]{1,0:T(8,128)(2,1)S(1)} %get-tuple-element.48), channel_id=1, source_target_pairs={{0,2},{1,3},{2,0},{3,1},{4,6},{5,7},{6,4},{7,5},{8,10},{9,11},{10,... | collective-permute-start | bytes 294920 | tf_op jit(solution)/shard_map/ppermute | solution.py:24
  51.2 1.4 %collective-permute-start.17 = (bf16[4,32,512]{2,1,0:T(8,128)(2,1)S(1)}, bf16[4,32,512]{2,1,0:T(8,128)(2,1)S(1)}, u32[]{:S(2)}, u32[]{:S(2)}) collective-permute-start(bf16[4,32,512]{2,1,0:T(8,128)(2,1)S(1)} %get-tuple-element.52), channel_id=1, source_target_pairs={{0,1},{1,0},{2,3},{3,2},{4,5},{5,4},{6,7},{7,6},{8,9},{9,8},{10,11... | collective-permute-start | bytes 393224 | tf_op jit(solution)/shard_map/ppermute | solution.py:24
  52.7 4.3 %collective-permute-start.18 = (bf16[2,32,512]{2,1,0:T(8,128)(2,1)S(1)}, bf16[2,32,512]{2,1,0:T(8,128)(2,1)S(1)}, u32[]{:S(2)}, u32[]{:S(2)}) collective-permute-start(bf16[2,32,512]{2,1,0:T(8,128)(2,1)S(1)} %get-tuple-element.54), channel_id=1, source_target_pairs={{0,2},{1,3},{2,0},{3,1},{4,6},{5,7},{6,4},{7,5},{8,10},{9,11},{10,... | collective-permute-start | bytes 196616 | tf_op jit(solution)/shard_map/ppermute | solution.py:24
  57.0 4.9 %collective-permute-start.19 = (bf16[32,512]{1,0:T(8,128)(2,1)S(1)}, bf16[32,512]{1,0:T(8,128)(2,1)S(1)}, u32[]{:S(2)}, u32[]{:S(2)}) collective-permute-start(bf16[32,512]{1,0:T(8,128)(2,1)S(1)} %get-tuple-element.55), channel_id=1, source_target_pairs={{0,4},{1,5},{2,6},{3,7},{4,0},{5,1},{6,2},{7,3},{8,12},{9,13},{10,... | collective-permute-start | bytes 98312 | tf_op jit(solution)/shard_map/ppermute | solution.py:24
